TPU v7x, 32 devices: a whole 2x2x4 slice. The times are simulated.
32 devices in a mesh: dp: 4 (over y, core), tensor: 8 (over z, x).
Axes of the slice: x: 2, y: 2, z: 4, core: 2. Of those that a mesh axis runs over, the one named last changes fastest.
Arguments:
- hidden_in: bfloat16 [4, 8, 128, 2, 4096], P('dp', None, None, None, 'tensor'), may hold values from -6 to 6
- conv_weight: bfloat16 [3, 3, 2, 4096], P(None, None, None, 'tensor'), may hold values from -2 to 2
- proj_weight: bfloat16 [4096, 2048], P('tensor'), may hold values from -0.125 to 0.125
- out_grad: bfloat16 [4, 8, 128, 2048], P('dp', 'tensor'), may hold values from -6 to 6
- sample_gate: float32 [4, 2048], P('dp'), may hold values from -4 to 4
Outputs:
- hidden_grad: bfloat16 [4, 8, 128, 2, 4096], P('dp', None, None, None, 'tensor')
- proj_grad: bfloat16 [4096, 2048], P('tensor')
- conv_grad: float32 [3, 3, 2, 4096], P(None, None, None, 'tensor')
All inputs are finite; a program needn't handle non-finite values.
Results may differ from a plain program's by a relative error of at most 0.0057.
Values may be sent and summed in bfloat16 or wider, within the bound.
No kernel may reach another device: no remote copies, remote signals or barrier semaphores. Data moves between devices by JAX's collectives and lax.ppermute only.
A program may use at most 128 MiB of HBM per device.

v0:
```python
import math

import jax
import jax.numpy as jnp
from jax import lax
from jax.sharding import PartitionSpec as P


def depthwise(volume, kernel, mirror):
    height = volume.shape[1]
    across = volume.shape[2]
    padded = jnp.pad(volume, ((0, 0), (1, 1), (1, 1), (0, 0), (0, 0)))
    summed = jnp.zeros(volume.shape, jnp.float32)
    for i in range(3):
        for j in range(3):
            a = 2 - i if mirror else i
            b = 2 - j if mirror else j
            summed = (
                summed
                + kernel[i, j].astype(jnp.float32) * padded[:, a : a + height, b : b + across]
            )
    return summed


def kernel_terms(grad_pre, volume):
    height = volume.shape[1]
    across = volume.shape[2]
    padded = jnp.pad(volume, ((0, 0), (1, 1), (1, 1), (0, 0), (0, 0)))
    rows_out = []
    for i in range(3):
        row_terms = []
        for j in range(3):
            row_terms.append(
                jnp.sum(grad_pre * padded[:, i : i + height, j : j + across], axis=(0, 1, 2))
            )
        rows_out.append(jnp.stack(row_terms))
    return jnp.stack(rows_out)


def on_device(hidden_in, conv_weight, proj_weight, out_grad, sample_gate):
    samples = hidden_in.shape[0]
    height = hidden_in.shape[1]
    across = hidden_in.shape[2]
    grad_scale = 1.0 / math.sqrt(lax.axis_size("dp") * samples * height * across)
    gated_grad = (out_grad.astype(jnp.float32) * sample_gate[:, None, None, :]).astype(jnp.bfloat16)
    conv_out = depthwise(hidden_in, conv_weight, False)
    value_part = conv_out[..., 0, :]
    gate_part = conv_out[..., 1, :]
    gate_sig = jax.nn.sigmoid(gate_part)
    mixed_act = (value_part * gate_part * gate_sig).astype(jnp.bfloat16)
    gathered = lax.all_gather(gated_grad, "tensor", axis=1, tiled=True)
    grad_mixed = jnp.einsum(
        "srwd,cd->srwc", gathered, proj_weight, preferred_element_type=jnp.float32
    )
    proj_sum = jnp.einsum("srwc,srwd->cd", mixed_act, gathered, preferred_element_type=jnp.float32)
    grad_pre = jnp.stack(
        [
            grad_mixed * gate_part * gate_sig,
            grad_mixed * value_part * gate_sig * (1.0 + gate_part * (1.0 - gate_sig)),
        ],
        axis=-2,
    )
    hidden_grad = depthwise(grad_pre, conv_weight, True).astype(jnp.bfloat16)
    kernel_sum = kernel_terms(grad_pre, hidden_in)
    proj_total, kernel_total = lax.psum((proj_sum, kernel_sum), "dp")
    proj_grad = (proj_total * grad_scale).astype(jnp.bfloat16)
    conv_grad = kernel_total * grad_scale
    return (hidden_grad, proj_grad, conv_grad)


def solution(mesh):
    in_specs = (
        P("dp", None, None, None, "tensor"),
        P(None, None, None, "tensor"),
        P("tensor", None),
        P("dp", "tensor", None, None),
        P("dp", None),
    )
    out_specs = (
        P("dp", None, None, None, "tensor"),
        P("tensor", None),
        P(None, None, None, "tensor"),
    )
    return jax.shard_map(
        on_device, mesh=mesh, in_specs=in_specs, out_specs=out_specs, check_vma=False
    )
```

profile of v0, /device:TPU:0, one launch (start us, length us, event | category | flops | bytes accessed | tf_op | source)
XLA Modules:
  0.0 190.3 jit_solution(7498614369889694965)
XLA Ops:
  7.2 0.0 copy-start
  7.2 0.0 copy-start.4
  7.2 0.0 all-gather.2.cloned.1.call-start
  7.2 2.1 %multiply_convert_fusion.3 = bf16[1,1,128,2048]{3,2,0,1:T(8,128)(2,1)} fusion(bf16[1,1,128,2048]{3,2,1,0:T(8,128)(2,1)} %param.8, f32[2048]{0:T(1024)} %bitcast.107), kind=kLoop, calls=%fused_computation.91 | loop fusion | flops 786432 | bytes 1056768 | tf_op jit(solution)/shard_map/convert_element_type | solution.py:45
  9.3 0.0 all-gather.2.cloned.1.call-update
  9.3 0.0 all-reduce.4.cloned.1.call-start
  9.4 2.0 %copy.13 = bf16[1,8,128,2,512]{4,2,1,3,0:T(8,128)(2,1)S(1)} copy(bf16[1,8,128,2,512]{4,3,2,1,0:T(2,128)(2,1)} %param.5) | data formatting | bytes 4194304 | tf_op args[0]
  11.4 0.0 copy-done.4
  11.4 0.0 copy-start.1
  11.4 1.3 copy-done.1
  12.7 9.6 %fusion.7 = f32[1,8,128,2,512]{4,2,1,3,0:T(8,128)} fusion(bf16[1,8,128,2,512]{4,2,1,3,0:T(8,128)(2,1)S(1)} %copy.13, f32[2,512]{1,0:T(2,128)S(1)} %get-tuple-element.31, f32[2,512]{1,0:T(2,128)S(1)} %get-tuple-element.32, f32[2,512]{1,0:T(2,128)S(1)} %get-tuple-element.25, f32[2,512]{1,0:T(2,128)S(1)} %get-tuple-element.26, ...), kind=kLoop, calls=%fused_computation.33 | loop fusion | flops 27262976 | bytes 6328320 | tf_op jit(solution)/shard_map/add | solution.py:19
  22.4 64.5 %all-gather.2.cloned.1.call-done = bf16[1,8,128,2048]{3,2,0,1:T(8,128)(2,1)} async-done(((bf16[1,1,128,2048]{3,2,0,1:T(8,128)(2,1)}), bf16[1,8,128,2048]{3,2,0,1:T(8,128)(2,1)}) %all-gather.2.cloned.1.call-update) | async-done | bytes 4194320 | tf_op jit(solution)/shard_map/all_gather | solution.py:51
  86.9 7.9 %fusion.38 = f32[512,2048]{1,0:T(8,128)} fusion(bf16[1,8,128,2048]{3,2,0,1:T(8,128)(2,1)} %all-gather.2.cloned.1.call-done, f32[1,8,128,2,512]{4,2,1,3,0:T(8,128)} %fusion.7), kind=kOutput, calls=%fused_computation.66 | convolution fusion | flops 2150629376 | bytes 12582912 | tf_op jit(solution)/shard_map/srwc,srwd->cd/dot_general | solution.py:55
  94.7 0.0 all-reduce.4.cloned.1.call-update
  94.8 0.0 copy-done
  94.8 0.0 copy-start.2
  94.8 0.0 copy-start.3
  94.8 6.5 %fusion.45 = (f32[1,8,128,1,512]{4,2,1,3,0:T(8,128)S(1)}, f32[1,8,128,1,512]{4,2,1,3,0:T(8,128)S(1)}) fusion(f32[1,8,128,2,512]{4,2,1,3,0:T(8,128)} %fusion.7, bf16[512,2048]{1,0:T(8,128)(2,1)S(1)} %copy-done, bf16[1,8,128,2048]{3,2,0,1:T(8,128)(2,1)} %all-gather.2.cloned.1.call-done), kind=kOutput, calls=%fused_computation.83 | convolution fusion | flops 2153250816 | bytes 14680064 | tf_op jit(solution)/shard_map/srwd,cd->srwc/dot_general | solution.py:52
  101.3 0.0 copy-done.2
  101.3 0.0 copy-done.3
  101.3 6.9 %fusion.8 = (f32[2,512]{1,0:T(2,128)S(1)}, f32[2,512]{1,0:T(2,128)S(1)}, f32[2,512]{1,0:T(2,128)S(1)}, f32[2,512]{1,0:T(2,128)S(1)}, f32[2,512]{1,0:T(2,128)S(1)...) fusion(bf16[1,8,128,2,512]{4,2,1,3,0:T(8,128)(2,1)S(1)} %copy-d, ...), kind=kLoop, calls=%fused_computation.34 | loop fusion | flops 29350912 | bytes 12619776 | tf_op jit(solution)/shard_map/reduce_sum | solution.py:34
  108.2 7.8 %fusion.26 = bf16[1,8,128,2,512]{4,2,1,3,0:T(8,128)(2,1)S(1)} fusion(f32[1,8,128,2,512]{4,2,1,3,0:T(8,128)S(1)} %get-tuple-element.23, f32[2,512]{1,0:T(2,128)S(1)} %get-tuple-element.31, f32[2,512]{1,0:T(2,128)S(1)} %get-tuple-element.32, f32[2,512]{1,0:T(2,128)S(1)} %get-tuple-element.25, f32[2,512]{1,0:T(2,128)S(1)} %get-tuple-element.26, ...), kind=kLoop, calls=%fused_computation.52 | loop fusion | flops 18874368 | bytes 6328320 | tf_op jit(solution)/shard_map/convert_element_type | solution.py:63
  116.0 3.5 %copy.16 = bf16[1,8,128,2,512]{4,3,2,1,0:T(2,128)(2,1)} copy(bf16[1,8,128,2,512]{4,2,1,3,0:T(8,128)(2,1)S(1)} %fusion.26) | data formatting | bytes 4194304
  119.5 12.9 %psum.15 = f32[3,3,2,512]{3,2,1,0:T(2,128)S(1)} all-reduce(f32[3,3,2,512]{3,2,1,0:T(2,128)S(1)} %pad_maximum_fusion.1), channel_id=1, replica_groups=mesh['dp'=4,'tensor'=8] {'dp'}, use_global_device_ids=true, to_apply=%region_10.11 | all-reduce | flops 9216 | bytes 73728 | tf_op jit(solution)/shard_map/psum | solution.py:65
  132.4 0.6 broadcast_multiply_fusion
  133.0 46.4 %all-reduce.4.cloned.1.call-done = f32[512,2048]{1,0:T(8,128)} async-done(((f32[512,2048]{1,0:T(8,128)}), f32[512,2048]{1,0:T(8,128)}) %all-reduce.4.cloned.1.call-update) | async-done | bytes 4194320 | tf_op jit(solution)/shard_map/psum | solution.py:65
  179.4 4.0 %multiply_convert_fusion = bf16[512,2048]{1,0:T(8,128)(2,1)} fusion(f32[512,2048]{1,0:T(8,128)} %all-reduce.4.cloned.1.call-done), kind=kLoop, calls=%fused_computation.65 | loop fusion | flops 2097152 | bytes 6291456 | tf_op jit(solution)/shard_map/convert_element_type | solution.py:66
  (4 shorter events, 0.1 us)
Async XLA Ops:
  7.2 87.6 %copy-start = (bf16[512,2048]{1,0:T(8,128)(2,1)S(1)}, bf16[512,2048]{1,0:T(8,128)(2,1)}, u32[]{:S(2)}) copy-start(bf16[512,2048]{1,0:T(8,128)(2,1)} %param.7) | copy-start | bytes 6291460
  7.2 4.2 %copy-start.4 = (bf16[3,3,2,512]{3,2,1,0:T(2,128)(2,1)S(1)}, bf16[3,3,2,512]{3,2,1,0:T(2,128)(2,1)}, u32[]{:S(2)}) copy-start(bf16[3,3,2,512]{3,2,1,0:T(2,128)(2,1)} %param.6) | copy-start | bytes 55300
  7.2 79.7 %all-gather.2.cloned.1.call-start = ((), (), s32[]{:S(2)}) async-start(), calls=%async_computation | async-start | bytes 4718592 | tf_op jit(solution)/shard_map/all_gather | solution.py:51
  9.3 170.1 %all-reduce.4.cloned.1.call-start = ((), (), s32[]{:S(2)}) async-start(), calls=%async_computation.1 | async-start | bytes 8388608 | tf_op jit(solution)/shard_map/psum | solution.py:65
  11.4 1.3 copy-start.1
  94.8 6.5 %copy-start.2 = (bf16[1,8,128,2,512]{4,2,1,3,0:T(8,128)(2,1)S(1)}, bf16[1,8,128,2,512]{4,2,1,3,0:T(8,128)(2,1)}, u32[]{:S(2)}) copy-start(bf16[1,8,128,2,512]{4,2,1,3,0:T(8,128)(2,1)} %copy-done.1) | copy-start | bytes 6291460
  94.8 6.5 %copy-start.3 = (bf16[1,8,128,2,512]{4,3,2,1,0:T(2,128)(2,1)S(1)}, bf16[1,8,128,2,512]{4,3,2,1,0:T(2,128)(2,1)}, u32[]{:S(2)}) copy-start(bf16[1,8,128,2,512]{4,3,2,1,0:T(2,128)(2,1)} %param.5) | copy-start | bytes 6291460
Sparse Core Ops, SparseCore 0:
  10.7 76.0 all-gather.1
  94.9 84.5 all-reduce.3
where the time goes:
time: 191 us; the launch traced here: 190 us
  waiting for transfers between devices  111 us (58%)
  other arithmetic  31 us (16%)
  matrix products  14.4 us (8%)
  between operations  14.2 us (7%)
  blocking collectives  12.9 us (7%)
  local copies, waits for them, and re-layouts  6.8 us (4%)
    all_gather x1, waiting for transfers between devices, on_device(): gathered = lax.all_gather(gated_grad, 'tensor', axis=1, tiled=True)  64.5 us
    psum x1, waiting for transfers between devices, on_device(): proj_total, kernel_total = lax.psum((proj_sum, kernel_sum), 'dp')  46.4 us
    psum x1, blocking collectives, on_device(): proj_total, kernel_total = lax.psum((proj_sum, kernel_sum), 'dp')  12.9 us
    add x1, other arithmetic, depthwise(): summed + kernel[i, j].astype(jnp.float32) * padded[:, a:a + height, b:b +...  9.63 us
    dot_general x1, matrix products, on_device(): jnp.einsum('srwc,srwd->cd', mixed_act, gathered, preferred_element_type=j...  7.87 us
    convert_element_type x1, other arithmetic, on_device(): hidden_grad = depthwise(grad_pre, conv_weight, True).astype(jnp.bfloat16)  7.75 us
    reduce_sum x1, other arithmetic, kernel_terms(): jnp.sum(grad_pre * padded[:, i:i + height, j:j + across], axis=(0, 1, 2))  6.87 us
    unnamed x12, local copies, waits for them, and re-layouts  6.8 us
  transfers between devices with their start and end apart: 2, of which 2 were waited for; matrix products, arithmetic and copies ran while one was open for 19% of the time, Pallas kernels for 0%

commit v1 on v0

v1 whole, which is shorter than its diff:
```python
import functools
import math

import jax
import jax.numpy as jnp
from jax import lax
from jax.experimental import pallas as pl
from jax.experimental.pallas import tpu as pltpu
from jax.sharding import PartitionSpec as P

F32 = jnp.float32
BF16 = jnp.bfloat16
PAD = 8
TILE = 16
LANES = 128
VMEM_BYTES = 48 * 1024 * 1024


def ring_order(n):
    return [2 * i if i < n // 2 else 2 * (n - 1 - i) + 1 for i in range(n)]


def at_ring(position, n):
    position = lax.rem(position + 2 * n, n)
    return jnp.where(position < n // 2, 2 * position, 2 * (n - 1 - position) + 1)


def ring_place(index, n):
    half = index // 2
    return jnp.where(lax.rem(index, 2) == 0, half, n - 1 - half)


def split_widths(depth):
    first = depth * 5 // 8 // 256 * 256
    return [first, depth - first]


def conv_kernel(hidden_ref, weight_ref, gate_ref, value_ref, mixed_ref, pad_ref):
    _, height, across, lanes = hidden_ref.shape
    for k in range(2):
        pad_ref[k, 0] = jnp.zeros(pad_ref.shape[2:], F32)
        pad_ref[k, height + 1] = jnp.zeros(pad_ref.shape[2:], F32)

    @pl.loop(0, height)
    def _(r):
        for k in range(2):
            pad_ref[k, r + 1, 0:PAD] = jnp.zeros((PAD, lanes), F32)
            pad_ref[k, r + 1, PAD + across : 2 * PAD + across] = jnp.zeros((PAD, lanes), F32)
            pad_ref[k, r + 1, PAD : PAD + across] = hidden_ref[k, r].astype(F32)

    weights = weight_ref[...]

    @pl.loop(0, height)
    def _(r):
        for t in range(across // TILE):
            w = t * TILE
            parts = []
            for k in range(2):
                total = None
                for i in range(3):
                    for j in range(3):
                        term = (
                            weights[(i * 3 + j) * 2 + k][None, :]
                            * pad_ref[k, r + i, PAD + w + j - 1 : PAD + w + j - 1 + TILE]
                        )
                        total = term if total is None else total + term
                parts.append(total)
            value, gate = parts
            sig = 1.0 / (1.0 + jnp.exp(-gate))
            gated = gate * sig
            gate_ref[r, w : w + TILE] = gated
            value_ref[r, w : w + TILE] = value * sig * (1.0 + gate * (1.0 - sig))
            mixed_ref[r, w : w + TILE] = (value * gated).astype(BF16)


def conv_parts(hidden, weights):
    _, height, across, channels = hidden.shape
    block = pl.BlockSpec((height, across, LANES), lambda c: (0, 0, c))
    return pl.pallas_call(
        conv_kernel,
        grid=(channels // LANES,),
        in_specs=[
            pl.BlockSpec((2, height, across, LANES), lambda c: (0, 0, 0, c)),
            pl.BlockSpec((18, LANES), lambda c: (0, c)),
        ],
        out_specs=[block, block, block],
        out_shape=[
            jax.ShapeDtypeStruct((height, across, channels), F32),
            jax.ShapeDtypeStruct((height, across, channels), F32),
            jax.ShapeDtypeStruct((height, across, channels), BF16),
        ],
        scratch_shapes=[pltpu.VMEM((2, height + 2, across + 2 * PAD, LANES), F32)],
        compiler_params=pltpu.CompilerParams(vmem_limit_bytes=VMEM_BYTES),
        cost_estimate=pl.CostEstimate(
            flops=height * across * channels * 60,
            bytes_accessed=height * across * channels * 14,
            transcendentals=height * across * channels,
        ),
    )(hidden, weights)


def matmul_kernel(n, first, place_ref, *refs):
    count = n + 1
    pieces, refs = refs[:count], refs[count:]
    gate_ref, weight_ref, mixed_ref = refs[:3]
    refs = refs[3:]
    if first:
        before_ref, refs = None, refs
    else:
        before_ref, refs = refs[0], refs[1:]
    grad_ref, send_ref, keep_ref, full_ref = refs
    across = pieces[0].shape[0]
    width = pieces[0].shape[1]
    me, core = place_ref[0], place_ref[1]
    spot = ring_place(me, n)
    gate = gate_ref[...]
    starts = []
    for step in range(n // 2):
        if step == 0:
            starts.append(at_ring(spot, n) * across)
        else:
            starts.append(at_ring(spot - step, n) * across)
            starts.append(at_ring(spot + step, n) * across)
    far = at_ring(spot + n // 2, n) * across
    starts.extend([far, far + across // 2])
    for piece, start in zip(pieces, starts):
        rows = piece.shape[0]
        full_ref[pl.ds(pl.multiple_of(start, rows), rows)] = (
            piece[...].astype(F32) * gate
        ).astype(BF16)
    tokens = full_ref.shape[0]
    half = width // 2
    slab = min(tokens, 512)

    @pl.loop(0, tokens // slab)
    def _(s):
        rows = pl.ds(pl.multiple_of(s * slab, slab), slab)
        product = lax.dot_general(
            full_ref[rows], weight_ref[...], (((1,), (1,)), ((), ())), preferred_element_type=F32
        )
        if before_ref is not None:
            product = product + before_ref[rows]
        grad_ref[rows] = product

    for out_ref, column in ((send_ref, 1 - core), (keep_ref, core)):
        columns = pl.ds(pl.multiple_of(column * half, LANES), half)
        out_ref[...] = lax.dot_general(
            mixed_ref[...],
            full_ref[:, columns],
            (((0,), (0,)), ((), ())),
            preferred_element_type=F32,
        ).astype(out_ref.dtype)


def matmul_parts(n, place, pieces, gate, weight, mixed, before):
    across, width = pieces[0].shape
    channels = weight.shape[0]
    tokens = mixed.shape[0]
    first = before is None
    vmem = pl.BlockSpec(memory_space=pltpu.VMEM)
    operands = [*pieces, gate, weight, mixed] + ([] if first else [before])
    return pl.pallas_call(
        functools.partial(matmul_kernel, n, first),
        in_specs=[pl.BlockSpec(memory_space=pltpu.SMEM)] + [vmem] * len(operands),
        out_specs=[vmem] * 3,
        out_shape=[
            jax.ShapeDtypeStruct((tokens, channels), F32),
            jax.ShapeDtypeStruct((channels, width // 2), BF16),
            jax.ShapeDtypeStruct((channels, width // 2), F32),
        ],
        scratch_shapes=[pltpu.VMEM((tokens, width), BF16)],
        compiler_params=pltpu.CompilerParams(vmem_limit_bytes=VMEM_BYTES),
        cost_estimate=pl.CostEstimate(
            flops=4 * tokens * channels * width,
            bytes_accessed=tokens * width * 2 + channels * width * 5 + tokens * channels * 10,
            transcendentals=0,
        ),
    )(place, *operands)


def grads_kernel(grad_ref, gate_ref, value_ref, hidden_ref, weight_ref, out_ref, term_ref, pad_ref):
    _, height, across, lanes = hidden_ref.shape
    for k in range(2):
        pad_ref[k, 0] = jnp.zeros(pad_ref.shape[2:], F32)
        pad_ref[k, height + 1] = jnp.zeros(pad_ref.shape[2:], F32)

    @pl.loop(0, height)
    def _(r):
        grad = grad_ref[r]
        for k, factor in enumerate((gate_ref, value_ref)):
            pad_ref[k, r + 1, 0:PAD] = jnp.zeros((PAD, lanes), F32)
            pad_ref[k, r + 1, PAD + across : 2 * PAD + across] = jnp.zeros((PAD, lanes), F32)
            pad_ref[k, r + 1, PAD : PAD + across] = grad * factor[r]

    weights = weight_ref[...]
    for k in range(2):

        def row(r, sums):
            sums = list(sums)
            for t in range(across // TILE):
                w = t * TILE
                own = hidden_ref[k, r, w : w + TILE].astype(F32)
                total = None
                for i in range(3):
                    for j in range(3):
                        view = pad_ref[k, r + 2 - i, PAD + w + 1 - j : PAD + w + 1 - j + TILE]
                        term = weights[(i * 3 + j) * 2 + k][None, :] * view
                        total = term if total is None else total + term
                        both = view * own
                        sums[i * 3 + j] = sums[i * 3 + j] + (both[:8] + both[8:])
                out_ref[k, r, w : w + TILE] = total.astype(BF16)
            return tuple(sums)

        sums = lax.fori_loop(0, height, row, tuple(jnp.zeros((8, lanes), F32) for _ in range(9)))
        for tap in range(9):
            term_ref[tap * 2 + k : tap * 2 + k + 1] = jnp.sum(sums[tap], axis=0, keepdims=True)


def grads(grad, gate_part, value_part, hidden, weights):
    _, height, across, channels = hidden.shape
    block = pl.BlockSpec((height, across, LANES), lambda c: (0, 0, c))
    pair = pl.BlockSpec((2, height, across, LANES), lambda c: (0, 0, 0, c))
    taps = pl.BlockSpec((18, LANES), lambda c: (0, c))
    return pl.pallas_call(
        grads_kernel,
        grid=(channels // LANES,),
        in_specs=[block, block, block, pair, taps],
        out_specs=[pair, taps],
        out_shape=[
            jax.ShapeDtypeStruct(hidden.shape, BF16),
            jax.ShapeDtypeStruct((18, channels), F32),
        ],
        scratch_shapes=[pltpu.VMEM((2, height + 2, across + 2 * PAD, LANES), F32)],
        compiler_params=pltpu.CompilerParams(vmem_limit_bytes=VMEM_BYTES),
        cost_estimate=pl.CostEstimate(
            flops=height * across * channels * 80,
            bytes_accessed=height * across * channels * 20,
            transcendentals=0,
        ),
    )(grad, gate_part, value_part, hidden, weights)


def place_kernel(place_ref, mine_ref, other_ref, whole_ref, out_ref):
    step = pl.program_id(0)

    @pl.when(step == 0)
    def _():
        out_ref[...] = mine_ref[...]

    @pl.when(step == 1)
    def _():
        out_ref[...] = other_ref[...]


def put(place, mine, other, whole, offset):
    channels, half = mine.shape
    unit = math.gcd(half, offset) if offset else half
    return pl.pallas_call(
        place_kernel,
        grid_spec=pltpu.PrefetchScalarGridSpec(
            num_scalar_prefetch=1,
            grid=(2, half // unit),
            in_specs=[
                pl.BlockSpec((channels, unit), lambda h, u, s: (0, u)),
                pl.BlockSpec((channels, unit), lambda h, u, s: (0, u)),
                pl.BlockSpec(memory_space=pl.ANY),
            ],
            out_specs=pl.BlockSpec(
                (channels, unit),
                lambda h, u, s: (
                    0,
                    offset // unit + (h + s[1] - 2 * h * s[1]) * (half // unit) + u,
                ),
            ),
        ),
        out_shape=jax.ShapeDtypeStruct(whole.shape, whole.dtype),
        input_output_aliases={3: 0},
        compiler_params=pltpu.CompilerParams(vmem_limit_bytes=VMEM_BYTES),
        cost_estimate=pl.CostEstimate(
            flops=0, bytes_accessed=channels * half * 8, transcendentals=0
        ),
    )(place, mine, other, whole)


def ring_gather(n, own, state):
    ring = ring_order(n)
    right = [(ring[i], ring[(i + 1) % n]) for i in range(n)]
    left = [(ring[i], ring[(i - 1) % n]) for i in range(n)]
    half = own.shape[0] // 2
    gathered = [own]
    up = down = own
    for step in range(1, n // 2):
        up = lax.ppermute(up, "tensor", right)
        down = lax.ppermute(down, "tensor", left)
        gathered += [up, down]
        state.append((up, down))
    gathered.append(lax.ppermute(up[:half], "tensor", right))
    gathered.append(lax.ppermute(down[half:], "tensor", left))
    return gathered


def swap(value, bit):
    n = lax.axis_size("dp")
    return lax.ppermute(value, "dp", [(i, i ^ bit) for i in range(n)])


def sum_rest(value, low=2):
    bit = low
    while bit < lax.axis_size("dp"):
        value = value.astype(F32) + swap(value, bit).astype(F32)
        if bit * 2 < lax.axis_size("dp"):
            value = value.astype(BF16)
        bit *= 2
    return value


def on_device(hidden_in, conv_weight, proj_weight, out_grad, sample_gate):
    samples, height, across, _, channels = hidden_in.shape
    depth = out_grad.shape[-1]
    n = lax.axis_size("tensor")
    dp = lax.axis_size("dp")
    assert samples == 1 and out_grad.shape[1] == 1 and n % 2 == 0 and dp & (dp - 1) == 0
    grad_scale = 1.0 / math.sqrt(dp * samples * height * across)
    place = jnp.stack([lax.axis_index("tensor"), lax.rem(lax.axis_index("dp"), 2)]).astype(
        jnp.int32
    )
    own = out_grad.reshape(across, depth)
    hidden = jnp.transpose(hidden_in.reshape(height, across, 2, channels), (2, 0, 1, 3))
    taps = conv_weight.astype(F32).reshape(18, channels)

    widths = split_widths(depth)
    offset = 0
    chunks = []
    previous = None
    for width in widths:
        block = own[:, offset : offset + width]
        if previous is not None:
            block = lax.optimization_barrier((block, *previous[1]))[0]
        state = []
        pieces = ring_gather(n, block, state)
        previous = state
        chunks.append((offset, width, pieces))
        offset += width

    gate_part, value_part, mixed = conv_parts(hidden, taps)
    mixed = mixed.reshape(height * across, channels)
    grad = None
    whole = jnp.zeros((channels, depth), BF16)
    for offset, width, pieces in chunks:
        grad, send, keep = matmul_parts(
            n,
            place,
            pieces,
            sample_gate[:, offset : offset + width],
            proj_weight[:, offset : offset + width],
            mixed,
            grad,
        )
        pair = (keep + swap(send, 1).astype(F32)).astype(BF16)
        mine = (sum_rest(pair) * grad_scale).astype(BF16)
        other = swap(mine, 1)
        whole = put(place, mine, other, whole, offset)

    hidden_grad, terms = grads(
        grad.reshape(height, across, channels), gate_part, value_part, hidden, taps
    )
    total = terms
    bit = 1
    while bit < dp:
        total = total + swap(total, bit)
        bit *= 2
    conv_grad = (total * grad_scale).reshape(3, 3, 2, channels)
    hidden_grad = jnp.transpose(hidden_grad, (1, 2, 0, 3))[None]
    return (hidden_grad, whole, conv_grad)


def solution(mesh):
    in_specs = (
        P("dp", None, None, None, "tensor"),
        P(None, None, None, "tensor"),
        P("tensor", None),
        P("dp", "tensor", None, None),
        P("dp", None),
    )
    out_specs = (
        P("dp", None, None, None, "tensor"),
        P("tensor", None),
        P(None, None, None, "tensor"),
    )
    return jax.shard_map(
        on_device, mesh=mesh, in_specs=in_specs, out_specs=out_specs, check_vma=False
    )
```

time: 191 us -> 127 us (0.66)
  waiting for transfers between devices: 111 us -> 55.9 us
  other arithmetic: 31 us -> 0.66 us
  Pallas kernels: 0 us -> 28.7 us
  starting transfers between devices: 0.08 us -> 23 us
  matrix products: 14.4 us -> 0 us
  between operations: 14.2 us -> 0.8 us
  blocking collectives: 12.9 us -> 0 us
  local copies, waits for them, and re-layouts: 6.8 us -> 17.4 us
    all_gather x1 -> x0, waiting for transfers between devices: 64.5 us -> none  [on_device(): gathered = lax.all_gather(gated_grad, 'tensor', axis=1, tiled=True)]
    ppermute x0 -> x24, waiting for transfers between devices: none -> 55.9 us  [the longest x6 30.1 us: ring_gather(): up = lax.ppermute(up, 'tensor', right)]
    psum x1 -> x0, waiting for transfers between devices: 46.4 us -> none  [on_device(): proj_total, kernel_total = lax.psum((proj_sum, kernel_sum), 'dp')]
    pallas_call x0 -> x6, Pallas kernels: none -> 28.7 us  [the longest x2 10.1 us: matmul_parts(): pl.pallas_call(functools.partial(matmul_kernel, n, first), in_specs=[pl.B...]
    ppermute x0 -> x24, starting transfers between devices: none -> 23 us  [the longest x6 10.5 us: ring_gather(): up = lax.ppermute(up, 'tensor', right)]
    dot_general x2 -> x0, matrix products: 14.4 us -> none  [the longest x1 7.87 us: on_device(): jnp.einsum('srwc,srwd->cd', mixed_act, gathered, preferred_element_type=j...]
    convert_element_type x4, other arithmetic: 13.9 us -> 0.57 us  [the longest x2 0.33 us: on_device(): mine = (sum_rest(pair) * grad_scale).astype(BF16)]
    psum x1 -> x0, blocking collectives: 12.9 us -> none  [on_device(): proj_total, kernel_total = lax.psum((proj_sum, kernel_sum), 'dp')]
  transfers between devices with their start and end apart: 2 -> 24, of which waited for: 2 -> 10; matrix products, arithmetic and copies ran while one was open for 19% -> 11% of each run, Pallas kernels for 0% -> 20%
where the time goes in v1:
time: 127 us; the launch traced here: 126 us
  waiting for transfers between devices  55.9 us (44%)
  Pallas kernels  28.7 us (23%)
  starting transfers between devices  23 us (18%)
  local copies, waits for them, and re-layouts  17.4 us (14%)
    ppermute x6, waiting for transfers between devices, ring_gather(): up = lax.ppermute(up, 'tensor', right)  30.1 us
    ppermute x8, waiting for transfers between devices, swap(): return lax.ppermute(value, 'dp', [(i, i ^ bit) for i in range(n)])  23 us
    ppermute x6, starting transfers between devices, ring_gather(): up = lax.ppermute(up, 'tensor', right)  10.5 us
    pallas_call x2, Pallas kernels, matmul_parts(): pl.pallas_call(functools.partial(matmul_kernel, n, first), in_specs=[pl.B...  10.1 us
    unnamed x12, local copies, waits for them, and re-layouts  9.5 us
    pallas_call x1, Pallas kernels, grads(): pl.pallas_call(grads_kernel, grid=(channels // LANES,), in_specs=[block,...  8 us
    pallas_call x1, Pallas kernels, conv_parts(): pl.pallas_call(conv_kernel, grid=(channels // LANES,), in_specs=[pl.Block...  6.01 us
    ppermute x8, starting transfers between devices, swap(): return lax.ppermute(value, 'dp', [(i, i ^ bit) for i in range(n)])  5.47 us
  transfers between devices with their start and end apart: 24, of which 10 were waited for; matrix products, arithmetic and copies ran while one was open for 11% of the time, Pallas kernels for 20%

profile of v1, /device:TPU:0, one launch (start us, length us, event | category | flops | bytes accessed | tf_op | source)
XLA Modules:
  0.0 126.4 jit_solution(17032603759828006057)
XLA Ops:
  1.6 3.1 %collective-permute-start = (bf16[128,1280]{1,0:T(8,128)(2,1)S(1)}, bf16[128,1280]{1,0:T(8,128)(2,1)S(1)}, u32[]{:S(2)}, u32[]{:S(2)}) collective-permute-start(bf16[128,1280]{1,0:T(8,128)(2,1)S(1)} %slice.41.refs_0_), channel_id=1, source_target_pairs={{0,2},{2,4},{4,6},{6,7},{7,5},{5,3},{3,1},{1,0},{8,10},{10,12},{12... | collective-permute-start | bytes 983048 | tf_op jit(solution)/shard_map/ppermute | solution.py:293
  4.7 7.6 %collective-permute-done.refs_1_ = bf16[128,1280]{1,0:T(8,128)(2,1)S(1)} collective-permute-done((bf16[128,1280]{1,0:T(8,128)(2,1)S(1)}, bf16[128,1280]{1,0:T(8,128)(2,1)S(1)}, u32[]{:S(2)}, u32[]{:S(2)}) %collective-permute-start) | collective-permute-done | bytes 327712 | tf_op jit(solution)/shard_map/ppermute | solution.py:293
  12.3 1.8 %collective-permute-start.1 = (bf16[128,1280]{1,0:T(8,128)(2,1)S(1)}, bf16[128,1280]{1,0:T(8,128)(2,1)S(1)}, u32[]{:S(2)}, u32[]{:S(2)}) collective-permute-start(bf16[128,1280]{1,0:T(8,128)(2,1)S(1)} %collective-permute-done.refs_1_), channel_id=1, source_target_pairs={{0,2},{2,4},{4,6},{6,7},{7,5},{5,3},{3,1},{1,0},{8,10},{10,12},{12... | collective-permute-start | bytes 983048 | tf_op jit(solution)/shard_map/ppermute | solution.py:293
  14.4 6.9 %collective-permute-done.1.refs_3_ = bf16[128,1280]{1,0:T(8,128)(2,1)S(1)} collective-permute-done((bf16[128,1280]{1,0:T(8,128)(2,1)S(1)}, bf16[128,1280]{1,0:T(8,128)(2,1)S(1)}, u32[]{:S(2)}, u32[]{:S(2)}) %collective-permute-start.1) | collective-permute-done | bytes 327712 | tf_op jit(solution)/shard_map/ppermute | solution.py:293
  21.2 1.5 %collective-permute-start.12 = (bf16[128,1280]{1,0:T(8,128)(2,1)S(1)}, bf16[128,1280]{1,0:T(8,128)(2,1)S(1)}, u32[]{:S(2)}, u32[]{:S(2)}) collective-permute-start(bf16[128,1280]{1,0:T(8,128)(2,1)S(1)} %collective-permute-done.1.refs_3_), channel_id=1, source_target_pairs={{0,2},{2,4},{4,6},{6,7},{7,5},{5,3},{3,1},{1,0},{8,10},{10,12},{12... | collective-permute-start | bytes 983048 | tf_op jit(solution)/shard_map/ppermute | solution.py:293
  23.3 5.9 %collective-permute-done.12.refs_5_ = bf16[128,1280]{1,0:T(8,128)(2,1)S(1)} collective-permute-done((bf16[128,1280]{1,0:T(8,128)(2,1)S(1)}, bf16[128,1280]{1,0:T(8,128)(2,1)S(1)}, u32[]{:S(2)}, u32[]{:S(2)}) %collective-permute-start.12) | collective-permute-done | bytes 327712 | tf_op jit(solution)/shard_map/ppermute | solution.py:293
  29.2 1.4 %collective-permute-start.14 = (bf16[64,1280]{1,0:T(8,128)(2,1)S(1)}, bf16[64,1280]{1,0:T(8,128)(2,1)S(1)}, u32[]{:S(2)}, u32[]{:S(2)}) collective-permute-start(bf16[64,1280]{1,0:T(8,128)(2,1)S(1)} %slice.44), channel_id=1, source_target_pairs={{0,2},{2,4},{4,6},{6,7},{7,5},{5,3},{3,1},{1,0},{8,10},{10,12},{12... | collective-permute-start | bytes 491528 | tf_op jit(solution)/shard_map/ppermute | solution.py:297
  32.3 3.3 %copy.13 = bf16[1,8,128,2,512]{4,2,1,3,0:T(8,128)(2,1)} copy(bf16[1,8,128,2,512]{4,3,2,1,0:T(2,128)(2,1)} %param.5) | data formatting | bytes 4194304 | tf_op args[0]
  35.7 2.5 %slice.39.refs_10_ = bf16[512,1280]{1,0:T(8,128)(2,1)} slice(bf16[512,2048]{1,0:T(8,128)(2,1)} %param.7), slice={[0:512], [0:1280]} | slice | bytes 2621440 | tf_op jit(solution)/shard_map/slice | solution.py:355
  38.2 6.0 %shard_map.76 = (f32[8,128,512]{2,1,0:T(8,128)S(1)}, f32[8,128,512]{2,1,0:T(8,128)S(1)}, bf16[8,128,512]{2,1,0:T(8,128)(2,1)S(1)}) custom-call(bf16[2,8,128,512]{3,2,1,0:T(8,128)(2,1)} %bitcast.17, f32[18,512]{1,0:T(8,128)S(1)} %reshape.34.weight_ref), custom_call_target="tpu_custom_call" | custom-call | flops 31457280 | bytes 7340032 | tf_op jit(solution)/shard_map/pallas_call | solution.py:79
  44.2 1.4 %copy-done = f32[8,128,512]{2,1,0:T(8,128)} copy-done((f32[8,128,512]{2,1,0:T(8,128)}, f32[8,128,512]{2,1,0:T(8,128)S(1)}, u32[]{:S(2)}) %copy-start) | copy-done | bytes 2097176
  45.6 1.3 %copy-done.1 = f32[8,128,512]{2,1,0:T(8,128)} copy-done((f32[8,128,512]{2,1,0:T(8,128)}, f32[8,128,512]{2,1,0:T(8,128)S(1)}, u32[]{:S(2)}) %copy-start.1) | copy-done | bytes 2097176
  47.0 1.3 %collective-permute-start.4 = (bf16[128,768]{1,0:T(8,128)(2,1)S(1)}, bf16[128,768]{1,0:T(8,128)(2,1)S(1)}, u32[]{:S(2)}, u32[]{:S(2)}) collective-permute-start(bf16[128,768]{1,0:T(8,128)(2,1)S(1)} %slice.40.refs_0_), channel_id=1, source_target_pairs={{0,2},{2,4},{4,6},{6,7},{7,5},{5,3},{3,1},{1,0},{8,10},{10,12},{12... | collective-permute-start | bytes 589832 | tf_op jit(solution)/shard_map/ppermute | solution.py:293
  49.0 5.3 %shard_map.77 = (f32[1024,512]{1,0:T(8,128)}, bf16[512,640]{1,0:T(8,128)(2,1)S(1)}, f32[512,640]{1,0:T(8,128)S(1)}) custom-call(s32[2]{0:T(128)S(1)} %pad_add_fusion.place_ref, bf16[128,1280]{1,0:T(8,128)(2,1)S(1)} %slice.41.refs_0_, bf16[128,1280]{1,0:T(8,128)(2,1)S(1)} %collective-permute-done.refs_1_, ...), custom_call_target="tpu_custom_call" | custom-call | flops 2684354560 | bytes 11141120 | tf_op jit(solution)/shard_map/pallas_call | solution.py:162
  54.4 1.4 %collective-permute-start.6 = (bf16[128,768]{1,0:T(8,128)(2,1)S(1)}, bf16[128,768]{1,0:T(8,128)(2,1)S(1)}, u32[]{:S(2)}, u32[]{:S(2)}) collective-permute-start(bf16[128,768]{1,0:T(8,128)(2,1)S(1)} %collective-permute-done.4.refs_1_), channel_id=1, source_target_pairs={{0,2},{2,4},{4,6},{6,7},{7,5},{5,3},{3,1},{1,0},{8,10},{10,12},{12... | collective-permute-start | bytes 589832 | tf_op jit(solution)/shard_map/ppermute | solution.py:293
  56.5 5.2 %collective-permute-done.6.refs_3_ = bf16[128,768]{1,0:T(8,128)(2,1)S(1)} collective-permute-done((bf16[128,768]{1,0:T(8,128)(2,1)S(1)}, bf16[128,768]{1,0:T(8,128)(2,1)S(1)}, u32[]{:S(2)}, u32[]{:S(2)}) %collective-permute-start.6) | collective-permute-done | bytes 196640 | tf_op jit(solution)/shard_map/ppermute | solution.py:293
  61.7 1.3 %collective-permute-start.8 = (bf16[128,768]{1,0:T(8,128)(2,1)S(1)}, bf16[128,768]{1,0:T(8,128)(2,1)S(1)}, u32[]{:S(2)}, u32[]{:S(2)}) collective-permute-start(bf16[128,768]{1,0:T(8,128)(2,1)S(1)} %collective-permute-done.6.refs_3_), channel_id=1, source_target_pairs={{0,2},{2,4},{4,6},{6,7},{7,5},{5,3},{3,1},{1,0},{8,10},{10,12},{12... | collective-permute-start | bytes 589832 | tf_op jit(solution)/shard_map/ppermute | solution.py:293
  63.7 4.4 %collective-permute-done.8.refs_5_ = bf16[128,768]{1,0:T(8,128)(2,1)S(1)} collective-permute-done((bf16[128,768]{1,0:T(8,128)(2,1)S(1)}, bf16[128,768]{1,0:T(8,128)(2,1)S(1)}, u32[]{:S(2)}, u32[]{:S(2)}) %collective-permute-start.8) | collective-permute-done | bytes 196640 | tf_op jit(solution)/shard_map/ppermute | solution.py:293
  68.2 1.4 %collective-permute-start.10 = (bf16[64,768]{1,0:T(8,128)(2,1)S(1)}, bf16[64,768]{1,0:T(8,128)(2,1)S(1)}, u32[]{:S(2)}, u32[]{:S(2)}) collective-permute-start(bf16[64,768]{1,0:T(8,128)(2,1)S(1)} %slice.42), channel_id=1, source_target_pairs={{0,2},{2,4},{4,6},{6,7},{7,5},{5,3},{3,1},{1,0},{8,10},{10,12},{12... | collective-permute-start | bytes 294920 | tf_op jit(solution)/shard_map/ppermute | solution.py:297
  71.5 1.3 %collective-permute-done.10.refs_7_ = bf16[64,768]{1,0:T(8,128)(2,1)S(1)} collective-permute-done((bf16[64,768]{1,0:T(8,128)(2,1)S(1)}, bf16[64,768]{1,0:T(8,128)(2,1)S(1)}, u32[]{:S(2)}, u32[]{:S(2)}) %collective-permute-start.10) | collective-permute-done | bytes 98336 | tf_op jit(solution)/shard_map/ppermute | solution.py:297
  72.8 1.4 %collective-permute-done.11.refs_8_ = bf16[64,768]{1,0:T(8,128)(2,1)S(1)} collective-permute-done((bf16[64,768]{1,0:T(8,128)(2,1)S(1)}, bf16[64,768]{1,0:T(8,128)(2,1)S(1)}, u32[]{:S(2)}, u32[]{:S(2)}) %collective-permute-start.11) | collective-permute-done | bytes 98336 | tf_op jit(solution)/shard_map/ppermute | solution.py:298
  74.3 4.8 %shard_map.78 = (f32[1024,512]{1,0:T(8,128)}, bf16[512,384]{1,0:T(8,128)(2,1)S(1)}, f32[512,384]{1,0:T(8,128)S(1)}) custom-call(s32[2]{0:T(128)S(1)} %pad_add_fusion.place_ref, bf16[128,768]{1,0:T(8,128)(2,1)S(1)} %slice.40.refs_0_, bf16[128,768]{1,0:T(8,128)(2,1)S(1)} %collective-permute-done.4.refs_1_, ...), custom_call_target="tpu_custom_call" | custom-call | flops 1610612736 | bytes 8781824 | tf_op jit(solution)/shard_map/pallas_call | solution.py:162
  79.2 1.6 %collective-permute-start.20 = (bf16[512,640]{1,0:T(8,128)(2,1)S(1)}, bf16[512,640]{1,0:T(8,128)(2,1)S(1)}, u32[]{:S(2)}, u32[]{:S(2)}) collective-permute-start(bf16[512,640]{1,0:T(8,128)(2,1)S(1)} %add_convert_fusion), channel_id=1, source_target_pairs={{0,16},{8,24},{16,0},{24,8},{1,17},{9,25},{17,1},{25,9},{2,18},{10... | collective-permute-start | bytes 1966088 | tf_op jit(solution)/shard_map/ppermute | solution.py:304
  80.9 1.5 %collective-permute-start.17 = (bf16[512,384]{1,0:T(8,128)(2,1)S(1)}, bf16[512,384]{1,0:T(8,128)(2,1)S(1)}, u32[]{:S(2)}, u32[]{:S(2)}) collective-permute-start(bf16[512,384]{1,0:T(8,128)(2,1)S(1)} %add_convert_fusion.1), channel_id=1, source_target_pairs={{0,16},{8,24},{16,0},{24,8},{1,17},{9,25},{17,1},{25,9},{2,18},{10... | collective-permute-start | bytes 1179656 | tf_op jit(solution)/shard_map/ppermute | solution.py:304
  82.5 14.4 %collective-permute-done.20 = bf16[512,640]{1,0:T(8,128)(2,1)S(1)} collective-permute-done((bf16[512,640]{1,0:T(8,128)(2,1)S(1)}, bf16[512,640]{1,0:T(8,128)(2,1)S(1)}, u32[]{:S(2)}, u32[]{:S(2)}) %collective-permute-start.20) | collective-permute-done | bytes 655392 | tf_op jit(solution)/shard_map/ppermute | solution.py:304
  97.1 7.8 %collective-permute-done.17 = bf16[512,384]{1,0:T(8,128)(2,1)S(1)} collective-permute-done((bf16[512,384]{1,0:T(8,128)(2,1)S(1)}, bf16[512,384]{1,0:T(8,128)(2,1)S(1)}, u32[]{:S(2)}, u32[]{:S(2)}) %collective-permute-start.17) | collective-permute-done | bytes 393248 | tf_op jit(solution)/shard_map/ppermute | solution.py:304
  105.1 8.0 %shard_map.79 = (bf16[2,8,128,512]{3,2,1,0:T(8,128)(2,1)S(1)}, f32[18,512]{1,0:T(8,128)S(1)}) custom-call(f32[8,128,512]{2,1,0:T(8,128)S(1)} %bitcast.14, f32[8,128,512]{2,1,0:T(8,128)} %copy-done, f32[8,128,512]{2,1,0:T(8,128)} %copy-done.1, bf16[2,8,128,512]{3,2,1,0:T(8,128)(2,1)} %bitcast.18, f32[18,512]{1,0:T(8,128)S(1)} %reshape.34.weight_ref), custom_call_target="tpu_custom_call" | custom-call | flops 41943040 | bytes 10485760 | tf_op jit(solution)/shard_map/pallas_call | solution.py:224
  114.5 1.6 %collective-permute-start.23 = (f32[18,512]{1,0:T(8,128)S(1)}, f32[18,512]{1,0:T(8,128)S(1)}, u32[]{:S(2)}, u32[]{:S(2)}) collective-permute-start(f32[18,512]{1,0:T(8,128)S(1)} %add.22), channel_id=1, source_target_pairs={{0,16},{8,24},{16,0},{24,8},{1,17},{9,25},{17,1},{25,9},{2,18},{10... | collective-permute-start | bytes 110600 | tf_op jit(solution)/shard_map/ppermute | solution.py:304
  116.1 3.5 %copy.11 = bf16[1,8,128,2,512]{4,3,2,1,0:T(2,128)(2,1)} copy(bf16[1,8,128,2,512]{4,2,1,3,0:T(8,128)(2,1)S(1)} %bitcast.13) | data formatting | bytes 4194304
  120.3 1.6 %broadcast_in_dim.7.whole_ref = bf16[512,2048]{1,0:T(8,128)(2,1)} broadcast(bf16[]{:T(256)} %constant.18.clone.1), dimensions={} | broadcast | bytes 2097154 | tf_op jit(solution)/shard_map/broadcast_in_dim | solution.py:348
  121.8 1.7 %shard_map.80.whole_ref = bf16[512,2048]{1,0:T(8,128)(2,1)} custom-call(s32[2]{0:T(128)S(1)} %pad_add_fusion.place_ref, bf16[512,640]{1,0:T(8,128)(2,1)S(1)} %multiply_convert_fusion.mine_ref, bf16[512,640]{1,0:T(8,128)(2,1)S(1)} %collective-permute-done.21.other_ref, bf16[512,2048]{1,0:T(8,128)(2,1)} %broadcast_in_dim.7.whole_ref), custom_call_target="tpu_custom_call", output_to_operand_aliasing={{}: (3, {})} | custom-call | bytes 2621440 | tf_op jit(solution)/shard_map/pallas_call | solution.py:258
  123.5 2.9 %shard_map.81 = bf16[512,2048]{1,0:T(8,128)(2,1)} custom-call(s32[2]{0:T(128)S(1)} %pad_add_fusion.place_ref, bf16[512,384]{1,0:T(8,128)(2,1)S(1)} %multiply_convert_fusion.1.mine_ref, bf16[512,384]{1,0:T(8,128)(2,1)S(1)} %collective-permute-done.18.other_ref, bf16[512,2048]{1,0:T(8,128)(2,1)} %shard_map.80.whole_ref), custom_call_target="tpu_custom_call", output_to_operand_aliasing={{}: (3, {})} | custom-call | bytes 1572864 | tf_op jit(solution)/shard_map/pallas_call | solution.py:258
  (54 shorter events, 10.4 us)
Async XLA Ops:
  1.6 10.7 %collective-permute-start = (bf16[128,1280]{1,0:T(8,128)(2,1)S(1)}, bf16[128,1280]{1,0:T(8,128)(2,1)S(1)}, u32[]{:S(2)}, u32[]{:S(2)}) collective-permute-start(bf16[128,1280]{1,0:T(8,128)(2,1)S(1)} %slice.41.refs_0_), channel_id=1, source_target_pairs={{0,2},{2,4},{4,6},{6,7},{7,5},{5,3},{3,1},{1,0},{8,10},{10,12},{12... | collective-permute-start | bytes 983048 | tf_op jit(solution)/shard_map/ppermute | solution.py:293
  4.7 9.5 %collective-permute-start.2 = (bf16[128,1280]{1,0:T(8,128)(2,1)S(1)}, bf16[128,1280]{1,0:T(8,128)(2,1)S(1)}, u32[]{:S(2)}, u32[]{:S(2)}) collective-permute-start(bf16[128,1280]{1,0:T(8,128)(2,1)S(1)} %slice.41.refs_0_), channel_id=1, source_target_pairs={{0,1},{2,0},{4,2},{6,4},{7,6},{5,7},{3,5},{1,3},{8,9},{10,8},{12,1... | collective-permute-start | bytes 983048 | tf_op jit(solution)/shard_map/ppermute | solution.py:294
  12.3 8.9 %collective-permute-start.1 = (bf16[128,1280]{1,0:T(8,128)(2,1)S(1)}, bf16[128,1280]{1,0:T(8,128)(2,1)S(1)}, u32[]{:S(2)}, u32[]{:S(2)}) collective-permute-start(bf16[128,1280]{1,0:T(8,128)(2,1)S(1)} %collective-permute-done.refs_1_), channel_id=1, source_target_pairs={{0,2},{2,4},{4,6},{6,7},{7,5},{5,3},{3,1},{1,0},{8,10},{10,12},{12... | collective-permute-start | bytes 983048 | tf_op jit(solution)/shard_map/ppermute | solution.py:293
  14.2 8.6 %collective-permute-start.3 = (bf16[128,1280]{1,0:T(8,128)(2,1)S(1)}, bf16[128,1280]{1,0:T(8,128)(2,1)S(1)}, u32[]{:S(2)}, u32[]{:S(2)}) collective-permute-start(bf16[128,1280]{1,0:T(8,128)(2,1)S(1)} %collective-permute-done.2.refs_2_), channel_id=1, source_target_pairs={{0,1},{2,0},{4,2},{6,4},{7,6},{5,7},{3,5},{1,3},{8,9},{10,8},{12,1... | collective-permute-start | bytes 983048 | tf_op jit(solution)/shard_map/ppermute | solution.py:294
  21.2 8.0 %collective-permute-start.12 = (bf16[128,1280]{1,0:T(8,128)(2,1)S(1)}, bf16[128,1280]{1,0:T(8,128)(2,1)S(1)}, u32[]{:S(2)}, u32[]{:S(2)}) collective-permute-start(bf16[128,1280]{1,0:T(8,128)(2,1)S(1)} %collective-permute-done.1.refs_3_), channel_id=1, source_target_pairs={{0,2},{2,4},{4,6},{6,7},{7,5},{5,3},{3,1},{1,0},{8,10},{10,12},{12... | collective-permute-start | bytes 983048 | tf_op jit(solution)/shard_map/ppermute | solution.py:293
  22.7 7.9 %collective-permute-start.13 = (bf16[128,1280]{1,0:T(8,128)(2,1)S(1)}, bf16[128,1280]{1,0:T(8,128)(2,1)S(1)}, u32[]{:S(2)}, u32[]{:S(2)}) collective-permute-start(bf16[128,1280]{1,0:T(8,128)(2,1)S(1)} %collective-permute-done.3.refs_4_), channel_id=1, source_target_pairs={{0,1},{2,0},{4,2},{6,4},{7,6},{5,7},{3,5},{1,3},{8,9},{10,8},{12,1... | collective-permute-start | bytes 983048 | tf_op jit(solution)/shard_map/ppermute | solution.py:294
  29.2 19.8 %collective-permute-start.14 = (bf16[64,1280]{1,0:T(8,128)(2,1)S(1)}, bf16[64,1280]{1,0:T(8,128)(2,1)S(1)}, u32[]{:S(2)}, u32[]{:S(2)}) collective-permute-start(bf16[64,1280]{1,0:T(8,128)(2,1)S(1)} %slice.44), channel_id=1, source_target_pairs={{0,2},{2,4},{4,6},{6,7},{7,5},{5,3},{3,1},{1,0},{8,10},{10,12},{12... | collective-permute-start | bytes 491528 | tf_op jit(solution)/shard_map/ppermute | solution.py:297
  30.6 18.4 %collective-permute-start.15 = (bf16[64,1280]{1,0:T(8,128)(2,1)S(1)}, bf16[64,1280]{1,0:T(8,128)(2,1)S(1)}, u32[]{:S(2)}, u32[]{:S(2)}) collective-permute-start(bf16[64,1280]{1,0:T(8,128)(2,1)S(1)} %slice.45), channel_id=1, source_target_pairs={{0,1},{2,0},{4,2},{6,4},{7,6},{5,7},{3,5},{1,3},{8,9},{10,8},{12,1... | collective-permute-start | bytes 491528 | tf_op jit(solution)/shard_map/ppermute | solution.py:298
  32.3 3.3 %copy-start.3 = (bf16[3,3,2,512]{3,2,1,0:T(2,128)(2,1)S(1)}, bf16[3,3,2,512]{3,2,1,0:T(2,128)(2,1)}, u32[]{:S(2)}) copy-start(bf16[3,3,2,512]{3,2,1,0:T(2,128)(2,1)} %param.6) | copy-start | bytes 55300
  35.7 2.5 %copy-start.4 = (f32[1,2048]{1,0:T(1,128)S(1)}, f32[1,2048]{1,0:T(1,128)}, u32[]{:S(2)}) copy-start(f32[1,2048]{1,0:T(1,128)} %param.9) | copy-start | bytes 24580
  44.2 1.4 %copy-start = (f32[8,128,512]{2,1,0:T(8,128)}, f32[8,128,512]{2,1,0:T(8,128)S(1)}, u32[]{:S(2)}) copy-start(f32[8,128,512]{2,1,0:T(8,128)S(1)} %get-tuple-element.19.gate_ref) | copy-start | bytes 6291460
  45.6 1.3 %copy-start.1 = (f32[8,128,512]{2,1,0:T(8,128)}, f32[8,128,512]{2,1,0:T(8,128)S(1)}, u32[]{:S(2)}) copy-start(f32[8,128,512]{2,1,0:T(8,128)S(1)} %get-tuple-element.20.value_ref) | copy-start | bytes 6291460
  47.0 7.4 %collective-permute-start.4 = (bf16[128,768]{1,0:T(8,128)(2,1)S(1)}, bf16[128,768]{1,0:T(8,128)(2,1)S(1)}, u32[]{:S(2)}, u32[]{:S(2)}) collective-permute-start(bf16[128,768]{1,0:T(8,128)(2,1)S(1)} %slice.40.refs_0_), channel_id=1, source_target_pairs={{0,2},{2,4},{4,6},{6,7},{7,5},{5,3},{3,1},{1,0},{8,10},{10,12},{12... | collective-permute-start | bytes 589832 | tf_op jit(solution)/shard_map/ppermute | solution.py:293
  48.3 7.5 %collective-permute-start.5 = (bf16[128,768]{1,0:T(8,128)(2,1)S(1)}, bf16[128,768]{1,0:T(8,128)(2,1)S(1)}, u32[]{:S(2)}, u32[]{:S(2)}) collective-permute-start(bf16[128,768]{1,0:T(8,128)(2,1)S(1)} %slice.40.refs_0_), channel_id=1, source_target_pairs={{0,1},{2,0},{4,2},{6,4},{7,6},{5,7},{3,5},{1,3},{8,9},{10,8},{12,1... | collective-permute-start | bytes 589832 | tf_op jit(solution)/shard_map/ppermute | solution.py:294
  54.3 24.8 %collective-permute-start.19 = (bf16[512,640]{1,0:T(8,128)(2,1)S(1)}, bf16[512,640]{1,0:T(8,128)(2,1)S(1)}, u32[]{:S(2)}, u32[]{:S(2)}) collective-permute-start(bf16[512,640]{1,0:T(8,128)(2,1)S(1)} %get-tuple-element.25), channel_id=1, source_target_pairs={{0,8},{8,0},{16,24},{24,16},{1,9},{9,1},{17,25},{25,17},{2,10},{10... | collective-permute-start | bytes 1966088 | tf_op jit(solution)/shard_map/ppermute | solution.py:304
  54.4 7.3 %collective-permute-start.6 = (bf16[128,768]{1,0:T(8,128)(2,1)S(1)}, bf16[128,768]{1,0:T(8,128)(2,1)S(1)}, u32[]{:S(2)}, u32[]{:S(2)}) collective-permute-start(bf16[128,768]{1,0:T(8,128)(2,1)S(1)} %collective-permute-done.4.refs_1_), channel_id=1, source_target_pairs={{0,2},{2,4},{4,6},{6,7},{7,5},{5,3},{3,1},{1,0},{8,10},{10,12},{12... | collective-permute-start | bytes 589832 | tf_op jit(solution)/shard_map/ppermute | solution.py:293
  55.8 7.2 %collective-permute-start.7 = (bf16[128,768]{1,0:T(8,128)(2,1)S(1)}, bf16[128,768]{1,0:T(8,128)(2,1)S(1)}, u32[]{:S(2)}, u32[]{:S(2)}) collective-permute-start(bf16[128,768]{1,0:T(8,128)(2,1)S(1)} %collective-permute-done.5.refs_2_), channel_id=1, source_target_pairs={{0,1},{2,0},{4,2},{6,4},{7,6},{5,7},{3,5},{1,3},{8,9},{10,8},{12,1... | collective-permute-start | bytes 589832 | tf_op jit(solution)/shard_map/ppermute | solution.py:294
  61.7 6.5 %collective-permute-start.8 = (bf16[128,768]{1,0:T(8,128)(2,1)S(1)}, bf16[128,768]{1,0:T(8,128)(2,1)S(1)}, u32[]{:S(2)}, u32[]{:S(2)}) collective-permute-start(bf16[128,768]{1,0:T(8,128)(2,1)S(1)} %collective-permute-done.6.refs_3_), channel_id=1, source_target_pairs={{0,2},{2,4},{4,6},{6,7},{7,5},{5,3},{3,1},{1,0},{8,10},{10,12},{12... | collective-permute-start | bytes 589832 | tf_op jit(solution)/shard_map/ppermute | solution.py:293
  63.1 6.5 %collective-permute-start.9 = (bf16[128,768]{1,0:T(8,128)(2,1)S(1)}, bf16[128,768]{1,0:T(8,128)(2,1)S(1)}, u32[]{:S(2)}, u32[]{:S(2)}) collective-permute-start(bf16[128,768]{1,0:T(8,128)(2,1)S(1)} %collective-permute-done.7.refs_4_), channel_id=1, source_target_pairs={{0,1},{2,0},{4,2},{6,4},{7,6},{5,7},{3,5},{1,3},{8,9},{10,8},{12,1... | collective-permute-start | bytes 589832 | tf_op jit(solution)/shard_map/ppermute | solution.py:294
  68.2 4.7 %collective-permute-start.10 = (bf16[64,768]{1,0:T(8,128)(2,1)S(1)}, bf16[64,768]{1,0:T(8,128)(2,1)S(1)}, u32[]{:S(2)}, u32[]{:S(2)}) collective-permute-start(bf16[64,768]{1,0:T(8,128)(2,1)S(1)} %slice.42), channel_id=1, source_target_pairs={{0,2},{2,4},{4,6},{6,7},{7,5},{5,3},{3,1},{1,0},{8,10},{10,12},{12... | collective-permute-start | bytes 294920 | tf_op jit(solution)/shard_map/ppermute | solution.py:297
  69.6 4.7 %collective-permute-start.11 = (bf16[64,768]{1,0:T(8,128)(2,1)S(1)}, bf16[64,768]{1,0:T(8,128)(2,1)S(1)}, u32[]{:S(2)}, u32[]{:S(2)}) collective-permute-start(bf16[64,768]{1,0:T(8,128)(2,1)S(1)} %slice.43), channel_id=1, source_target_pairs={{0,1},{2,0},{4,2},{6,4},{7,6},{5,7},{3,5},{1,3},{8,9},{10,8},{12,1... | collective-permute-start | bytes 294920 | tf_op jit(solution)/shard_map/ppermute | solution.py:298
  79.1 1.8 %collective-permute-start.16 = (bf16[512,384]{1,0:T(8,128)(2,1)S(1)}, bf16[512,384]{1,0:T(8,128)(2,1)S(1)}, u32[]{:S(2)}, u32[]{:S(2)}) collective-permute-start(bf16[512,384]{1,0:T(8,128)(2,1)S(1)} %get-tuple-element.23), channel_id=1, source_target_pairs={{0,8},{8,0},{16,24},{24,16},{1,9},{9,1},{17,25},{25,17},{2,10},{10... | collective-permute-start | bytes 1179656 | tf_op jit(solution)/shard_map/ppermute | solution.py:304
  79.2 17.6 %collective-permute-start.20 = (bf16[512,640]{1,0:T(8,128)(2,1)S(1)}, bf16[512,640]{1,0:T(8,128)(2,1)S(1)}, u32[]{:S(2)}, u32[]{:S(2)}) collective-permute-start(bf16[512,640]{1,0:T(8,128)(2,1)S(1)} %add_convert_fusion), channel_id=1, source_target_pairs={{0,16},{8,24},{16,0},{24,8},{1,17},{9,25},{17,1},{25,9},{2,18},{10... | collective-permute-start | bytes 1966088 | tf_op jit(solution)/shard_map/ppermute | solution.py:304
  80.8 24.3 %copy-start.2 = (f32[1024,512]{1,0:T(8,128)S(1)}, f32[1024,512]{1,0:T(8,128)}, u32[]{:S(2)}) copy-start(f32[1024,512]{1,0:T(8,128)} %get-tuple-element.18) | copy-start | bytes 6291460
  80.9 24.0 %collective-permute-start.17 = (bf16[512,384]{1,0:T(8,128)(2,1)S(1)}, bf16[512,384]{1,0:T(8,128)(2,1)S(1)}, u32[]{:S(2)}, u32[]{:S(2)}) collective-permute-start(bf16[512,384]{1,0:T(8,128)(2,1)S(1)} %add_convert_fusion.1), channel_id=1, source_target_pairs={{0,16},{8,24},{16,0},{24,8},{1,17},{9,25},{17,1},{25,9},{2,18},{10... | collective-permute-start | bytes 1179656 | tf_op jit(solution)/shard_map/ppermute | solution.py:304
  97.0 23.2 %collective-permute-start.21 = (bf16[512,640]{1,0:T(8,128)(2,1)S(1)}, bf16[512,640]{1,0:T(8,128)(2,1)S(1)}, u32[]{:S(2)}, u32[]{:S(2)}) collective-permute-start(bf16[512,640]{1,0:T(8,128)(2,1)S(1)} %multiply_convert_fusion.mine_ref), channel_id=1, source_target_pairs={{0,8},{8,0},{16,24},{24,16},{1,9},{9,1},{17,25},{25,17},{2,10},{10... | collective-permute-start | bytes 1966088 | tf_op jit(solution)/shard_map/ppermute | solution.py:304
  105.0 18.5 %collective-permute-start.18 = (bf16[512,384]{1,0:T(8,128)(2,1)S(1)}, bf16[512,384]{1,0:T(8,128)(2,1)S(1)}, u32[]{:S(2)}, u32[]{:S(2)}) collective-permute-start(bf16[512,384]{1,0:T(8,128)(2,1)S(1)} %multiply_convert_fusion.1.mine_ref), channel_id=1, source_target_pairs={{0,8},{8,0},{16,24},{24,16},{1,9},{9,1},{17,25},{25,17},{2,10},{10... | collective-permute-start | bytes 1179656 | tf_op jit(solution)/shard_map/ppermute | solution.py:304
  113.1 1.4 %collective-permute-start.22 = (f32[18,512]{1,0:T(8,128)S(1)}, f32[18,512]{1,0:T(8,128)S(1)}, u32[]{:S(2)}, u32[]{:S(2)}) collective-permute-start(f32[18,512]{1,0:T(8,128)S(1)} %get-tuple-element.26), channel_id=1, source_target_pairs={{0,8},{8,0},{16,24},{24,16},{1,9},{9,1},{17,25},{25,17},{2,10},{10... | collective-permute-start | bytes 110600 | tf_op jit(solution)/shard_map/ppermute | solution.py:304
  114.5 5.1 %collective-permute-start.23 = (f32[18,512]{1,0:T(8,128)S(1)}, f32[18,512]{1,0:T(8,128)S(1)}, u32[]{:S(2)}, u32[]{:S(2)}) collective-permute-start(f32[18,512]{1,0:T(8,128)S(1)} %add.22), channel_id=1, source_target_pairs={{0,16},{8,24},{16,0},{24,8},{1,17},{9,25},{17,1},{25,9},{2,18},{10... | collective-permute-start | bytes 110600 | tf_op jit(solution)/shard_map/ppermute | solution.py:304

commit v2 on v0

v2 whole, which is shorter than its diff:
```python
import functools
import math

import jax
import jax.numpy as jnp
from jax import lax
from jax.experimental import pallas as pl
from jax.experimental.pallas import tpu as pltpu
from jax.sharding import PartitionSpec as P

F32 = jnp.float32
BF16 = jnp.bfloat16
PAD = 8
TILE = 16
LANES = 128
VMEM_BYTES = 20 * 1024 * 1024
VMEM = pl.BlockSpec(memory_space=pltpu.VMEM)
SMEM = pl.BlockSpec(memory_space=pltpu.SMEM)


def ring_order(n):
    return [2 * i if i < n // 2 else 2 * (n - 1 - i) + 1 for i in range(n)]


def at_ring(position, n):
    position = lax.rem(position + 2 * n, n)
    return jnp.where(position < n // 2, 2 * position, 2 * (n - 1 - position) + 1)


def ring_place(index, n):
    half = index // 2
    return jnp.where(lax.rem(index, 2) == 0, half, n - 1 - half)


def split_widths(depth):
    return [depth // 2, depth // 2]


def params(limit=VMEM_BYTES):
    return pltpu.CompilerParams(vmem_limit_bytes=limit)


def cost(flops, moved, transcendentals=0):
    return pl.CostEstimate(flops=flops, bytes_accessed=moved, transcendentals=transcendentals)


def clear_edges(pad_ref, height, across):
    lanes = pad_ref.shape[-1]
    for k in range(2):
        pad_ref[k, 0] = jnp.zeros(pad_ref.shape[2:], F32)
        pad_ref[k, height + 1] = jnp.zeros(pad_ref.shape[2:], F32)

        @pl.loop(0, height)
        def _(r):
            pad_ref[k, r + 1, 0:PAD] = jnp.zeros((PAD, lanes), F32)
            pad_ref[k, r + 1, PAD + across : 2 * PAD + across] = jnp.zeros((PAD, lanes), F32)


def conv_kernel(hidden_ref, weight_ref, gate_ref, value_ref, mixed_ref, pad_ref):
    _, height, across, channels = hidden_ref.shape
    clear_edges(pad_ref, height, across)

    @pl.loop(0, channels // LANES)
    def _(c):
        lanes = pl.ds(pl.multiple_of(c * LANES, LANES), LANES)

        @pl.loop(0, height)
        def _(r):
            for k in range(2):
                pad_ref[k, r + 1, PAD : PAD + across] = hidden_ref[k, r, :, lanes].astype(F32)

        weights = weight_ref[:, lanes]

        @pl.loop(0, height)
        def _(r):
            mixed = []
            for t in range(across // TILE):
                w = t * TILE
                parts = []
                for k in range(2):
                    total = None
                    for i in range(3):
                        for j in range(3):
                            view = pad_ref[k, r + i, PAD + w + j - 1 : PAD + w + j - 1 + TILE]
                            term = weights[(i * 3 + j) * 2 + k][None, :] * view
                            total = term if total is None else total + term
                    parts.append(total)
                value, gate = parts
                sig = 1.0 / (1.0 + jnp.exp(-gate))
                gated = gate * sig
                gate_ref[r, w : w + TILE, lanes] = gated.astype(BF16)
                value_ref[r, w : w + TILE, lanes] = (
                    value * sig * (1.0 + gate * (1.0 - sig))
                ).astype(BF16)
                mixed.append((value * gated).astype(BF16))
            tokens = pl.ds(pl.multiple_of(r * across, LANES), across)
            mixed_ref[lanes, tokens] = jnp.concatenate(mixed, axis=0).T


def conv_parts(hidden, weights):
    _, height, across, channels = hidden.shape
    size = height * across * channels
    return pl.pallas_call(
        conv_kernel,
        in_specs=[VMEM, VMEM],
        out_specs=[VMEM] * 3,
        out_shape=[
            jax.ShapeDtypeStruct((height, across, channels), BF16),
            jax.ShapeDtypeStruct((height, across, channels), BF16),
            jax.ShapeDtypeStruct((channels, height * across), BF16),
        ],
        scratch_shapes=[pltpu.VMEM((2, height + 2, across + 2 * PAD, LANES), F32)],
        compiler_params=params(),
        cost_estimate=cost(size * 60, size * 14, size),
    )(hidden, weights)


def gather_rows(n, place_ref, pieces, full_ref):
    across = pieces[0].shape[0]
    spot = ring_place(place_ref[0], n)
    starts = [at_ring(spot, n) * across]
    for step in range(1, n // 2):
        starts.append(at_ring(spot - step, n) * across)
        starts.append(at_ring(spot + step, n) * across)
    far = at_ring(spot + n // 2, n) * across
    starts.extend([far, far + across // 2])
    for piece, start in zip(pieces, starts):
        rows = piece.shape[0]
        full_ref[pl.ds(pl.multiple_of(start, rows), rows)] = piece[...]


def column_sums(place_ref, mixed_ref, full_ref, send_ref, keep_ref):
    core = place_ref[1]
    half = full_ref.shape[1] // 2
    for out_ref, column in ((send_ref, 1 - core), (keep_ref, core)):
        columns = pl.ds(pl.multiple_of(column * half, LANES), half)
        out_ref[...] = jnp.dot(
            mixed_ref[...], full_ref[:, columns], preferred_element_type=F32
        ).astype(out_ref.dtype)


def row_products(offset, full_ref, weight_ref, before_ref, grad_ref):
    tokens, width = full_ref.shape
    slab = min(tokens, 512)

    @pl.loop(0, tokens // slab)
    def _(s):
        rows = pl.ds(pl.multiple_of(s * slab, slab), slab)
        grad = lax.dot_general(
            full_ref[rows],
            weight_ref[:, offset : offset + width],
            (((1,), (1,)), ((), ())),
            preferred_element_type=F32,
        )
        if before_ref is not None:
            grad = grad + before_ref[rows]
        grad_ref[rows] = grad


def chunk_kernel(n, offset, product, added, place_ref, *refs):
    pieces, refs = refs[: n + 1], refs[n + 1 :]
    full_ref = refs[-1]
    gather_rows(n, place_ref, pieces, full_ref)
    if not product:
        mixed_ref, send_ref, keep_ref = refs[:3]
    elif added:
        mixed_ref, weight_ref, before_ref, send_ref, keep_ref, grad_ref = refs[:6]
    else:
        mixed_ref, weight_ref, send_ref, keep_ref, grad_ref = refs[:5]
        before_ref = None
    column_sums(place_ref, mixed_ref, full_ref, send_ref, keep_ref)
    if product:
        row_products(offset, full_ref, weight_ref, before_ref, grad_ref)


def chunk_parts(n, place, pieces, offset, mixed, weight=None, before=None):
    across, width = pieces[0].shape
    channels, tokens = mixed.shape
    product, added = weight is not None, before is not None
    operands = [*pieces, mixed] + [v for v in (weight, before) if v is not None]
    out_shape = [
        jax.ShapeDtypeStruct((channels, width // 2), BF16),
        jax.ShapeDtypeStruct((channels, width // 2), F32),
    ]
    if product:
        out_shape.append(jax.ShapeDtypeStruct((tokens, channels), F32))
    return pl.pallas_call(
        functools.partial(chunk_kernel, n, offset, product, added),
        in_specs=[SMEM] + [VMEM] * len(operands),
        out_specs=[VMEM] * len(out_shape),
        out_shape=out_shape,
        scratch_shapes=[pltpu.VMEM((tokens, width), BF16)],
        compiler_params=params(),
        cost_estimate=cost(
            2 * (1 + product) * tokens * channels * width,
            tokens * width * 2 + channels * width * 5 + tokens * channels * 10,
        ),
    )(place, *operands)


def grads_kernel(n, offset, place_ref, *refs):
    pieces, refs = refs[: n + 1], refs[n + 1 :]
    weight_ref, before_ref, gate_ref, value_ref, hidden_ref, taps_ref = refs[:6]
    out_ref, term_ref, full_ref, grad_ref, pad_ref = refs[6:]
    _, height, across, channels = hidden_ref.shape
    gather_rows(n, place_ref, pieces, full_ref)
    row_products(offset, full_ref, weight_ref, before_ref, grad_ref)
    clear_edges(pad_ref, height, across)

    @pl.loop(0, channels // LANES)
    def _(c):
        lanes = pl.ds(pl.multiple_of(c * LANES, LANES), LANES)

        @pl.loop(0, height)
        def _(r):
            grad = grad_ref[pl.ds(pl.multiple_of(r * across, across), across), lanes]
            for k, factor in enumerate((gate_ref, value_ref)):
                pad_ref[k, r + 1, PAD : PAD + across] = grad * factor[r, :, lanes].astype(F32)

        weights = taps_ref[:, lanes]
        for k in range(2):

            def row(r, sums):
                sums = list(sums)
                for t in range(across // TILE):
                    w = t * TILE
                    own = hidden_ref[k, r, w : w + TILE, lanes].astype(F32)
                    total = None
                    for i in range(3):
                        for j in range(3):
                            view = pad_ref[k, r + 2 - i, PAD + w + 1 - j : PAD + w + 1 - j + TILE]
                            term = weights[(i * 3 + j) * 2 + k][None, :] * view
                            total = term if total is None else total + term
                            both = view * own
                            sums[i * 3 + j] = sums[i * 3 + j] + (both[:8] + both[8:])
                    out_ref[k, r, w : w + TILE, lanes] = total.astype(BF16)
                return tuple(sums)

            sums = lax.fori_loop(0, height, row, tuple(jnp.zeros((8, LANES), F32) for _ in range(9)))
            for tap in range(9):
                term_ref[tap * 2 + k : tap * 2 + k + 1, lanes] = jnp.sum(
                    sums[tap], axis=0, keepdims=True
                )


def grads(n, place, pieces, offset, weight, before, gate_part, value_part, hidden, taps):
    _, height, across, channels = hidden.shape
    width = pieces[0].shape[1]
    tokens = height * across
    size = tokens * channels
    operands = [*pieces, weight, before, gate_part, value_part, hidden, taps]
    return pl.pallas_call(
        functools.partial(grads_kernel, n, offset),
        in_specs=[SMEM] + [VMEM] * len(operands),
        out_specs=[VMEM, VMEM],
        out_shape=[
            jax.ShapeDtypeStruct(hidden.shape, BF16),
            jax.ShapeDtypeStruct((18, channels), F32),
        ],
        scratch_shapes=[
            pltpu.VMEM((tokens, width), BF16),
            pltpu.VMEM((tokens, channels), F32),
            pltpu.VMEM((2, height + 2, across + 2 * PAD, LANES), F32),
        ],
        compiler_params=params(),
        cost_estimate=cost(size * 80, size * 20),
    )(place, *operands)


def put_kernel(offset, place_ref, mine_ref, other_ref, *refs):
    out_ref, sems = refs[-2:]
    half = mine_ref.shape[1]
    copies = []
    for slot, (ref, column) in enumerate(((mine_ref, place_ref[1]), (other_ref, 1 - place_ref[1]))):
        columns = pl.ds(pl.multiple_of(offset + column * half, LANES), half)
        copies.append(pltpu.make_async_copy(ref, out_ref.at[:, columns], sems.at[slot]))
    for copy in copies:
        copy.start()
    for copy in copies:
        copy.wait()


def put(place, mine, other, whole, offset, shape):
    hbm = pl.BlockSpec(memory_space=pl.ANY)
    arrays = [mine, other] + ([] if whole is None else [whole])
    return pl.pallas_call(
        functools.partial(put_kernel, offset),
        in_specs=[SMEM] + [hbm] * len(arrays),
        out_specs=hbm,
        out_shape=jax.ShapeDtypeStruct(shape, BF16),
        scratch_shapes=[pltpu.SemaphoreType.DMA((2,))],
        input_output_aliases={} if whole is None else {3: 0},
        compiler_params=params(),
        cost_estimate=cost(0, mine.size * 8),
    )(place, *arrays)


class Ring:
    def __init__(self, n):
        ring = ring_order(n)
        self.right = [(ring[i], ring[(i + 1) % n]) for i in range(n)]
        self.left = [(ring[i], ring[(i - 1) % n]) for i in range(n)]
        self.last = n // 2
        self.stage = 0

    def begin(self, own):
        self.edge = [own, own]
        self.pieces = [own]

    def step(self):
        self.stage += 1
        up, down = self.edge
        if self.stage == self.last:
            half = up.shape[0] // 2
            up, down = up[:half], down[half:]
        up = lax.ppermute(up, "tensor", self.right)
        down = lax.ppermute(down, "tensor", self.left)
        self.edge = [up, down]
        self.pieces += [up, down]


class Order:
    def __init__(self, token):
        self.token = token

    def after(self, values, waited):
        flat, tree = jax.tree.flatten((values, waited, self.token))
        values, _, self.token = jax.tree.unflatten(tree, lax.optimization_barrier(flat))
        return values


def swap(value, bit):
    n = lax.axis_size("dp")
    return lax.ppermute(value, "dp", [(i, i ^ bit) for i in range(n)])


def sum_rest(value, low=2):
    bit = low
    while bit < lax.axis_size("dp"):
        value = value.astype(F32) + swap(value, bit).astype(F32)
        if bit * 2 < lax.axis_size("dp"):
            value = value.astype(BF16)
        bit *= 2
    return value


def on_device(hidden_in, conv_weight, proj_weight, out_grad, sample_gate):
    samples, height, across, _, channels = hidden_in.shape
    depth = out_grad.shape[-1]
    n = lax.axis_size("tensor")
    dp = lax.axis_size("dp")
    assert samples == 1 and out_grad.shape[1] == 1 and n % 2 == 0 and dp & (dp - 1) == 0
    grad_scale = 1.0 / math.sqrt(dp * samples * height * across)
    place = jnp.stack([lax.axis_index("tensor"), lax.rem(lax.axis_index("dp"), 2)]).astype(
        jnp.int32
    )
    own = out_grad.reshape(across, depth)
    hidden = jnp.transpose(hidden_in.reshape(height, across, 2, channels), (2, 0, 1, 3))
    taps = conv_weight.astype(F32).reshape(18, channels)

    widths = split_widths(depth)
    offsets = [sum(widths[:k]) for k in range(len(widths))]
    first, second = Ring(n), Ring(n)
    last = n // 2
    order = Order(place)

    def block(k):
        columns = slice(offsets[k], offsets[k] + widths[k])
        return (own[:, columns].astype(F32) * sample_gate[:, columns]).astype(BF16)

    def move(ring, waited=()):
        ring.edge = order.after(ring.edge, waited)
        ring.step()

    first.begin(block(0))
    first.step()
    hidden, source = order.after((hidden, block(1)), ())
    second.begin(source)
    move(first, (first.edge, hidden))
    hidden = order.after(hidden, ())
    conv = conv_parts(hidden, taps)
    for step in range(3, last + 1):
        move(second, (second.edge, conv))
        move(first, first.edge)
    move(second, second.edge)
    pieces = order.after(first.pieces, first.edge)
    send, keep, grad = chunk_parts(n, order.token, pieces, offsets[0], conv[2], proj_weight)
    if second.stage < last:
        second.edge = order.after(second.edge, (second.edge, grad))
        second.step()
    send = order.after(send, grad)
    pair0 = (keep + swap(send, 1).astype(F32)).astype(BF16)
    pair0 = order.after(pair0, ())
    units = 2
    unit = pair0.shape[1] // units
    sums0 = [sum_rest(pair0[:, u * unit : (u + 1) * unit]) for u in range(units)]

    pieces = order.after(second.pieces, second.edge)
    gate_part, value_part, mixed = conv
    send, keep = chunk_parts(n, order.token, pieces, offsets[1], mixed)
    send = order.after(send, keep)
    pair1 = (keep + swap(send, 1).astype(F32)).astype(BF16)
    pair1 = order.after(pair1, sums0[0])
    sums1 = [sum_rest(pair1[:, u * unit : (u + 1) * unit]) for u in range(units)]
    grad = order.after(grad, ())
    hidden_grad, terms = grads(
        n,
        order.token,
        pieces,
        offsets[1],
        proj_weight,
        grad,
        gate_part,
        value_part,
        hidden,
        taps,
    )
    total = order.after(terms, ())
    bit = 1
    while bit < dp:
        total = total + swap(total, bit)
        bit *= 2
    conv_grad = (total * grad_scale).reshape(3, 3, 2, channels)
    hidden_grad = jnp.transpose(hidden_grad, (1, 2, 0, 3))[None]
    whole = None
    for k, sums in ((0, sums0), (1, sums1)):
        mine = (jnp.concatenate(sums, axis=1) * grad_scale).astype(BF16)
        mine = order.after(mine, ())
        whole = put(order.token, mine, swap(mine, 1), whole, offsets[k], (channels, depth))
    return (hidden_grad, whole, conv_grad)


def solution(mesh):
    in_specs = (
        P("dp", None, None, None, "tensor"),
        P(None, None, None, "tensor"),
        P("tensor", None),
        P("dp", "tensor", None, None),
        P("dp", None),
    )
    out_specs = (
        P("dp", None, None, None, "tensor"),
        P("tensor", None),
        P(None, None, None, "tensor"),
    )
    return jax.shard_map(
        on_device, mesh=mesh, in_specs=in_specs, out_specs=out_specs, check_vma=False
    )
```

time: 191 us -> 91.9 us (0.48)
  waiting for transfers between devices: 111 us -> 34.2 us
  other arithmetic: 31 us -> 1.92 us
  starting transfers between devices: 0.08 us -> 24 us
  Pallas kernels: 0 us -> 23.8 us
  matrix products: 14.4 us -> 0 us
  between operations: 14.2 us -> 0.84 us
  blocking collectives: 12.9 us -> 0 us
    all_gather x1 -> x0, waiting for transfers between devices: 64.5 us -> none  [on_device(): gathered = lax.all_gather(gated_grad, 'tensor', axis=1, tiled=True)]
    psum x1 -> x0, waiting for transfers between devices: 46.4 us -> none  [on_device(): proj_total, kernel_total = lax.psum((proj_sum, kernel_sum), 'dp')]
    ppermute x0 -> x26, waiting for transfers between devices: none -> 34.2 us  [the longest x8 13.8 us: step(): up = lax.ppermute(up, 'tensor', self.right)]
    ppermute x0 -> x26, starting transfers between devices: none -> 24 us  [the longest x8 14.8 us: step(): up = lax.ppermute(up, 'tensor', self.right)]
    pallas_call x0 -> x6, Pallas kernels: none -> 23.8 us  [the longest x1 8.84 us: grads(): pl.pallas_call(functools.partial(grads_kernel, n, offset), in_specs=[SMEM...]
    dot_general x2 -> x0, matrix products: 14.4 us -> none  [the longest x1 7.87 us: on_device(): jnp.einsum('srwc,srwd->cd', mixed_act, gathered, preferred_element_type=j...]
    psum x1 -> x0, blocking collectives: 12.9 us -> none  [on_device(): proj_total, kernel_total = lax.psum((proj_sum, kernel_sum), 'dp')]
    convert_element_type x4 -> x5, other arithmetic: 13.9 us -> 1.62 us  [the longest x1 1.13 us: block(): return (own[:, columns].astype(F32) * sample_gate[:, columns]).astype(BF16)]
  transfers between devices with their start and end apart: 2 -> 26, of which waited for: 2 -> 17; matrix products, arithmetic and copies ran while one was open for 19% -> 7% of each run, Pallas kernels for 0% -> 24%
where the time goes in v2:
time: 91.9 us; the launch traced here: 91.7 us
  waiting for transfers between devices  34.2 us (37%)
  starting transfers between devices  24 us (26%)
  Pallas kernels  23.8 us (26%)
  local copies, waits for them, and re-layouts  6.96 us (8%)
  other arithmetic  1.92 us (2%)
    ppermute x8, starting transfers between devices, step(): up = lax.ppermute(up, 'tensor', self.right)  14.8 us
    ppermute x8, waiting for transfers between devices, step(): up = lax.ppermute(up, 'tensor', self.right)  13.8 us
    ppermute x10, waiting for transfers between devices, swap(): return lax.ppermute(value, 'dp', [(i, i ^ bit) for i in range(n)])  10.4 us
    ppermute x8, waiting for transfers between devices, step(): down = lax.ppermute(down, 'tensor', self.left)  9.99 us
    pallas_call x1, Pallas kernels, grads(): pl.pallas_call(functools.partial(grads_kernel, n, offset), in_specs=[SMEM...  8.84 us
    ppermute x10, starting transfers between devices, swap(): return lax.ppermute(value, 'dp', [(i, i ^ bit) for i in range(n)])  6.48 us
    pallas_call x1, Pallas kernels, conv_parts(): pl.pallas_call(conv_kernel, in_specs=[VMEM, VMEM], out_specs=[VMEM] * 3,...  6.01 us
    pallas_call x2, Pallas kernels, chunk_parts(): pl.pallas_call(functools.partial(chunk_kernel, n, offset, product, added)...  5.87 us
  transfers between devices with their start and end apart: 26, of which 17 were waited for; matrix products, arithmetic and copies ran while one was open for 7% of the time, Pallas kernels for 24%

profile of v2, /device:TPU:0, one launch (start us, length us, event | category | flops | bytes accessed | tf_op | source)
XLA Modules:
  0.0 91.7 jit_solution(17779797241991387030)
XLA Ops:
  2.5 3.1 %collective-permute-start = (bf16[128,1024]{1,0:T(8,128)(2,1)S(1)}, bf16[128,1024]{1,0:T(8,128)(2,1)S(1)}, u32[]{:S(2)}, u32[]{:S(2)}) collective-permute-start(bf16[128,1024]{1,0:T(8,128)(2,1)S(1)} %get-tuple-element.100.refs_0_), channel_id=1, source_target_pairs={{0,2},{2,4},{4,6},{6,7},{7,5},{5,3},{3,1},{1,0},{8,10},{10,12},{12... | collective-permute-start | bytes 786440 | tf_op jit(solution)/shard_map/ppermute | solution.py:316
  5.6 2.0 %copy.12 = bf16[1,8,128,2,512]{4,2,1,3,0:T(8,128)(2,1)S(1)} copy(bf16[1,8,128,2,512]{4,3,2,1,0:T(2,128)(2,1)} %param.5) | data formatting | bytes 4194304 | tf_op args[0]
  7.7 4.1 %collective-permute-done.refs_1_ = bf16[128,1024]{1,0:T(8,128)(2,1)S(1)} collective-permute-done((bf16[128,1024]{1,0:T(8,128)(2,1)S(1)}, bf16[128,1024]{1,0:T(8,128)(2,1)S(1)}, u32[]{:S(2)}, u32[]{:S(2)}) %collective-permute-start) | collective-permute-done | bytes 262176 | tf_op jit(solution)/shard_map/ppermute | solution.py:316
  11.8 1.5 %collective-permute-done.1.refs_2_ = bf16[128,1024]{1,0:T(8,128)(2,1)S(1)} collective-permute-done((bf16[128,1024]{1,0:T(8,128)(2,1)S(1)}, bf16[128,1024]{1,0:T(8,128)(2,1)S(1)}, u32[]{:S(2)}, u32[]{:S(2)}) %collective-permute-start.1) | collective-permute-done | bytes 262176 | tf_op jit(solution)/shard_map/ppermute | solution.py:317
  13.3 1.6 %collective-permute-start.2 = (bf16[128,1024]{1,0:T(8,128)(2,1)S(1)}, bf16[128,1024]{1,0:T(8,128)(2,1)S(1)}, u32[]{:S(2)}, u32[]{:S(2)}) collective-permute-start(bf16[128,1024]{1,0:T(8,128)(2,1)S(1)} %collective-permute-done.refs_1_), channel_id=1, source_target_pairs={{0,2},{2,4},{4,6},{6,7},{7,5},{5,3},{3,1},{1,0},{8,10},{10,12},{12... | collective-permute-start | bytes 786440 | tf_op jit(solution)/shard_map/ppermute | solution.py:316
  15.4 6.0 %shard_map.76 = (bf16[8,128,512]{2,1,0:T(8,128)(2,1)S(1)}, bf16[8,128,512]{2,1,0:T(8,128)(2,1)S(1)}, bf16[512,1024]{1,0:T(8,128)(2,1)S(1)}) custom-call(bf16[2,8,128,512]{3,2,1,0:T(8,128)(2,1)S(1)} %bitcast.13, f32[18,512]{1,0:T(8,128)S(1)} %reshape.26.weight_ref.refs_14_), custom_call_target="tpu_custom_call" | custom-call | flops 31457280 | bytes 7340032 | tf_op jit(solution)/shard_map/pallas_call | solution.py:103
  21.4 1.6 %collective-permute-start.6 = (bf16[128,1024]{1,0:T(8,128)(2,1)S(1)}, bf16[128,1024]{1,0:T(8,128)(2,1)S(1)}, u32[]{:S(2)}, u32[]{:S(2)}) collective-permute-start(bf16[128,1024]{1,0:T(8,128)(2,1)S(1)} %get-tuple-element.121.refs_0_), channel_id=1, source_target_pairs={{0,2},{2,4},{4,6},{6,7},{7,5},{5,3},{3,1},{1,0},{8,10},{10,12},{12... | collective-permute-start | bytes 786440 | tf_op jit(solution)/shard_map/ppermute | solution.py:316
  23.5 1.6 %collective-permute-start.4 = (bf16[128,1024]{1,0:T(8,128)(2,1)S(1)}, bf16[128,1024]{1,0:T(8,128)(2,1)S(1)}, u32[]{:S(2)}, u32[]{:S(2)}) collective-permute-start(bf16[128,1024]{1,0:T(8,128)(2,1)S(1)} %collective-permute-done.2.refs_3_), channel_id=1, source_target_pairs={{0,2},{2,4},{4,6},{6,7},{7,5},{5,3},{3,1},{1,0},{8,10},{10,12},{12... | collective-permute-start | bytes 786440 | tf_op jit(solution)/shard_map/ppermute | solution.py:316
  25.5 5.2 %collective-permute-done.6.refs_1_ = bf16[128,1024]{1,0:T(8,128)(2,1)S(1)} collective-permute-done((bf16[128,1024]{1,0:T(8,128)(2,1)S(1)}, bf16[128,1024]{1,0:T(8,128)(2,1)S(1)}, u32[]{:S(2)}, u32[]{:S(2)}) %collective-permute-start.6) | collective-permute-done | bytes 262176 | tf_op jit(solution)/shard_map/ppermute | solution.py:316
  30.7 1.6 %collective-permute-done.7.refs_2_ = bf16[128,1024]{1,0:T(8,128)(2,1)S(1)} collective-permute-done((bf16[128,1024]{1,0:T(8,128)(2,1)S(1)}, bf16[128,1024]{1,0:T(8,128)(2,1)S(1)}, u32[]{:S(2)}, u32[]{:S(2)}) %collective-permute-start.7) | collective-permute-done | bytes 262176 | tf_op jit(solution)/shard_map/ppermute | solution.py:317
  32.3 1.6 %collective-permute-start.10 = (bf16[128,1024]{1,0:T(8,128)(2,1)S(1)}, bf16[128,1024]{1,0:T(8,128)(2,1)S(1)}, u32[]{:S(2)}, u32[]{:S(2)}) collective-permute-start(bf16[128,1024]{1,0:T(8,128)(2,1)S(1)} %collective-permute-done.6.refs_1_), channel_id=1, source_target_pairs={{0,2},{2,4},{4,6},{6,7},{7,5},{5,3},{3,1},{1,0},{8,10},{10,12},{12... | collective-permute-start | bytes 786440 | tf_op jit(solution)/shard_map/ppermute | solution.py:316
  34.3 2.0 %collective-permute-done.4.refs_5_ = bf16[128,1024]{1,0:T(8,128)(2,1)S(1)} collective-permute-done((bf16[128,1024]{1,0:T(8,128)(2,1)S(1)}, bf16[128,1024]{1,0:T(8,128)(2,1)S(1)}, u32[]{:S(2)}, u32[]{:S(2)}) %collective-permute-start.4) | collective-permute-done | bytes 262176 | tf_op jit(solution)/shard_map/ppermute | solution.py:316
  36.3 1.6 %collective-permute-done.5.refs_6_ = bf16[128,1024]{1,0:T(8,128)(2,1)S(1)} collective-permute-done((bf16[128,1024]{1,0:T(8,128)(2,1)}, bf16[128,1024]{1,0:T(8,128)(2,1)S(1)}, u32[]{:S(2)}, u32[]{:S(2)}) %collective-permute-start.5) | collective-permute-done | bytes 262176 | tf_op jit(solution)/shard_map/ppermute | solution.py:317
  37.9 1.6 %collective-permute-start.8 = (bf16[64,1024]{1,0:T(8,128)(2,1)S(1)}, bf16[64,1024]{1,0:T(8,128)(2,1)S(1)}, u32[]{:S(2)}, u32[]{:S(2)}) collective-permute-start(bf16[64,1024]{1,0:T(8,128)(2,1)S(1)} %slice.40), channel_id=1, source_target_pairs={{0,2},{2,4},{4,6},{6,7},{7,5},{5,3},{3,1},{1,0},{8,10},{10,12},{12... | collective-permute-start | bytes 393224 | tf_op jit(solution)/shard_map/ppermute | solution.py:316
  42.2 1.7 %collective-permute-start.12 = (bf16[128,1024]{1,0:T(8,128)(2,1)S(1)}, bf16[128,1024]{1,0:T(8,128)(2,1)S(1)}, u32[]{:S(2)}, u32[]{:S(2)}) collective-permute-start(bf16[128,1024]{1,0:T(8,128)(2,1)S(1)} %collective-permute-done.10.refs_3_), channel_id=1, source_target_pairs={{0,2},{2,4},{4,6},{6,7},{7,5},{5,3},{3,1},{1,0},{8,10},{10,12},{12... | collective-permute-start | bytes 786440 | tf_op jit(solution)/shard_map/ppermute | solution.py:316
  44.4 1.5 %collective-permute-done.9.refs_8_ = bf16[64,1024]{1,0:T(8,128)(2,1)S(1)} collective-permute-done((bf16[64,1024]{1,0:T(8,128)(2,1)S(1)}, bf16[64,1024]{1,0:T(8,128)(2,1)S(1)}, u32[]{:S(2)}, u32[]{:S(2)}) %collective-permute-start.9) | collective-permute-done | bytes 131104 | tf_op jit(solution)/shard_map/ppermute | solution.py:317
  45.9 3.9 %shard_map.77 = (bf16[512,512]{1,0:T(8,128)(2,1)S(1)}, f32[512,512]{1,0:T(8,128)S(1)}, f32[1024,512]{1,0:T(8,128)S(1)}) custom-call(s32[2]{0:T(128)S(1)} %pad_add_fusion.place_ref, bf16[128,1024]{1,0:T(8,128)(2,1)S(1)} %get-tuple-element.100.refs_0_, bf16[128,1024]{1,0:T(8,128)(2,1)S(1)} %collective-permute-done.refs_1_, ...), custom_call_target="tpu_custom_call" | custom-call | flops 2147483648 | bytes 9961472 | tf_op jit(solution)/shard_map/pallas_call | solution.py:187
  50.5 2.1 %collective-permute-start.14 = (bf16[64,1024]{1,0:T(8,128)(2,1)S(1)}, bf16[64,1024]{1,0:T(8,128)(2,1)S(1)}, u32[]{:S(2)}, u32[]{:S(2)}) collective-permute-start(bf16[64,1024]{1,0:T(8,128)(2,1)S(1)} %slice.42), channel_id=1, source_target_pairs={{0,2},{2,4},{4,6},{6,7},{7,5},{5,3},{3,1},{1,0},{8,10},{10,12},{12... | collective-permute-start | bytes 393224 | tf_op jit(solution)/shard_map/ppermute | solution.py:316
  52.9 1.6 %collective-permute-start.18 = (bf16[512,256]{1,0:T(8,128)(2,1)S(1)}, bf16[512,256]{1,0:T(8,128)(2,1)S(1)}, u32[]{:S(2)}, u32[]{:S(2)}) collective-permute-start(bf16[512,256]{1,0:T(8,128)(2,1)S(1)} %get-tuple-element.153), channel_id=1, source_target_pairs={{0,16},{8,24},{16,0},{24,8},{1,17},{9,25},{17,1},{25,9},{2,18},{10... | collective-permute-start | bytes 786440 | tf_op jit(solution)/shard_map/ppermute | solution.py:334
  55.0 1.5 %collective-permute-done.14.refs_7_ = bf16[64,1024]{1,0:T(8,128)(2,1)S(1)} collective-permute-done((bf16[64,1024]{1,0:T(8,128)(2,1)S(1)}, bf16[64,1024]{1,0:T(8,128)(2,1)S(1)}, u32[]{:S(2)}, u32[]{:S(2)}) %collective-permute-start.14) | collective-permute-done | bytes 131104 | tf_op jit(solution)/shard_map/ppermute | solution.py:316
  56.5 1.8 %collective-permute-done.15.refs_8_ = bf16[64,1024]{1,0:T(8,128)(2,1)S(1)} collective-permute-done((bf16[64,1024]{1,0:T(8,128)(2,1)S(1)}, bf16[64,1024]{1,0:T(8,128)(2,1)S(1)}, u32[]{:S(2)}, u32[]{:S(2)}) %collective-permute-start.15) | collective-permute-done | bytes 131104 | tf_op jit(solution)/shard_map/ppermute | solution.py:317
  58.3 2.0 %shard_map.78 = (bf16[512,512]{1,0:T(8,128)(2,1)S(1)}, f32[512,512]{1,0:T(8,128)S(1)}) custom-call(s32[2]{0:T(128)S(1)} %pad_add_fusion.place_ref, bf16[128,1024]{1,0:T(8,128)(2,1)S(1)} %get-tuple-element.121.refs_0_, bf16[128,1024]{1,0:T(8,128)(2,1)S(1)} %collective-permute-done.6.refs_1_, bf16[128,1024]{1,0:T(8,128)(2,1)S(1)} %collective-permute-done.7.refs_2_, ...), custom_call_target="tpu_custom_call" | custom-call | flops 1073741824 | bytes 9961472 | tf_op jit(solution)/shard_map/pallas_call | solution.py:187
  60.3 1.8 %collective-permute-done.18 = bf16[512,256]{1,0:T(8,128)(2,1)S(1)} collective-permute-done((bf16[512,256]{1,0:T(8,128)(2,1)S(1)}, bf16[512,256]{1,0:T(8,128)(2,1)S(1)}, u32[]{:S(2)}, u32[]{:S(2)}) %collective-permute-start.18) | collective-permute-done | bytes 262176 | tf_op jit(solution)/shard_map/ppermute | solution.py:334
  62.1 4.9 %collective-permute-done.21 = bf16[512,256]{1,0:T(8,128)(2,1)S(1)} collective-permute-done((bf16[512,256]{1,0:T(8,128)(2,1)S(1)}, bf16[512,256]{1,0:T(8,128)(2,1)S(1)}, u32[]{:S(2)}, u32[]{:S(2)}) %collective-permute-start.21) | collective-permute-done | bytes 262176 | tf_op jit(solution)/shard_map/ppermute | solution.py:334
  67.3 1.6 %collective-permute-start.19 = (bf16[512,256]{1,0:T(8,128)(2,1)S(1)}, bf16[512,256]{1,0:T(8,128)(2,1)S(1)}, u32[]{:S(2)}, u32[]{:S(2)}) collective-permute-start(bf16[512,256]{1,0:T(8,128)(2,1)S(1)} %get-tuple-element.156), channel_id=1, source_target_pairs={{0,16},{8,24},{16,0},{24,8},{1,17},{9,25},{17,1},{25,9},{2,18},{10... | collective-permute-start | bytes 786440 | tf_op jit(solution)/shard_map/ppermute | solution.py:334
  69.5 8.8 %shard_map.79 = (bf16[2,8,128,512]{3,2,1,0:T(8,128)(2,1)S(1)}, f32[18,512]{1,0:T(8,128)S(1)}) custom-call(s32[2]{0:T(128)S(1)} %pad_add_fusion.place_ref, bf16[128,1024]{1,0:T(8,128)(2,1)S(1)} %get-tuple-element.121.refs_0_, bf16[128,1024]{1,0:T(8,128)(2,1)S(1)} %collective-permute-done.6.refs_1_, bf16[128,1024]{1,0:T(8,128)(2,1)S(1)} %collective-permute-done.7.refs_2_, ...), custom_call_target="tpu_custom_call" | custom-call | flops 41943040 | bytes 10485760 | tf_op jit(solution)/shard_map/pallas_call | solution.py:252
  78.4 2.2 %collective-permute-done.20 = bf16[512,256]{1,0:T(8,128)(2,1)S(1)} collective-permute-done((bf16[512,256]{1,0:T(8,128)(2,1)S(1)}, bf16[512,256]{1,0:T(8,128)(2,1)S(1)}, u32[]{:S(2)}, u32[]{:S(2)}) %collective-permute-start.20) | collective-permute-done | bytes 262176 | tf_op jit(solution)/shard_map/ppermute | solution.py:334
  81.4 1.5 %collective-permute-done.24 = f32[18,512]{1,0:T(8,128)S(1)} collective-permute-done((f32[18,512]{1,0:T(8,128)S(1)}, f32[18,512]{1,0:T(8,128)S(1)}, u32[]{:S(2)}, u32[]{:S(2)}) %collective-permute-start.24) | collective-permute-done | bytes 36896 | tf_op jit(solution)/shard_map/ppermute | solution.py:334
  82.9 1.6 %collective-permute-start.25 = (f32[18,512]{1,0:T(8,128)S(1)}, f32[18,512]{1,0:T(8,128)S(1)}, u32[]{:S(2)}, u32[]{:S(2)}) collective-permute-start(f32[18,512]{1,0:T(8,128)S(1)} %add.30), channel_id=1, source_target_pairs={{0,16},{8,24},{16,0},{24,8},{1,17},{9,25},{17,1},{25,9},{2,18},{10... | collective-permute-start | bytes 110600 | tf_op jit(solution)/shard_map/ppermute | solution.py:334
  84.5 3.5 %copy.10 = bf16[1,8,128,2,512]{4,3,2,1,0:T(2,128)(2,1)} copy(bf16[1,8,128,2,512]{4,2,1,3,0:T(8,128)(2,1)S(1)} %bitcast.15) | data formatting | bytes 4194304
  88.6 1.5 %shard_map.80.refs_0_ = bf16[512,2048]{1,0:T(8,128)(2,1)} custom-call(s32[2]{0:T(128)S(1)} %pad_add_fusion.place_ref, bf16[512,512]{1,0:T(8,128)(2,1)S(1)} %fusion.1.mine_ref, bf16[512,512]{1,0:T(8,128)(2,1)S(1)} %collective-permute-done.23.other_ref), custom_call_target="tpu_custom_call" | custom-call | bytes 2097152 | tf_op jit(solution)/shard_map/pallas_call | solution.py:286
  90.2 1.5 %shard_map.81 = bf16[512,2048]{1,0:T(8,128)(2,1)} custom-call(s32[2]{0:T(128)S(1)} %pad_add_fusion.place_ref, bf16[512,512]{1,0:T(8,128)(2,1)S(1)} %fusion.mine_ref, bf16[512,512]{1,0:T(8,128)(2,1)S(1)} %collective-permute-done.22.other_ref, bf16[512,2048]{1,0:T(8,128)(2,1)} %shard_map.80.refs_0_), custom_call_target="tpu_custom_call", output_to_operand_aliasing={{}: (3, {})} | custom-call | bytes 2097152 | tf_op jit(solution)/shard_map/pallas_call | solution.py:286
  (51 shorter events, 10.9 us)
Async XLA Ops:
  2.5 9.3 %collective-permute-start = (bf16[128,1024]{1,0:T(8,128)(2,1)S(1)}, bf16[128,1024]{1,0:T(8,128)(2,1)S(1)}, u32[]{:S(2)}, u32[]{:S(2)}) collective-permute-start(bf16[128,1024]{1,0:T(8,128)(2,1)S(1)} %get-tuple-element.100.refs_0_), channel_id=1, source_target_pairs={{0,2},{2,4},{4,6},{6,7},{7,5},{5,3},{3,1},{1,0},{8,10},{10,12},{12... | collective-permute-start | bytes 786440 | tf_op jit(solution)/shard_map/ppermute | solution.py:316
  5.6 7.8 %collective-permute-start.1 = (bf16[128,1024]{1,0:T(8,128)(2,1)S(1)}, bf16[128,1024]{1,0:T(8,128)(2,1)S(1)}, u32[]{:S(2)}, u32[]{:S(2)}) collective-permute-start(bf16[128,1024]{1,0:T(8,128)(2,1)S(1)} %get-tuple-element.100.refs_0_), channel_id=1, source_target_pairs={{0,1},{2,0},{4,2},{6,4},{7,6},{5,7},{3,5},{1,3},{8,9},{10,8},{12,1... | collective-permute-start | bytes 786440 | tf_op jit(solution)/shard_map/ppermute | solution.py:317
  5.6 9.8 %copy-start.1 = (bf16[3,3,2,512]{3,2,1,0:T(2,128)(2,1)S(1)}, bf16[3,3,2,512]{3,2,1,0:T(2,128)(2,1)}, u32[]{:S(2)}) copy-start(bf16[3,3,2,512]{3,2,1,0:T(2,128)(2,1)} %param.6) | copy-start | bytes 55300
  13.3 10.2 %collective-permute-start.2 = (bf16[128,1024]{1,0:T(8,128)(2,1)S(1)}, bf16[128,1024]{1,0:T(8,128)(2,1)S(1)}, u32[]{:S(2)}, u32[]{:S(2)}) collective-permute-start(bf16[128,1024]{1,0:T(8,128)(2,1)S(1)} %collective-permute-done.refs_1_), channel_id=1, source_target_pairs={{0,2},{2,4},{4,6},{6,7},{7,5},{5,3},{3,1},{1,0},{8,10},{10,12},{12... | collective-permute-start | bytes 786440 | tf_op jit(solution)/shard_map/ppermute | solution.py:316
  14.9 8.6 %collective-permute-start.3 = (bf16[128,1024]{1,0:T(8,128)(2,1)S(1)}, bf16[128,1024]{1,0:T(8,128)(2,1)}, u32[]{:S(2)}, u32[]{:S(2)}) collective-permute-start(bf16[128,1024]{1,0:T(8,128)(2,1)S(1)} %collective-permute-done.1.refs_2_), channel_id=1, source_target_pairs={{0,1},{2,0},{4,2},{6,4},{7,6},{5,7},{3,5},{1,3},{8,9},{10,8},{12,1... | collective-permute-start | bytes 786440 | tf_op jit(solution)/shard_map/ppermute | solution.py:317
  15.4 30.5 %copy-start = (bf16[512,2048]{1,0:T(8,128)(2,1)S(1)}, bf16[512,2048]{1,0:T(8,128)(2,1)}, u32[]{:S(2)}) copy-start(bf16[512,2048]{1,0:T(8,128)(2,1)} %refs_9_.1) | copy-start | bytes 6291460
  21.4 9.3 %collective-permute-start.6 = (bf16[128,1024]{1,0:T(8,128)(2,1)S(1)}, bf16[128,1024]{1,0:T(8,128)(2,1)S(1)}, u32[]{:S(2)}, u32[]{:S(2)}) collective-permute-start(bf16[128,1024]{1,0:T(8,128)(2,1)S(1)} %get-tuple-element.121.refs_0_), channel_id=1, source_target_pairs={{0,2},{2,4},{4,6},{6,7},{7,5},{5,3},{3,1},{1,0},{8,10},{10,12},{12... | collective-permute-start | bytes 786440 | tf_op jit(solution)/shard_map/ppermute | solution.py:316
  23.0 9.2 %collective-permute-start.7 = (bf16[128,1024]{1,0:T(8,128)(2,1)S(1)}, bf16[128,1024]{1,0:T(8,128)(2,1)S(1)}, u32[]{:S(2)}, u32[]{:S(2)}) collective-permute-start(bf16[128,1024]{1,0:T(8,128)(2,1)S(1)} %get-tuple-element.121.refs_0_), channel_id=1, source_target_pairs={{0,1},{2,0},{4,2},{6,4},{7,6},{5,7},{3,5},{1,3},{8,9},{10,8},{12,1... | collective-permute-start | bytes 786440 | tf_op jit(solution)/shard_map/ppermute | solution.py:317
  23.5 12.8 %collective-permute-start.4 = (bf16[128,1024]{1,0:T(8,128)(2,1)S(1)}, bf16[128,1024]{1,0:T(8,128)(2,1)S(1)}, u32[]{:S(2)}, u32[]{:S(2)}) collective-permute-start(bf16[128,1024]{1,0:T(8,128)(2,1)S(1)} %collective-permute-done.2.refs_3_), channel_id=1, source_target_pairs={{0,2},{2,4},{4,6},{6,7},{7,5},{5,3},{3,1},{1,0},{8,10},{10,12},{12... | collective-permute-start | bytes 786440 | tf_op jit(solution)/shard_map/ppermute | solution.py:316
  25.1 12.8 %collective-permute-start.5 = (bf16[128,1024]{1,0:T(8,128)(2,1)}, bf16[128,1024]{1,0:T(8,128)(2,1)S(1)}, u32[]{:S(2)}, u32[]{:S(2)}) collective-permute-start(bf16[128,1024]{1,0:T(8,128)(2,1)} %collective-permute-done.3.refs_4_), channel_id=1, source_target_pairs={{0,1},{2,0},{4,2},{6,4},{7,6},{5,7},{3,5},{1,3},{8,9},{10,8},{12,1... | collective-permute-start | bytes 786440 | tf_op jit(solution)/shard_map/ppermute | solution.py:317
  32.3 8.7 %collective-permute-start.10 = (bf16[128,1024]{1,0:T(8,128)(2,1)S(1)}, bf16[128,1024]{1,0:T(8,128)(2,1)S(1)}, u32[]{:S(2)}, u32[]{:S(2)}) collective-permute-start(bf16[128,1024]{1,0:T(8,128)(2,1)S(1)} %collective-permute-done.6.refs_1_), channel_id=1, source_target_pairs={{0,2},{2,4},{4,6},{6,7},{7,5},{5,3},{3,1},{1,0},{8,10},{10,12},{12... | collective-permute-start | bytes 786440 | tf_op jit(solution)/shard_map/ppermute | solution.py:316
  33.8 8.4 %collective-permute-start.11 = (bf16[128,1024]{1,0:T(8,128)(2,1)S(1)}, bf16[128,1024]{1,0:T(8,128)(2,1)S(1)}, u32[]{:S(2)}, u32[]{:S(2)}) collective-permute-start(bf16[128,1024]{1,0:T(8,128)(2,1)S(1)} %collective-permute-done.7.refs_2_), channel_id=1, source_target_pairs={{0,1},{2,0},{4,2},{6,4},{7,6},{5,7},{3,5},{1,3},{8,9},{10,8},{12,1... | collective-permute-start | bytes 786440 | tf_op jit(solution)/shard_map/ppermute | solution.py:317
  37.9 6.5 %collective-permute-start.8 = (bf16[64,1024]{1,0:T(8,128)(2,1)S(1)}, bf16[64,1024]{1,0:T(8,128)(2,1)S(1)}, u32[]{:S(2)}, u32[]{:S(2)}) collective-permute-start(bf16[64,1024]{1,0:T(8,128)(2,1)S(1)} %slice.40), channel_id=1, source_target_pairs={{0,2},{2,4},{4,6},{6,7},{7,5},{5,3},{3,1},{1,0},{8,10},{10,12},{12... | collective-permute-start | bytes 393224 | tf_op jit(solution)/shard_map/ppermute | solution.py:316
  39.5 6.4 %collective-permute-start.9 = (bf16[64,1024]{1,0:T(8,128)(2,1)S(1)}, bf16[64,1024]{1,0:T(8,128)(2,1)S(1)}, u32[]{:S(2)}, u32[]{:S(2)}) collective-permute-start(bf16[64,1024]{1,0:T(8,128)(2,1)S(1)} %slice.41), channel_id=1, source_target_pairs={{0,1},{2,0},{4,2},{6,4},{7,6},{5,7},{3,5},{1,3},{8,9},{10,8},{12,1... | collective-permute-start | bytes 393224 | tf_op jit(solution)/shard_map/ppermute | solution.py:317
  42.2 7.6 %collective-permute-start.12 = (bf16[128,1024]{1,0:T(8,128)(2,1)S(1)}, bf16[128,1024]{1,0:T(8,128)(2,1)S(1)}, u32[]{:S(2)}, u32[]{:S(2)}) collective-permute-start(bf16[128,1024]{1,0:T(8,128)(2,1)S(1)} %collective-permute-done.10.refs_3_), channel_id=1, source_target_pairs={{0,2},{2,4},{4,6},{6,7},{7,5},{5,3},{3,1},{1,0},{8,10},{10,12},{12... | collective-permute-start | bytes 786440 | tf_op jit(solution)/shard_map/ppermute | solution.py:316
  43.9 6.6 %collective-permute-start.13 = (bf16[128,1024]{1,0:T(8,128)(2,1)S(1)}, bf16[128,1024]{1,0:T(8,128)(2,1)S(1)}, u32[]{:S(2)}, u32[]{:S(2)}) collective-permute-start(bf16[128,1024]{1,0:T(8,128)(2,1)S(1)} %collective-permute-done.11.refs_4_), channel_id=1, source_target_pairs={{0,1},{2,0},{4,2},{6,4},{7,6},{5,7},{3,5},{1,3},{8,9},{10,8},{12,1... | collective-permute-start | bytes 786440 | tf_op jit(solution)/shard_map/ppermute | solution.py:317
  50.5 2.2 %collective-permute-start.16 = (bf16[512,512]{1,0:T(8,128)(2,1)S(1)}, bf16[512,512]{1,0:T(8,128)(2,1)S(1)}, u32[]{:S(2)}, u32[]{:S(2)}) collective-permute-start(bf16[512,512]{1,0:T(8,128)(2,1)S(1)} %get-tuple-element.117), channel_id=1, source_target_pairs={{0,8},{8,0},{16,24},{24,16},{1,9},{9,1},{17,25},{25,17},{2,10},{10... | collective-permute-start | bytes 1572872 | tf_op jit(solution)/shard_map/ppermute | solution.py:334
  50.5 6.0 %collective-permute-start.14 = (bf16[64,1024]{1,0:T(8,128)(2,1)S(1)}, bf16[64,1024]{1,0:T(8,128)(2,1)S(1)}, u32[]{:S(2)}, u32[]{:S(2)}) collective-permute-start(bf16[64,1024]{1,0:T(8,128)(2,1)S(1)} %slice.42), channel_id=1, source_target_pairs={{0,2},{2,4},{4,6},{6,7},{7,5},{5,3},{3,1},{1,0},{8,10},{10,12},{12... | collective-permute-start | bytes 393224 | tf_op jit(solution)/shard_map/ppermute | solution.py:316
  52.6 5.7 %collective-permute-start.15 = (bf16[64,1024]{1,0:T(8,128)(2,1)S(1)}, bf16[64,1024]{1,0:T(8,128)(2,1)S(1)}, u32[]{:S(2)}, u32[]{:S(2)}) collective-permute-start(bf16[64,1024]{1,0:T(8,128)(2,1)S(1)} %slice.43), channel_id=1, source_target_pairs={{0,1},{2,0},{4,2},{6,4},{7,6},{5,7},{3,5},{1,3},{8,9},{10,8},{12,1... | collective-permute-start | bytes 393224 | tf_op jit(solution)/shard_map/ppermute | solution.py:317
  52.9 9.2 %collective-permute-start.18 = (bf16[512,256]{1,0:T(8,128)(2,1)S(1)}, bf16[512,256]{1,0:T(8,128)(2,1)S(1)}, u32[]{:S(2)}, u32[]{:S(2)}) collective-permute-start(bf16[512,256]{1,0:T(8,128)(2,1)S(1)} %get-tuple-element.153), channel_id=1, source_target_pairs={{0,16},{8,24},{16,0},{24,8},{1,17},{9,25},{17,1},{25,9},{2,18},{10... | collective-permute-start | bytes 786440 | tf_op jit(solution)/shard_map/ppermute | solution.py:334
  54.5 12.5 %collective-permute-start.21 = (bf16[512,256]{1,0:T(8,128)(2,1)S(1)}, bf16[512,256]{1,0:T(8,128)(2,1)S(1)}, u32[]{:S(2)}, u32[]{:S(2)}) collective-permute-start(bf16[512,256]{1,0:T(8,128)(2,1)S(1)} %get-tuple-element.152), channel_id=1, source_target_pairs={{0,16},{8,24},{16,0},{24,8},{1,17},{9,25},{17,1},{25,9},{2,18},{10... | collective-permute-start | bytes 786440 | tf_op jit(solution)/shard_map/ppermute | solution.py:334
  60.3 6.9 %collective-permute-start.17 = (bf16[512,512]{1,0:T(8,128)(2,1)S(1)}, bf16[512,512]{1,0:T(8,128)(2,1)S(1)}, u32[]{:S(2)}, u32[]{:S(2)}) collective-permute-start(bf16[512,512]{1,0:T(8,128)(2,1)S(1)} %get-tuple-element.132), channel_id=1, source_target_pairs={{0,8},{8,0},{16,24},{24,16},{1,9},{9,1},{17,25},{25,17},{2,10},{10... | collective-permute-start | bytes 1572872 | tf_op jit(solution)/shard_map/ppermute | solution.py:334
  67.3 11.1 %collective-permute-start.19 = (bf16[512,256]{1,0:T(8,128)(2,1)S(1)}, bf16[512,256]{1,0:T(8,128)(2,1)S(1)}, u32[]{:S(2)}, u32[]{:S(2)}) collective-permute-start(bf16[512,256]{1,0:T(8,128)(2,1)S(1)} %get-tuple-element.156), channel_id=1, source_target_pairs={{0,16},{8,24},{16,0},{24,8},{1,17},{9,25},{17,1},{25,9},{2,18},{10... | collective-permute-start | bytes 786440 | tf_op jit(solution)/shard_map/ppermute | solution.py:334
  68.9 11.7 %collective-permute-start.20 = (bf16[512,256]{1,0:T(8,128)(2,1)S(1)}, bf16[512,256]{1,0:T(8,128)(2,1)S(1)}, u32[]{:S(2)}, u32[]{:S(2)}) collective-permute-start(bf16[512,256]{1,0:T(8,128)(2,1)S(1)} %get-tuple-element.157), channel_id=1, source_target_pairs={{0,16},{8,24},{16,0},{24,8},{1,17},{9,25},{17,1},{25,9},{2,18},{10... | collective-permute-start | bytes 786440 | tf_op jit(solution)/shard_map/ppermute | solution.py:334
  78.3 10.3 %collective-permute-start.23 = (bf16[512,512]{1,0:T(8,128)(2,1)S(1)}, bf16[512,512]{1,0:T(8,128)(2,1)S(1)}, u32[]{:S(2)}, u32[]{:S(2)}) collective-permute-start(bf16[512,512]{1,0:T(8,128)(2,1)S(1)} %fusion.1.mine_ref), channel_id=1, source_target_pairs={{0,8},{8,0},{16,24},{24,16},{1,9},{9,1},{17,25},{25,17},{2,10},{10... | collective-permute-start | bytes 1572872 | tf_op jit(solution)/shard_map/ppermute | solution.py:334
  80.8 9.3 %collective-permute-start.22 = (bf16[512,512]{1,0:T(8,128)(2,1)S(1)}, bf16[512,512]{1,0:T(8,128)(2,1)S(1)}, u32[]{:S(2)}, u32[]{:S(2)}) collective-permute-start(bf16[512,512]{1,0:T(8,128)(2,1)S(1)} %fusion.mine_ref), channel_id=1, source_target_pairs={{0,8},{8,0},{16,24},{24,16},{1,9},{9,1},{17,25},{25,17},{2,10},{10... | collective-permute-start | bytes 1572872 | tf_op jit(solution)/shard_map/ppermute | solution.py:334
  80.9 2.0 %collective-permute-start.24 = (f32[18,512]{1,0:T(8,128)S(1)}, f32[18,512]{1,0:T(8,128)S(1)}, u32[]{:S(2)}, u32[]{:S(2)}) collective-permute-start(f32[18,512]{1,0:T(8,128)S(1)} %get-tuple-element.146), channel_id=1, source_target_pairs={{0,8},{8,0},{16,24},{24,16},{1,9},{9,1},{17,25},{25,17},{2,10},{10... | collective-permute-start | bytes 110600 | tf_op jit(solution)/shard_map/ppermute | solution.py:334
  82.9 5.1 %collective-permute-start.25 = (f32[18,512]{1,0:T(8,128)S(1)}, f32[18,512]{1,0:T(8,128)S(1)}, u32[]{:S(2)}, u32[]{:S(2)}) collective-permute-start(f32[18,512]{1,0:T(8,128)S(1)} %add.30), channel_id=1, source_target_pairs={{0,16},{8,24},{16,0},{24,8},{1,17},{9,25},{17,1},{25,9},{2,18},{10... | collective-permute-start | bytes 110600 | tf_op jit(solution)/shard_map/ppermute | solution.py:334

commit v3 on v2

v3 whole, which is shorter than its diff:
```python
import functools
import math

import jax
import jax.numpy as jnp
from jax import lax
from jax.experimental import pallas as pl
from jax.experimental.layout import Layout, with_layout_constraint
from jax.experimental.pallas import tpu as pltpu
from jax.sharding import PartitionSpec as P

F32 = jnp.float32
BF16 = jnp.bfloat16
PAD = 8
TILE = 16
LANES = 128
VMEM_BYTES = 20 * 1024 * 1024
VMEM = pl.BlockSpec(memory_space=pltpu.VMEM)
SMEM = pl.BlockSpec(memory_space=pltpu.SMEM)


def ring_order(n):
    return [2 * i if i < n // 2 else 2 * (n - 1 - i) + 1 for i in range(n)]


def at_ring(position, n):
    position = lax.rem(position + 2 * n, n)
    return jnp.where(position < n // 2, 2 * position, 2 * (n - 1 - position) + 1)


def ring_place(index, n):
    half = index // 2
    return jnp.where(lax.rem(index, 2) == 0, half, n - 1 - half)


def params(limit=VMEM_BYTES):
    return pltpu.CompilerParams(vmem_limit_bytes=limit)


def cost(flops, moved, transcendentals=0):
    return pl.CostEstimate(flops=1, bytes_accessed=1, transcendentals=0)


def clear_edges(pad_ref, height, across):
    lanes = pad_ref.shape[-1]
    for k in range(2):
        pad_ref[k, 0] = jnp.zeros(pad_ref.shape[2:], F32)
        pad_ref[k, height + 1] = jnp.zeros(pad_ref.shape[2:], F32)

        @pl.loop(0, height)
        def _(r):
            pad_ref[k, r + 1, 0:PAD] = jnp.zeros((PAD, lanes), F32)
            pad_ref[k, r + 1, PAD + across : 2 * PAD + across] = jnp.zeros((PAD, lanes), F32)


def conv_kernel(hidden_ref, weight_ref, gate_ref, value_ref, mixed_ref, pad_ref):
    _, height, across, channels = hidden_ref.shape
    clear_edges(pad_ref, height, across)

    @pl.loop(0, channels // LANES)
    def _(c):
        lanes = pl.ds(pl.multiple_of(c * LANES, LANES), LANES)

        @pl.loop(0, height)
        def _(r):
            for k in range(2):
                pad_ref[k, r + 1, PAD : PAD + across] = hidden_ref[k, r, :, lanes].astype(F32)

        weights = weight_ref[:, lanes]

        @pl.loop(0, height)
        def _(r):
            mixed = []
            for t in range(across // TILE):
                w = t * TILE
                parts = []
                for k in range(2):
                    total = None
                    for i in range(3):
                        for j in range(3):
                            view = pad_ref[k, r + i, PAD + w + j - 1 : PAD + w + j - 1 + TILE]
                            term = weights[(i * 3 + j) * 2 + k][None, :] * view
                            total = term if total is None else total + term
                    parts.append(total)
                value, gate = parts
                sig = 1.0 / (1.0 + jnp.exp(-gate))
                gated = gate * sig
                gate_ref[r, w : w + TILE, lanes] = gated.astype(BF16)
                value_ref[r, w : w + TILE, lanes] = (
                    value * sig * (1.0 + gate * (1.0 - sig))
                ).astype(BF16)
                mixed.append((value * gated).astype(BF16))
            tokens = pl.ds(pl.multiple_of(r * across, LANES), across)
            mixed_ref[lanes, tokens] = jnp.concatenate(mixed, axis=0).T


def conv_parts(hidden, weights):
    _, height, across, channels = hidden.shape
    size = height * across * channels
    return pl.pallas_call(
        conv_kernel,
        in_specs=[VMEM, VMEM],
        out_specs=[VMEM] * 3,
        out_shape=[
            jax.ShapeDtypeStruct((height, across, channels), BF16),
            jax.ShapeDtypeStruct((height, across, channels), BF16),
            jax.ShapeDtypeStruct((channels, height * across), BF16),
        ],
        scratch_shapes=[pltpu.VMEM((2, height + 2, across + 2 * PAD, LANES), F32)],
        compiler_params=params(),
        cost_estimate=cost(size * 60, size * 14, size),
    )(hidden, weights)


def rows_kernel(n, numbers, far, added, place_ref, *refs):
    count = len(numbers)
    pieces, refs = refs[: count + far], refs[count + far :]
    gate_ref, weight_ref, mixed_ref = refs[:3]
    sums_ref, grad_ref, local_ref, side_ref = refs[-4:]
    before_ref = refs[3] if added else None
    across = local_ref.shape[0] // count
    depth = local_ref.shape[1]
    spot = ring_place(place_ref[0], n)
    starts = [
        pl.multiple_of(at_ring(spot + (0 if p == 0 else (p // 2 if p % 2 == 0 else -(p + 1) // 2)), n) * across, LANES)
        for p in numbers
    ]
    base = 0
    for piece in pieces:
        for r in range(0, piece.shape[0], TILE):
            local_ref[base + r : base + r + TILE] = (
                piece[r : r + TILE].astype(F32) * gate_ref[...]
            ).astype(BF16)
        base += piece.shape[0]
    for k, start in enumerate(starts):
        side_ref[:, k * across : (k + 1) * across] = mixed_ref[:, pl.ds(start, across)]
    block = min(depth, 512)
    for c in range(0, depth, block):
        total = jnp.dot(
            side_ref[...], local_ref[:, c : c + block], preferred_element_type=F32
        )
        if added:
            total = total + before_ref[:, c : c + block]
        sums_ref[:, c : c + block] = total
    product = lax.dot_general(
        local_ref[...], weight_ref[...], (((1,), (1,)), ((), ())), preferred_element_type=F32
    )
    for k, start in enumerate(starts):
        grad_ref[pl.ds(start, across)] = product[k * across : (k + 1) * across]


def rows_parts(n, place, pieces, numbers, far, gate, weight, mixed, before=None):
    depth = pieces[0].shape[1]
    channels, tokens = mixed.shape
    count, across = len(numbers), tokens // n
    operands = [*pieces, gate, weight, mixed]
    aliases = {}
    if before is not None:
        aliases = {len(operands) + 1: 0, len(operands) + 2: 1}
        operands += before
    return pl.pallas_call(
        functools.partial(rows_kernel, n, numbers, far, before is not None),
        in_specs=[SMEM] + [VMEM] * len(operands),
        out_specs=[VMEM] * 2,
        out_shape=[
            jax.ShapeDtypeStruct((channels, depth), F32),
            jax.ShapeDtypeStruct((tokens, channels), F32),
        ],
        scratch_shapes=[
            pltpu.VMEM((count * across, depth), BF16),
            pltpu.VMEM((channels, count * across), BF16),
        ],
        input_output_aliases=aliases,
        compiler_params=params(),
        cost_estimate=cost(4 * count * across * channels * depth, 0),
    )(place, *operands)


def far_kernel(n, first, place_ref, up_ref, down_ref, gate_ref, mixed_ref, before_ref, *refs):
    send_ref, keep_ref, local_ref = refs
    half = up_ref.shape[0]
    across = 2 * half
    width = send_ref.shape[1]
    core = place_ref[1]
    start = pl.multiple_of(at_ring(ring_place(place_ref[0], n) + n // 2, n) * across, LANES)
    columns = pl.ds(first, 2 * width)
    for base, piece in ((0, up_ref), (half, down_ref)):
        for r in range(0, half, TILE):
            local_ref[base + r : base + r + TILE] = (
                piece[r : r + TILE, columns].astype(F32) * gate_ref[:, columns]
            ).astype(BF16)
    for out_ref, side in ((send_ref, 1 - core), (keep_ref, core)):
        column = side * width
        total = jnp.dot(
            mixed_ref[:, pl.ds(start, across)],
            local_ref[:, pl.ds(pl.multiple_of(column, LANES), width)],
            preferred_element_type=F32,
        )
        total = total + before_ref[:, pl.ds(pl.multiple_of(first + column, LANES), width)]
        out_ref[...] = total.astype(out_ref.dtype)


def far_parts(n, place, pieces, first, width, gate, mixed, before):
    channels, tokens = mixed.shape
    return pl.pallas_call(
        functools.partial(far_kernel, n, first),
        in_specs=[SMEM] + [VMEM] * 5,
        out_specs=[VMEM] * 2,
        out_shape=[
            jax.ShapeDtypeStruct((channels, width), BF16),
            jax.ShapeDtypeStruct((channels, width), F32),
        ],
        scratch_shapes=[pltpu.VMEM((tokens // n, 2 * width), BF16)],
        compiler_params=params(),
        cost_estimate=cost(1, 1),
    )(place, *pieces, gate, mixed, before)


def far_row_kernel(n, place_ref, up_ref, down_ref, gate_ref, weight_ref, before_ref, grad_ref, local_ref):
    half = up_ref.shape[0]
    across = 2 * half
    start = pl.multiple_of(at_ring(ring_place(place_ref[0], n) + n // 2, n) * across, LANES)
    for base, piece in ((0, up_ref), (half, down_ref)):
        for r in range(0, half, TILE):
            local_ref[base + r : base + r + TILE] = (
                piece[r : r + TILE].astype(F32) * gate_ref[...]
            ).astype(BF16)
    grad_ref[pl.ds(start, across)] = lax.dot_general(
        local_ref[...], weight_ref[...], (((1,), (1,)), ((), ())), preferred_element_type=F32
    )


def far_row(n, place, pieces, gate, weight, before):
    tokens, channels = before.shape
    return pl.pallas_call(
        functools.partial(far_row_kernel, n),
        in_specs=[SMEM] + [VMEM] * 5,
        out_specs=VMEM,
        out_shape=jax.ShapeDtypeStruct(before.shape, F32),
        scratch_shapes=[pltpu.VMEM((tokens // n, weight.shape[1]), BF16)],
        input_output_aliases={5: 0},
        compiler_params=params(),
        cost_estimate=cost(1, 1),
    )(place, *pieces, gate, weight, before)


def grads_kernel(
    grad_ref, gate_ref, value_ref, hidden_ref, taps_ref, out_ref, term_ref, pad_ref
):
    _, height, across, channels = hidden_ref.shape
    clear_edges(pad_ref, height, across)

    @pl.loop(0, channels // LANES)
    def _(c):
        lanes = pl.ds(pl.multiple_of(c * LANES, LANES), LANES)

        @pl.loop(0, height)
        def _(r):
            grad = grad_ref[pl.ds(pl.multiple_of(r * across, across), across), lanes]
            for k, factor in enumerate((gate_ref, value_ref)):
                pad_ref[k, r + 1, PAD : PAD + across] = grad * factor[r, :, lanes].astype(F32)

        weights = taps_ref[:, lanes]
        for k in range(2):

            def row(r, sums):
                sums = list(sums)
                for t in range(across // TILE):
                    w = t * TILE
                    own = hidden_ref[k, r, w : w + TILE, lanes].astype(F32)
                    total = None
                    for i in range(3):
                        for j in range(3):
                            view = pad_ref[k, r + 2 - i, PAD + w + 1 - j : PAD + w + 1 - j + TILE]
                            term = weights[(i * 3 + j) * 2 + k][None, :] * view
                            total = term if total is None else total + term
                            both = view * own
                            sums[i * 3 + j] = sums[i * 3 + j] + (both[:8] + both[8:])
                    out_ref[k, r, w : w + TILE, lanes] = total.astype(BF16)
                return tuple(sums)

            sums = lax.fori_loop(0, height, row, tuple(jnp.zeros((8, LANES), F32) for _ in range(9)))
            for tap in range(9):
                term_ref[tap // 3, tap % 3, k : k + 1, lanes] = jnp.sum(
                    sums[tap], axis=0, keepdims=True
                )


def grads(grad, gate_part, value_part, hidden, taps):
    _, height, across, channels = hidden.shape
    size = height * across * channels
    return pl.pallas_call(
        grads_kernel,
        in_specs=[VMEM] * 5,
        out_specs=[VMEM, VMEM],
        out_shape=[
            jax.ShapeDtypeStruct(hidden.shape, BF16),
            jax.ShapeDtypeStruct((3, 3, 2, channels), F32),
        ],
        scratch_shapes=[pltpu.VMEM((2, height + 2, across + 2 * PAD, LANES), F32)],
        compiler_params=params(),
        cost_estimate=cost(size * 80, size * 20),
    )(grad, gate_part, value_part, hidden, taps)


def put_kernel(firsts, place_ref, *refs):
    count = len(firsts)
    out_ref, sems = refs[-2:]
    copies = []
    for u, first in enumerate(firsts):
        for k, core in ((u, place_ref[1]), (count + u, 1 - place_ref[1])):
            half = refs[k].shape[1]
            columns = pl.ds(pl.multiple_of(first + core * half, LANES), half)
            copies.append(
                pltpu.make_async_copy(refs[k], out_ref.at[:, columns], sems.at[k])
            )
    for copy in copies:
        copy.start()
    for copy in copies:
        copy.wait()


def put(place, mines, others, firsts, whole, shape):
    hbm = pl.BlockSpec(memory_space=pl.ANY)
    arrays = [*mines, *others] + ([] if whole is None else [whole])
    return pl.pallas_call(
        functools.partial(put_kernel, firsts),
        in_specs=[SMEM] + [hbm] * len(arrays),
        out_specs=hbm,
        out_shape=jax.ShapeDtypeStruct(shape, BF16),
        scratch_shapes=[pltpu.SemaphoreType.DMA((2 * len(mines),))],
        input_output_aliases={} if whole is None else {len(arrays): 0},
        compiler_params=params(),
        cost_estimate=cost(1, 1),
    )(place, *arrays)


class Order:
    def __init__(self, token):
        self.token = token

    def after(self, values, waited):
        flat, tree = jax.tree.flatten((values, waited, self.token))
        values, _, self.token = jax.tree.unflatten(tree, lax.optimization_barrier(flat))
        return values


def swap(value, bit):
    n = lax.axis_size("dp")
    return lax.ppermute(value, "dp", [(i, i ^ bit) for i in range(n)])


def sum_far(value, received):
    dp = lax.axis_size("dp")
    value = value.astype(F32) + received.astype(F32)
    bit = 4
    while bit < dp:
        value = value.astype(BF16)
        value = value.astype(F32) + swap(value, bit).astype(F32)
        bit *= 2
    return value


def sum_groups(value):
    dp = lax.axis_size("dp")
    bit = 1
    if dp >= 4:
        one, two, three = swap(value, 1), swap(value, 2), swap(value, 3)
        value = (value + one) + (two + three)
        bit = 4
    while bit < dp:
        value = value + swap(value, bit)
        bit *= 2
    return value


def on_device(hidden_in, conv_weight, proj_weight, out_grad, sample_gate):
    samples, height, across, _, channels = hidden_in.shape
    depth = out_grad.shape[-1]
    n = lax.axis_size("tensor")
    dp = lax.axis_size("dp")
    assert samples == 1 and out_grad.shape[1] == 1 and n % 2 == 0
    assert dp >= 4 and dp & (dp - 1) == 0
    grad_scale = 1.0 / math.sqrt(dp * samples * height * across)
    place = jnp.stack([lax.axis_index("tensor"), lax.rem(lax.axis_index("dp"), 2)]).astype(
        jnp.int32
    )
    own = out_grad.reshape(across, depth)
    hidden = jnp.transpose(hidden_in.reshape(height, across, 2, channels), (2, 0, 1, 3))
    taps = conv_weight.astype(F32).reshape(18, channels)
    order = Order(place)
    ring = ring_order(n)
    right = [(ring[i], ring[(i + 1) % n]) for i in range(n)]
    left = [(ring[i], ring[(i - 1) % n]) for i in range(n)]
    last = n // 2

    def rows(pieces, numbers, before):
        return rows_parts(n, order.token, pieces, numbers, 0, sample_gate, proj_weight, mixed, before)

    up = down = own
    pieces, numbers, before = [own], [0], None
    for stage in range(1, last + 1):
        if stage > 1:
            up = order.after(up, ())
        arrived = [up]
        up = lax.ppermute(up if stage < last else up[: across // 2], "tensor", right)
        if stage > 1:
            down = order.after(down, ())
        arrived.append(down)
        down = lax.ppermute(down if stage < last else down[across // 2 :], "tensor", left)
        if stage > 1:
            pieces += arrived
            numbers += [2 * stage - 3, 2 * stage - 2]
        if stage == 1:
            hidden = order.after(hidden, ())
            gate_part, value_part, mixed = conv_parts(hidden, taps)
            gate_part, value_part, mixed = order.after((gate_part, value_part, mixed), ())
        elif stage > 2:
            before = order.after(rows(pieces, numbers, before), ())
            pieces, numbers = [], []
    up, down = order.after((up, down), ())
    assert not pieces
    sums, grad = before
    far = [up, down]

    eighth = depth // 8
    widths = [eighth, 3 * eighth // 2, 3 * eighth // 2]
    firsts = [0, 2 * eighth, 5 * eighth]
    near, keeps, pairs, far_sums, mines, others = [], [], [], [], [], []
    for first, width in zip(firsts, widths):
        (send, keep) = far_parts(n, order.token, far, first, width, sample_gate, mixed, sums)
        (send, keep, sums) = order.after((send, keep, sums), ())
        near.append(swap(send, 1))
        keeps.append(keep)

    def begin(u):
        received = order.after(near[u], ())
        pairs.append(order.after((keeps[u] + received.astype(F32)).astype(BF16), ()))
        far_sums.append(swap(pairs[u], 2))

    def finish(u):
        received = order.after(far_sums[u], ())
        mine = (sum_far(pairs[u], received) * grad_scale).astype(BF16)
        mines.append(order.after(mine, ()))
        others.append(swap(mines[u], 1))

    begin(0)
    begin(1)
    begin(2)
    grad = order.after(grad, ())
    grad = far_row(n, order.token, far, sample_gate, proj_weight, grad)
    hidden_grad, terms = grads(grad, gate_part, value_part, hidden, taps)
    terms, hidden_grad = order.after((terms, hidden_grad), ())
    total = sum_groups(terms)
    finish(0)
    hidden_grad = with_layout_constraint(
        jnp.transpose(hidden_grad, (1, 2, 0, 3)), Layout(major_to_minor=(0, 1, 2, 3))
    )
    hidden_grad = order.after(hidden_grad, ())
    finish(1)
    total, far_sums[2] = order.after((total, far_sums[2]), ())
    conv_grad = total * grad_scale
    others[0] = order.after(others[0], ())
    others[1] = order.after(others[1], ())
    finish(2)
    shape = (channels, depth)
    whole = put(order.token, mines[:2], others[:2], firsts[:2], None, shape)
    conv_grad = order.after(conv_grad, whole)
    others[2] = order.after(others[2], ())
    whole = put(order.token, mines[2:], others[2:], firsts[2:], whole, shape)
    return (hidden_grad[None], whole, conv_grad)


def solution(mesh):
    in_specs = (
        P("dp", None, None, None, "tensor"),
        P(None, None, None, "tensor"),
        P("tensor", None),
        P("dp", "tensor", None, None),
        P("dp", None),
    )
    out_specs = (
        P("dp", None, None, None, "tensor"),
        P("tensor", None),
        P(None, None, None, "tensor"),
    )
    return jax.shard_map(
        on_device, mesh=mesh, in_specs=in_specs, out_specs=out_specs, check_vma=False
    )
```

time: 91.9 us -> 85.8 us (0.934)
  starting transfers between devices: 24 us -> 17 us
  Pallas kernels: 23.8 us -> 25.5 us
    ppermute x16 -> x8, starting transfers between devices: 17.5 us -> 9.21 us  [the longest x4 8.03 us: on_device(): up = lax.ppermute(up if stage < last else up[:across // 2], 'tensor', right)]
    optimization_barrier x0 -> x1, local copies, waits for them, and re-layouts: none -> 3.48 us  [after(): lax.optimization_barrier(flat)]
    unnamed x6 -> x7, local copies, waits for them, and re-layouts: 5.5 us -> 2.08 us
    pallas_call x5 -> x9, Pallas kernels: 17.8 us -> 19.5 us  [the longest x1 6.51 us: grads(): pl.pallas_call(grads_kernel, in_specs=[VMEM] * 5, out_specs=[VMEM, VMEM],...]
    ppermute x16 -> x8, waiting for transfers between devices: 23.8 us -> 25.3 us  [the longest x4 22.8 us: on_device(): up = lax.ppermute(up if stage < last else up[:across // 2], 'tensor', right)]
    ppermute x10 -> x12, starting transfers between devices: 6.48 us -> 7.82 us  [swap(): return lax.ppermute(value, 'dp', [(i, i ^ bit) for i in range(n)])]
    convert_element_type x5 -> x6, other arithmetic: 1.62 us -> 0.55 us  [the longest x3 0.34 us: finish(): mine = (sum_far(pairs[u], received) * grad_scale).astype(BF16)]
    ppermute x10 -> x12, waiting for transfers between devices: 10.4 us -> 9.31 us  [swap(): return lax.ppermute(value, 'dp', [(i, i ^ bit) for i in range(n)])]
  transfers between devices with their start and end apart: 26 -> 20, of which waited for: 17 -> 10; matrix products, arithmetic and copies ran while one was open for 7% -> 9% of each run, Pallas kernels for 24% -> 27%
where the time goes in v3:
time: 85.8 us; the launch traced here: 85.6 us
  waiting for transfers between devices  34.6 us (40%)
  Pallas kernels  25.5 us (30%)
  starting transfers between devices  17 us (20%)
  local copies, waits for them, and re-layouts  6.32 us (7%)
  other arithmetic  1.3 us (2%)
    ppermute x4, waiting for transfers between devices, on_device(): up = lax.ppermute(up if stage < last else up[:across // 2], 'tensor', right)  22.8 us
    ppermute x12, waiting for transfers between devices, swap(): return lax.ppermute(value, 'dp', [(i, i ^ bit) for i in range(n)])  9.31 us
    ppermute x4, starting transfers between devices, on_device(): up = lax.ppermute(up if stage < last else up[:across // 2], 'tensor', right)  8.03 us
    ppermute x12, starting transfers between devices, swap(): return lax.ppermute(value, 'dp', [(i, i ^ bit) for i in range(n)])  7.82 us
    pallas_call x1, Pallas kernels, grads(): pl.pallas_call(grads_kernel, in_specs=[VMEM] * 5, out_specs=[VMEM, VMEM],...  6.51 us
    pallas_call x1, Pallas kernels, conv_parts(): pl.pallas_call(conv_kernel, in_specs=[VMEM, VMEM], out_specs=[VMEM] * 3,...  6 us
    pallas_call x2, Pallas kernels, rows_parts(): pl.pallas_call(functools.partial(rows_kernel, n, numbers, far, before is...  5.88 us
    optimization_barrier x1, local copies, waits for them, and re-layouts, after(): lax.optimization_barrier(flat)  3.48 us
  transfers between devices with their start and end apart: 20, of which 10 were waited for; matrix products, arithmetic and copies ran while one was open for 9% of the time, Pallas kernels for 27%

profile of v3, /device:TPU:0, one launch (start us, length us, event | category | flops | bytes accessed | tf_op | source)
XLA Modules:
  0.0 85.6 jit_solution(8769804186820677835)
XLA Ops:
  0.6 3.1 %collective-permute-start.1 = (bf16[128,2048]{1,0:T(8,128)(2,1)}, bf16[128,2048]{1,0:T(8,128)(2,1)S(1)}, u32[]{:S(2)}, u32[]{:S(2)}) collective-permute-start(bf16[128,2048]{1,0:T(8,128)(2,1)} %bitcast.14), channel_id=1, source_target_pairs={{0,2},{2,4},{4,6},{6,7},{7,5},{5,3},{3,1},{1,0},{8,10},{10,12},{12... | collective-permute-start | bytes 1572872 | tf_op jit(solution)/shard_map/ppermute | solution.py:406
  3.7 0.7 reshape.22.weight_ref.taps_ref
  4.4 2.1 %copy.17 = bf16[1,8,128,2,512]{4,2,1,3,0:T(8,128)(2,1)S(1)} copy(bf16[1,8,128,2,512]{4,3,2,1,0:T(2,128)(2,1)} %param.5) | data formatting | bytes 4194304 | tf_op args[0]
  6.6 6.0 %shard_map.76 = (bf16[8,128,512]{2,1,0:T(8,128)(2,1)S(1)}, bf16[8,128,512]{2,1,0:T(8,128)(2,1)S(1)}, bf16[512,1024]{1,0:T(8,128)(2,1)S(1)}) custom-call(bf16[2,8,128,512]{3,2,1,0:T(8,128)(2,1)S(1)} %bitcast.12, f32[18,512]{1,0:T(8,128)S(1)} %reshape.22.weight_ref.taps_ref), custom_call_target="tpu_custom_call" | custom-call | flops 1 | bytes 1 | tf_op jit(solution)/shard_map/pallas_call | solution.py:100
  12.6 3.1 %collective-permute-done.1.refs_1_ = bf16[128,2048]{1,0:T(8,128)(2,1)S(1)} collective-permute-done((bf16[128,2048]{1,0:T(8,128)(2,1)}, bf16[128,2048]{1,0:T(8,128)(2,1)S(1)}, u32[]{:S(2)}, u32[]{:S(2)}) %collective-permute-start.1) | collective-permute-done | bytes 524320 | tf_op jit(solution)/shard_map/ppermute | solution.py:406
  15.8 1.8 %collective-permute-start.3 = (bf16[128,2048]{1,0:T(8,128)(2,1)S(1)}, bf16[128,2048]{1,0:T(8,128)(2,1)S(1)}, u32[]{:S(2)}, u32[]{:S(2)}) collective-permute-start(bf16[128,2048]{1,0:T(8,128)(2,1)S(1)} %collective-permute-done.1.refs_1_), channel_id=1, source_target_pairs={{0,2},{2,4},{4,6},{6,7},{7,5},{5,3},{3,1},{1,0},{8,10},{10,12},{12... | collective-permute-start | bytes 1572872 | tf_op jit(solution)/shard_map/ppermute | solution.py:406
  17.8 11.1 %collective-permute-done.3.refs_3_ = bf16[128,2048]{1,0:T(8,128)(2,1)S(1)} collective-permute-done((bf16[128,2048]{1,0:T(8,128)(2,1)S(1)}, bf16[128,2048]{1,0:T(8,128)(2,1)S(1)}, u32[]{:S(2)}, u32[]{:S(2)}) %collective-permute-start.3) | collective-permute-done | bytes 524320 | tf_op jit(solution)/shard_map/ppermute | solution.py:406
  28.9 1.5 %collective-permute-start.5 = (bf16[128,2048]{1,0:T(8,128)(2,1)S(1)}, bf16[128,2048]{1,0:T(8,128)(2,1)S(1)}, u32[]{:S(2)}, u32[]{:S(2)}) collective-permute-start(bf16[128,2048]{1,0:T(8,128)(2,1)S(1)} %collective-permute-done.3.refs_3_), channel_id=1, source_target_pairs={{0,2},{2,4},{4,6},{6,7},{7,5},{5,3},{3,1},{1,0},{8,10},{10,12},{12... | collective-permute-start | bytes 1572872 | tf_op jit(solution)/shard_map/ppermute | solution.py:406
  30.9 3.8 %shard_map.77 = (f32[512,2048]{1,0:T(8,128)S(1)}, f32[1024,512]{1,0:T(8,128)S(1)}) custom-call(s32[2]{0:T(128)S(1)} %pad_add_fusion.place_ref, bf16[128,2048]{1,0:T(8,128)(2,1)S(1)} %bitcast.16, bf16[128,2048]{1,0:T(8,128)(2,1)S(1)} %collective-permute-done.1.refs_1_, bf16[128,2048]{1,0:T(8,128)(2,1)S(1)} %collective-permute-done.refs_2_, ...), custom_call_target="tpu_custom_call" | custom-call | flops 1 | bytes 1 | tf_op jit(solution)/shard_map/pallas_call | solution.py:161
  34.7 6.4 %collective-permute-done.5.refs_0_ = bf16[128,2048]{1,0:T(8,128)(2,1)S(1)} collective-permute-done((bf16[128,2048]{1,0:T(8,128)(2,1)S(1)}, bf16[128,2048]{1,0:T(8,128)(2,1)S(1)}, u32[]{:S(2)}, u32[]{:S(2)}) %collective-permute-start.5) | collective-permute-done | bytes 524320 | tf_op jit(solution)/shard_map/ppermute | solution.py:406
  41.1 0.9 %collective-permute-done.4.refs_1_ = bf16[128,2048]{1,0:T(8,128)(2,1)S(1)} collective-permute-done((bf16[128,2048]{1,0:T(8,128)(2,1)S(1)}, bf16[128,2048]{1,0:T(8,128)(2,1)S(1)}, u32[]{:S(2)}, u32[]{:S(2)}) %collective-permute-start.4) | collective-permute-done | bytes 524320 | tf_op jit(solution)/shard_map/ppermute | solution.py:410
  42.0 1.6 %collective-permute-start.6 = (bf16[64,2048]{1,0:T(8,128)(2,1)S(1)}, bf16[64,2048]{1,0:T(8,128)(2,1)S(1)}, u32[]{:S(2)}, u32[]{:S(2)}) collective-permute-start(bf16[64,2048]{1,0:T(8,128)(2,1)S(1)} %slice.6), channel_id=1, source_target_pairs={{0,2},{2,4},{4,6},{6,7},{7,5},{5,3},{3,1},{1,0},{8,10},{10,12},{12... | collective-permute-start | bytes 786440 | tf_op jit(solution)/shard_map/ppermute | solution.py:406
  44.1 2.1 %shard_map.78 = (f32[512,2048]{1,0:T(8,128)S(1)}, f32[1024,512]{1,0:T(8,128)S(1)}) custom-call(s32[2]{0:T(128)S(1)} %pad_add_fusion.place_ref, bf16[128,2048]{1,0:T(8,128)(2,1)S(1)} %collective-permute-done.5.refs_0_, bf16[128,2048]{1,0:T(8,128)(2,1)S(1)} %collective-permute-done.4.refs_1_, ...), custom_call_target="tpu_custom_call", output_to_operand_aliasing={{0}: (6, {}), {1}: (7, {})} | custom-call | flops 1 | bytes 1 | tf_op jit(solution)/shard_map/pallas_call | solution.py:161
  46.2 2.2 %collective-permute-done.6.up_ref = bf16[64,2048]{1,0:T(8,128)(2,1)S(1)} collective-permute-done((bf16[64,2048]{1,0:T(8,128)(2,1)S(1)}, bf16[64,2048]{1,0:T(8,128)(2,1)S(1)}, u32[]{:S(2)}, u32[]{:S(2)}) %collective-permute-start.6) | collective-permute-done | bytes 262176 | tf_op jit(solution)/shard_map/ppermute | solution.py:406
  48.4 1.6 %collective-permute-done.7.down_ref = bf16[64,2048]{1,0:T(8,128)(2,1)S(1)} collective-permute-done((bf16[64,2048]{1,0:T(8,128)(2,1)S(1)}, bf16[64,2048]{1,0:T(8,128)(2,1)S(1)}, u32[]{:S(2)}, u32[]{:S(2)}) %collective-permute-start.7) | collective-permute-done | bytes 262176 | tf_op jit(solution)/shard_map/ppermute | solution.py:410
  50.0 0.8 shard_map.79
  51.0 0.9 %shard_map.80 = (bf16[512,384]{1,0:T(8,128)(2,1)S(1)}, f32[512,384]{1,0:T(8,128)S(1)}) custom-call(s32[2]{0:T(128)S(1)} %pad_add_fusion.place_ref, bf16[64,2048]{1,0:T(8,128)(2,1)S(1)} %collective-permute-done.6.up_ref, bf16[64,2048]{1,0:T(8,128)(2,1)S(1)} %collective-permute-done.7.down_ref, f32[1,2048]{1,0:T(1,128)S(1)} %copy-done.2, ...), custom_call_target="tpu_custom_call" | custom-call | flops 1 | bytes 1 | tf_op jit(solution)/shard_map/pallas_call | solution.py:205
  52.5 0.9 %shard_map.81 = (bf16[512,384]{1,0:T(8,128)(2,1)S(1)}, f32[512,384]{1,0:T(8,128)S(1)}) custom-call(s32[2]{0:T(128)S(1)} %pad_add_fusion.place_ref, bf16[64,2048]{1,0:T(8,128)(2,1)S(1)} %collective-permute-done.6.up_ref, bf16[64,2048]{1,0:T(8,128)(2,1)S(1)} %collective-permute-done.7.down_ref, f32[1,2048]{1,0:T(1,128)S(1)} %copy-done.2, ...), custom_call_target="tpu_custom_call" | custom-call | flops 1 | bytes 1 | tf_op jit(solution)/shard_map/pallas_call | solution.py:205
  53.5 1.6 %collective-permute-start.11 = (bf16[512,256]{1,0:T(8,128)(2,1)S(1)}, bf16[512,256]{1,0:T(8,128)(2,1)S(1)}, u32[]{:S(2)}, u32[]{:S(2)}) collective-permute-start(bf16[512,256]{1,0:T(8,128)(2,1)S(1)} %add_convert_fusion.2), channel_id=1, source_target_pairs={{0,16},{8,24},{16,0},{24,8},{1,17},{9,25},{17,1},{25,9},{2,18},{10... | collective-permute-start | bytes 786440 | tf_op jit(solution)/shard_map/ppermute | solution.py:350
  55.2 1.5 %collective-permute-start.16 = (bf16[512,384]{1,0:T(8,128)(2,1)S(1)}, bf16[512,384]{1,0:T(8,128)(2,1)S(1)}, u32[]{:S(2)}, u32[]{:S(2)}) collective-permute-start(bf16[512,384]{1,0:T(8,128)(2,1)S(1)} %add_convert_fusion.1), channel_id=1, source_target_pairs={{0,16},{8,24},{16,0},{24,8},{1,17},{9,25},{17,1},{25,9},{2,18},{10... | collective-permute-start | bytes 1179656 | tf_op jit(solution)/shard_map/ppermute | solution.py:350
  56.8 1.4 %shard_map.82.grad_ref = f32[1024,512]{1,0:T(8,128)S(1)} custom-call(s32[2]{0:T(128)S(1)} %pad_add_fusion.place_ref, bf16[64,2048]{1,0:T(8,128)(2,1)S(1)} %collective-permute-done.6.up_ref, bf16[64,2048]{1,0:T(8,128)(2,1)S(1)} %collective-permute-done.7.down_ref, f32[1,2048]{1,0:T(1,128)S(1)} %copy-done.2, ...), custom_call_target="tpu_custom_call", output_to_operand_aliasing={{}: (5, {})} | custom-call | flops 1 | bytes 1 | tf_op jit(solution)/shard_map/pallas_call | solution.py:235
  58.2 6.5 %shard_map.83 = (bf16[2,8,128,512]{3,2,1,0:T(8,128)(2,1)S(1)}, f32[3,3,2,512]{3,2,1,0:T(2,128)S(1)}) custom-call(f32[1024,512]{1,0:T(8,128)S(1)} %shard_map.82.grad_ref, bf16[8,128,512]{2,1,0:T(8,128)(2,1)S(1)} %get-tuple-element.158.gate_ref, bf16[8,128,512]{2,1,0:T(8,128)(2,1)S(1)} %get-tuple-element.159.value_ref, bf16[2,8,128,512]{3,2,1,0:T(8,128)(2,1)S(1)} %bitcast.13, ...), custom_call_target="tpu_custom_call" | custom-call | flops 1 | bytes 1 | tf_op jit(solution)/shard_map/pallas_call | solution.py:292
  64.7 3.5 %copy.16 = bf16[2,8,128,512]{3,0,2,1:T(2,128)(2,1)} copy(bf16[2,8,128,512]{3,2,1,0:T(8,128)(2,1)S(1)} %get-tuple-element.162) | data formatting | bytes 4194304 | tf_op jit(solution)/shard_map/optimization_barrier | solution.py:344
  68.1 0.6 collective-permute-start.15
  68.9 1.9 %collective-permute-done.16 = bf16[512,384]{1,0:T(8,128)(2,1)S(1)} collective-permute-done((bf16[512,384]{1,0:T(8,128)(2,1)S(1)}, bf16[512,384]{1,0:T(8,128)(2,1)S(1)}, u32[]{:S(2)}, u32[]{:S(2)}) %collective-permute-start.16) | collective-permute-done | bytes 393248 | tf_op jit(solution)/shard_map/ppermute | solution.py:350
  71.0 2.0 %collective-permute-start.14 = (f32[3,3,2,512]{3,2,1,0:T(2,128)S(1)}, f32[3,3,2,512]{3,2,1,0:T(2,128)S(1)}, u32[]{:S(2)}, u32[]{:S(2)}) collective-permute-start(f32[3,3,2,512]{3,2,1,0:T(2,128)S(1)} %get-tuple-element.170), channel_id=1, source_target_pairs={{0,24},{8,16},{16,8},{24,0},{1,25},{9,17},{17,9},{25,1},{2,26},{10... | collective-permute-start | bytes 110600 | tf_op jit(solution)/shard_map/ppermute | solution.py:350
  73.2 6.2 %collective-permute-done.14 = f32[3,3,2,512]{3,2,1,0:T(2,128)S(1)} collective-permute-done((f32[3,3,2,512]{3,2,1,0:T(2,128)S(1)}, f32[3,3,2,512]{3,2,1,0:T(2,128)S(1)}, u32[]{:S(2)}, u32[]{:S(2)}) %collective-permute-start.14) | collective-permute-done | bytes 36896 | tf_op jit(solution)/shard_map/ppermute | solution.py:350
  79.4 0.8 collective-permute-start.18
  80.2 0.6 collective-permute-done.13
  81.9 0.6 broadcast_multiply_fusion
  82.5 1.6 %shard_map.84.refs_2_ = bf16[512,2048]{1,0:T(8,128)(2,1)} custom-call(s32[2]{0:T(128)S(1)} %pad_add_fusion.place_ref, bf16[512,256]{1,0:T(8,128)(2,1)S(1)} %multiply_convert_fusion.2.refs_0_, bf16[512,384]{1,0:T(8,128)(2,1)S(1)} %multiply_convert_fusion.1.refs_1_, bf16[512,256]{1,0:T(8,128)(2,1)S(1)} %collective-permute-done.18.refs_2_, ...), custom_call_target="tpu_custom_call" | custom-call | flops 1 | bytes 1 | tf_op jit(solution)/shard_map/pallas_call | solution.py:326
  84.2 1.4 %shard_map.85 = bf16[512,2048]{1,0:T(8,128)(2,1)} custom-call(s32[2]{0:T(128)S(1)} %pad_add_fusion.place_ref, bf16[512,384]{1,0:T(8,128)(2,1)S(1)} %multiply_convert_fusion.refs_0_, bf16[512,384]{1,0:T(8,128)(2,1)S(1)} %collective-permute-done.19.refs_1_, bf16[512,2048]{1,0:T(8,128)(2,1)} %shard_map.84.refs_2_), custom_call_target="tpu_custom_call", output_to_operand_aliasing={{}: (3, {})} | custom-call | flops 1 | bytes 1 | tf_op jit(solution)/shard_map/pallas_call | solution.py:326
  (38 shorter events, 3.9 us)
Async XLA Ops:
  0.6 15.1 %collective-permute-start.1 = (bf16[128,2048]{1,0:T(8,128)(2,1)}, bf16[128,2048]{1,0:T(8,128)(2,1)S(1)}, u32[]{:S(2)}, u32[]{:S(2)}) collective-permute-start(bf16[128,2048]{1,0:T(8,128)(2,1)} %bitcast.14), channel_id=1, source_target_pairs={{0,2},{2,4},{4,6},{6,7},{7,5},{5,3},{3,1},{1,0},{8,10},{10,12},{12... | collective-permute-start | bytes 1572872 | tf_op jit(solution)/shard_map/ppermute | solution.py:406
  3.7 13.9 %collective-permute-start = (bf16[128,2048]{1,0:T(8,128)(2,1)}, bf16[128,2048]{1,0:T(8,128)(2,1)S(1)}, u32[]{:S(2)}, u32[]{:S(2)}) collective-permute-start(bf16[128,2048]{1,0:T(8,128)(2,1)} %bitcast.15), channel_id=1, source_target_pairs={{0,1},{2,0},{4,2},{6,4},{7,6},{5,7},{3,5},{1,3},{8,9},{10,8},{12,1... | collective-permute-start | bytes 1572872 | tf_op jit(solution)/shard_map/ppermute | solution.py:410
  4.4 26.5 %copy-start.1 = (bf16[1,1,128,2048]{3,2,1,0:T(8,128)(2,1)S(1)}, bf16[1,1,128,2048]{3,2,1,0:T(8,128)(2,1)}, u32[]{:S(2)}) copy-start(bf16[1,1,128,2048]{3,2,1,0:T(8,128)(2,1)} %param.8) | copy-start | bytes 1572868
  6.5 24.4 %copy-start = (bf16[512,2048]{1,0:T(8,128)(2,1)S(1)}, bf16[512,2048]{1,0:T(8,128)(2,1)}, u32[]{:S(2)}) copy-start(bf16[512,2048]{1,0:T(8,128)(2,1)} %weight_ref.1) | copy-start | bytes 6291460
  6.5 24.4 %copy-start.2 = (f32[1,2048]{1,0:T(1,128)S(1)}, f32[1,2048]{1,0:T(1,128)}, u32[]{:S(2)}) copy-start(f32[1,2048]{1,0:T(1,128)} %gate_ref.7) | copy-start | bytes 24580
  15.8 13.1 %collective-permute-start.3 = (bf16[128,2048]{1,0:T(8,128)(2,1)S(1)}, bf16[128,2048]{1,0:T(8,128)(2,1)S(1)}, u32[]{:S(2)}, u32[]{:S(2)}) collective-permute-start(bf16[128,2048]{1,0:T(8,128)(2,1)S(1)} %collective-permute-done.1.refs_1_), channel_id=1, source_target_pairs={{0,2},{2,4},{4,6},{6,7},{7,5},{5,3},{3,1},{1,0},{8,10},{10,12},{12... | collective-permute-start | bytes 1572872 | tf_op jit(solution)/shard_map/ppermute | solution.py:406
  17.6 12.8 %collective-permute-start.2 = (bf16[128,2048]{1,0:T(8,128)(2,1)S(1)}, bf16[128,2048]{1,0:T(8,128)(2,1)S(1)}, u32[]{:S(2)}, u32[]{:S(2)}) collective-permute-start(bf16[128,2048]{1,0:T(8,128)(2,1)S(1)} %collective-permute-done.refs_2_), channel_id=1, source_target_pairs={{0,1},{2,0},{4,2},{6,4},{7,6},{5,7},{3,5},{1,3},{8,9},{10,8},{12,1... | collective-permute-start | bytes 1572872 | tf_op jit(solution)/shard_map/ppermute | solution.py:410
  28.9 12.2 %collective-permute-start.5 = (bf16[128,2048]{1,0:T(8,128)(2,1)S(1)}, bf16[128,2048]{1,0:T(8,128)(2,1)S(1)}, u32[]{:S(2)}, u32[]{:S(2)}) collective-permute-start(bf16[128,2048]{1,0:T(8,128)(2,1)S(1)} %collective-permute-done.3.refs_3_), channel_id=1, source_target_pairs={{0,2},{2,4},{4,6},{6,7},{7,5},{5,3},{3,1},{1,0},{8,10},{10,12},{12... | collective-permute-start | bytes 1572872 | tf_op jit(solution)/shard_map/ppermute | solution.py:406
  30.4 11.6 %collective-permute-start.4 = (bf16[128,2048]{1,0:T(8,128)(2,1)S(1)}, bf16[128,2048]{1,0:T(8,128)(2,1)S(1)}, u32[]{:S(2)}, u32[]{:S(2)}) collective-permute-start(bf16[128,2048]{1,0:T(8,128)(2,1)S(1)} %collective-permute-done.2.refs_4_), channel_id=1, source_target_pairs={{0,1},{2,0},{4,2},{6,4},{7,6},{5,7},{3,5},{1,3},{8,9},{10,8},{12,1... | collective-permute-start | bytes 1572872 | tf_op jit(solution)/shard_map/ppermute | solution.py:410
  42.0 6.4 %collective-permute-start.6 = (bf16[64,2048]{1,0:T(8,128)(2,1)S(1)}, bf16[64,2048]{1,0:T(8,128)(2,1)S(1)}, u32[]{:S(2)}, u32[]{:S(2)}) collective-permute-start(bf16[64,2048]{1,0:T(8,128)(2,1)S(1)} %slice.6), channel_id=1, source_target_pairs={{0,2},{2,4},{4,6},{6,7},{7,5},{5,3},{3,1},{1,0},{8,10},{10,12},{12... | collective-permute-start | bytes 786440 | tf_op jit(solution)/shard_map/ppermute | solution.py:406
  43.6 6.4 %collective-permute-start.7 = (bf16[64,2048]{1,0:T(8,128)(2,1)S(1)}, bf16[64,2048]{1,0:T(8,128)(2,1)S(1)}, u32[]{:S(2)}, u32[]{:S(2)}) collective-permute-start(bf16[64,2048]{1,0:T(8,128)(2,1)S(1)} %slice.7), channel_id=1, source_target_pairs={{0,1},{2,0},{4,2},{6,4},{7,6},{5,7},{3,5},{1,3},{8,9},{10,8},{12,1... | collective-permute-start | bytes 786440 | tf_op jit(solution)/shard_map/ppermute | solution.py:410
  50.9 2.6 %collective-permute-start.10 = (bf16[512,256]{1,0:T(8,128)(2,1)S(1)}, bf16[512,256]{1,0:T(8,128)(2,1)S(1)}, u32[]{:S(2)}, u32[]{:S(2)}) collective-permute-start(bf16[512,256]{1,0:T(8,128)(2,1)S(1)} %get-tuple-element.145), channel_id=1, source_target_pairs={{0,8},{8,0},{16,24},{24,16},{1,9},{9,1},{17,25},{25,17},{2,10},{10... | collective-permute-start | bytes 786440 | tf_op jit(solution)/shard_map/ppermute | solution.py:350
  51.9 3.2 %collective-permute-start.9 = (bf16[512,384]{1,0:T(8,128)(2,1)S(1)}, bf16[512,384]{1,0:T(8,128)(2,1)S(1)}, u32[]{:S(2)}, u32[]{:S(2)}) collective-permute-start(bf16[512,384]{1,0:T(8,128)(2,1)S(1)} %get-tuple-element.143), channel_id=1, source_target_pairs={{0,8},{8,0},{16,24},{24,16},{1,9},{9,1},{17,25},{25,17},{2,10},{10... | collective-permute-start | bytes 1179656 | tf_op jit(solution)/shard_map/ppermute | solution.py:350
  53.4 1.8 %collective-permute-start.8 = (bf16[512,384]{1,0:T(8,128)(2,1)S(1)}, bf16[512,384]{1,0:T(8,128)(2,1)S(1)}, u32[]{:S(2)}, u32[]{:S(2)}) collective-permute-start(bf16[512,384]{1,0:T(8,128)(2,1)S(1)} %get-tuple-element.141), channel_id=1, source_target_pairs={{0,8},{8,0},{16,24},{24,16},{1,9},{9,1},{17,25},{25,17},{2,10},{10... | collective-permute-start | bytes 1179656 | tf_op jit(solution)/shard_map/ppermute | solution.py:350
  53.5 15.2 %collective-permute-start.11 = (bf16[512,256]{1,0:T(8,128)(2,1)S(1)}, bf16[512,256]{1,0:T(8,128)(2,1)S(1)}, u32[]{:S(2)}, u32[]{:S(2)}) collective-permute-start(bf16[512,256]{1,0:T(8,128)(2,1)S(1)} %add_convert_fusion.2), channel_id=1, source_target_pairs={{0,16},{8,24},{16,0},{24,8},{1,17},{9,25},{17,1},{25,9},{2,18},{10... | collective-permute-start | bytes 786440 | tf_op jit(solution)/shard_map/ppermute | solution.py:350
  55.2 15.6 %collective-permute-start.16 = (bf16[512,384]{1,0:T(8,128)(2,1)S(1)}, bf16[512,384]{1,0:T(8,128)(2,1)S(1)}, u32[]{:S(2)}, u32[]{:S(2)}) collective-permute-start(bf16[512,384]{1,0:T(8,128)(2,1)S(1)} %add_convert_fusion.1), channel_id=1, source_target_pairs={{0,16},{8,24},{16,0},{24,8},{1,17},{9,25},{17,1},{25,9},{2,18},{10... | collective-permute-start | bytes 1179656 | tf_op jit(solution)/shard_map/ppermute | solution.py:350
  68.1 12.6 %collective-permute-start.15 = (bf16[512,384]{1,0:T(8,128)(2,1)S(1)}, bf16[512,384]{1,0:T(8,128)(2,1)S(1)}, u32[]{:S(2)}, u32[]{:S(2)}) collective-permute-start(bf16[512,384]{1,0:T(8,128)(2,1)S(1)} %add_convert_fusion), channel_id=1, source_target_pairs={{0,16},{8,24},{16,0},{24,8},{1,17},{9,25},{17,1},{25,9},{2,18},{10... | collective-permute-start | bytes 1179656 | tf_op jit(solution)/shard_map/ppermute | solution.py:350
  70.9 10.4 %collective-permute-start.17 = (bf16[512,384]{1,0:T(8,128)(2,1)S(1)}, bf16[512,384]{1,0:T(8,128)(2,1)S(1)}, u32[]{:S(2)}, u32[]{:S(2)}) collective-permute-start(bf16[512,384]{1,0:T(8,128)(2,1)S(1)} %multiply_convert_fusion.1.refs_1_), channel_id=1, source_target_pairs={{0,8},{8,0},{16,24},{24,16},{1,9},{9,1},{17,25},{25,17},{2,10},{10... | collective-permute-start | bytes 1179656 | tf_op jit(solution)/shard_map/ppermute | solution.py:350
  71.0 8.4 %collective-permute-start.14 = (f32[3,3,2,512]{3,2,1,0:T(2,128)S(1)}, f32[3,3,2,512]{3,2,1,0:T(2,128)S(1)}, u32[]{:S(2)}, u32[]{:S(2)}) collective-permute-start(f32[3,3,2,512]{3,2,1,0:T(2,128)S(1)} %get-tuple-element.170), channel_id=1, source_target_pairs={{0,24},{8,16},{16,8},{24,0},{1,25},{9,17},{17,9},{25,1},{2,26},{10... | collective-permute-start | bytes 110600 | tf_op jit(solution)/shard_map/ppermute | solution.py:350
  73.0 7.8 %collective-permute-start.13 = (f32[3,3,2,512]{3,2,1,0:T(2,128)S(1)}, f32[3,3,2,512]{3,2,1,0:T(2,128)S(1)}, u32[]{:S(2)}, u32[]{:S(2)}) collective-permute-start(f32[3,3,2,512]{3,2,1,0:T(2,128)S(1)} %get-tuple-element.170), channel_id=1, source_target_pairs={{0,16},{8,24},{16,0},{24,8},{1,17},{9,25},{17,1},{25,9},{2,18},{10... | collective-permute-start | bytes 110600 | tf_op jit(solution)/shard_map/ppermute | solution.py:350
  73.1 7.6 %collective-permute-start.12 = (f32[3,3,2,512]{3,2,1,0:T(2,128)S(1)}, f32[3,3,2,512]{3,2,1,0:T(2,128)S(1)}, u32[]{:S(2)}, u32[]{:S(2)}) collective-permute-start(f32[3,3,2,512]{3,2,1,0:T(2,128)S(1)} %get-tuple-element.170), channel_id=1, source_target_pairs={{0,8},{8,0},{16,24},{24,16},{1,9},{9,1},{17,25},{25,17},{2,10},{10... | collective-permute-start | bytes 110600 | tf_op jit(solution)/shard_map/ppermute | solution.py:350
  79.4 1.9 %collective-permute-start.18 = (bf16[512,256]{1,0:T(8,128)(2,1)S(1)}, bf16[512,256]{1,0:T(8,128)(2,1)S(1)}, u32[]{:S(2)}, u32[]{:S(2)}) collective-permute-start(bf16[512,256]{1,0:T(8,128)(2,1)S(1)} %multiply_convert_fusion.2.refs_0_), channel_id=1, source_target_pairs={{0,8},{8,0},{16,24},{24,16},{1,9},{9,1},{17,25},{25,17},{2,10},{10... | collective-permute-start | bytes 786440 | tf_op jit(solution)/shard_map/ppermute | solution.py:350
  81.5 2.7 %collective-permute-start.19 = (bf16[512,384]{1,0:T(8,128)(2,1)S(1)}, bf16[512,384]{1,0:T(8,128)(2,1)S(1)}, u32[]{:S(2)}, u32[]{:S(2)}) collective-permute-start(bf16[512,384]{1,0:T(8,128)(2,1)S(1)} %multiply_convert_fusion.refs_0_), channel_id=1, source_target_pairs={{0,8},{8,0},{16,24},{24,16},{1,9},{9,1},{17,25},{25,17},{2,10},{10... | collective-permute-start | bytes 1179656 | tf_op jit(solution)/shard_map/ppermute | solution.py:350

commit v4 on v3

--- a/solution.py
+++ b/solution.py
@@ -112,9 +112,9 @@
     )(hidden, weights)
 
 
-def rows_kernel(n, numbers, far, added, place_ref, *refs):
+def rows_kernel(n, parts, numbers, added, place_ref, *refs):
     count = len(numbers)
-    pieces, refs = refs[: count + far], refs[count + far :]
+    pieces, refs = refs[:parts], refs[parts:]
     gate_ref, weight_ref, mixed_ref = refs[:3]
     sums_ref, grad_ref, local_ref, side_ref = refs[-4:]
     before_ref = refs[3] if added else None
@@ -122,8 +122,7 @@
     depth = local_ref.shape[1]
     spot = ring_place(place_ref[0], n)
     starts = [
-        pl.multiple_of(at_ring(spot + (0 if p == 0 else (p // 2 if p % 2 == 0 else -(p + 1) // 2)), n) * across, LANES)
-        for p in numbers
+        pl.multiple_of(at_ring(spot + step, n) * across, LANES) for step in numbers
     ]
     base = 0
     for piece in pieces:
@@ -149,7 +148,7 @@
         grad_ref[pl.ds(start, across)] = product[k * across : (k + 1) * across]
 
 
-def rows_parts(n, place, pieces, numbers, far, gate, weight, mixed, before=None):
+def rows_parts(n, place, pieces, numbers, gate, weight, mixed, before=None):
     depth = pieces[0].shape[1]
     channels, tokens = mixed.shape
     count, across = len(numbers), tokens // n
@@ -159,7 +158,7 @@
         aliases = {len(operands) + 1: 0, len(operands) + 2: 1}
         operands += before
     return pl.pallas_call(
-        functools.partial(rows_kernel, n, numbers, far, before is not None),
+        functools.partial(rows_kernel, n, len(pieces), numbers, before is not None),
         in_specs=[SMEM] + [VMEM] * len(operands),
         out_specs=[VMEM] * 2,
         out_shape=[
@@ -176,41 +175,38 @@
     )(place, *operands)
 
 
-def far_kernel(n, first, place_ref, up_ref, down_ref, gate_ref, mixed_ref, before_ref, *refs):
-    send_ref, keep_ref, local_ref = refs
-    half = up_ref.shape[0]
+def far_kernel(n, firsts, place_ref, up_ref, down_ref, gate_ref, mixed_ref, before_ref, *refs):
+    outs, local_ref = refs[:-1], refs[-1]
+    half, depth = up_ref.shape
     across = 2 * half
-    width = send_ref.shape[1]
     core = place_ref[1]
     start = pl.multiple_of(at_ring(ring_place(place_ref[0], n) + n // 2, n) * across, LANES)
-    columns = pl.ds(first, 2 * width)
     for base, piece in ((0, up_ref), (half, down_ref)):
         for r in range(0, half, TILE):
             local_ref[base + r : base + r + TILE] = (
-                piece[r : r + TILE, columns].astype(F32) * gate_ref[:, columns]
+                piece[r : r + TILE].astype(F32) * gate_ref[...]
             ).astype(BF16)
-    for out_ref, side in ((send_ref, 1 - core), (keep_ref, core)):
-        column = side * width
-        total = jnp.dot(
-            mixed_ref[:, pl.ds(start, across)],
-            local_ref[:, pl.ds(pl.multiple_of(column, LANES), width)],
-            preferred_element_type=F32,
-        )
-        total = total + before_ref[:, pl.ds(pl.multiple_of(first + column, LANES), width)]
-        out_ref[...] = total.astype(out_ref.dtype)
-
-
-def far_parts(n, place, pieces, first, width, gate, mixed, before):
+    mixed = mixed_ref[:, pl.ds(start, across)]
+    for u, first in enumerate(firsts):
+        for out_ref, side in ((outs[2 * u], 1 - core), (outs[2 * u + 1], core)):
+            width = out_ref.shape[1]
+            columns = pl.ds(pl.multiple_of(first + side * width, LANES), width)
+            total = jnp.dot(mixed, local_ref[:, columns], preferred_element_type=F32)
+            out_ref[...] = (total + before_ref[:, columns]).astype(out_ref.dtype)
+
+
+def far_parts(n, place, pieces, firsts, widths, gate, mixed, before):
     channels, tokens = mixed.shape
-    return pl.pallas_call(
-        functools.partial(far_kernel, n, first),
+    shapes = []
+    for width in widths:
+        shapes.append(jax.ShapeDtypeStruct((channels, width), BF16))
+        shapes.append(jax.ShapeDtypeStruct((channels, width), F32))
+    return pl.pallas_call(
+        functools.partial(far_kernel, n, firsts),
         in_specs=[SMEM] + [VMEM] * 5,
-        out_specs=[VMEM] * 2,
-        out_shape=[
-            jax.ShapeDtypeStruct((channels, width), BF16),
-            jax.ShapeDtypeStruct((channels, width), F32),
-        ],
-        scratch_shapes=[pltpu.VMEM((tokens // n, 2 * width), BF16)],
+        out_specs=[VMEM] * len(shapes),
+        out_shape=shapes,
+        scratch_shapes=[pltpu.VMEM((tokens // n, before.shape[1]), BF16)],
         compiler_params=params(),
         cost_estimate=cost(1, 1),
     )(place, *pieces, gate, mixed, before)
@@ -245,7 +241,7 @@
 
 
 def grads_kernel(
-    grad_ref, gate_ref, value_ref, hidden_ref, taps_ref, out_ref, term_ref, pad_ref
+    scale, grad_ref, gate_ref, value_ref, hidden_ref, taps_ref, out_ref, term_ref, pad_ref
 ):
     _, height, across, channels = hidden_ref.shape
     clear_edges(pad_ref, height, across)
@@ -281,16 +277,16 @@
 
             sums = lax.fori_loop(0, height, row, tuple(jnp.zeros((8, LANES), F32) for _ in range(9)))
             for tap in range(9):
-                term_ref[tap // 3, tap % 3, k : k + 1, lanes] = jnp.sum(
+                term_ref[tap // 3, tap % 3, k : k + 1, lanes] = scale * jnp.sum(
                     sums[tap], axis=0, keepdims=True
                 )
 
 
-def grads(grad, gate_part, value_part, hidden, taps):
+def grads(grad, gate_part, value_part, hidden, taps, scale):
     _, height, across, channels = hidden.shape
     size = height * across * channels
     return pl.pallas_call(
-        grads_kernel,
+        functools.partial(grads_kernel, scale),
         in_specs=[VMEM] * 5,
         out_specs=[VMEM, VMEM],
         out_shape=[
@@ -395,43 +391,38 @@
     last = n // 2
 
     def rows(pieces, numbers, before):
-        return rows_parts(n, order.token, pieces, numbers, 0, sample_gate, proj_weight, mixed, before)
-
-    up = down = own
+        return rows_parts(n, order.token, pieces, numbers, sample_gate, proj_weight, mixed, before)
+
+    half = across // 2
+    state = {("up", 0): own[:half], ("down", 1): own[half:], ("up", 1): own[half:], ("down", 0): own[:half]}
     pieces, numbers, before = [own], [0], None
     for stage in range(1, last + 1):
+        arrived = {}
+        for way, part in state:
+            if stage == last and (way, part) not in (("up", 0), ("down", 1)):
+                arrived[way, part] = order.after(state[way, part], ())
+                continue
+            if stage > 1:
+                state[way, part] = order.after(state[way, part], ())
+            arrived[way, part] = state[way, part]
+            state[way, part] = lax.ppermute(state[way, part], "tensor", right if way == "up" else left)
         if stage > 1:
-            up = order.after(up, ())
-        arrived = [up]
-        up = lax.ppermute(up if stage < last else up[: across // 2], "tensor", right)
-        if stage > 1:
-            down = order.after(down, ())
-        arrived.append(down)
-        down = lax.ppermute(down if stage < last else down[across // 2 :], "tensor", left)
-        if stage > 1:
-            pieces += arrived
-            numbers += [2 * stage - 3, 2 * stage - 2]
+            pieces += [arrived[way, part] for way in ("up", "down") for part in (0, 1)]
+            numbers += [1 - stage, stage - 1]
         if stage == 1:
             hidden = order.after(hidden, ())
             gate_part, value_part, mixed = conv_parts(hidden, taps)
             gate_part, value_part, mixed = order.after((gate_part, value_part, mixed), ())
-        elif stage > 2:
+        else:
             before = order.after(rows(pieces, numbers, before), ())
             pieces, numbers = [], []
-    up, down = order.after((up, down), ())
-    assert not pieces
+    far = list(order.after((state["up", 0], state["down", 1]), ()))
     sums, grad = before
-    far = [up, down]
 
     eighth = depth // 8
     widths = [eighth, 3 * eighth // 2, 3 * eighth // 2]
     firsts = [0, 2 * eighth, 5 * eighth]
-    near, keeps, pairs, far_sums, mines, others = [], [], [], [], [], []
-    for first, width in zip(firsts, widths):
-        (send, keep) = far_parts(n, order.token, far, first, width, sample_gate, mixed, sums)
-        (send, keep, sums) = order.after((send, keep, sums), ())
-        near.append(swap(send, 1))
-        keeps.append(keep)
+    pairs, far_sums, mines, others = [], [], [], []
 
     def begin(u):
         received = order.after(near[u], ())
@@ -444,12 +435,18 @@
         mines.append(order.after(mine, ()))
         others.append(swap(mines[u], 1))
 
+    parts = far_parts(n, order.token, far, firsts, widths, sample_gate, mixed, sums)
+    parts = order.after(parts, ())
+    near = [swap(part, 1) for part in parts[::2]]
+    keeps = parts[1::2]
     begin(0)
     begin(1)
     begin(2)
     grad = order.after(grad, ())
     grad = far_row(n, order.token, far, sample_gate, proj_weight, grad)
-    hidden_grad, terms = grads(grad, gate_part, value_part, hidden, taps)
+    hidden_grad, terms = grads(
+        grad, gate_part, value_part, hidden, taps, grad_scale
+    )
     terms, hidden_grad = order.after((terms, hidden_grad), ())
     total = sum_groups(terms)
     finish(0)
@@ -459,7 +456,7 @@
     hidden_grad = order.after(hidden_grad, ())
     finish(1)
     total, far_sums[2] = order.after((total, far_sums[2]), ())
-    conv_grad = total * grad_scale
+    conv_grad = total
     others[0] = order.after(others[0], ())
     others[1] = order.after(others[1], ())
     finish(2)

time: 85.8 us -> 81.4 us (0.949)
  waiting for transfers between devices: 34.6 us -> 23.2 us
  starting transfers between devices: 17 us -> 23.1 us
  local copies, waits for them, and re-layouts: 6.32 us -> 7.36 us
    ppermute x8 -> x14, waiting for transfers between devices: 25.3 us -> 14.1 us  [on_device(): lax.ppermute(state[way, part], 'tensor', right if way == 'up' else left)]
    ppermute x8 -> x14, starting transfers between devices: 9.21 us -> 15.3 us  [on_device(): lax.ppermute(state[way, part], 'tensor', right if way == 'up' else left)]
    slice x2 -> x1, local copies, waits for them, and re-layouts: 0.04 us -> 1.07 us  [on_device(): own[half:]]
    pallas_call x6 -> x5, Pallas kernels: 15.1 us -> 14.8 us  [the longest x3 6.9 us: rows_parts(): pl.pallas_call(functools.partial(rows_kernel, n, len(pieces), numbers, be...]
  transfers between devices with their start and end apart: 20 -> 26, of which waited for: 10 -> 12; matrix products, arithmetic and copies ran while one was open for 9% -> 9% of each run, Pallas kernels for 27% -> 28%
where the time goes in v4:
time: 81.4 us; the launch traced here: 81.2 us
  Pallas kernels  25.2 us (31%)
  waiting for transfers between devices  23.2 us (29%)
  starting transfers between devices  23.1 us (28%)
  local copies, waits for them, and re-layouts  7.36 us (9%)
  other arithmetic  1.32 us (2%)
  between operations  0.98 us (1%)
    ppermute x14, starting transfers between devices, on_device(): lax.ppermute(state[way, part], 'tensor', right if way == 'up' else left)  15.3 us
    ppermute x14, waiting for transfers between devices, on_device(): lax.ppermute(state[way, part], 'tensor', right if way == 'up' else left)  14.1 us
    ppermute x12, waiting for transfers between devices, swap(): return lax.ppermute(value, 'dp', [(i, i ^ bit) for i in range(n)])  9.15 us
    ppermute x12, starting transfers between devices, swap(): return lax.ppermute(value, 'dp', [(i, i ^ bit) for i in range(n)])  7.85 us
    pallas_call x3, Pallas kernels, rows_parts(): pl.pallas_call(functools.partial(rows_kernel, n, len(pieces), numbers, be...  6.9 us
    pallas_call x1, Pallas kernels, grads(): pl.pallas_call(functools.partial(grads_kernel, scale), in_specs=[VMEM] *...  6.52 us
    pallas_call x1, Pallas kernels, conv_parts(): pl.pallas_call(conv_kernel, in_specs=[VMEM, VMEM], out_specs=[VMEM] * 3,...  6 us
    optimization_barrier x1, local copies, waits for them, and re-layouts, after(): lax.optimization_barrier(flat)  3.48 us
  transfers between devices with their start and end apart: 26, of which 12 were waited for; matrix products, arithmetic and copies ran while one was open for 9% of the time, Pallas kernels for 28%

profile of v4, /device:TPU:0, one launch (start us, length us, event | category | flops | bytes accessed | tf_op | source)
XLA Modules:
  0.0 81.2 jit_solution(11534280033785209420)
XLA Ops:
  0.6 1.1 %slice_bitcast_fusion = (bf16[64,2048]{1,0:T(8,128)(2,1)S(1)}, bf16[64,2048]{1,0:T(8,128)(2,1)S(1)}) fusion(bf16[1,1,128,2048]{3,2,1,0:T(8,128)(2,1)} %param.8), kind=kLoop, calls=%fused_computation.8 | loop fusion | bytes 1048576 | tf_op jit(solution)/shard_map/slice | solution.py:397
  1.7 3.1 %collective-permute-start.3 = (bf16[64,2048]{1,0:T(8,128)(2,1)S(1)}, bf16[64,2048]{1,0:T(8,128)(2,1)S(1)}, u32[]{:S(2)}, u32[]{:S(2)}) collective-permute-start(bf16[64,2048]{1,0:T(8,128)(2,1)S(1)} %get-tuple-element.220), channel_id=1, source_target_pairs={{0,2},{2,4},{4,6},{6,7},{7,5},{5,3},{3,1},{1,0},{8,10},{10,12},{12... | collective-permute-start | bytes 786440 | tf_op jit(solution)/shard_map/ppermute | solution.py:408
  4.8 2.0 %collective-permute-start.1 = (bf16[64,2048]{1,0:T(8,128)(2,1)S(1)}, bf16[64,2048]{1,0:T(8,128)(2,1)S(1)}, u32[]{:S(2)}, u32[]{:S(2)}) collective-permute-start(bf16[64,2048]{1,0:T(8,128)(2,1)S(1)} %get-tuple-element.219), channel_id=1, source_target_pairs={{0,2},{2,4},{4,6},{6,7},{7,5},{5,3},{3,1},{1,0},{8,10},{10,12},{12... | collective-permute-start | bytes 786440 | tf_op jit(solution)/shard_map/ppermute | solution.py:408
  7.6 2.1 %copy.19 = bf16[1,8,128,2,512]{4,2,1,3,0:T(8,128)(2,1)S(1)} copy(bf16[1,8,128,2,512]{4,3,2,1,0:T(2,128)(2,1)} %param.5) | data formatting | bytes 4194304 | tf_op args[0]
  9.7 6.0 %shard_map.76 = (bf16[8,128,512]{2,1,0:T(8,128)(2,1)S(1)}, bf16[8,128,512]{2,1,0:T(8,128)(2,1)S(1)}, bf16[512,1024]{1,0:T(8,128)(2,1)S(1)}) custom-call(bf16[2,8,128,512]{3,2,1,0:T(8,128)(2,1)S(1)} %bitcast.16, f32[18,512]{1,0:T(8,128)S(1)} %reshape.24.weight_ref.taps_ref), custom_call_target="tpu_custom_call" | custom-call | flops 1 | bytes 1 | tf_op jit(solution)/shard_map/pallas_call | solution.py:100
  15.7 2.1 %collective-permute-start.7 = (bf16[64,2048]{1,0:T(8,128)(2,1)S(1)}, bf16[64,2048]{1,0:T(8,128)(2,1)S(1)}, u32[]{:S(2)}, u32[]{:S(2)}) collective-permute-start(bf16[64,2048]{1,0:T(8,128)(2,1)S(1)} %collective-permute-done.3.refs_1_), channel_id=1, source_target_pairs={{0,2},{2,4},{4,6},{6,7},{7,5},{5,3},{3,1},{1,0},{8,10},{10,12},{12... | collective-permute-start | bytes 786440 | tf_op jit(solution)/shard_map/ppermute | solution.py:408
  18.2 1.7 %collective-permute-start.5 = (bf16[64,2048]{1,0:T(8,128)(2,1)S(1)}, bf16[64,2048]{1,0:T(8,128)(2,1)S(1)}, u32[]{:S(2)}, u32[]{:S(2)}) collective-permute-start(bf16[64,2048]{1,0:T(8,128)(2,1)S(1)} %collective-permute-done.1.refs_2_), channel_id=1, source_target_pairs={{0,2},{2,4},{4,6},{6,7},{7,5},{5,3},{3,1},{1,0},{8,10},{10,12},{12... | collective-permute-start | bytes 786440 | tf_op jit(solution)/shard_map/ppermute | solution.py:408
  20.2 2.7 %shard_map.77 = (f32[512,2048]{1,0:T(8,128)S(1)}, f32[1024,512]{1,0:T(8,128)S(1)}) custom-call(s32[2]{0:T(128)S(1)} %pad_add_fusion.place_ref, bf16[128,2048]{1,0:T(8,128)(2,1)S(1)} %bitcast.18, bf16[64,2048]{1,0:T(8,128)(2,1)S(1)} %collective-permute-done.3.refs_1_, bf16[64,2048]{1,0:T(8,128)(2,1)S(1)} %collective-permute-done.1.refs_2_, ...), custom_call_target="tpu_custom_call" | custom-call | flops 1 | bytes 1 | tf_op jit(solution)/shard_map/pallas_call | solution.py:160
  22.9 2.2 %collective-permute-done.7.refs_0_ = bf16[64,2048]{1,0:T(8,128)(2,1)S(1)} collective-permute-done((bf16[64,2048]{1,0:T(8,128)(2,1)S(1)}, bf16[64,2048]{1,0:T(8,128)(2,1)S(1)}, u32[]{:S(2)}, u32[]{:S(2)}) %collective-permute-start.7) | collective-permute-done | bytes 262176 | tf_op jit(solution)/shard_map/ppermute | solution.py:408
  25.0 2.0 %collective-permute-start.11 = (bf16[64,2048]{1,0:T(8,128)(2,1)S(1)}, bf16[64,2048]{1,0:T(8,128)(2,1)S(1)}, u32[]{:S(2)}, u32[]{:S(2)}) collective-permute-start(bf16[64,2048]{1,0:T(8,128)(2,1)S(1)} %collective-permute-done.7.refs_0_), channel_id=1, source_target_pairs={{0,2},{2,4},{4,6},{6,7},{7,5},{5,3},{3,1},{1,0},{8,10},{10,12},{12... | collective-permute-start | bytes 786440 | tf_op jit(solution)/shard_map/ppermute | solution.py:408
  27.1 3.6 %collective-permute-done.5.refs_1_ = bf16[64,2048]{1,0:T(8,128)(2,1)S(1)} collective-permute-done((bf16[64,2048]{1,0:T(8,128)(2,1)S(1)}, bf16[64,2048]{1,0:T(8,128)(2,1)S(1)}, u32[]{:S(2)}, u32[]{:S(2)}) %collective-permute-start.5) | collective-permute-done | bytes 262176 | tf_op jit(solution)/shard_map/ppermute | solution.py:408
  30.7 2.0 %collective-permute-done.4.refs_2_ = bf16[64,2048]{1,0:T(8,128)(2,1)S(1)} collective-permute-done((bf16[64,2048]{1,0:T(8,128)(2,1)S(1)}, bf16[64,2048]{1,0:T(8,128)(2,1)S(1)}, u32[]{:S(2)}, u32[]{:S(2)}) %collective-permute-start.4) | collective-permute-done | bytes 262176 | tf_op jit(solution)/shard_map/ppermute | solution.py:408
  32.7 2.0 %collective-permute-start.9 = (bf16[64,2048]{1,0:T(8,128)(2,1)S(1)}, bf16[64,2048]{1,0:T(8,128)(2,1)S(1)}, u32[]{:S(2)}, u32[]{:S(2)}) collective-permute-start(bf16[64,2048]{1,0:T(8,128)(2,1)S(1)} %collective-permute-done.5.refs_1_), channel_id=1, source_target_pairs={{0,2},{2,4},{4,6},{6,7},{7,5},{5,3},{3,1},{1,0},{8,10},{10,12},{12... | collective-permute-start | bytes 786440 | tf_op jit(solution)/shard_map/ppermute | solution.py:408
  34.7 2.1 %shard_map.78 = (f32[512,2048]{1,0:T(8,128)S(1)}, f32[1024,512]{1,0:T(8,128)S(1)}) custom-call(s32[2]{0:T(128)S(1)} %pad_add_fusion.place_ref, bf16[64,2048]{1,0:T(8,128)(2,1)S(1)} %collective-permute-done.7.refs_0_, bf16[64,2048]{1,0:T(8,128)(2,1)S(1)} %collective-permute-done.5.refs_1_, ...), custom_call_target="tpu_custom_call", output_to_operand_aliasing={{0}: (8, {}), {1}: (9, {})} | custom-call | flops 1 | bytes 1 | tf_op jit(solution)/shard_map/pallas_call | solution.py:160
  36.8 1.4 %collective-permute-done.10.refs_3_ = bf16[64,2048]{1,0:T(8,128)(2,1)S(1)} collective-permute-done((bf16[64,2048]{1,0:T(8,128)(2,1)S(1)}, bf16[64,2048]{1,0:T(8,128)(2,1)S(1)}, u32[]{:S(2)}, u32[]{:S(2)}) %collective-permute-start.10) | collective-permute-done | bytes 262176 | tf_op jit(solution)/shard_map/ppermute | solution.py:408
  38.3 2.0 %collective-permute-start.12 = (bf16[64,2048]{1,0:T(8,128)(2,1)S(1)}, bf16[64,2048]{1,0:T(8,128)(2,1)S(1)}, u32[]{:S(2)}, u32[]{:S(2)}) collective-permute-start(bf16[64,2048]{1,0:T(8,128)(2,1)S(1)} %collective-permute-done.11.refs_0_), channel_id=1, source_target_pairs={{0,2},{2,4},{4,6},{6,7},{7,5},{5,3},{3,1},{1,0},{8,10},{10,12},{12... | collective-permute-start | bytes 786440 | tf_op jit(solution)/shard_map/ppermute | solution.py:408
  40.3 1.6 %collective-permute-done.9.refs_1_ = bf16[64,2048]{1,0:T(8,128)(2,1)S(1)} collective-permute-done((bf16[64,2048]{1,0:T(8,128)(2,1)S(1)}, bf16[64,2048]{1,0:T(8,128)(2,1)S(1)}, u32[]{:S(2)}, u32[]{:S(2)}) %collective-permute-start.9) | collective-permute-done | bytes 262176 | tf_op jit(solution)/shard_map/ppermute | solution.py:408
  41.9 2.0 %collective-permute-done.8.refs_2_ = bf16[64,2048]{1,0:T(8,128)(2,1)S(1)} collective-permute-done((bf16[64,2048]{1,0:T(8,128)(2,1)S(1)}, bf16[64,2048]{1,0:T(8,128)(2,1)S(1)}, u32[]{:S(2)}, u32[]{:S(2)}) %collective-permute-start.8) | collective-permute-done | bytes 262176 | tf_op jit(solution)/shard_map/ppermute | solution.py:408
  43.9 2.1 %shard_map.79 = (f32[512,2048]{1,0:T(8,128)S(1)}, f32[1024,512]{1,0:T(8,128)S(1)}) custom-call(s32[2]{0:T(128)S(1)} %pad_add_fusion.place_ref, bf16[64,2048]{1,0:T(8,128)(2,1)S(1)} %collective-permute-done.11.refs_0_, bf16[64,2048]{1,0:T(8,128)(2,1)S(1)} %collective-permute-done.9.refs_1_, ...), custom_call_target="tpu_custom_call", output_to_operand_aliasing={{0}: (8, {}), {1}: (9, {})} | custom-call | flops 1 | bytes 1 | tf_op jit(solution)/shard_map/pallas_call | solution.py:160
  46.9 1.3 %shard_map.80 = (bf16[512,256]{1,0:T(8,128)(2,1)S(1)}, f32[512,256]{1,0:T(8,128)S(1)}, bf16[512,384]{1,0:T(8,128)(2,1)S(1)}, f32[512,384]{1,0:T(8,128)S(1)}, bf1...) custom-call(s32[2]{0:T(128)S(1)} %pad_add_fusion.place_ref, bf16[64,2048]{1,0:T(8,128)(2,1)S(1)} %collective-permute-done.12.up_ref, ...), custom_call_target="tpu_custom_call" | custom-call | flops 1 | bytes 1 | tf_op jit(solution)/shard_map/pallas_call | solution.py:204
  48.9 0.9 %collective-permute-done.16 = bf16[512,256]{1,0:T(8,128)(2,1)S(1)} collective-permute-done((bf16[512,256]{1,0:T(8,128)(2,1)S(1)}, bf16[512,256]{1,0:T(8,128)(2,1)S(1)}, u32[]{:S(2)}, u32[]{:S(2)}) %collective-permute-start.16) | collective-permute-done | bytes 262176 | tf_op jit(solution)/shard_map/ppermute | solution.py:346
  50.0 1.6 %collective-permute-start.17 = (bf16[512,256]{1,0:T(8,128)(2,1)S(1)}, bf16[512,256]{1,0:T(8,128)(2,1)S(1)}, u32[]{:S(2)}, u32[]{:S(2)}) collective-permute-start(bf16[512,256]{1,0:T(8,128)(2,1)S(1)} %add_convert_fusion.2), channel_id=1, source_target_pairs={{0,16},{8,24},{16,0},{24,8},{1,17},{9,25},{17,1},{25,9},{2,18},{10... | collective-permute-start | bytes 786440 | tf_op jit(solution)/shard_map/ppermute | solution.py:346
  51.6 0.9 %collective-permute-start.22 = (bf16[512,384]{1,0:T(8,128)(2,1)S(1)}, bf16[512,384]{1,0:T(8,128)(2,1)S(1)}, u32[]{:S(2)}, u32[]{:S(2)}) collective-permute-start(bf16[512,384]{1,0:T(8,128)(2,1)S(1)} %add_convert_fusion.1), channel_id=1, source_target_pairs={{0,16},{8,24},{16,0},{24,8},{1,17},{9,25},{17,1},{25,9},{2,18},{10... | collective-permute-start | bytes 1179656 | tf_op jit(solution)/shard_map/ppermute | solution.py:346
  52.6 1.4 %shard_map.81.grad_ref = f32[1024,512]{1,0:T(8,128)S(1)} custom-call(s32[2]{0:T(128)S(1)} %pad_add_fusion.place_ref, bf16[64,2048]{1,0:T(8,128)(2,1)S(1)} %collective-permute-done.12.up_ref, bf16[64,2048]{1,0:T(8,128)(2,1)S(1)} %collective-permute-done.13.down_ref, f32[1,2048]{1,0:T(1,128)S(1)} %copy-done.2, ...), custom_call_target="tpu_custom_call", output_to_operand_aliasing={{}: (5, {})} | custom-call | flops 1 | bytes 1 | tf_op jit(solution)/shard_map/pallas_call | solution.py:231
  54.0 6.5 %shard_map.82 = (bf16[2,8,128,512]{3,2,1,0:T(8,128)(2,1)S(1)}, f32[3,3,2,512]{3,2,1,0:T(2,128)S(1)}) custom-call(f32[1024,512]{1,0:T(8,128)S(1)} %shard_map.81.grad_ref, bf16[8,128,512]{2,1,0:T(8,128)(2,1)S(1)} %get-tuple-element.184.gate_ref, bf16[8,128,512]{2,1,0:T(8,128)(2,1)S(1)} %get-tuple-element.185.value_ref, bf16[2,8,128,512]{3,2,1,0:T(8,128)(2,1)S(1)} %bitcast.17, ...), custom_call_target="tpu_custom_call" | custom-call | flops 1 | bytes 1 | tf_op jit(solution)/shard_map/pallas_call | solution.py:288
  60.5 3.5 %copy.18 = bf16[2,8,128,512]{3,0,2,1:T(2,128)(2,1)} copy(bf16[2,8,128,512]{3,2,1,0:T(8,128)(2,1)S(1)} %get-tuple-element.188) | data formatting | bytes 4194304 | tf_op jit(solution)/shard_map/optimization_barrier | solution.py:340
  64.0 1.2 %collective-permute-start.21 = (bf16[512,384]{1,0:T(8,128)(2,1)S(1)}, bf16[512,384]{1,0:T(8,128)(2,1)S(1)}, u32[]{:S(2)}, u32[]{:S(2)}) collective-permute-start(bf16[512,384]{1,0:T(8,128)(2,1)S(1)} %add_convert_fusion), channel_id=1, source_target_pairs={{0,16},{8,24},{16,0},{24,8},{1,17},{9,25},{17,1},{25,9},{2,18},{10... | collective-permute-start | bytes 1179656 | tf_op jit(solution)/shard_map/ppermute | solution.py:346
  65.3 1.7 %collective-permute-done.22 = bf16[512,384]{1,0:T(8,128)(2,1)S(1)} collective-permute-done((bf16[512,384]{1,0:T(8,128)(2,1)S(1)}, bf16[512,384]{1,0:T(8,128)(2,1)S(1)}, u32[]{:S(2)}, u32[]{:S(2)}) %collective-permute-start.22) | collective-permute-done | bytes 393248 | tf_op jit(solution)/shard_map/ppermute | solution.py:346
  67.2 2.2 %collective-permute-start.20 = (f32[3,3,2,512]{3,2,1,0:T(2,128)S(1)}, f32[3,3,2,512]{3,2,1,0:T(2,128)S(1)}, u32[]{:S(2)}, u32[]{:S(2)}) collective-permute-start(f32[3,3,2,512]{3,2,1,0:T(2,128)S(1)} %get-tuple-element.196), channel_id=1, source_target_pairs={{0,24},{8,16},{16,8},{24,0},{1,25},{9,17},{17,9},{25,1},{2,26},{10... | collective-permute-start | bytes 110600 | tf_op jit(solution)/shard_map/ppermute | solution.py:346
  69.6 5.9 %collective-permute-done.20 = f32[3,3,2,512]{3,2,1,0:T(2,128)S(1)} collective-permute-done((f32[3,3,2,512]{3,2,1,0:T(2,128)S(1)}, f32[3,3,2,512]{3,2,1,0:T(2,128)S(1)}, u32[]{:S(2)}, u32[]{:S(2)}) %collective-permute-start.20) | collective-permute-done | bytes 36896 | tf_op jit(solution)/shard_map/ppermute | solution.py:346
  78.0 1.6 %shard_map.83.refs_2_ = bf16[512,2048]{1,0:T(8,128)(2,1)} custom-call(s32[2]{0:T(128)S(1)} %pad_add_fusion.place_ref, bf16[512,256]{1,0:T(8,128)(2,1)S(1)} %multiply_convert_fusion.2.refs_0_, bf16[512,384]{1,0:T(8,128)(2,1)S(1)} %multiply_convert_fusion.1.refs_1_, bf16[512,256]{1,0:T(8,128)(2,1)S(1)} %collective-permute-done.24.refs_2_, ...), custom_call_target="tpu_custom_call" | custom-call | flops 1 | bytes 1 | tf_op jit(solution)/shard_map/pallas_call | solution.py:322
  79.6 1.4 %shard_map.84 = bf16[512,2048]{1,0:T(8,128)(2,1)} custom-call(s32[2]{0:T(128)S(1)} %pad_add_fusion.place_ref, bf16[512,384]{1,0:T(8,128)(2,1)S(1)} %multiply_convert_fusion.refs_0_, bf16[512,384]{1,0:T(8,128)(2,1)S(1)} %collective-permute-done.25.refs_1_, bf16[512,2048]{1,0:T(8,128)(2,1)} %shard_map.83.refs_2_), custom_call_target="tpu_custom_call", output_to_operand_aliasing={{}: (3, {})} | custom-call | flops 1 | bytes 1 | tf_op jit(solution)/shard_map/pallas_call | solution.py:322
  (47 shorter events, 6.2 us)
Async XLA Ops:
  1.7 14.0 %collective-permute-start.3 = (bf16[64,2048]{1,0:T(8,128)(2,1)S(1)}, bf16[64,2048]{1,0:T(8,128)(2,1)S(1)}, u32[]{:S(2)}, u32[]{:S(2)}) collective-permute-start(bf16[64,2048]{1,0:T(8,128)(2,1)S(1)} %get-tuple-element.220), channel_id=1, source_target_pairs={{0,2},{2,4},{4,6},{6,7},{7,5},{5,3},{3,1},{1,0},{8,10},{10,12},{12... | collective-permute-start | bytes 786440 | tf_op jit(solution)/shard_map/ppermute | solution.py:408
  4.8 13.0 %collective-permute-start.2 = (bf16[64,2048]{1,0:T(8,128)(2,1)S(1)}, bf16[64,2048]{1,0:T(8,128)(2,1)S(1)}, u32[]{:S(2)}, u32[]{:S(2)}) collective-permute-start(bf16[64,2048]{1,0:T(8,128)(2,1)S(1)} %get-tuple-element.219), channel_id=1, source_target_pairs={{0,1},{2,0},{4,2},{6,4},{7,6},{5,7},{3,5},{1,3},{8,9},{10,8},{12,1... | collective-permute-start | bytes 786440 | tf_op jit(solution)/shard_map/ppermute | solution.py:408
  4.8 13.0 %collective-permute-start.1 = (bf16[64,2048]{1,0:T(8,128)(2,1)S(1)}, bf16[64,2048]{1,0:T(8,128)(2,1)S(1)}, u32[]{:S(2)}, u32[]{:S(2)}) collective-permute-start(bf16[64,2048]{1,0:T(8,128)(2,1)S(1)} %get-tuple-element.219), channel_id=1, source_target_pairs={{0,2},{2,4},{4,6},{6,7},{7,5},{5,3},{3,1},{1,0},{8,10},{10,12},{12... | collective-permute-start | bytes 786440 | tf_op jit(solution)/shard_map/ppermute | solution.py:408
  6.8 11.4 %collective-permute-start = (bf16[64,2048]{1,0:T(8,128)(2,1)S(1)}, bf16[64,2048]{1,0:T(8,128)(2,1)S(1)}, u32[]{:S(2)}, u32[]{:S(2)}) collective-permute-start(bf16[64,2048]{1,0:T(8,128)(2,1)S(1)} %get-tuple-element.220), channel_id=1, source_target_pairs={{0,1},{2,0},{4,2},{6,4},{7,6},{5,7},{3,5},{1,3},{8,9},{10,8},{12,1... | collective-permute-start | bytes 786440 | tf_op jit(solution)/shard_map/ppermute | solution.py:408
  7.6 12.6 %copy-start.1 = (bf16[1,1,128,2048]{3,2,1,0:T(8,128)(2,1)S(1)}, bf16[1,1,128,2048]{3,2,1,0:T(8,128)(2,1)}, u32[]{:S(2)}) copy-start(bf16[1,1,128,2048]{3,2,1,0:T(8,128)(2,1)} %param.8) | copy-start | bytes 1572868
  9.7 10.5 %copy-start = (bf16[512,2048]{1,0:T(8,128)(2,1)S(1)}, bf16[512,2048]{1,0:T(8,128)(2,1)}, u32[]{:S(2)}) copy-start(bf16[512,2048]{1,0:T(8,128)(2,1)} %weight_ref.1) | copy-start | bytes 6291460
  9.7 10.5 %copy-start.2 = (f32[1,2048]{1,0:T(1,128)S(1)}, f32[1,2048]{1,0:T(1,128)}, u32[]{:S(2)}) copy-start(f32[1,2048]{1,0:T(1,128)} %gate_ref.3) | copy-start | bytes 24580
  15.7 9.3 %collective-permute-start.7 = (bf16[64,2048]{1,0:T(8,128)(2,1)S(1)}, bf16[64,2048]{1,0:T(8,128)(2,1)S(1)}, u32[]{:S(2)}, u32[]{:S(2)}) collective-permute-start(bf16[64,2048]{1,0:T(8,128)(2,1)S(1)} %collective-permute-done.3.refs_1_), channel_id=1, source_target_pairs={{0,2},{2,4},{4,6},{6,7},{7,5},{5,3},{3,1},{1,0},{8,10},{10,12},{12... | collective-permute-start | bytes 786440 | tf_op jit(solution)/shard_map/ppermute | solution.py:408
  17.8 9.2 %collective-permute-start.6 = (bf16[64,2048]{1,0:T(8,128)(2,1)S(1)}, bf16[64,2048]{1,0:T(8,128)(2,1)S(1)}, u32[]{:S(2)}, u32[]{:S(2)}) collective-permute-start(bf16[64,2048]{1,0:T(8,128)(2,1)S(1)} %collective-permute-done.2.refs_4_), channel_id=1, source_target_pairs={{0,1},{2,0},{4,2},{6,4},{7,6},{5,7},{3,5},{1,3},{8,9},{10,8},{12,1... | collective-permute-start | bytes 786440 | tf_op jit(solution)/shard_map/ppermute | solution.py:408
  18.2 12.5 %collective-permute-start.5 = (bf16[64,2048]{1,0:T(8,128)(2,1)S(1)}, bf16[64,2048]{1,0:T(8,128)(2,1)S(1)}, u32[]{:S(2)}, u32[]{:S(2)}) collective-permute-start(bf16[64,2048]{1,0:T(8,128)(2,1)S(1)} %collective-permute-done.1.refs_2_), channel_id=1, source_target_pairs={{0,2},{2,4},{4,6},{6,7},{7,5},{5,3},{3,1},{1,0},{8,10},{10,12},{12... | collective-permute-start | bytes 786440 | tf_op jit(solution)/shard_map/ppermute | solution.py:408
  19.9 12.8 %collective-permute-start.4 = (bf16[64,2048]{1,0:T(8,128)(2,1)S(1)}, bf16[64,2048]{1,0:T(8,128)(2,1)S(1)}, u32[]{:S(2)}, u32[]{:S(2)}) collective-permute-start(bf16[64,2048]{1,0:T(8,128)(2,1)S(1)} %collective-permute-done.refs_3_), channel_id=1, source_target_pairs={{0,1},{2,0},{4,2},{6,4},{7,6},{5,7},{3,5},{1,3},{8,9},{10,8},{12,1... | collective-permute-start | bytes 786440 | tf_op jit(solution)/shard_map/ppermute | solution.py:408
  25.0 11.8 %collective-permute-start.11 = (bf16[64,2048]{1,0:T(8,128)(2,1)S(1)}, bf16[64,2048]{1,0:T(8,128)(2,1)S(1)}, u32[]{:S(2)}, u32[]{:S(2)}) collective-permute-start(bf16[64,2048]{1,0:T(8,128)(2,1)S(1)} %collective-permute-done.7.refs_0_), channel_id=1, source_target_pairs={{0,2},{2,4},{4,6},{6,7},{7,5},{5,3},{3,1},{1,0},{8,10},{10,12},{12... | collective-permute-start | bytes 786440 | tf_op jit(solution)/shard_map/ppermute | solution.py:408
  27.1 11.2 %collective-permute-start.10 = (bf16[64,2048]{1,0:T(8,128)(2,1)S(1)}, bf16[64,2048]{1,0:T(8,128)(2,1)S(1)}, u32[]{:S(2)}, u32[]{:S(2)}) collective-permute-start(bf16[64,2048]{1,0:T(8,128)(2,1)S(1)} %collective-permute-done.6.refs_3_), channel_id=1, source_target_pairs={{0,1},{2,0},{4,2},{6,4},{7,6},{5,7},{3,5},{1,3},{8,9},{10,8},{12,1... | collective-permute-start | bytes 786440 | tf_op jit(solution)/shard_map/ppermute | solution.py:408
  32.7 11.2 %collective-permute-start.8 = (bf16[64,2048]{1,0:T(8,128)(2,1)S(1)}, bf16[64,2048]{1,0:T(8,128)(2,1)S(1)}, u32[]{:S(2)}, u32[]{:S(2)}) collective-permute-start(bf16[64,2048]{1,0:T(8,128)(2,1)S(1)} %collective-permute-done.4.refs_2_), channel_id=1, source_target_pairs={{0,1},{2,0},{4,2},{6,4},{7,6},{5,7},{3,5},{1,3},{8,9},{10,8},{12,1... | collective-permute-start | bytes 786440 | tf_op jit(solution)/shard_map/ppermute | solution.py:408
  32.7 9.2 %collective-permute-start.9 = (bf16[64,2048]{1,0:T(8,128)(2,1)S(1)}, bf16[64,2048]{1,0:T(8,128)(2,1)S(1)}, u32[]{:S(2)}, u32[]{:S(2)}) collective-permute-start(bf16[64,2048]{1,0:T(8,128)(2,1)S(1)} %collective-permute-done.5.refs_1_), channel_id=1, source_target_pairs={{0,2},{2,4},{4,6},{6,7},{7,5},{5,3},{3,1},{1,0},{8,10},{10,12},{12... | collective-permute-start | bytes 786440 | tf_op jit(solution)/shard_map/ppermute | solution.py:408
  38.3 8.6 %collective-permute-start.13 = (bf16[64,2048]{1,0:T(8,128)(2,1)S(1)}, bf16[64,2048]{1,0:T(8,128)(2,1)S(1)}, u32[]{:S(2)}, u32[]{:S(2)}) collective-permute-start(bf16[64,2048]{1,0:T(8,128)(2,1)S(1)} %collective-permute-done.10.refs_3_), channel_id=1, source_target_pairs={{0,1},{2,0},{4,2},{6,4},{7,6},{5,7},{3,5},{1,3},{8,9},{10,8},{12,1... | collective-permute-start | bytes 786440 | tf_op jit(solution)/shard_map/ppermute | solution.py:408
  38.3 8.6 %collective-permute-start.12 = (bf16[64,2048]{1,0:T(8,128)(2,1)S(1)}, bf16[64,2048]{1,0:T(8,128)(2,1)S(1)}, u32[]{:S(2)}, u32[]{:S(2)}) collective-permute-start(bf16[64,2048]{1,0:T(8,128)(2,1)S(1)} %collective-permute-done.11.refs_0_), channel_id=1, source_target_pairs={{0,2},{2,4},{4,6},{6,7},{7,5},{5,3},{3,1},{1,0},{8,10},{10,12},{12... | collective-permute-start | bytes 786440 | tf_op jit(solution)/shard_map/ppermute | solution.py:408
  48.3 1.6 %collective-permute-start.16 = (bf16[512,256]{1,0:T(8,128)(2,1)S(1)}, bf16[512,256]{1,0:T(8,128)(2,1)S(1)}, u32[]{:S(2)}, u32[]{:S(2)}) collective-permute-start(bf16[512,256]{1,0:T(8,128)(2,1)S(1)} %get-tuple-element.171), channel_id=1, source_target_pairs={{0,8},{8,0},{16,24},{24,16},{1,9},{9,1},{17,25},{25,17},{2,10},{10... | collective-permute-start | bytes 786440 | tf_op jit(solution)/shard_map/ppermute | solution.py:346
  48.4 3.2 %collective-permute-start.15 = (bf16[512,384]{1,0:T(8,128)(2,1)S(1)}, bf16[512,384]{1,0:T(8,128)(2,1)S(1)}, u32[]{:S(2)}, u32[]{:S(2)}) collective-permute-start(bf16[512,384]{1,0:T(8,128)(2,1)S(1)} %get-tuple-element.169), channel_id=1, source_target_pairs={{0,8},{8,0},{16,24},{24,16},{1,9},{9,1},{17,25},{25,17},{2,10},{10... | collective-permute-start | bytes 1179656 | tf_op jit(solution)/shard_map/ppermute | solution.py:346
  48.9 2.8 %collective-permute-start.14 = (bf16[512,384]{1,0:T(8,128)(2,1)S(1)}, bf16[512,384]{1,0:T(8,128)(2,1)S(1)}, u32[]{:S(2)}, u32[]{:S(2)}) collective-permute-start(bf16[512,384]{1,0:T(8,128)(2,1)S(1)} %get-tuple-element.167), channel_id=1, source_target_pairs={{0,8},{8,0},{16,24},{24,16},{1,9},{9,1},{17,25},{25,17},{2,10},{10... | collective-permute-start | bytes 1179656 | tf_op jit(solution)/shard_map/ppermute | solution.py:346
  50.0 15.3 %collective-permute-start.17 = (bf16[512,256]{1,0:T(8,128)(2,1)S(1)}, bf16[512,256]{1,0:T(8,128)(2,1)S(1)}, u32[]{:S(2)}, u32[]{:S(2)}) collective-permute-start(bf16[512,256]{1,0:T(8,128)(2,1)S(1)} %add_convert_fusion.2), channel_id=1, source_target_pairs={{0,16},{8,24},{16,0},{24,8},{1,17},{9,25},{17,1},{25,9},{2,18},{10... | collective-permute-start | bytes 786440 | tf_op jit(solution)/shard_map/ppermute | solution.py:346
  51.6 15.4 %collective-permute-start.22 = (bf16[512,384]{1,0:T(8,128)(2,1)S(1)}, bf16[512,384]{1,0:T(8,128)(2,1)S(1)}, u32[]{:S(2)}, u32[]{:S(2)}) collective-permute-start(bf16[512,384]{1,0:T(8,128)(2,1)S(1)} %add_convert_fusion.1), channel_id=1, source_target_pairs={{0,16},{8,24},{16,0},{24,8},{1,17},{9,25},{17,1},{25,9},{2,18},{10... | collective-permute-start | bytes 1179656 | tf_op jit(solution)/shard_map/ppermute | solution.py:346
  64.0 13.4 %collective-permute-start.21 = (bf16[512,384]{1,0:T(8,128)(2,1)S(1)}, bf16[512,384]{1,0:T(8,128)(2,1)S(1)}, u32[]{:S(2)}, u32[]{:S(2)}) collective-permute-start(bf16[512,384]{1,0:T(8,128)(2,1)S(1)} %add_convert_fusion), channel_id=1, source_target_pairs={{0,16},{8,24},{16,0},{24,8},{1,17},{9,25},{17,1},{25,9},{2,18},{10... | collective-permute-start | bytes 1179656 | tf_op jit(solution)/shard_map/ppermute | solution.py:346
  67.2 10.3 %collective-permute-start.23 = (bf16[512,384]{1,0:T(8,128)(2,1)S(1)}, bf16[512,384]{1,0:T(8,128)(2,1)S(1)}, u32[]{:S(2)}, u32[]{:S(2)}) collective-permute-start(bf16[512,384]{1,0:T(8,128)(2,1)S(1)} %multiply_convert_fusion.1.refs_1_), channel_id=1, source_target_pairs={{0,8},{8,0},{16,24},{24,16},{1,9},{9,1},{17,25},{25,17},{2,10},{10... | collective-permute-start | bytes 1179656 | tf_op jit(solution)/shard_map/ppermute | solution.py:346
  67.2 8.2 %collective-permute-start.20 = (f32[3,3,2,512]{3,2,1,0:T(2,128)S(1)}, f32[3,3,2,512]{3,2,1,0:T(2,128)S(1)}, u32[]{:S(2)}, u32[]{:S(2)}) collective-permute-start(f32[3,3,2,512]{3,2,1,0:T(2,128)S(1)} %get-tuple-element.196), channel_id=1, source_target_pairs={{0,24},{8,16},{16,8},{24,0},{1,25},{9,17},{17,9},{25,1},{2,26},{10... | collective-permute-start | bytes 110600 | tf_op jit(solution)/shard_map/ppermute | solution.py:346
  69.4 7.4 %collective-permute-start.19 = (f32[3,3,2,512]{3,2,1,0:T(2,128)S(1)}, f32[3,3,2,512]{3,2,1,0:T(2,128)S(1)}, u32[]{:S(2)}, u32[]{:S(2)}) collective-permute-start(f32[3,3,2,512]{3,2,1,0:T(2,128)S(1)} %get-tuple-element.196), channel_id=1, source_target_pairs={{0,16},{8,24},{16,0},{24,8},{1,17},{9,25},{17,1},{25,9},{2,18},{10... | collective-permute-start | bytes 110600 | tf_op jit(solution)/shard_map/ppermute | solution.py:346
  69.5 7.3 %collective-permute-start.18 = (f32[3,3,2,512]{3,2,1,0:T(2,128)S(1)}, f32[3,3,2,512]{3,2,1,0:T(2,128)S(1)}, u32[]{:S(2)}, u32[]{:S(2)}) collective-permute-start(f32[3,3,2,512]{3,2,1,0:T(2,128)S(1)} %get-tuple-element.196), channel_id=1, source_target_pairs={{0,8},{8,0},{16,24},{24,16},{1,9},{9,1},{17,25},{25,17},{2,10},{10... | collective-permute-start | bytes 110600 | tf_op jit(solution)/shard_map/ppermute | solution.py:346
  75.4 2.0 %collective-permute-start.24 = (bf16[512,256]{1,0:T(8,128)(2,1)S(1)}, bf16[512,256]{1,0:T(8,128)(2,1)S(1)}, u32[]{:S(2)}, u32[]{:S(2)}) collective-permute-start(bf16[512,256]{1,0:T(8,128)(2,1)S(1)} %multiply_convert_fusion.2.refs_0_), channel_id=1, source_target_pairs={{0,8},{8,0},{16,24},{24,16},{1,9},{9,1},{17,25},{25,17},{2,10},{10... | collective-permute-start | bytes 786440 | tf_op jit(solution)/shard_map/ppermute | solution.py:346
  77.6 2.0 %collective-permute-start.25 = (bf16[512,384]{1,0:T(8,128)(2,1)S(1)}, bf16[512,384]{1,0:T(8,128)(2,1)S(1)}, u32[]{:S(2)}, u32[]{:S(2)}) collective-permute-start(bf16[512,384]{1,0:T(8,128)(2,1)S(1)} %multiply_convert_fusion.refs_0_), channel_id=1, source_target_pairs={{0,8},{8,0},{16,24},{24,16},{1,9},{9,1},{17,25},{25,17},{2,10},{10... | collective-permute-start | bytes 1179656 | tf_op jit(solution)/shard_map/ppermute | solution.py:346

commit v5 on v4

--- a/solution.py
+++ b/solution.py
@@ -53,11 +53,12 @@
             pad_ref[k, r + 1, PAD + across : 2 * PAD + across] = jnp.zeros((PAD, lanes), F32)
 
 
-def conv_kernel(hidden_ref, weight_ref, gate_ref, value_ref, mixed_ref, pad_ref):
+def conv_kernel(first, count, hidden_ref, weight_ref, *refs):
+    gate_ref, value_ref, mixed_ref, pad_ref = refs[-4:]
     _, height, across, channels = hidden_ref.shape
     clear_edges(pad_ref, height, across)
 
-    @pl.loop(0, channels // LANES)
+    @pl.loop(first, first + count)
     def _(c):
         lanes = pl.ds(pl.multiple_of(c * LANES, LANES), LANES)
 
@@ -94,12 +95,11 @@
             mixed_ref[lanes, tokens] = jnp.concatenate(mixed, axis=0).T
 
 
-def conv_parts(hidden, weights):
+def conv_parts(hidden, weights, first, count, before=()):
     _, height, across, channels = hidden.shape
-    size = height * across * channels
-    return pl.pallas_call(
-        conv_kernel,
-        in_specs=[VMEM, VMEM],
+    return pl.pallas_call(
+        functools.partial(conv_kernel, first, count),
+        in_specs=[VMEM] * (2 + len(before)),
         out_specs=[VMEM] * 3,
         out_shape=[
             jax.ShapeDtypeStruct((height, across, channels), BF16),
@@ -107,9 +107,10 @@
             jax.ShapeDtypeStruct((channels, height * across), BF16),
         ],
         scratch_shapes=[pltpu.VMEM((2, height + 2, across + 2 * PAD, LANES), F32)],
-        compiler_params=params(),
-        cost_estimate=cost(size * 60, size * 14, size),
-    )(hidden, weights)
+        input_output_aliases={2 + k: k for k in range(len(before))},
+        compiler_params=params(),
+        cost_estimate=cost(1, 1),
+    )(hidden, weights, *before)
 
 
 def rows_kernel(n, parts, numbers, added, place_ref, *refs):
@@ -299,33 +300,30 @@
     )(grad, gate_part, value_part, hidden, taps)
 
 
-def put_kernel(firsts, place_ref, *refs):
+def put_kernel(firsts, given, place_ref, *refs):
     count = len(firsts)
     out_ref, sems = refs[-2:]
     copies = []
-    for u, first in enumerate(firsts):
-        for k, core in ((u, place_ref[1]), (count + u, 1 - place_ref[1])):
-            half = refs[k].shape[1]
-            columns = pl.ds(pl.multiple_of(first + core * half, LANES), half)
-            copies.append(
-                pltpu.make_async_copy(refs[k], out_ref.at[:, columns], sems.at[k])
-            )
+    for k in range(count + given):
+        half = refs[k].shape[1]
+        core = place_ref[1] if k < count else 1 - place_ref[1]
+        columns = pl.ds(pl.multiple_of(firsts[k % count] + core * half, LANES), half)
+        copies.append(pltpu.make_async_copy(refs[k], out_ref.at[:, columns], sems.at[k]))
     for copy in copies:
         copy.start()
     for copy in copies:
         copy.wait()
 
 
-def put(place, mines, others, firsts, whole, shape):
+def put(place, mines, others, firsts, shape):
     hbm = pl.BlockSpec(memory_space=pl.ANY)
-    arrays = [*mines, *others] + ([] if whole is None else [whole])
-    return pl.pallas_call(
-        functools.partial(put_kernel, firsts),
+    arrays = [*mines, *others]
+    return pl.pallas_call(
+        functools.partial(put_kernel, firsts, len(others)),
         in_specs=[SMEM] + [hbm] * len(arrays),
         out_specs=hbm,
         out_shape=jax.ShapeDtypeStruct(shape, BF16),
-        scratch_shapes=[pltpu.SemaphoreType.DMA((2 * len(mines),))],
-        input_output_aliases={} if whole is None else {len(arrays): 0},
+        scratch_shapes=[pltpu.SemaphoreType.DMA((len(arrays),))],
         compiler_params=params(),
         cost_estimate=cost(1, 1),
     )(place, *arrays)
@@ -353,19 +351,6 @@
     while bit < dp:
         value = value.astype(BF16)
         value = value.astype(F32) + swap(value, bit).astype(F32)
-        bit *= 2
-    return value
-
-
-def sum_groups(value):
-    dp = lax.axis_size("dp")
-    bit = 1
-    if dp >= 4:
-        one, two, three = swap(value, 1), swap(value, 2), swap(value, 3)
-        value = (value + one) + (two + three)
-        bit = 4
-    while bit < dp:
-        value = value + swap(value, bit)
         bit *= 2
     return value
 
@@ -396,6 +381,8 @@
     half = across // 2
     state = {("up", 0): own[:half], ("down", 1): own[half:], ("up", 1): own[half:], ("down", 0): own[:half]}
     pieces, numbers, before = [own], [0], None
+    blocks = channels // LANES
+    early = blocks - blocks // 4
     for stage in range(1, last + 1):
         arrived = {}
         for way, part in state:
@@ -411,9 +398,11 @@
             numbers += [1 - stage, stage - 1]
         if stage == 1:
             hidden = order.after(hidden, ())
-            gate_part, value_part, mixed = conv_parts(hidden, taps)
-            gate_part, value_part, mixed = order.after((gate_part, value_part, mixed), ())
+            conv = order.after(conv_parts(hidden, taps, 0, early), ())
         else:
+            if stage == 2 and early < blocks:
+                conv = order.after(conv_parts(hidden, taps, early, blocks - early, conv), ())
+            gate_part, value_part, mixed = conv
             before = order.after(rows(pieces, numbers, before), ())
             pieces, numbers = [], []
     far = list(order.after((state["up", 0], state["down", 1]), ()))
@@ -448,23 +437,30 @@
         grad, gate_part, value_part, hidden, taps, grad_scale
     )
     terms, hidden_grad = order.after((terms, hidden_grad), ())
-    total = sum_groups(terms)
+    received = swap(terms, 1)
     finish(0)
     hidden_grad = with_layout_constraint(
         jnp.transpose(hidden_grad, (1, 2, 0, 3)), Layout(major_to_minor=(0, 1, 2, 3))
     )
     hidden_grad = order.after(hidden_grad, ())
     finish(1)
-    total, far_sums[2] = order.after((total, far_sums[2]), ())
-    conv_grad = total
+    received = order.after(received, ())
+    terms = order.after(terms + received, ())
+    received = swap(terms, 2)
+    received, far_sums[2] = order.after((received, far_sums[2]), ())
+    conv_grad = terms + received
+    bit = 4
+    while bit < dp:
+        conv_grad = conv_grad + swap(conv_grad, bit)
+        bit *= 2
     others[0] = order.after(others[0], ())
     others[1] = order.after(others[1], ())
     finish(2)
     shape = (channels, depth)
-    whole = put(order.token, mines[:2], others[:2], firsts[:2], None, shape)
-    conv_grad = order.after(conv_grad, whole)
-    others[2] = order.after(others[2], ())
-    whole = put(order.token, mines[2:], others[2:], firsts[2:], whole, shape)
+    whole = put(order.token, mines, others[:2], firsts, shape)
+    whole, others[2] = order.after((whole, others[2]), ())
+    column = firsts[2] + (1 - place[1]) * widths[2]
+    whole = lax.dynamic_update_slice(whole, others[2], (0, column))
     return (hidden_grad[None], whole, conv_grad)
 
 

time: 81.4 us -> 79 us (0.971)
  Pallas kernels: 25.2 us -> 24 us
  waiting for transfers between devices: 23.2 us -> 22 us
    pallas_call x3, Pallas kernels: 9.07 us -> 7.86 us  [the longest x2 6.09 us: conv_parts(): pl.pallas_call(functools.partial(conv_kernel, first, count), in_specs=[VM...]
    ppermute x14, waiting for transfers between devices: 14.1 us -> 13.2 us  [on_device(): lax.ppermute(state[way, part], 'tensor', right if way == 'up' else left)]
    ppermute x12 -> x11, starting transfers between devices: 7.85 us -> 7.15 us  [swap(): return lax.ppermute(value, 'dp', [(i, i ^ bit) for i in range(n)])]
    ppermute x12 -> x11, waiting for transfers between devices: 9.15 us -> 8.77 us  [swap(): return lax.ppermute(value, 'dp', [(i, i ^ bit) for i in range(n)])]
  transfers between devices with their start and end apart: 26 -> 25, of which waited for: 12 -> 12; matrix products, arithmetic and copies ran while one was open for 9% -> 9% of each run, Pallas kernels for 28% -> 29%
where the time goes in v5:
time: 79 us; the launch traced here: 78.8 us
  Pallas kernels  24 us (30%)
  starting transfers between devices  22.5 us (28%)
  waiting for transfers between devices  22 us (28%)
  local copies, waits for them, and re-layouts  8.09 us (10%)
  other arithmetic  1.29 us (2%)
  between operations  0.86 us (1%)
    ppermute x14, starting transfers between devices, on_device(): lax.ppermute(state[way, part], 'tensor', right if way == 'up' else left)  15.3 us
    ppermute x14, waiting for transfers between devices, on_device(): lax.ppermute(state[way, part], 'tensor', right if way == 'up' else left)  13.2 us
    ppermute x11, waiting for transfers between devices, swap(): return lax.ppermute(value, 'dp', [(i, i ^ bit) for i in range(n)])  8.77 us
    ppermute x11, starting transfers between devices, swap(): return lax.ppermute(value, 'dp', [(i, i ^ bit) for i in range(n)])  7.15 us
    pallas_call x3, Pallas kernels, rows_parts(): pl.pallas_call(functools.partial(rows_kernel, n, len(pieces), numbers, be...  6.93 us
    pallas_call x1, Pallas kernels, grads(): pl.pallas_call(functools.partial(grads_kernel, scale), in_specs=[VMEM] *...  6.52 us
    pallas_call x2, Pallas kernels, conv_parts(): pl.pallas_call(functools.partial(conv_kernel, first, count), in_specs=[VM...  6.09 us
    optimization_barrier x1, local copies, waits for them, and re-layouts, after(): lax.optimization_barrier(flat)  3.48 us
  transfers between devices with their start and end apart: 25, of which 12 were waited for; matrix products, arithmetic and copies ran while one was open for 9% of the time, Pallas kernels for 29%

profile of v5, /device:TPU:0, one launch (start us, length us, event | category | flops | bytes accessed | tf_op | source)
XLA Modules:
  0.0 78.8 jit_solution(7048766201962878937)
XLA Ops:
  0.6 1.1 %slice_bitcast_fusion = (bf16[64,2048]{1,0:T(8,128)(2,1)S(1)}, bf16[64,2048]{1,0:T(8,128)(2,1)S(1)}) fusion(bf16[1,1,128,2048]{3,2,1,0:T(8,128)(2,1)} %param.8), kind=kLoop, calls=%fused_computation.8 | loop fusion | bytes 1048576 | tf_op jit(solution)/shard_map/slice | solution.py:382
  1.7 3.1 %collective-permute-start.3 = (bf16[64,2048]{1,0:T(8,128)(2,1)S(1)}, bf16[64,2048]{1,0:T(8,128)(2,1)S(1)}, u32[]{:S(2)}, u32[]{:S(2)}) collective-permute-start(bf16[64,2048]{1,0:T(8,128)(2,1)S(1)} %get-tuple-element.238), channel_id=1, source_target_pairs={{0,2},{2,4},{4,6},{6,7},{7,5},{5,3},{3,1},{1,0},{8,10},{10,12},{12... | collective-permute-start | bytes 786440 | tf_op jit(solution)/shard_map/ppermute | solution.py:395
  4.8 2.0 %collective-permute-start.1 = (bf16[64,2048]{1,0:T(8,128)(2,1)S(1)}, bf16[64,2048]{1,0:T(8,128)(2,1)S(1)}, u32[]{:S(2)}, u32[]{:S(2)}) collective-permute-start(bf16[64,2048]{1,0:T(8,128)(2,1)S(1)} %get-tuple-element.237), channel_id=1, source_target_pairs={{0,2},{2,4},{4,6},{6,7},{7,5},{5,3},{3,1},{1,0},{8,10},{10,12},{12... | collective-permute-start | bytes 786440 | tf_op jit(solution)/shard_map/ppermute | solution.py:395
  7.6 2.0 %copy.21 = bf16[1,8,128,2,512]{4,2,1,3,0:T(8,128)(2,1)S(1)} copy(bf16[1,8,128,2,512]{4,3,2,1,0:T(2,128)(2,1)} %param.5) | data formatting | bytes 4194304 | tf_op args[0]
  9.6 4.5 %shard_map.76 = (bf16[8,128,512]{2,1,0:T(8,128)(2,1)S(1)}, bf16[8,128,512]{2,1,0:T(8,128)(2,1)S(1)}, bf16[512,1024]{1,0:T(8,128)(2,1)S(1)}) custom-call(bf16[2,8,128,512]{3,2,1,0:T(8,128)(2,1)S(1)} %bitcast.16, f32[18,512]{1,0:T(8,128)S(1)} %reshape.24.weight_ref.taps_ref), custom_call_target="tpu_custom_call" | custom-call | flops 1 | bytes 1 | tf_op jit(solution)/shard_map/pallas_call | solution.py:100
  14.2 2.1 %collective-permute-start.7 = (bf16[64,2048]{1,0:T(8,128)(2,1)S(1)}, bf16[64,2048]{1,0:T(8,128)(2,1)S(1)}, u32[]{:S(2)}, u32[]{:S(2)}) collective-permute-start(bf16[64,2048]{1,0:T(8,128)(2,1)S(1)} %collective-permute-done.3.refs_1_), channel_id=1, source_target_pairs={{0,2},{2,4},{4,6},{6,7},{7,5},{5,3},{3,1},{1,0},{8,10},{10,12},{12... | collective-permute-start | bytes 786440 | tf_op jit(solution)/shard_map/ppermute | solution.py:395
  16.3 1.6 %shard_map.77 = (bf16[8,128,512]{2,1,0:T(8,128)(2,1)S(1)}, bf16[8,128,512]{2,1,0:T(8,128)(2,1)S(1)}, bf16[512,1024]{1,0:T(8,128)(2,1)S(1)}) custom-call(bf16[2,8,128,512]{3,2,1,0:T(8,128)(2,1)S(1)} %bitcast.17, f32[18,512]{1,0:T(8,128)S(1)} %reshape.24.weight_ref.taps_ref, ...), custom_call_target="tpu_custom_call", output_to_operand_aliasing={{0}: (2, {}), {1}: (3, {}), {2}: (4, {})} | custom-call | flops 1 | bytes 1 | tf_op jit(solution)/shard_map/pallas_call | solution.py:100
  17.9 1.1 %collective-permute-done.refs_3_ = bf16[64,2048]{1,0:T(8,128)(2,1)S(1)} collective-permute-done((bf16[64,2048]{1,0:T(8,128)(2,1)S(1)}, bf16[64,2048]{1,0:T(8,128)(2,1)S(1)}, u32[]{:S(2)}, u32[]{:S(2)}) %collective-permute-start) | collective-permute-done | bytes 262176 | tf_op jit(solution)/shard_map/ppermute | solution.py:395
  19.9 1.1 %collective-permute-start.5 = (bf16[64,2048]{1,0:T(8,128)(2,1)S(1)}, bf16[64,2048]{1,0:T(8,128)(2,1)S(1)}, u32[]{:S(2)}, u32[]{:S(2)}) collective-permute-start(bf16[64,2048]{1,0:T(8,128)(2,1)S(1)} %collective-permute-done.1.refs_2_), channel_id=1, source_target_pairs={{0,2},{2,4},{4,6},{6,7},{7,5},{5,3},{3,1},{1,0},{8,10},{10,12},{12... | collective-permute-start | bytes 786440 | tf_op jit(solution)/shard_map/ppermute | solution.py:395
  21.0 2.7 %shard_map.78 = (f32[512,2048]{1,0:T(8,128)S(1)}, f32[1024,512]{1,0:T(8,128)S(1)}) custom-call(s32[2]{0:T(128)S(1)} %pad_add_fusion.place_ref, bf16[128,2048]{1,0:T(8,128)(2,1)S(1)} %bitcast.19, bf16[64,2048]{1,0:T(8,128)(2,1)S(1)} %collective-permute-done.3.refs_1_, bf16[64,2048]{1,0:T(8,128)(2,1)S(1)} %collective-permute-done.1.refs_2_, ...), custom_call_target="tpu_custom_call" | custom-call | flops 1 | bytes 1 | tf_op jit(solution)/shard_map/pallas_call | solution.py:161
  23.6 1.9 %collective-permute-start.11 = (bf16[64,2048]{1,0:T(8,128)(2,1)S(1)}, bf16[64,2048]{1,0:T(8,128)(2,1)S(1)}, u32[]{:S(2)}, u32[]{:S(2)}) collective-permute-start(bf16[64,2048]{1,0:T(8,128)(2,1)S(1)} %collective-permute-done.7.refs_0_), channel_id=1, source_target_pairs={{0,2},{2,4},{4,6},{6,7},{7,5},{5,3},{3,1},{1,0},{8,10},{10,12},{12... | collective-permute-start | bytes 786440 | tf_op jit(solution)/shard_map/ppermute | solution.py:395
  25.7 3.4 %collective-permute-done.5.refs_1_ = bf16[64,2048]{1,0:T(8,128)(2,1)S(1)} collective-permute-done((bf16[64,2048]{1,0:T(8,128)(2,1)S(1)}, bf16[64,2048]{1,0:T(8,128)(2,1)S(1)}, u32[]{:S(2)}, u32[]{:S(2)}) %collective-permute-start.5) | collective-permute-done | bytes 262176 | tf_op jit(solution)/shard_map/ppermute | solution.py:395
  29.1 2.0 %collective-permute-done.4.refs_2_ = bf16[64,2048]{1,0:T(8,128)(2,1)S(1)} collective-permute-done((bf16[64,2048]{1,0:T(8,128)(2,1)S(1)}, bf16[64,2048]{1,0:T(8,128)(2,1)S(1)}, u32[]{:S(2)}, u32[]{:S(2)}) %collective-permute-start.4) | collective-permute-done | bytes 262176 | tf_op jit(solution)/shard_map/ppermute | solution.py:395
  31.2 2.0 %collective-permute-start.9 = (bf16[64,2048]{1,0:T(8,128)(2,1)S(1)}, bf16[64,2048]{1,0:T(8,128)(2,1)S(1)}, u32[]{:S(2)}, u32[]{:S(2)}) collective-permute-start(bf16[64,2048]{1,0:T(8,128)(2,1)S(1)} %collective-permute-done.5.refs_1_), channel_id=1, source_target_pairs={{0,2},{2,4},{4,6},{6,7},{7,5},{5,3},{3,1},{1,0},{8,10},{10,12},{12... | collective-permute-start | bytes 786440 | tf_op jit(solution)/shard_map/ppermute | solution.py:395
  33.2 2.1 %shard_map.79 = (f32[512,2048]{1,0:T(8,128)S(1)}, f32[1024,512]{1,0:T(8,128)S(1)}) custom-call(s32[2]{0:T(128)S(1)} %pad_add_fusion.place_ref, bf16[64,2048]{1,0:T(8,128)(2,1)S(1)} %collective-permute-done.7.refs_0_, bf16[64,2048]{1,0:T(8,128)(2,1)S(1)} %collective-permute-done.5.refs_1_, ...), custom_call_target="tpu_custom_call", output_to_operand_aliasing={{0}: (8, {}), {1}: (9, {})} | custom-call | flops 1 | bytes 1 | tf_op jit(solution)/shard_map/pallas_call | solution.py:161
  35.3 1.4 %collective-permute-done.10.refs_3_ = bf16[64,2048]{1,0:T(8,128)(2,1)S(1)} collective-permute-done((bf16[64,2048]{1,0:T(8,128)(2,1)S(1)}, bf16[64,2048]{1,0:T(8,128)(2,1)S(1)}, u32[]{:S(2)}, u32[]{:S(2)}) %collective-permute-start.10) | collective-permute-done | bytes 262176 | tf_op jit(solution)/shard_map/ppermute | solution.py:395
  36.8 2.0 %collective-permute-start.12 = (bf16[64,2048]{1,0:T(8,128)(2,1)S(1)}, bf16[64,2048]{1,0:T(8,128)(2,1)S(1)}, u32[]{:S(2)}, u32[]{:S(2)}) collective-permute-start(bf16[64,2048]{1,0:T(8,128)(2,1)S(1)} %collective-permute-done.11.refs_0_), channel_id=1, source_target_pairs={{0,2},{2,4},{4,6},{6,7},{7,5},{5,3},{3,1},{1,0},{8,10},{10,12},{12... | collective-permute-start | bytes 786440 | tf_op jit(solution)/shard_map/ppermute | solution.py:395
  38.8 1.6 %collective-permute-done.9.refs_1_ = bf16[64,2048]{1,0:T(8,128)(2,1)S(1)} collective-permute-done((bf16[64,2048]{1,0:T(8,128)(2,1)S(1)}, bf16[64,2048]{1,0:T(8,128)(2,1)S(1)}, u32[]{:S(2)}, u32[]{:S(2)}) %collective-permute-start.9) | collective-permute-done | bytes 262176 | tf_op jit(solution)/shard_map/ppermute | solution.py:395
  40.4 2.0 %collective-permute-done.8.refs_2_ = bf16[64,2048]{1,0:T(8,128)(2,1)S(1)} collective-permute-done((bf16[64,2048]{1,0:T(8,128)(2,1)S(1)}, bf16[64,2048]{1,0:T(8,128)(2,1)S(1)}, u32[]{:S(2)}, u32[]{:S(2)}) %collective-permute-start.8) | collective-permute-done | bytes 262176 | tf_op jit(solution)/shard_map/ppermute | solution.py:395
  42.4 2.1 %shard_map.80 = (f32[512,2048]{1,0:T(8,128)S(1)}, f32[1024,512]{1,0:T(8,128)S(1)}) custom-call(s32[2]{0:T(128)S(1)} %pad_add_fusion.place_ref, bf16[64,2048]{1,0:T(8,128)(2,1)S(1)} %collective-permute-done.11.refs_0_, bf16[64,2048]{1,0:T(8,128)(2,1)S(1)} %collective-permute-done.9.refs_1_, ...), custom_call_target="tpu_custom_call", output_to_operand_aliasing={{0}: (8, {}), {1}: (9, {})} | custom-call | flops 1 | bytes 1 | tf_op jit(solution)/shard_map/pallas_call | solution.py:161
  44.5 1.7 %collective-permute-done.13.down_ref = bf16[64,2048]{1,0:T(8,128)(2,1)S(1)} collective-permute-done((bf16[64,2048]{1,0:T(8,128)(2,1)S(1)}, bf16[64,2048]{1,0:T(8,128)(2,1)S(1)}, u32[]{:S(2)}, u32[]{:S(2)}) %collective-permute-start.13) | collective-permute-done | bytes 262176 | tf_op jit(solution)/shard_map/ppermute | solution.py:395
  46.3 1.3 %shard_map.81 = (bf16[512,256]{1,0:T(8,128)(2,1)S(1)}, f32[512,256]{1,0:T(8,128)S(1)}, bf16[512,384]{1,0:T(8,128)(2,1)S(1)}, f32[512,384]{1,0:T(8,128)S(1)}, bf1...) custom-call(s32[2]{0:T(128)S(1)} %pad_add_fusion.place_ref, bf16[64,2048]{1,0:T(8,128)(2,1)S(1)} %collective-permute-done.12.up_ref, ...), custom_call_target="tpu_custom_call" | custom-call | flops 1 | bytes 1 | tf_op jit(solution)/shard_map/pallas_call | solution.py:205
  49.3 1.6 %collective-permute-start.17 = (bf16[512,256]{1,0:T(8,128)(2,1)S(1)}, bf16[512,256]{1,0:T(8,128)(2,1)S(1)}, u32[]{:S(2)}, u32[]{:S(2)}) collective-permute-start(bf16[512,256]{1,0:T(8,128)(2,1)S(1)} %add_convert_fusion.2), channel_id=1, source_target_pairs={{0,16},{8,24},{16,0},{24,8},{1,17},{9,25},{17,1},{25,9},{2,18},{10... | collective-permute-start | bytes 786440 | tf_op jit(solution)/shard_map/ppermute | solution.py:344
  51.9 1.4 %shard_map.82.grad_ref = f32[1024,512]{1,0:T(8,128)S(1)} custom-call(s32[2]{0:T(128)S(1)} %pad_add_fusion.place_ref, bf16[64,2048]{1,0:T(8,128)(2,1)S(1)} %collective-permute-done.12.up_ref, bf16[64,2048]{1,0:T(8,128)(2,1)S(1)} %collective-permute-done.13.down_ref, f32[1,2048]{1,0:T(1,128)S(1)} %copy-done.2, ...), custom_call_target="tpu_custom_call", output_to_operand_aliasing={{}: (5, {})} | custom-call | flops 1 | bytes 1 | tf_op jit(solution)/shard_map/pallas_call | solution.py:232
  53.3 6.5 %shard_map.83 = (bf16[2,8,128,512]{3,2,1,0:T(8,128)(2,1)S(1)}, f32[3,3,2,512]{3,2,1,0:T(2,128)S(1)}) custom-call(f32[1024,512]{1,0:T(8,128)S(1)} %shard_map.82.grad_ref, bf16[8,128,512]{2,1,0:T(8,128)(2,1)S(1)} %get-tuple-element.200.gate_ref, bf16[8,128,512]{2,1,0:T(8,128)(2,1)S(1)} %get-tuple-element.201.value_ref, bf16[2,8,128,512]{3,2,1,0:T(8,128)(2,1)S(1)} %bitcast.18, ...), custom_call_target="tpu_custom_call" | custom-call | flops 1 | bytes 1 | tf_op jit(solution)/shard_map/pallas_call | solution.py:289
  59.8 3.5 %copy.20 = bf16[2,8,128,512]{3,0,2,1:T(2,128)(2,1)} copy(bf16[2,8,128,512]{3,2,1,0:T(8,128)(2,1)S(1)} %get-tuple-element.204) | data formatting | bytes 4194304 | tf_op jit(solution)/shard_map/optimization_barrier | solution.py:338
  63.3 1.2 %collective-permute-start.21 = (bf16[512,384]{1,0:T(8,128)(2,1)S(1)}, bf16[512,384]{1,0:T(8,128)(2,1)S(1)}, u32[]{:S(2)}, u32[]{:S(2)}) collective-permute-start(bf16[512,384]{1,0:T(8,128)(2,1)S(1)} %add_convert_fusion), channel_id=1, source_target_pairs={{0,16},{8,24},{16,0},{24,8},{1,17},{9,25},{17,1},{25,9},{2,18},{10... | collective-permute-start | bytes 1179656 | tf_op jit(solution)/shard_map/ppermute | solution.py:344
  64.6 1.8 %collective-permute-done.19 = bf16[512,384]{1,0:T(8,128)(2,1)S(1)} collective-permute-done((bf16[512,384]{1,0:T(8,128)(2,1)S(1)}, bf16[512,384]{1,0:T(8,128)(2,1)S(1)}, u32[]{:S(2)}, u32[]{:S(2)}) %collective-permute-start.19) | collective-permute-done | bytes 393248 | tf_op jit(solution)/shard_map/ppermute | solution.py:344
  67.2 1.6 %collective-permute-done.18 = f32[3,3,2,512]{3,2,1,0:T(2,128)S(1)} collective-permute-done((f32[3,3,2,512]{3,2,1,0:T(2,128)S(1)}, f32[3,3,2,512]{3,2,1,0:T(2,128)S(1)}, u32[]{:S(2)}, u32[]{:S(2)}) %collective-permute-start.18) | collective-permute-done | bytes 36896 | tf_op jit(solution)/shard_map/ppermute | solution.py:344
  68.8 2.1 %collective-permute-start.20 = (f32[3,3,2,512]{3,2,1,0:T(2,128)S(1)}, f32[3,3,2,512]{3,2,1,0:T(2,128)S(1)}, u32[]{:S(2)}, u32[]{:S(2)}) collective-permute-start(f32[3,3,2,512]{3,2,1,0:T(2,128)S(1)} %add.34), channel_id=1, source_target_pairs={{0,16},{8,24},{16,0},{24,8},{1,17},{9,25},{17,1},{25,9},{2,18},{10... | collective-permute-start | bytes 110600 | tf_op jit(solution)/shard_map/ppermute | solution.py:344
  70.9 4.1 %collective-permute-done.21 = bf16[512,384]{1,0:T(8,128)(2,1)S(1)} collective-permute-done((bf16[512,384]{1,0:T(8,128)(2,1)S(1)}, bf16[512,384]{1,0:T(8,128)(2,1)S(1)}, u32[]{:S(2)}, u32[]{:S(2)}) %collective-permute-start.21) | collective-permute-done | bytes 393248 | tf_op jit(solution)/shard_map/ppermute | solution.py:344
  76.2 1.8 %shard_map.84 = bf16[512,2048]{1,0:T(8,128)(2,1)} custom-call(s32[2]{0:T(128)S(1)} %pad_add_fusion.place_ref, bf16[512,256]{1,0:T(8,128)(2,1)S(1)} %multiply_convert_fusion.2.refs_0_, bf16[512,384]{1,0:T(8,128)(2,1)S(1)} %multiply_convert_fusion.1.refs_1_, bf16[512,384]{1,0:T(8,128)(2,1)S(1)} %multiply_convert_fusion.refs_2_, ...), custom_call_target="tpu_custom_call" | custom-call | flops 1 | bytes 1 | tf_op jit(solution)/shard_map/pallas_call | solution.py:321
  (47 shorter events, 7.6 us)
Async XLA Ops:
  1.7 12.5 %collective-permute-start.3 = (bf16[64,2048]{1,0:T(8,128)(2,1)S(1)}, bf16[64,2048]{1,0:T(8,128)(2,1)S(1)}, u32[]{:S(2)}, u32[]{:S(2)}) collective-permute-start(bf16[64,2048]{1,0:T(8,128)(2,1)S(1)} %get-tuple-element.238), channel_id=1, source_target_pairs={{0,2},{2,4},{4,6},{6,7},{7,5},{5,3},{3,1},{1,0},{8,10},{10,12},{12... | collective-permute-start | bytes 786440 | tf_op jit(solution)/shard_map/ppermute | solution.py:395
  4.8 11.5 %collective-permute-start.2 = (bf16[64,2048]{1,0:T(8,128)(2,1)S(1)}, bf16[64,2048]{1,0:T(8,128)(2,1)S(1)}, u32[]{:S(2)}, u32[]{:S(2)}) collective-permute-start(bf16[64,2048]{1,0:T(8,128)(2,1)S(1)} %get-tuple-element.237), channel_id=1, source_target_pairs={{0,1},{2,0},{4,2},{6,4},{7,6},{5,7},{3,5},{1,3},{8,9},{10,8},{12,1... | collective-permute-start | bytes 786440 | tf_op jit(solution)/shard_map/ppermute | solution.py:395
  4.8 13.1 %collective-permute-start.1 = (bf16[64,2048]{1,0:T(8,128)(2,1)S(1)}, bf16[64,2048]{1,0:T(8,128)(2,1)S(1)}, u32[]{:S(2)}, u32[]{:S(2)}) collective-permute-start(bf16[64,2048]{1,0:T(8,128)(2,1)S(1)} %get-tuple-element.237), channel_id=1, source_target_pairs={{0,2},{2,4},{4,6},{6,7},{7,5},{5,3},{3,1},{1,0},{8,10},{10,12},{12... | collective-permute-start | bytes 786440 | tf_op jit(solution)/shard_map/ppermute | solution.py:395
  6.8 12.1 %collective-permute-start = (bf16[64,2048]{1,0:T(8,128)(2,1)S(1)}, bf16[64,2048]{1,0:T(8,128)(2,1)S(1)}, u32[]{:S(2)}, u32[]{:S(2)}) collective-permute-start(bf16[64,2048]{1,0:T(8,128)(2,1)S(1)} %get-tuple-element.238), channel_id=1, source_target_pairs={{0,1},{2,0},{4,2},{6,4},{7,6},{5,7},{3,5},{1,3},{8,9},{10,8},{12,1... | collective-permute-start | bytes 786440 | tf_op jit(solution)/shard_map/ppermute | solution.py:395
  14.2 6.8 %copy-start = (bf16[512,2048]{1,0:T(8,128)(2,1)S(1)}, bf16[512,2048]{1,0:T(8,128)(2,1)}, u32[]{:S(2)}) copy-start(bf16[512,2048]{1,0:T(8,128)(2,1)} %weight_ref.1) | copy-start | bytes 6291460
  14.2 6.8 %copy-start.1 = (bf16[1,1,128,2048]{3,2,1,0:T(8,128)(2,1)S(1)}, bf16[1,1,128,2048]{3,2,1,0:T(8,128)(2,1)}, u32[]{:S(2)}) copy-start(bf16[1,1,128,2048]{3,2,1,0:T(8,128)(2,1)} %param.8) | copy-start | bytes 1572868
  14.2 6.8 %copy-start.2 = (f32[1,2048]{1,0:T(1,128)S(1)}, f32[1,2048]{1,0:T(1,128)}, u32[]{:S(2)}) copy-start(f32[1,2048]{1,0:T(1,128)} %gate_ref.3) | copy-start | bytes 24580
  14.2 9.4 %collective-permute-start.7 = (bf16[64,2048]{1,0:T(8,128)(2,1)S(1)}, bf16[64,2048]{1,0:T(8,128)(2,1)S(1)}, u32[]{:S(2)}, u32[]{:S(2)}) collective-permute-start(bf16[64,2048]{1,0:T(8,128)(2,1)S(1)} %collective-permute-done.3.refs_1_), channel_id=1, source_target_pairs={{0,2},{2,4},{4,6},{6,7},{7,5},{5,3},{3,1},{1,0},{8,10},{10,12},{12... | collective-permute-start | bytes 786440 | tf_op jit(solution)/shard_map/ppermute | solution.py:395
  16.3 9.2 %collective-permute-start.6 = (bf16[64,2048]{1,0:T(8,128)(2,1)S(1)}, bf16[64,2048]{1,0:T(8,128)(2,1)S(1)}, u32[]{:S(2)}, u32[]{:S(2)}) collective-permute-start(bf16[64,2048]{1,0:T(8,128)(2,1)S(1)} %collective-permute-done.2.refs_4_), channel_id=1, source_target_pairs={{0,1},{2,0},{4,2},{6,4},{7,6},{5,7},{3,5},{1,3},{8,9},{10,8},{12,1... | collective-permute-start | bytes 786440 | tf_op jit(solution)/shard_map/ppermute | solution.py:395
  18.9 12.2 %collective-permute-start.4 = (bf16[64,2048]{1,0:T(8,128)(2,1)S(1)}, bf16[64,2048]{1,0:T(8,128)(2,1)S(1)}, u32[]{:S(2)}, u32[]{:S(2)}) collective-permute-start(bf16[64,2048]{1,0:T(8,128)(2,1)S(1)} %collective-permute-done.refs_3_), channel_id=1, source_target_pairs={{0,1},{2,0},{4,2},{6,4},{7,6},{5,7},{3,5},{1,3},{8,9},{10,8},{12,1... | collective-permute-start | bytes 786440 | tf_op jit(solution)/shard_map/ppermute | solution.py:395
  19.9 9.2 %collective-permute-start.5 = (bf16[64,2048]{1,0:T(8,128)(2,1)S(1)}, bf16[64,2048]{1,0:T(8,128)(2,1)S(1)}, u32[]{:S(2)}, u32[]{:S(2)}) collective-permute-start(bf16[64,2048]{1,0:T(8,128)(2,1)S(1)} %collective-permute-done.1.refs_2_), channel_id=1, source_target_pairs={{0,2},{2,4},{4,6},{6,7},{7,5},{5,3},{3,1},{1,0},{8,10},{10,12},{12... | collective-permute-start | bytes 786440 | tf_op jit(solution)/shard_map/ppermute | solution.py:395
  23.6 11.7 %collective-permute-start.11 = (bf16[64,2048]{1,0:T(8,128)(2,1)S(1)}, bf16[64,2048]{1,0:T(8,128)(2,1)S(1)}, u32[]{:S(2)}, u32[]{:S(2)}) collective-permute-start(bf16[64,2048]{1,0:T(8,128)(2,1)S(1)} %collective-permute-done.7.refs_0_), channel_id=1, source_target_pairs={{0,2},{2,4},{4,6},{6,7},{7,5},{5,3},{3,1},{1,0},{8,10},{10,12},{12... | collective-permute-start | bytes 786440 | tf_op jit(solution)/shard_map/ppermute | solution.py:395
  25.5 11.2 %collective-permute-start.10 = (bf16[64,2048]{1,0:T(8,128)(2,1)S(1)}, bf16[64,2048]{1,0:T(8,128)(2,1)S(1)}, u32[]{:S(2)}, u32[]{:S(2)}) collective-permute-start(bf16[64,2048]{1,0:T(8,128)(2,1)S(1)} %collective-permute-done.6.refs_3_), channel_id=1, source_target_pairs={{0,1},{2,0},{4,2},{6,4},{7,6},{5,7},{3,5},{1,3},{8,9},{10,8},{12,1... | collective-permute-start | bytes 786440 | tf_op jit(solution)/shard_map/ppermute | solution.py:395
  31.2 11.2 %collective-permute-start.8 = (bf16[64,2048]{1,0:T(8,128)(2,1)S(1)}, bf16[64,2048]{1,0:T(8,128)(2,1)S(1)}, u32[]{:S(2)}, u32[]{:S(2)}) collective-permute-start(bf16[64,2048]{1,0:T(8,128)(2,1)S(1)} %collective-permute-done.4.refs_2_), channel_id=1, source_target_pairs={{0,1},{2,0},{4,2},{6,4},{7,6},{5,7},{3,5},{1,3},{8,9},{10,8},{12,1... | collective-permute-start | bytes 786440 | tf_op jit(solution)/shard_map/ppermute | solution.py:395
  31.2 9.2 %collective-permute-start.9 = (bf16[64,2048]{1,0:T(8,128)(2,1)S(1)}, bf16[64,2048]{1,0:T(8,128)(2,1)S(1)}, u32[]{:S(2)}, u32[]{:S(2)}) collective-permute-start(bf16[64,2048]{1,0:T(8,128)(2,1)S(1)} %collective-permute-done.5.refs_1_), channel_id=1, source_target_pairs={{0,2},{2,4},{4,6},{6,7},{7,5},{5,3},{3,1},{1,0},{8,10},{10,12},{12... | collective-permute-start | bytes 786440 | tf_op jit(solution)/shard_map/ppermute | solution.py:395
  36.8 9.5 %collective-permute-start.13 = (bf16[64,2048]{1,0:T(8,128)(2,1)S(1)}, bf16[64,2048]{1,0:T(8,128)(2,1)S(1)}, u32[]{:S(2)}, u32[]{:S(2)}) collective-permute-start(bf16[64,2048]{1,0:T(8,128)(2,1)S(1)} %collective-permute-done.10.refs_3_), channel_id=1, source_target_pairs={{0,1},{2,0},{4,2},{6,4},{7,6},{5,7},{3,5},{1,3},{8,9},{10,8},{12,1... | collective-permute-start | bytes 786440 | tf_op jit(solution)/shard_map/ppermute | solution.py:395
  36.8 9.5 %collective-permute-start.12 = (bf16[64,2048]{1,0:T(8,128)(2,1)S(1)}, bf16[64,2048]{1,0:T(8,128)(2,1)S(1)}, u32[]{:S(2)}, u32[]{:S(2)}) collective-permute-start(bf16[64,2048]{1,0:T(8,128)(2,1)S(1)} %collective-permute-done.11.refs_0_), channel_id=1, source_target_pairs={{0,2},{2,4},{4,6},{6,7},{7,5},{5,3},{3,1},{1,0},{8,10},{10,12},{12... | collective-permute-start | bytes 786440 | tf_op jit(solution)/shard_map/ppermute | solution.py:395
  47.6 1.6 %collective-permute-start.16 = (bf16[512,256]{1,0:T(8,128)(2,1)S(1)}, bf16[512,256]{1,0:T(8,128)(2,1)S(1)}, u32[]{:S(2)}, u32[]{:S(2)}) collective-permute-start(bf16[512,256]{1,0:T(8,128)(2,1)S(1)} %get-tuple-element.187), channel_id=1, source_target_pairs={{0,8},{8,0},{16,24},{24,16},{1,9},{9,1},{17,25},{25,17},{2,10},{10... | collective-permute-start | bytes 786440 | tf_op jit(solution)/shard_map/ppermute | solution.py:344
  47.7 3.2 %collective-permute-start.15 = (bf16[512,384]{1,0:T(8,128)(2,1)S(1)}, bf16[512,384]{1,0:T(8,128)(2,1)S(1)}, u32[]{:S(2)}, u32[]{:S(2)}) collective-permute-start(bf16[512,384]{1,0:T(8,128)(2,1)S(1)} %get-tuple-element.185), channel_id=1, source_target_pairs={{0,8},{8,0},{16,24},{24,16},{1,9},{9,1},{17,25},{25,17},{2,10},{10... | collective-permute-start | bytes 1179656 | tf_op jit(solution)/shard_map/ppermute | solution.py:344
  48.2 2.8 %collective-permute-start.14 = (bf16[512,384]{1,0:T(8,128)(2,1)S(1)}, bf16[512,384]{1,0:T(8,128)(2,1)S(1)}, u32[]{:S(2)}, u32[]{:S(2)}) collective-permute-start(bf16[512,384]{1,0:T(8,128)(2,1)S(1)} %get-tuple-element.183), channel_id=1, source_target_pairs={{0,8},{8,0},{16,24},{24,16},{1,9},{9,1},{17,25},{25,17},{2,10},{10... | collective-permute-start | bytes 1179656 | tf_op jit(solution)/shard_map/ppermute | solution.py:344
  49.3 15.2 %collective-permute-start.17 = (bf16[512,256]{1,0:T(8,128)(2,1)S(1)}, bf16[512,256]{1,0:T(8,128)(2,1)S(1)}, u32[]{:S(2)}, u32[]{:S(2)}) collective-permute-start(bf16[512,256]{1,0:T(8,128)(2,1)S(1)} %add_convert_fusion.2), channel_id=1, source_target_pairs={{0,16},{8,24},{16,0},{24,8},{1,17},{9,25},{17,1},{25,9},{2,18},{10... | collective-permute-start | bytes 786440 | tf_op jit(solution)/shard_map/ppermute | solution.py:344
  51.0 15.4 %collective-permute-start.19 = (bf16[512,384]{1,0:T(8,128)(2,1)S(1)}, bf16[512,384]{1,0:T(8,128)(2,1)S(1)}, u32[]{:S(2)}, u32[]{:S(2)}) collective-permute-start(bf16[512,384]{1,0:T(8,128)(2,1)S(1)} %add_convert_fusion.1), channel_id=1, source_target_pairs={{0,16},{8,24},{16,0},{24,8},{1,17},{9,25},{17,1},{25,9},{2,18},{10... | collective-permute-start | bytes 1179656 | tf_op jit(solution)/shard_map/ppermute | solution.py:344
  63.3 11.6 %collective-permute-start.21 = (bf16[512,384]{1,0:T(8,128)(2,1)S(1)}, bf16[512,384]{1,0:T(8,128)(2,1)S(1)}, u32[]{:S(2)}, u32[]{:S(2)}) collective-permute-start(bf16[512,384]{1,0:T(8,128)(2,1)S(1)} %add_convert_fusion), channel_id=1, source_target_pairs={{0,16},{8,24},{16,0},{24,8},{1,17},{9,25},{17,1},{25,9},{2,18},{10... | collective-permute-start | bytes 1179656 | tf_op jit(solution)/shard_map/ppermute | solution.py:344
  66.5 8.8 %collective-permute-start.22 = (bf16[512,384]{1,0:T(8,128)(2,1)S(1)}, bf16[512,384]{1,0:T(8,128)(2,1)S(1)}, u32[]{:S(2)}, u32[]{:S(2)}) collective-permute-start(bf16[512,384]{1,0:T(8,128)(2,1)S(1)} %multiply_convert_fusion.1.refs_1_), channel_id=1, source_target_pairs={{0,8},{8,0},{16,24},{24,16},{1,9},{9,1},{17,25},{25,17},{2,10},{10... | collective-permute-start | bytes 1179656 | tf_op jit(solution)/shard_map/ppermute | solution.py:344
  66.6 8.7 %collective-permute-start.23 = (bf16[512,256]{1,0:T(8,128)(2,1)S(1)}, bf16[512,256]{1,0:T(8,128)(2,1)S(1)}, u32[]{:S(2)}, u32[]{:S(2)}) collective-permute-start(bf16[512,256]{1,0:T(8,128)(2,1)S(1)} %multiply_convert_fusion.2.refs_0_), channel_id=1, source_target_pairs={{0,8},{8,0},{16,24},{24,16},{1,9},{9,1},{17,25},{25,17},{2,10},{10... | collective-permute-start | bytes 786440 | tf_op jit(solution)/shard_map/ppermute | solution.py:344
  67.1 1.6 %collective-permute-start.18 = (f32[3,3,2,512]{3,2,1,0:T(2,128)S(1)}, f32[3,3,2,512]{3,2,1,0:T(2,128)S(1)}, u32[]{:S(2)}, u32[]{:S(2)}) collective-permute-start(f32[3,3,2,512]{3,2,1,0:T(2,128)S(1)} %get-tuple-element.212), channel_id=1, source_target_pairs={{0,8},{8,0},{16,24},{24,16},{1,9},{9,1},{17,25},{25,17},{2,10},{10... | collective-permute-start | bytes 110600 | tf_op jit(solution)/shard_map/ppermute | solution.py:344
  68.8 6.6 %collective-permute-start.20 = (f32[3,3,2,512]{3,2,1,0:T(2,128)S(1)}, f32[3,3,2,512]{3,2,1,0:T(2,128)S(1)}, u32[]{:S(2)}, u32[]{:S(2)}) collective-permute-start(f32[3,3,2,512]{3,2,1,0:T(2,128)S(1)} %add.34), channel_id=1, source_target_pairs={{0,16},{8,24},{16,0},{24,8},{1,17},{9,25},{17,1},{25,9},{2,18},{10... | collective-permute-start | bytes 110600 | tf_op jit(solution)/shard_map/ppermute | solution.py:344
  75.5 2.5 %collective-permute-start.24 = (bf16[512,384]{1,0:T(8,128)(2,1)S(1)}, bf16[512,384]{1,0:T(8,128)(2,1)S(1)}, u32[]{:S(2)}, u32[]{:S(2)}) collective-permute-start(bf16[512,384]{1,0:T(8,128)(2,1)S(1)} %multiply_convert_fusion.refs_2_), channel_id=1, source_target_pairs={{0,8},{8,0},{16,24},{24,16},{1,9},{9,1},{17,25},{25,17},{2,10},{10... | collective-permute-start | bytes 1179656 | tf_op jit(solution)/shard_map/ppermute | solution.py:344

commit v6 on v5

--- a/solution.py
+++ b/solution.py
@@ -302,7 +302,13 @@
 
 def put_kernel(firsts, given, place_ref, *refs):
     count = len(firsts)
-    out_ref, sems = refs[-2:]
+    one_ref, two_ref, out_ref, total_ref, shares_ref, sems, share_sems = refs[-7:]
+    shares = [
+        pltpu.make_async_copy(ref, shares_ref.at[k], share_sems.at[k])
+        for k, ref in enumerate((one_ref, two_ref))
+    ]
+    for copy in shares:
+        copy.start()
     copies = []
     for k in range(count + given):
         half = refs[k].shape[1]
@@ -311,22 +317,32 @@
         copies.append(pltpu.make_async_copy(refs[k], out_ref.at[:, columns], sems.at[k]))
     for copy in copies:
         copy.start()
+    for copy in shares:
+        copy.wait()
+    shares_ref[2] = shares_ref[0] + shares_ref[1]
+    total = pltpu.make_async_copy(shares_ref.at[2], total_ref, share_sems.at[2])
+    total.start()
     for copy in copies:
         copy.wait()
-
-
-def put(place, mines, others, firsts, shape):
+    total.wait()
+
+
+def put(place, mines, others, firsts, shape, one, two):
     hbm = pl.BlockSpec(memory_space=pl.ANY)
     arrays = [*mines, *others]
     return pl.pallas_call(
         functools.partial(put_kernel, firsts, len(others)),
-        in_specs=[SMEM] + [hbm] * len(arrays),
-        out_specs=hbm,
-        out_shape=jax.ShapeDtypeStruct(shape, BF16),
-        scratch_shapes=[pltpu.SemaphoreType.DMA((len(arrays),))],
+        in_specs=[SMEM] + [hbm] * (len(arrays) + 2),
+        out_specs=[hbm, hbm],
+        out_shape=[jax.ShapeDtypeStruct(shape, BF16), jax.ShapeDtypeStruct(one.shape, F32)],
+        scratch_shapes=[
+            pltpu.VMEM((3, *one.shape), F32),
+            pltpu.SemaphoreType.DMA((len(arrays),)),
+            pltpu.SemaphoreType.DMA((3,)),
+        ],
         compiler_params=params(),
         cost_estimate=cost(1, 1),
-    )(place, *arrays)
+    )(place, *arrays, one, two)
 
 
 class Order:
@@ -409,8 +425,8 @@
     sums, grad = before
 
     eighth = depth // 8
-    widths = [eighth, 3 * eighth // 2, 3 * eighth // 2]
-    firsts = [0, 2 * eighth, 5 * eighth]
+    widths = [2 * eighth // 2, 3 * eighth // 2, 3 * eighth // 2]
+    firsts = [sum(widths[:u]) * 2 for u in range(len(widths))]
     pairs, far_sums, mines, others = [], [], [], []
 
     def begin(u):
@@ -448,16 +464,17 @@
     terms = order.after(terms + received, ())
     received = swap(terms, 2)
     received, far_sums[2] = order.after((received, far_sums[2]), ())
-    conv_grad = terms + received
+    others[0] = order.after(others[0], ())
+    others[1] = order.after(others[1], ())
+    finish(2)
+    shape = (channels, depth)
+    whole, conv_grad = put(
+        order.token, mines, others[:2], firsts, shape, terms, received
+    )
     bit = 4
     while bit < dp:
         conv_grad = conv_grad + swap(conv_grad, bit)
         bit *= 2
-    others[0] = order.after(others[0], ())
-    others[1] = order.after(others[1], ())
-    finish(2)
-    shape = (channels, depth)
-    whole = put(order.token, mines, others[:2], firsts, shape)
     whole, others[2] = order.after((whole, others[2]), ())
     column = firsts[2] + (1 - place[1]) * widths[2]
     whole = lax.dynamic_update_slice(whole, others[2], (0, column))

time: 79 us -> 78.5 us (level)
  no operation moved by 1% of the time
where the time goes in v6:
time: 78.5 us; the launch traced here: 78.3 us
  Pallas kernels  24.2 us (31%)
  starting transfers between devices  22.5 us (29%)
  waiting for transfers between devices  22 us (28%)
  local copies, waits for them, and re-layouts  8.09 us (10%)
  between operations  0.86 us (1%)
    ppermute x14, starting transfers between devices, on_device(): lax.ppermute(state[way, part], 'tensor', right if way == 'up' else left)  15.3 us
    ppermute x14, waiting for transfers between devices, on_device(): lax.ppermute(state[way, part], 'tensor', right if way == 'up' else left)  13.2 us
    ppermute x11, waiting for transfers between devices, swap(): return lax.ppermute(value, 'dp', [(i, i ^ bit) for i in range(n)])  8.77 us
    ppermute x11, starting transfers between devices, swap(): return lax.ppermute(value, 'dp', [(i, i ^ bit) for i in range(n)])  7.15 us
    pallas_call x3, Pallas kernels, rows_parts(): pl.pallas_call(functools.partial(rows_kernel, n, len(pieces), numbers, be...  6.93 us
    pallas_call x1, Pallas kernels, grads(): pl.pallas_call(functools.partial(grads_kernel, scale), in_specs=[VMEM] *...  6.52 us
    pallas_call x2, Pallas kernels, conv_parts(): pl.pallas_call(functools.partial(conv_kernel, first, count), in_specs=[VM...  6.09 us
    optimization_barrier x1, local copies, waits for them, and re-layouts, after(): lax.optimization_barrier(flat)  3.48 us
  transfers between devices with their start and end apart: 25, of which 12 were waited for; matrix products, arithmetic and copies ran while one was open for 9% of the time, Pallas kernels for 29%

profile of v6, /device:TPU:0, one launch (start us, length us, event | category | flops | bytes accessed | tf_op | source)
XLA Modules:
  0.0 78.3 jit_solution(5784955911756162131)
XLA Ops:
  0.6 1.1 %slice_bitcast_fusion = (bf16[64,2048]{1,0:T(8,128)(2,1)S(1)}, bf16[64,2048]{1,0:T(8,128)(2,1)S(1)}) fusion(bf16[1,1,128,2048]{3,2,1,0:T(8,128)(2,1)} %param.8), kind=kLoop, calls=%fused_computation.8 | loop fusion | bytes 1048576 | tf_op jit(solution)/shard_map/slice | solution.py:398
  1.7 3.1 %collective-permute-start.3 = (bf16[64,2048]{1,0:T(8,128)(2,1)S(1)}, bf16[64,2048]{1,0:T(8,128)(2,1)S(1)}, u32[]{:S(2)}, u32[]{:S(2)}) collective-permute-start(bf16[64,2048]{1,0:T(8,128)(2,1)S(1)} %get-tuple-element.242), channel_id=1, source_target_pairs={{0,2},{2,4},{4,6},{6,7},{7,5},{5,3},{3,1},{1,0},{8,10},{10,12},{12... | collective-permute-start | bytes 786440 | tf_op jit(solution)/shard_map/ppermute | solution.py:411
  4.8 2.0 %collective-permute-start.1 = (bf16[64,2048]{1,0:T(8,128)(2,1)S(1)}, bf16[64,2048]{1,0:T(8,128)(2,1)S(1)}, u32[]{:S(2)}, u32[]{:S(2)}) collective-permute-start(bf16[64,2048]{1,0:T(8,128)(2,1)S(1)} %get-tuple-element.241), channel_id=1, source_target_pairs={{0,2},{2,4},{4,6},{6,7},{7,5},{5,3},{3,1},{1,0},{8,10},{10,12},{12... | collective-permute-start | bytes 786440 | tf_op jit(solution)/shard_map/ppermute | solution.py:411
  7.6 2.0 %copy.21 = bf16[1,8,128,2,512]{4,2,1,3,0:T(8,128)(2,1)S(1)} copy(bf16[1,8,128,2,512]{4,3,2,1,0:T(2,128)(2,1)} %param.5) | data formatting | bytes 4194304 | tf_op args[0]
  9.6 4.5 %shard_map.76 = (bf16[8,128,512]{2,1,0:T(8,128)(2,1)S(1)}, bf16[8,128,512]{2,1,0:T(8,128)(2,1)S(1)}, bf16[512,1024]{1,0:T(8,128)(2,1)S(1)}) custom-call(bf16[2,8,128,512]{3,2,1,0:T(8,128)(2,1)S(1)} %bitcast.16, f32[18,512]{1,0:T(8,128)S(1)} %reshape.24.weight_ref.taps_ref), custom_call_target="tpu_custom_call" | custom-call | flops 1 | bytes 1 | tf_op jit(solution)/shard_map/pallas_call | solution.py:100
  14.2 2.1 %collective-permute-start.7 = (bf16[64,2048]{1,0:T(8,128)(2,1)S(1)}, bf16[64,2048]{1,0:T(8,128)(2,1)S(1)}, u32[]{:S(2)}, u32[]{:S(2)}) collective-permute-start(bf16[64,2048]{1,0:T(8,128)(2,1)S(1)} %collective-permute-done.3.refs_1_), channel_id=1, source_target_pairs={{0,2},{2,4},{4,6},{6,7},{7,5},{5,3},{3,1},{1,0},{8,10},{10,12},{12... | collective-permute-start | bytes 786440 | tf_op jit(solution)/shard_map/ppermute | solution.py:411
  16.3 1.6 %shard_map.77 = (bf16[8,128,512]{2,1,0:T(8,128)(2,1)S(1)}, bf16[8,128,512]{2,1,0:T(8,128)(2,1)S(1)}, bf16[512,1024]{1,0:T(8,128)(2,1)S(1)}) custom-call(bf16[2,8,128,512]{3,2,1,0:T(8,128)(2,1)S(1)} %bitcast.17, f32[18,512]{1,0:T(8,128)S(1)} %reshape.24.weight_ref.taps_ref, ...), custom_call_target="tpu_custom_call", output_to_operand_aliasing={{0}: (2, {}), {1}: (3, {}), {2}: (4, {})} | custom-call | flops 1 | bytes 1 | tf_op jit(solution)/shard_map/pallas_call | solution.py:100
  17.9 1.1 %collective-permute-done.refs_3_ = bf16[64,2048]{1,0:T(8,128)(2,1)S(1)} collective-permute-done((bf16[64,2048]{1,0:T(8,128)(2,1)S(1)}, bf16[64,2048]{1,0:T(8,128)(2,1)S(1)}, u32[]{:S(2)}, u32[]{:S(2)}) %collective-permute-start) | collective-permute-done | bytes 262176 | tf_op jit(solution)/shard_map/ppermute | solution.py:411
  19.9 1.1 %collective-permute-start.5 = (bf16[64,2048]{1,0:T(8,128)(2,1)S(1)}, bf16[64,2048]{1,0:T(8,128)(2,1)S(1)}, u32[]{:S(2)}, u32[]{:S(2)}) collective-permute-start(bf16[64,2048]{1,0:T(8,128)(2,1)S(1)} %collective-permute-done.1.refs_2_), channel_id=1, source_target_pairs={{0,2},{2,4},{4,6},{6,7},{7,5},{5,3},{3,1},{1,0},{8,10},{10,12},{12... | collective-permute-start | bytes 786440 | tf_op jit(solution)/shard_map/ppermute | solution.py:411
  21.0 2.7 %shard_map.78 = (f32[512,2048]{1,0:T(8,128)S(1)}, f32[1024,512]{1,0:T(8,128)S(1)}) custom-call(s32[2]{0:T(128)S(1)} %pad_add_fusion.place_ref, bf16[128,2048]{1,0:T(8,128)(2,1)S(1)} %bitcast.19, bf16[64,2048]{1,0:T(8,128)(2,1)S(1)} %collective-permute-done.3.refs_1_, bf16[64,2048]{1,0:T(8,128)(2,1)S(1)} %collective-permute-done.1.refs_2_, ...), custom_call_target="tpu_custom_call" | custom-call | flops 1 | bytes 1 | tf_op jit(solution)/shard_map/pallas_call | solution.py:161
  23.6 1.9 %collective-permute-start.11 = (bf16[64,2048]{1,0:T(8,128)(2,1)S(1)}, bf16[64,2048]{1,0:T(8,128)(2,1)S(1)}, u32[]{:S(2)}, u32[]{:S(2)}) collective-permute-start(bf16[64,2048]{1,0:T(8,128)(2,1)S(1)} %collective-permute-done.7.refs_0_), channel_id=1, source_target_pairs={{0,2},{2,4},{4,6},{6,7},{7,5},{5,3},{3,1},{1,0},{8,10},{10,12},{12... | collective-permute-start | bytes 786440 | tf_op jit(solution)/shard_map/ppermute | solution.py:411
  25.7 3.4 %collective-permute-done.5.refs_1_ = bf16[64,2048]{1,0:T(8,128)(2,1)S(1)} collective-permute-done((bf16[64,2048]{1,0:T(8,128)(2,1)S(1)}, bf16[64,2048]{1,0:T(8,128)(2,1)S(1)}, u32[]{:S(2)}, u32[]{:S(2)}) %collective-permute-start.5) | collective-permute-done | bytes 262176 | tf_op jit(solution)/shard_map/ppermute | solution.py:411
  29.1 2.0 %collective-permute-done.4.refs_2_ = bf16[64,2048]{1,0:T(8,128)(2,1)S(1)} collective-permute-done((bf16[64,2048]{1,0:T(8,128)(2,1)S(1)}, bf16[64,2048]{1,0:T(8,128)(2,1)S(1)}, u32[]{:S(2)}, u32[]{:S(2)}) %collective-permute-start.4) | collective-permute-done | bytes 262176 | tf_op jit(solution)/shard_map/ppermute | solution.py:411
  31.2 2.0 %collective-permute-start.9 = (bf16[64,2048]{1,0:T(8,128)(2,1)S(1)}, bf16[64,2048]{1,0:T(8,128)(2,1)S(1)}, u32[]{:S(2)}, u32[]{:S(2)}) collective-permute-start(bf16[64,2048]{1,0:T(8,128)(2,1)S(1)} %collective-permute-done.5.refs_1_), channel_id=1, source_target_pairs={{0,2},{2,4},{4,6},{6,7},{7,5},{5,3},{3,1},{1,0},{8,10},{10,12},{12... | collective-permute-start | bytes 786440 | tf_op jit(solution)/shard_map/ppermute | solution.py:411
  33.2 2.1 %shard_map.79 = (f32[512,2048]{1,0:T(8,128)S(1)}, f32[1024,512]{1,0:T(8,128)S(1)}) custom-call(s32[2]{0:T(128)S(1)} %pad_add_fusion.place_ref, bf16[64,2048]{1,0:T(8,128)(2,1)S(1)} %collective-permute-done.7.refs_0_, bf16[64,2048]{1,0:T(8,128)(2,1)S(1)} %collective-permute-done.5.refs_1_, ...), custom_call_target="tpu_custom_call", output_to_operand_aliasing={{0}: (8, {}), {1}: (9, {})} | custom-call | flops 1 | bytes 1 | tf_op jit(solution)/shard_map/pallas_call | solution.py:161
  35.3 1.4 %collective-permute-done.10.refs_3_ = bf16[64,2048]{1,0:T(8,128)(2,1)S(1)} collective-permute-done((bf16[64,2048]{1,0:T(8,128)(2,1)S(1)}, bf16[64,2048]{1,0:T(8,128)(2,1)S(1)}, u32[]{:S(2)}, u32[]{:S(2)}) %collective-permute-start.10) | collective-permute-done | bytes 262176 | tf_op jit(solution)/shard_map/ppermute | solution.py:411
  36.8 2.0 %collective-permute-start.12 = (bf16[64,2048]{1,0:T(8,128)(2,1)S(1)}, bf16[64,2048]{1,0:T(8,128)(2,1)S(1)}, u32[]{:S(2)}, u32[]{:S(2)}) collective-permute-start(bf16[64,2048]{1,0:T(8,128)(2,1)S(1)} %collective-permute-done.11.refs_0_), channel_id=1, source_target_pairs={{0,2},{2,4},{4,6},{6,7},{7,5},{5,3},{3,1},{1,0},{8,10},{10,12},{12... | collective-permute-start | bytes 786440 | tf_op jit(solution)/shard_map/ppermute | solution.py:411
  38.8 1.6 %collective-permute-done.9.refs_1_ = bf16[64,2048]{1,0:T(8,128)(2,1)S(1)} collective-permute-done((bf16[64,2048]{1,0:T(8,128)(2,1)S(1)}, bf16[64,2048]{1,0:T(8,128)(2,1)S(1)}, u32[]{:S(2)}, u32[]{:S(2)}) %collective-permute-start.9) | collective-permute-done | bytes 262176 | tf_op jit(solution)/shard_map/ppermute | solution.py:411
  40.4 2.0 %collective-permute-done.8.refs_2_ = bf16[64,2048]{1,0:T(8,128)(2,1)S(1)} collective-permute-done((bf16[64,2048]{1,0:T(8,128)(2,1)S(1)}, bf16[64,2048]{1,0:T(8,128)(2,1)S(1)}, u32[]{:S(2)}, u32[]{:S(2)}) %collective-permute-start.8) | collective-permute-done | bytes 262176 | tf_op jit(solution)/shard_map/ppermute | solution.py:411
  42.4 2.1 %shard_map.80 = (f32[512,2048]{1,0:T(8,128)S(1)}, f32[1024,512]{1,0:T(8,128)S(1)}) custom-call(s32[2]{0:T(128)S(1)} %pad_add_fusion.place_ref, bf16[64,2048]{1,0:T(8,128)(2,1)S(1)} %collective-permute-done.11.refs_0_, bf16[64,2048]{1,0:T(8,128)(2,1)S(1)} %collective-permute-done.9.refs_1_, ...), custom_call_target="tpu_custom_call", output_to_operand_aliasing={{0}: (8, {}), {1}: (9, {})} | custom-call | flops 1 | bytes 1 | tf_op jit(solution)/shard_map/pallas_call | solution.py:161
  44.5 1.7 %collective-permute-done.13.down_ref = bf16[64,2048]{1,0:T(8,128)(2,1)S(1)} collective-permute-done((bf16[64,2048]{1,0:T(8,128)(2,1)S(1)}, bf16[64,2048]{1,0:T(8,128)(2,1)S(1)}, u32[]{:S(2)}, u32[]{:S(2)}) %collective-permute-start.13) | collective-permute-done | bytes 262176 | tf_op jit(solution)/shard_map/ppermute | solution.py:411
  46.3 1.3 %shard_map.81 = (bf16[512,256]{1,0:T(8,128)(2,1)S(1)}, f32[512,256]{1,0:T(8,128)S(1)}, bf16[512,384]{1,0:T(8,128)(2,1)S(1)}, f32[512,384]{1,0:T(8,128)S(1)}, bf1...) custom-call(s32[2]{0:T(128)S(1)} %pad_add_fusion.place_ref, bf16[64,2048]{1,0:T(8,128)(2,1)S(1)} %collective-permute-done.12.up_ref, ...), custom_call_target="tpu_custom_call" | custom-call | flops 1 | bytes 1 | tf_op jit(solution)/shard_map/pallas_call | solution.py:205
  49.3 1.6 %collective-permute-start.17 = (bf16[512,256]{1,0:T(8,128)(2,1)S(1)}, bf16[512,256]{1,0:T(8,128)(2,1)S(1)}, u32[]{:S(2)}, u32[]{:S(2)}) collective-permute-start(bf16[512,256]{1,0:T(8,128)(2,1)S(1)} %add_convert_fusion.2), channel_id=1, source_target_pairs={{0,16},{8,24},{16,0},{24,8},{1,17},{9,25},{17,1},{25,9},{2,18},{10... | collective-permute-start | bytes 786440 | tf_op jit(solution)/shard_map/ppermute | solution.py:360
  51.9 1.4 %shard_map.82.grad_ref = f32[1024,512]{1,0:T(8,128)S(1)} custom-call(s32[2]{0:T(128)S(1)} %pad_add_fusion.place_ref, bf16[64,2048]{1,0:T(8,128)(2,1)S(1)} %collective-permute-done.12.up_ref, bf16[64,2048]{1,0:T(8,128)(2,1)S(1)} %collective-permute-done.13.down_ref, f32[1,2048]{1,0:T(1,128)S(1)} %copy-done.2, ...), custom_call_target="tpu_custom_call", output_to_operand_aliasing={{}: (5, {})} | custom-call | flops 1 | bytes 1 | tf_op jit(solution)/shard_map/pallas_call | solution.py:232
  53.3 6.5 %shard_map.83 = (bf16[2,8,128,512]{3,2,1,0:T(8,128)(2,1)S(1)}, f32[3,3,2,512]{3,2,1,0:T(2,128)S(1)}) custom-call(f32[1024,512]{1,0:T(8,128)S(1)} %shard_map.82.grad_ref, bf16[8,128,512]{2,1,0:T(8,128)(2,1)S(1)} %get-tuple-element.202.gate_ref, bf16[8,128,512]{2,1,0:T(8,128)(2,1)S(1)} %get-tuple-element.203.value_ref, bf16[2,8,128,512]{3,2,1,0:T(8,128)(2,1)S(1)} %bitcast.18, ...), custom_call_target="tpu_custom_call" | custom-call | flops 1 | bytes 1 | tf_op jit(solution)/shard_map/pallas_call | solution.py:289
  59.8 3.5 %copy.20 = bf16[2,8,128,512]{3,0,2,1:T(2,128)(2,1)} copy(bf16[2,8,128,512]{3,2,1,0:T(8,128)(2,1)S(1)} %get-tuple-element.206) | data formatting | bytes 4194304 | tf_op jit(solution)/shard_map/optimization_barrier | solution.py:354
  63.3 1.2 %collective-permute-start.21 = (bf16[512,384]{1,0:T(8,128)(2,1)S(1)}, bf16[512,384]{1,0:T(8,128)(2,1)S(1)}, u32[]{:S(2)}, u32[]{:S(2)}) collective-permute-start(bf16[512,384]{1,0:T(8,128)(2,1)S(1)} %add_convert_fusion), channel_id=1, source_target_pairs={{0,16},{8,24},{16,0},{24,8},{1,17},{9,25},{17,1},{25,9},{2,18},{10... | collective-permute-start | bytes 1179656 | tf_op jit(solution)/shard_map/ppermute | solution.py:360
  64.6 1.8 %collective-permute-done.19 = bf16[512,384]{1,0:T(8,128)(2,1)S(1)} collective-permute-done((bf16[512,384]{1,0:T(8,128)(2,1)S(1)}, bf16[512,384]{1,0:T(8,128)(2,1)S(1)}, u32[]{:S(2)}, u32[]{:S(2)}) %collective-permute-start.19) | collective-permute-done | bytes 393248 | tf_op jit(solution)/shard_map/ppermute | solution.py:360
  67.2 1.6 %collective-permute-done.18 = f32[3,3,2,512]{3,2,1,0:T(2,128)S(1)} collective-permute-done((f32[3,3,2,512]{3,2,1,0:T(2,128)S(1)}, f32[3,3,2,512]{3,2,1,0:T(2,128)S(1)}, u32[]{:S(2)}, u32[]{:S(2)}) %collective-permute-start.18) | collective-permute-done | bytes 36896 | tf_op jit(solution)/shard_map/ppermute | solution.py:360
  68.8 2.1 %collective-permute-start.20 = (f32[3,3,2,512]{3,2,1,0:T(2,128)S(1)}, f32[3,3,2,512]{3,2,1,0:T(2,128)S(1)}, u32[]{:S(2)}, u32[]{:S(2)}) collective-permute-start(f32[3,3,2,512]{3,2,1,0:T(2,128)S(1)} %add.31.refs_5_), channel_id=1, source_target_pairs={{0,16},{8,24},{16,0},{24,8},{1,17},{9,25},{17,1},{25,9},{2,18},{10... | collective-permute-start | bytes 110600 | tf_op jit(solution)/shard_map/ppermute | solution.py:360
  70.9 4.1 %collective-permute-done.21 = bf16[512,384]{1,0:T(8,128)(2,1)S(1)} collective-permute-done((bf16[512,384]{1,0:T(8,128)(2,1)S(1)}, bf16[512,384]{1,0:T(8,128)(2,1)S(1)}, u32[]{:S(2)}, u32[]{:S(2)}) %collective-permute-start.21) | collective-permute-done | bytes 393248 | tf_op jit(solution)/shard_map/ppermute | solution.py:360
  75.6 1.9 %shard_map.84 = (bf16[512,2048]{1,0:T(8,128)(2,1)}, f32[3,3,2,512]{3,2,1,0:T(2,128)}) custom-call(s32[2]{0:T(128)S(1)} %pad_add_fusion.place_ref, bf16[512,256]{1,0:T(8,128)(2,1)S(1)} %multiply_convert_fusion.2.refs_0_, bf16[512,384]{1,0:T(8,128)(2,1)S(1)} %multiply_convert_fusion.1.refs_1_, bf16[512,384]{1,0:T(8,128)(2,1)S(1)} %multiply_convert_fusion.refs_2_, ...), custom_call_target="tpu_custom_call" | custom-call | flops 1 | bytes 1 | tf_op jit(solution)/shard_map/pallas_call | solution.py:333
  (46 shorter events, 7.0 us)
Async XLA Ops:
  1.7 12.5 %collective-permute-start.3 = (bf16[64,2048]{1,0:T(8,128)(2,1)S(1)}, bf16[64,2048]{1,0:T(8,128)(2,1)S(1)}, u32[]{:S(2)}, u32[]{:S(2)}) collective-permute-start(bf16[64,2048]{1,0:T(8,128)(2,1)S(1)} %get-tuple-element.242), channel_id=1, source_target_pairs={{0,2},{2,4},{4,6},{6,7},{7,5},{5,3},{3,1},{1,0},{8,10},{10,12},{12... | collective-permute-start | bytes 786440 | tf_op jit(solution)/shard_map/ppermute | solution.py:411
  4.8 11.5 %collective-permute-start.2 = (bf16[64,2048]{1,0:T(8,128)(2,1)S(1)}, bf16[64,2048]{1,0:T(8,128)(2,1)S(1)}, u32[]{:S(2)}, u32[]{:S(2)}) collective-permute-start(bf16[64,2048]{1,0:T(8,128)(2,1)S(1)} %get-tuple-element.241), channel_id=1, source_target_pairs={{0,1},{2,0},{4,2},{6,4},{7,6},{5,7},{3,5},{1,3},{8,9},{10,8},{12,1... | collective-permute-start | bytes 786440 | tf_op jit(solution)/shard_map/ppermute | solution.py:411
  4.8 13.1 %collective-permute-start.1 = (bf16[64,2048]{1,0:T(8,128)(2,1)S(1)}, bf16[64,2048]{1,0:T(8,128)(2,1)S(1)}, u32[]{:S(2)}, u32[]{:S(2)}) collective-permute-start(bf16[64,2048]{1,0:T(8,128)(2,1)S(1)} %get-tuple-element.241), channel_id=1, source_target_pairs={{0,2},{2,4},{4,6},{6,7},{7,5},{5,3},{3,1},{1,0},{8,10},{10,12},{12... | collective-permute-start | bytes 786440 | tf_op jit(solution)/shard_map/ppermute | solution.py:411
  6.8 12.1 %collective-permute-start = (bf16[64,2048]{1,0:T(8,128)(2,1)S(1)}, bf16[64,2048]{1,0:T(8,128)(2,1)S(1)}, u32[]{:S(2)}, u32[]{:S(2)}) collective-permute-start(bf16[64,2048]{1,0:T(8,128)(2,1)S(1)} %get-tuple-element.242), channel_id=1, source_target_pairs={{0,1},{2,0},{4,2},{6,4},{7,6},{5,7},{3,5},{1,3},{8,9},{10,8},{12,1... | collective-permute-start | bytes 786440 | tf_op jit(solution)/shard_map/ppermute | solution.py:411
  14.2 6.8 %copy-start = (bf16[512,2048]{1,0:T(8,128)(2,1)S(1)}, bf16[512,2048]{1,0:T(8,128)(2,1)}, u32[]{:S(2)}) copy-start(bf16[512,2048]{1,0:T(8,128)(2,1)} %weight_ref.1) | copy-start | bytes 6291460
  14.2 6.8 %copy-start.1 = (bf16[1,1,128,2048]{3,2,1,0:T(8,128)(2,1)S(1)}, bf16[1,1,128,2048]{3,2,1,0:T(8,128)(2,1)}, u32[]{:S(2)}) copy-start(bf16[1,1,128,2048]{3,2,1,0:T(8,128)(2,1)} %param.8) | copy-start | bytes 1572868
  14.2 6.8 %copy-start.2 = (f32[1,2048]{1,0:T(1,128)S(1)}, f32[1,2048]{1,0:T(1,128)}, u32[]{:S(2)}) copy-start(f32[1,2048]{1,0:T(1,128)} %gate_ref.3) | copy-start | bytes 24580
  14.2 9.4 %collective-permute-start.7 = (bf16[64,2048]{1,0:T(8,128)(2,1)S(1)}, bf16[64,2048]{1,0:T(8,128)(2,1)S(1)}, u32[]{:S(2)}, u32[]{:S(2)}) collective-permute-start(bf16[64,2048]{1,0:T(8,128)(2,1)S(1)} %collective-permute-done.3.refs_1_), channel_id=1, source_target_pairs={{0,2},{2,4},{4,6},{6,7},{7,5},{5,3},{3,1},{1,0},{8,10},{10,12},{12... | collective-permute-start | bytes 786440 | tf_op jit(solution)/shard_map/ppermute | solution.py:411
  16.3 9.2 %collective-permute-start.6 = (bf16[64,2048]{1,0:T(8,128)(2,1)S(1)}, bf16[64,2048]{1,0:T(8,128)(2,1)S(1)}, u32[]{:S(2)}, u32[]{:S(2)}) collective-permute-start(bf16[64,2048]{1,0:T(8,128)(2,1)S(1)} %collective-permute-done.2.refs_4_), channel_id=1, source_target_pairs={{0,1},{2,0},{4,2},{6,4},{7,6},{5,7},{3,5},{1,3},{8,9},{10,8},{12,1... | collective-permute-start | bytes 786440 | tf_op jit(solution)/shard_map/ppermute | solution.py:411
  18.9 12.2 %collective-permute-start.4 = (bf16[64,2048]{1,0:T(8,128)(2,1)S(1)}, bf16[64,2048]{1,0:T(8,128)(2,1)S(1)}, u32[]{:S(2)}, u32[]{:S(2)}) collective-permute-start(bf16[64,2048]{1,0:T(8,128)(2,1)S(1)} %collective-permute-done.refs_3_), channel_id=1, source_target_pairs={{0,1},{2,0},{4,2},{6,4},{7,6},{5,7},{3,5},{1,3},{8,9},{10,8},{12,1... | collective-permute-start | bytes 786440 | tf_op jit(solution)/shard_map/ppermute | solution.py:411
  19.9 9.2 %collective-permute-start.5 = (bf16[64,2048]{1,0:T(8,128)(2,1)S(1)}, bf16[64,2048]{1,0:T(8,128)(2,1)S(1)}, u32[]{:S(2)}, u32[]{:S(2)}) collective-permute-start(bf16[64,2048]{1,0:T(8,128)(2,1)S(1)} %collective-permute-done.1.refs_2_), channel_id=1, source_target_pairs={{0,2},{2,4},{4,6},{6,7},{7,5},{5,3},{3,1},{1,0},{8,10},{10,12},{12... | collective-permute-start | bytes 786440 | tf_op jit(solution)/shard_map/ppermute | solution.py:411
  23.6 11.7 %collective-permute-start.11 = (bf16[64,2048]{1,0:T(8,128)(2,1)S(1)}, bf16[64,2048]{1,0:T(8,128)(2,1)S(1)}, u32[]{:S(2)}, u32[]{:S(2)}) collective-permute-start(bf16[64,2048]{1,0:T(8,128)(2,1)S(1)} %collective-permute-done.7.refs_0_), channel_id=1, source_target_pairs={{0,2},{2,4},{4,6},{6,7},{7,5},{5,3},{3,1},{1,0},{8,10},{10,12},{12... | collective-permute-start | bytes 786440 | tf_op jit(solution)/shard_map/ppermute | solution.py:411
  25.5 11.2 %collective-permute-start.10 = (bf16[64,2048]{1,0:T(8,128)(2,1)S(1)}, bf16[64,2048]{1,0:T(8,128)(2,1)S(1)}, u32[]{:S(2)}, u32[]{:S(2)}) collective-permute-start(bf16[64,2048]{1,0:T(8,128)(2,1)S(1)} %collective-permute-done.6.refs_3_), channel_id=1, source_target_pairs={{0,1},{2,0},{4,2},{6,4},{7,6},{5,7},{3,5},{1,3},{8,9},{10,8},{12,1... | collective-permute-start | bytes 786440 | tf_op jit(solution)/shard_map/ppermute | solution.py:411
  31.2 11.2 %collective-permute-start.8 = (bf16[64,2048]{1,0:T(8,128)(2,1)S(1)}, bf16[64,2048]{1,0:T(8,128)(2,1)S(1)}, u32[]{:S(2)}, u32[]{:S(2)}) collective-permute-start(bf16[64,2048]{1,0:T(8,128)(2,1)S(1)} %collective-permute-done.4.refs_2_), channel_id=1, source_target_pairs={{0,1},{2,0},{4,2},{6,4},{7,6},{5,7},{3,5},{1,3},{8,9},{10,8},{12,1... | collective-permute-start | bytes 786440 | tf_op jit(solution)/shard_map/ppermute | solution.py:411
  31.2 9.2 %collective-permute-start.9 = (bf16[64,2048]{1,0:T(8,128)(2,1)S(1)}, bf16[64,2048]{1,0:T(8,128)(2,1)S(1)}, u32[]{:S(2)}, u32[]{:S(2)}) collective-permute-start(bf16[64,2048]{1,0:T(8,128)(2,1)S(1)} %collective-permute-done.5.refs_1_), channel_id=1, source_target_pairs={{0,2},{2,4},{4,6},{6,7},{7,5},{5,3},{3,1},{1,0},{8,10},{10,12},{12... | collective-permute-start | bytes 786440 | tf_op jit(solution)/shard_map/ppermute | solution.py:411
  36.8 9.5 %collective-permute-start.13 = (bf16[64,2048]{1,0:T(8,128)(2,1)S(1)}, bf16[64,2048]{1,0:T(8,128)(2,1)S(1)}, u32[]{:S(2)}, u32[]{:S(2)}) collective-permute-start(bf16[64,2048]{1,0:T(8,128)(2,1)S(1)} %collective-permute-done.10.refs_3_), channel_id=1, source_target_pairs={{0,1},{2,0},{4,2},{6,4},{7,6},{5,7},{3,5},{1,3},{8,9},{10,8},{12,1... | collective-permute-start | bytes 786440 | tf_op jit(solution)/shard_map/ppermute | solution.py:411
  36.8 9.5 %collective-permute-start.12 = (bf16[64,2048]{1,0:T(8,128)(2,1)S(1)}, bf16[64,2048]{1,0:T(8,128)(2,1)S(1)}, u32[]{:S(2)}, u32[]{:S(2)}) collective-permute-start(bf16[64,2048]{1,0:T(8,128)(2,1)S(1)} %collective-permute-done.11.refs_0_), channel_id=1, source_target_pairs={{0,2},{2,4},{4,6},{6,7},{7,5},{5,3},{3,1},{1,0},{8,10},{10,12},{12... | collective-permute-start | bytes 786440 | tf_op jit(solution)/shard_map/ppermute | solution.py:411
  47.6 1.6 %collective-permute-start.16 = (bf16[512,256]{1,0:T(8,128)(2,1)S(1)}, bf16[512,256]{1,0:T(8,128)(2,1)S(1)}, u32[]{:S(2)}, u32[]{:S(2)}) collective-permute-start(bf16[512,256]{1,0:T(8,128)(2,1)S(1)} %get-tuple-element.189), channel_id=1, source_target_pairs={{0,8},{8,0},{16,24},{24,16},{1,9},{9,1},{17,25},{25,17},{2,10},{10... | collective-permute-start | bytes 786440 | tf_op jit(solution)/shard_map/ppermute | solution.py:360
  47.7 3.2 %collective-permute-start.15 = (bf16[512,384]{1,0:T(8,128)(2,1)S(1)}, bf16[512,384]{1,0:T(8,128)(2,1)S(1)}, u32[]{:S(2)}, u32[]{:S(2)}) collective-permute-start(bf16[512,384]{1,0:T(8,128)(2,1)S(1)} %get-tuple-element.187), channel_id=1, source_target_pairs={{0,8},{8,0},{16,24},{24,16},{1,9},{9,1},{17,25},{25,17},{2,10},{10... | collective-permute-start | bytes 1179656 | tf_op jit(solution)/shard_map/ppermute | solution.py:360
  48.2 2.8 %collective-permute-start.14 = (bf16[512,384]{1,0:T(8,128)(2,1)S(1)}, bf16[512,384]{1,0:T(8,128)(2,1)S(1)}, u32[]{:S(2)}, u32[]{:S(2)}) collective-permute-start(bf16[512,384]{1,0:T(8,128)(2,1)S(1)} %get-tuple-element.185), channel_id=1, source_target_pairs={{0,8},{8,0},{16,24},{24,16},{1,9},{9,1},{17,25},{25,17},{2,10},{10... | collective-permute-start | bytes 1179656 | tf_op jit(solution)/shard_map/ppermute | solution.py:360
  49.3 15.2 %collective-permute-start.17 = (bf16[512,256]{1,0:T(8,128)(2,1)S(1)}, bf16[512,256]{1,0:T(8,128)(2,1)S(1)}, u32[]{:S(2)}, u32[]{:S(2)}) collective-permute-start(bf16[512,256]{1,0:T(8,128)(2,1)S(1)} %add_convert_fusion.2), channel_id=1, source_target_pairs={{0,16},{8,24},{16,0},{24,8},{1,17},{9,25},{17,1},{25,9},{2,18},{10... | collective-permute-start | bytes 786440 | tf_op jit(solution)/shard_map/ppermute | solution.py:360
  51.0 15.4 %collective-permute-start.19 = (bf16[512,384]{1,0:T(8,128)(2,1)S(1)}, bf16[512,384]{1,0:T(8,128)(2,1)S(1)}, u32[]{:S(2)}, u32[]{:S(2)}) collective-permute-start(bf16[512,384]{1,0:T(8,128)(2,1)S(1)} %add_convert_fusion.1), channel_id=1, source_target_pairs={{0,16},{8,24},{16,0},{24,8},{1,17},{9,25},{17,1},{25,9},{2,18},{10... | collective-permute-start | bytes 1179656 | tf_op jit(solution)/shard_map/ppermute | solution.py:360
  63.3 11.6 %collective-permute-start.21 = (bf16[512,384]{1,0:T(8,128)(2,1)S(1)}, bf16[512,384]{1,0:T(8,128)(2,1)S(1)}, u32[]{:S(2)}, u32[]{:S(2)}) collective-permute-start(bf16[512,384]{1,0:T(8,128)(2,1)S(1)} %add_convert_fusion), channel_id=1, source_target_pairs={{0,16},{8,24},{16,0},{24,8},{1,17},{9,25},{17,1},{25,9},{2,18},{10... | collective-permute-start | bytes 1179656 | tf_op jit(solution)/shard_map/ppermute | solution.py:360
  66.5 8.8 %collective-permute-start.22 = (bf16[512,384]{1,0:T(8,128)(2,1)S(1)}, bf16[512,384]{1,0:T(8,128)(2,1)S(1)}, u32[]{:S(2)}, u32[]{:S(2)}) collective-permute-start(bf16[512,384]{1,0:T(8,128)(2,1)S(1)} %multiply_convert_fusion.1.refs_1_), channel_id=1, source_target_pairs={{0,8},{8,0},{16,24},{24,16},{1,9},{9,1},{17,25},{25,17},{2,10},{10... | collective-permute-start | bytes 1179656 | tf_op jit(solution)/shard_map/ppermute | solution.py:360
  66.6 8.7 %collective-permute-start.23 = (bf16[512,256]{1,0:T(8,128)(2,1)S(1)}, bf16[512,256]{1,0:T(8,128)(2,1)S(1)}, u32[]{:S(2)}, u32[]{:S(2)}) collective-permute-start(bf16[512,256]{1,0:T(8,128)(2,1)S(1)} %multiply_convert_fusion.2.refs_0_), channel_id=1, source_target_pairs={{0,8},{8,0},{16,24},{24,16},{1,9},{9,1},{17,25},{25,17},{2,10},{10... | collective-permute-start | bytes 786440 | tf_op jit(solution)/shard_map/ppermute | solution.py:360
  67.1 1.6 %collective-permute-start.18 = (f32[3,3,2,512]{3,2,1,0:T(2,128)S(1)}, f32[3,3,2,512]{3,2,1,0:T(2,128)S(1)}, u32[]{:S(2)}, u32[]{:S(2)}) collective-permute-start(f32[3,3,2,512]{3,2,1,0:T(2,128)S(1)} %get-tuple-element.214), channel_id=1, source_target_pairs={{0,8},{8,0},{16,24},{24,16},{1,9},{9,1},{17,25},{25,17},{2,10},{10... | collective-permute-start | bytes 110600 | tf_op jit(solution)/shard_map/ppermute | solution.py:360
  68.8 6.6 %collective-permute-start.20 = (f32[3,3,2,512]{3,2,1,0:T(2,128)S(1)}, f32[3,3,2,512]{3,2,1,0:T(2,128)S(1)}, u32[]{:S(2)}, u32[]{:S(2)}) collective-permute-start(f32[3,3,2,512]{3,2,1,0:T(2,128)S(1)} %add.31.refs_5_), channel_id=1, source_target_pairs={{0,16},{8,24},{16,0},{24,8},{1,17},{9,25},{17,1},{25,9},{2,18},{10... | collective-permute-start | bytes 110600 | tf_op jit(solution)/shard_map/ppermute | solution.py:360
  75.5 2.0 %collective-permute-start.24 = (bf16[512,384]{1,0:T(8,128)(2,1)S(1)}, bf16[512,384]{1,0:T(8,128)(2,1)S(1)}, u32[]{:S(2)}, u32[]{:S(2)}) collective-permute-start(bf16[512,384]{1,0:T(8,128)(2,1)S(1)} %multiply_convert_fusion.refs_2_), channel_id=1, source_target_pairs={{0,8},{8,0},{16,24},{24,16},{1,9},{9,1},{17,25},{25,17},{2,10},{10... | collective-permute-start | bytes 1179656 | tf_op jit(solution)/shard_map/ppermute | solution.py:360

commit v7 on v6

--- a/solution.py
+++ b/solution.py
@@ -16,7 +16,6 @@
 LANES = 128
 VMEM_BYTES = 20 * 1024 * 1024
 VMEM = pl.BlockSpec(memory_space=pltpu.VMEM)
-SMEM = pl.BlockSpec(memory_space=pltpu.SMEM)
 
 
 def ring_order(n):
@@ -26,6 +25,10 @@
 def at_ring(position, n):
     position = lax.rem(position + 2 * n, n)
     return jnp.where(position < n // 2, 2 * position, 2 * (n - 1 - position) + 1)
+
+
+def this_core():
+    return lax.rem(lax.axis_index("dp"), 2)
 
 
 def ring_place(index, n):
@@ -113,7 +116,7 @@
     )(hidden, weights, *before)
 
 
-def rows_kernel(n, parts, numbers, added, place_ref, *refs):
+def rows_kernel(n, parts, numbers, added, *refs):
     count = len(numbers)
     pieces, refs = refs[:parts], refs[parts:]
     gate_ref, weight_ref, mixed_ref = refs[:3]
@@ -121,7 +124,7 @@
     before_ref = refs[3] if added else None
     across = local_ref.shape[0] // count
     depth = local_ref.shape[1]
-    spot = ring_place(place_ref[0], n)
+    spot = ring_place(lax.axis_index("tensor"), n)
     starts = [
         pl.multiple_of(at_ring(spot + step, n) * across, LANES) for step in numbers
     ]
@@ -149,18 +152,18 @@
         grad_ref[pl.ds(start, across)] = product[k * across : (k + 1) * across]
 
 
-def rows_parts(n, place, pieces, numbers, gate, weight, mixed, before=None):
+def rows_parts(n, pieces, numbers, gate, weight, mixed, before=None):
     depth = pieces[0].shape[1]
     channels, tokens = mixed.shape
     count, across = len(numbers), tokens // n
     operands = [*pieces, gate, weight, mixed]
     aliases = {}
     if before is not None:
-        aliases = {len(operands) + 1: 0, len(operands) + 2: 1}
+        aliases = {len(operands): 0, len(operands) + 1: 1}
         operands += before
     return pl.pallas_call(
         functools.partial(rows_kernel, n, len(pieces), numbers, before is not None),
-        in_specs=[SMEM] + [VMEM] * len(operands),
+        in_specs=[VMEM] * len(operands),
         out_specs=[VMEM] * 2,
         out_shape=[
             jax.ShapeDtypeStruct((channels, depth), F32),
@@ -173,30 +176,39 @@
         input_output_aliases=aliases,
         compiler_params=params(),
         cost_estimate=cost(4 * count * across * channels * depth, 0),
-    )(place, *operands)
-
-
-def far_kernel(n, firsts, place_ref, up_ref, down_ref, gate_ref, mixed_ref, before_ref, *refs):
+    )(*operands)
+
+
+def far_kernel(n, firsts, up_ref, down_ref, gate_ref, mixed_ref, before_ref, *refs):
     outs, local_ref = refs[:-1], refs[-1]
-    half, depth = up_ref.shape
+    half = up_ref.shape[0]
     across = 2 * half
-    core = place_ref[1]
-    start = pl.multiple_of(at_ring(ring_place(place_ref[0], n) + n // 2, n) * across, LANES)
+    width = local_ref.shape[1]
+    core = this_core()
+    start = pl.multiple_of(
+        at_ring(ring_place(lax.axis_index("tensor"), n) + n // 2, n) * across, LANES
+    )
+    columns = slice(firsts[0], firsts[0] + width)
     for base, piece in ((0, up_ref), (half, down_ref)):
         for r in range(0, half, TILE):
             local_ref[base + r : base + r + TILE] = (
-                piece[r : r + TILE].astype(F32) * gate_ref[...]
+                piece[r : r + TILE, columns].astype(F32) * gate_ref[:, columns]
             ).astype(BF16)
     mixed = mixed_ref[:, pl.ds(start, across)]
     for u, first in enumerate(firsts):
         for out_ref, side in ((outs[2 * u], 1 - core), (outs[2 * u + 1], core)):
-            width = out_ref.shape[1]
-            columns = pl.ds(pl.multiple_of(first + side * width, LANES), width)
-            total = jnp.dot(mixed, local_ref[:, columns], preferred_element_type=F32)
-            out_ref[...] = (total + before_ref[:, columns]).astype(out_ref.dtype)
-
-
-def far_parts(n, place, pieces, firsts, widths, gate, mixed, before):
+            part = out_ref.shape[1]
+            column = first + side * part
+            total = jnp.dot(
+                mixed,
+                local_ref[:, pl.ds(pl.multiple_of(column - firsts[0], LANES), part)],
+                preferred_element_type=F32,
+            )
+            total = total + before_ref[:, pl.ds(pl.multiple_of(column, LANES), part)]
+            out_ref[...] = total.astype(out_ref.dtype)
+
+
+def far_parts(n, pieces, firsts, widths, gate, mixed, before):
     channels, tokens = mixed.shape
     shapes = []
     for width in widths:
@@ -204,19 +216,19 @@
         shapes.append(jax.ShapeDtypeStruct((channels, width), F32))
     return pl.pallas_call(
         functools.partial(far_kernel, n, firsts),
-        in_specs=[SMEM] + [VMEM] * 5,
+        in_specs=[VMEM] * 5,
         out_specs=[VMEM] * len(shapes),
         out_shape=shapes,
-        scratch_shapes=[pltpu.VMEM((tokens // n, before.shape[1]), BF16)],
+        scratch_shapes=[pltpu.VMEM((tokens // n, 2 * sum(widths)), BF16)],
         compiler_params=params(),
         cost_estimate=cost(1, 1),
-    )(place, *pieces, gate, mixed, before)
-
-
-def far_row_kernel(n, place_ref, up_ref, down_ref, gate_ref, weight_ref, before_ref, grad_ref, local_ref):
+    )(*pieces, gate, mixed, before)
+
+
+def far_row_kernel(n, up_ref, down_ref, gate_ref, weight_ref, before_ref, grad_ref, local_ref):
     half = up_ref.shape[0]
     across = 2 * half
-    start = pl.multiple_of(at_ring(ring_place(place_ref[0], n) + n // 2, n) * across, LANES)
+    start = pl.multiple_of(at_ring(ring_place(lax.axis_index("tensor"), n) + n // 2, n) * across, LANES)
     for base, piece in ((0, up_ref), (half, down_ref)):
         for r in range(0, half, TILE):
             local_ref[base + r : base + r + TILE] = (
@@ -227,18 +239,18 @@
     )
 
 
-def far_row(n, place, pieces, gate, weight, before):
+def far_row(n, pieces, gate, weight, before):
     tokens, channels = before.shape
     return pl.pallas_call(
         functools.partial(far_row_kernel, n),
-        in_specs=[SMEM] + [VMEM] * 5,
+        in_specs=[VMEM] * 5,
         out_specs=VMEM,
         out_shape=jax.ShapeDtypeStruct(before.shape, F32),
         scratch_shapes=[pltpu.VMEM((tokens // n, weight.shape[1]), BF16)],
-        input_output_aliases={5: 0},
+        input_output_aliases={4: 0},
         compiler_params=params(),
         cost_estimate=cost(1, 1),
-    )(place, *pieces, gate, weight, before)
+    )(*pieces, gate, weight, before)
 
 
 def grads_kernel(
@@ -300,9 +312,9 @@
     )(grad, gate_part, value_part, hidden, taps)
 
 
-def put_kernel(firsts, given, place_ref, *refs):
+def put_kernel(firsts, given, *refs):
     count = len(firsts)
-    one_ref, two_ref, out_ref, total_ref, shares_ref, sems, share_sems = refs[-7:]
+    one_ref, two_ref, _, out_ref, total_ref, shares_ref, sems, share_sems = refs[-8:]
     shares = [
         pltpu.make_async_copy(ref, shares_ref.at[k], share_sems.at[k])
         for k, ref in enumerate((one_ref, two_ref))
@@ -312,7 +324,7 @@
     copies = []
     for k in range(count + given):
         half = refs[k].shape[1]
-        core = place_ref[1] if k < count else 1 - place_ref[1]
+        core = this_core() if k < count else 1 - this_core()
         columns = pl.ds(pl.multiple_of(firsts[k % count] + core * half, LANES), half)
         copies.append(pltpu.make_async_copy(refs[k], out_ref.at[:, columns], sems.at[k]))
     for copy in copies:
@@ -327,12 +339,12 @@
     total.wait()
 
 
-def put(place, mines, others, firsts, shape, one, two):
+def put(token, mines, others, firsts, shape, one, two):
     hbm = pl.BlockSpec(memory_space=pl.ANY)
     arrays = [*mines, *others]
     return pl.pallas_call(
         functools.partial(put_kernel, firsts, len(others)),
-        in_specs=[SMEM] + [hbm] * (len(arrays) + 2),
+        in_specs=[hbm] * (len(arrays) + 3),
         out_specs=[hbm, hbm],
         out_shape=[jax.ShapeDtypeStruct(shape, BF16), jax.ShapeDtypeStruct(one.shape, F32)],
         scratch_shapes=[
@@ -342,7 +354,7 @@
         ],
         compiler_params=params(),
         cost_estimate=cost(1, 1),
-    )(place, *arrays, one, two)
+    )(*arrays, one, two, token)
 
 
 class Order:
@@ -392,7 +404,7 @@
     last = n // 2
 
     def rows(pieces, numbers, before):
-        return rows_parts(n, order.token, pieces, numbers, sample_gate, proj_weight, mixed, before)
+        return rows_parts(n, pieces, numbers, sample_gate, proj_weight, mixed, before)
 
     half = across // 2
     state = {("up", 0): own[:half], ("down", 1): own[half:], ("up", 1): own[half:], ("down", 0): own[:half]}
@@ -440,15 +452,17 @@
         mines.append(order.after(mine, ()))
         others.append(swap(mines[u], 1))
 
-    parts = far_parts(n, order.token, far, firsts, widths, sample_gate, mixed, sums)
-    parts = order.after(parts, ())
-    near = [swap(part, 1) for part in parts[::2]]
-    keeps = parts[1::2]
+    near, keeps = [], []
+    for units in (slice(0, 1), slice(1, None)):
+        parts = far_parts(n, far, firsts[units], widths[units], sample_gate, mixed, sums)
+        parts, sums = order.after((parts, sums), ())
+        near += [swap(part, 1) for part in parts[::2]]
+        keeps += parts[1::2]
     begin(0)
     begin(1)
     begin(2)
     grad = order.after(grad, ())
-    grad = far_row(n, order.token, far, sample_gate, proj_weight, grad)
+    grad = far_row(n, far, sample_gate, proj_weight, grad)
     hidden_grad, terms = grads(
         grad, gate_part, value_part, hidden, taps, grad_scale
     )

time: 78.5 us -> 77.3 us (0.985)
  Pallas kernels: 24.2 us -> 21.1 us
  waiting for transfers between devices: 22 us -> 23.8 us
    ppermute x14, waiting for transfers between devices: 13.2 us -> 14.9 us  [on_device(): lax.ppermute(state[way, part], 'tensor', right if way == 'up' else left)]
    pallas_call x3, Pallas kernels: 6.93 us -> 5.34 us  [rows_parts(): pl.pallas_call(functools.partial(rows_kernel, n, len(pieces), numbers, be...]
    pallas_call x2 -> x3, Pallas kernels: 2.71 us -> 1.82 us  [the longest x2 0.99 us: far_parts(): pl.pallas_call(functools.partial(far_kernel, n, firsts), in_specs=[VMEM]...]
  transfers between devices with their start and end apart: 25 -> 25, of which waited for: 12 -> 14; matrix products, arithmetic and copies ran while one was open for 9% -> 9% of each run, Pallas kernels for 29% -> 27%
where the time goes in v7:
time: 77.3 us; the launch traced here: 77.1 us
  waiting for transfers between devices  23.8 us (31%)
  starting transfers between devices  22.5 us (29%)
  Pallas kernels  21.1 us (27%)
  local copies, waits for them, and re-layouts  8.09 us (10%)
  between operations  0.85 us (1%)
    ppermute x14, starting transfers between devices, on_device(): lax.ppermute(state[way, part], 'tensor', right if way == 'up' else left)  15.3 us
    ppermute x14, waiting for transfers between devices, on_device(): lax.ppermute(state[way, part], 'tensor', right if way == 'up' else left)  14.9 us
    ppermute x11, waiting for transfers between devices, swap(): return lax.ppermute(value, 'dp', [(i, i ^ bit) for i in range(n)])  8.96 us
    ppermute x11, starting transfers between devices, swap(): return lax.ppermute(value, 'dp', [(i, i ^ bit) for i in range(n)])  7.25 us
    pallas_call x1, Pallas kernels, grads(): pl.pallas_call(functools.partial(grads_kernel, scale), in_specs=[VMEM] *...  6.52 us
    pallas_call x2, Pallas kernels, conv_parts(): pl.pallas_call(functools.partial(conv_kernel, first, count), in_specs=[VM...  6.09 us
    pallas_call x3, Pallas kernels, rows_parts(): pl.pallas_call(functools.partial(rows_kernel, n, len(pieces), numbers, be...  5.34 us
    optimization_barrier x1, local copies, waits for them, and re-layouts, after(): lax.optimization_barrier(flat)  3.48 us
  transfers between devices with their start and end apart: 25, of which 14 were waited for; matrix products, arithmetic and copies ran while one was open for 9% of the time, Pallas kernels for 27%

profile of v7, /device:TPU:0, one launch (start us, length us, event | category | flops | bytes accessed | tf_op | source)
XLA Modules:
  0.0 77.1 jit_solution(14698783728398180535)
XLA Ops:
  0.6 1.1 %slice_bitcast_fusion = (bf16[64,2048]{1,0:T(8,128)(2,1)S(1)}, bf16[64,2048]{1,0:T(8,128)(2,1)S(1)}) fusion(bf16[1,1,128,2048]{3,2,1,0:T(8,128)(2,1)} %param.8), kind=kLoop, calls=%fused_computation.8 | loop fusion | bytes 1048576 | tf_op jit(solution)/shard_map/slice | solution.py:410
  1.7 3.1 %collective-permute-start = (bf16[64,2048]{1,0:T(8,128)(2,1)S(1)}, bf16[64,2048]{1,0:T(8,128)(2,1)S(1)}, u32[]{:S(2)}, u32[]{:S(2)}) collective-permute-start(bf16[64,2048]{1,0:T(8,128)(2,1)S(1)} %get-tuple-element.246), channel_id=1, source_target_pairs={{0,2},{2,4},{4,6},{6,7},{7,5},{5,3},{3,1},{1,0},{8,10},{10,12},{12... | collective-permute-start | bytes 786440 | tf_op jit(solution)/shard_map/ppermute | solution.py:423
  4.8 2.0 %collective-permute-start.2 = (bf16[64,2048]{1,0:T(8,128)(2,1)S(1)}, bf16[64,2048]{1,0:T(8,128)(2,1)S(1)}, u32[]{:S(2)}, u32[]{:S(2)}) collective-permute-start(bf16[64,2048]{1,0:T(8,128)(2,1)S(1)} %get-tuple-element.245), channel_id=1, source_target_pairs={{0,2},{2,4},{4,6},{6,7},{7,5},{5,3},{3,1},{1,0},{8,10},{10,12},{12... | collective-permute-start | bytes 786440 | tf_op jit(solution)/shard_map/ppermute | solution.py:423
  7.6 2.0 %copy.21 = bf16[1,8,128,2,512]{4,2,1,3,0:T(8,128)(2,1)S(1)} copy(bf16[1,8,128,2,512]{4,3,2,1,0:T(2,128)(2,1)} %param.5) | data formatting | bytes 4194304 | tf_op args[0]
  9.6 4.5 %shard_map.76 = (bf16[8,128,512]{2,1,0:T(8,128)(2,1)S(1)}, bf16[8,128,512]{2,1,0:T(8,128)(2,1)S(1)}, bf16[512,1024]{1,0:T(8,128)(2,1)S(1)}) custom-call(bf16[2,8,128,512]{3,2,1,0:T(8,128)(2,1)S(1)} %bitcast.16, f32[18,512]{1,0:T(8,128)S(1)} %reshape.24.weight_ref.taps_ref), custom_call_target="tpu_custom_call" | custom-call | flops 1 | bytes 1 | tf_op jit(solution)/shard_map/pallas_call | solution.py:103
  14.2 2.1 %collective-permute-start.1 = (bf16[64,2048]{1,0:T(8,128)(2,1)S(1)}, bf16[64,2048]{1,0:T(8,128)(2,1)S(1)}, u32[]{:S(2)}, u32[]{:S(2)}) collective-permute-start(bf16[64,2048]{1,0:T(8,128)(2,1)S(1)} %collective-permute-done.refs_1_), channel_id=1, source_target_pairs={{0,2},{2,4},{4,6},{6,7},{7,5},{5,3},{3,1},{1,0},{8,10},{10,12},{12... | collective-permute-start | bytes 786440 | tf_op jit(solution)/shard_map/ppermute | solution.py:423
  16.3 1.6 %shard_map.77 = (bf16[8,128,512]{2,1,0:T(8,128)(2,1)S(1)}, bf16[8,128,512]{2,1,0:T(8,128)(2,1)S(1)}, bf16[512,1024]{1,0:T(8,128)(2,1)S(1)}) custom-call(bf16[2,8,128,512]{3,2,1,0:T(8,128)(2,1)S(1)} %bitcast.17, f32[18,512]{1,0:T(8,128)S(1)} %reshape.24.weight_ref.taps_ref, ...), custom_call_target="tpu_custom_call", output_to_operand_aliasing={{0}: (2, {}), {1}: (3, {}), {2}: (4, {})} | custom-call | flops 1 | bytes 1 | tf_op jit(solution)/shard_map/pallas_call | solution.py:103
  17.9 1.1 %collective-permute-done.4.refs_3_ = bf16[64,2048]{1,0:T(8,128)(2,1)S(1)} collective-permute-done((bf16[64,2048]{1,0:T(8,128)(2,1)S(1)}, bf16[64,2048]{1,0:T(8,128)(2,1)S(1)}, u32[]{:S(2)}, u32[]{:S(2)}) %collective-permute-start.4) | collective-permute-done | bytes 262176 | tf_op jit(solution)/shard_map/ppermute | solution.py:423
  18.9 0.9 %collective-permute-start.8 = (bf16[64,2048]{1,0:T(8,128)(2,1)S(1)}, bf16[64,2048]{1,0:T(8,128)(2,1)S(1)}, u32[]{:S(2)}, u32[]{:S(2)}) collective-permute-start(bf16[64,2048]{1,0:T(8,128)(2,1)S(1)} %collective-permute-done.4.refs_3_), channel_id=1, source_target_pairs={{0,1},{2,0},{4,2},{6,4},{7,6},{5,7},{3,5},{1,3},{8,9},{10,8},{12,1... | collective-permute-start | bytes 786440 | tf_op jit(solution)/shard_map/ppermute | solution.py:423
  19.9 1.1 %collective-permute-start.6 = (bf16[64,2048]{1,0:T(8,128)(2,1)S(1)}, bf16[64,2048]{1,0:T(8,128)(2,1)S(1)}, u32[]{:S(2)}, u32[]{:S(2)}) collective-permute-start(bf16[64,2048]{1,0:T(8,128)(2,1)S(1)} %collective-permute-done.2.refs_2_), channel_id=1, source_target_pairs={{0,2},{2,4},{4,6},{6,7},{7,5},{5,3},{3,1},{1,0},{8,10},{10,12},{12... | collective-permute-start | bytes 786440 | tf_op jit(solution)/shard_map/ppermute | solution.py:423
  21.0 2.1 %shard_map.78 = (f32[512,2048]{1,0:T(8,128)S(1)}, f32[1024,512]{1,0:T(8,128)S(1)}) custom-call(bf16[128,2048]{1,0:T(8,128)(2,1)S(1)} %bitcast.19, bf16[64,2048]{1,0:T(8,128)(2,1)S(1)} %collective-permute-done.refs_1_, bf16[64,2048]{1,0:T(8,128)(2,1)S(1)} %collective-permute-done.2.refs_2_, bf16[64,2048]{1,0:T(8,128)(2,1)S(1)} %collective-permute-done.4.refs_3_, ...), custom_call_target="tpu_custom_call" | custom-call | flops 1 | bytes 1 | tf_op jit(solution)/shard_map/pallas_call | solution.py:164
  23.5 2.0 %collective-permute-start.5 = (bf16[64,2048]{1,0:T(8,128)(2,1)S(1)}, bf16[64,2048]{1,0:T(8,128)(2,1)S(1)}, u32[]{:S(2)}, u32[]{:S(2)}) collective-permute-start(bf16[64,2048]{1,0:T(8,128)(2,1)S(1)} %collective-permute-done.1.refs_0_), channel_id=1, source_target_pairs={{0,2},{2,4},{4,6},{6,7},{7,5},{5,3},{3,1},{1,0},{8,10},{10,12},{12... | collective-permute-start | bytes 786440 | tf_op jit(solution)/shard_map/ppermute | solution.py:423
  25.5 3.6 %collective-permute-done.6.refs_1_ = bf16[64,2048]{1,0:T(8,128)(2,1)S(1)} collective-permute-done((bf16[64,2048]{1,0:T(8,128)(2,1)S(1)}, bf16[64,2048]{1,0:T(8,128)(2,1)S(1)}, u32[]{:S(2)}, u32[]{:S(2)}) %collective-permute-start.6) | collective-permute-done | bytes 262176 | tf_op jit(solution)/shard_map/ppermute | solution.py:423
  29.1 2.0 %collective-permute-done.8.refs_2_ = bf16[64,2048]{1,0:T(8,128)(2,1)S(1)} collective-permute-done((bf16[64,2048]{1,0:T(8,128)(2,1)S(1)}, bf16[64,2048]{1,0:T(8,128)(2,1)S(1)}, u32[]{:S(2)}, u32[]{:S(2)}) %collective-permute-start.8) | collective-permute-done | bytes 262176 | tf_op jit(solution)/shard_map/ppermute | solution.py:423
  31.2 2.0 %collective-permute-start.12 = (bf16[64,2048]{1,0:T(8,128)(2,1)S(1)}, bf16[64,2048]{1,0:T(8,128)(2,1)S(1)}, u32[]{:S(2)}, u32[]{:S(2)}) collective-permute-start(bf16[64,2048]{1,0:T(8,128)(2,1)S(1)} %collective-permute-done.6.refs_1_), channel_id=1, source_target_pairs={{0,2},{2,4},{4,6},{6,7},{7,5},{5,3},{3,1},{1,0},{8,10},{10,12},{12... | collective-permute-start | bytes 786440 | tf_op jit(solution)/shard_map/ppermute | solution.py:423
  33.2 1.6 %shard_map.79 = (f32[512,2048]{1,0:T(8,128)S(1)}, f32[1024,512]{1,0:T(8,128)S(1)}) custom-call(bf16[64,2048]{1,0:T(8,128)(2,1)S(1)} %collective-permute-done.1.refs_0_, bf16[64,2048]{1,0:T(8,128)(2,1)S(1)} %collective-permute-done.6.refs_1_, bf16[64,2048]{1,0:T(8,128)(2,1)S(1)} %collective-permute-done.8.refs_2_, ...), custom_call_target="tpu_custom_call", output_to_operand_aliasing={{0}: (7, {}), {1}: (8, {})} | custom-call | flops 1 | bytes 1 | tf_op jit(solution)/shard_map/pallas_call | solution.py:164
  34.8 2.0 %collective-permute-done.10.refs_3_ = bf16[64,2048]{1,0:T(8,128)(2,1)S(1)} collective-permute-done((bf16[64,2048]{1,0:T(8,128)(2,1)S(1)}, bf16[64,2048]{1,0:T(8,128)(2,1)S(1)}, u32[]{:S(2)}, u32[]{:S(2)}) %collective-permute-start.10) | collective-permute-done | bytes 262176 | tf_op jit(solution)/shard_map/ppermute | solution.py:423
  36.8 2.0 %collective-permute-start.9 = (bf16[64,2048]{1,0:T(8,128)(2,1)S(1)}, bf16[64,2048]{1,0:T(8,128)(2,1)S(1)}, u32[]{:S(2)}, u32[]{:S(2)}) collective-permute-start(bf16[64,2048]{1,0:T(8,128)(2,1)S(1)} %collective-permute-done.5.refs_0_), channel_id=1, source_target_pairs={{0,2},{2,4},{4,6},{6,7},{7,5},{5,3},{3,1},{1,0},{8,10},{10,12},{12... | collective-permute-start | bytes 786440 | tf_op jit(solution)/shard_map/ppermute | solution.py:423
  38.8 1.6 %collective-permute-done.12.refs_1_ = bf16[64,2048]{1,0:T(8,128)(2,1)S(1)} collective-permute-done((bf16[64,2048]{1,0:T(8,128)(2,1)S(1)}, bf16[64,2048]{1,0:T(8,128)(2,1)S(1)}, u32[]{:S(2)}, u32[]{:S(2)}) %collective-permute-start.12) | collective-permute-done | bytes 262176 | tf_op jit(solution)/shard_map/ppermute | solution.py:423
  40.4 2.0 %collective-permute-done.13.refs_2_ = bf16[64,2048]{1,0:T(8,128)(2,1)S(1)} collective-permute-done((bf16[64,2048]{1,0:T(8,128)(2,1)S(1)}, bf16[64,2048]{1,0:T(8,128)(2,1)S(1)}, u32[]{:S(2)}, u32[]{:S(2)}) %collective-permute-start.13) | collective-permute-done | bytes 262176 | tf_op jit(solution)/shard_map/ppermute | solution.py:423
  42.4 1.6 %shard_map.80 = (f32[512,2048]{1,0:T(8,128)S(1)}, f32[1024,512]{1,0:T(8,128)S(1)}) custom-call(bf16[64,2048]{1,0:T(8,128)(2,1)S(1)} %collective-permute-done.5.refs_0_, bf16[64,2048]{1,0:T(8,128)(2,1)S(1)} %collective-permute-done.12.refs_1_, bf16[64,2048]{1,0:T(8,128)(2,1)S(1)} %collective-permute-done.13.refs_2_, ...), custom_call_target="tpu_custom_call", output_to_operand_aliasing={{0}: (7, {}), {1}: (8, {})} | custom-call | flops 1 | bytes 1 | tf_op jit(solution)/shard_map/pallas_call | solution.py:164
  44.0 2.3 %collective-permute-done.11.down_ref = bf16[64,2048]{1,0:T(8,128)(2,1)S(1)} collective-permute-done((bf16[64,2048]{1,0:T(8,128)(2,1)S(1)}, bf16[64,2048]{1,0:T(8,128)(2,1)S(1)}, u32[]{:S(2)}, u32[]{:S(2)}) %collective-permute-start.11) | collective-permute-done | bytes 262176 | tf_op jit(solution)/shard_map/ppermute | solution.py:423
  48.3 1.6 %collective-permute-start.17 = (bf16[512,256]{1,0:T(8,128)(2,1)S(1)}, bf16[512,256]{1,0:T(8,128)(2,1)S(1)}, u32[]{:S(2)}, u32[]{:S(2)}) collective-permute-start(bf16[512,256]{1,0:T(8,128)(2,1)S(1)} %add_convert_fusion.2), channel_id=1, source_target_pairs={{0,16},{8,24},{16,0},{24,8},{1,17},{9,25},{17,1},{25,9},{2,18},{10... | collective-permute-start | bytes 786440 | tf_op jit(solution)/shard_map/ppermute | solution.py:372
  49.9 1.4 %collective-permute-start.18 = (bf16[512,384]{1,0:T(8,128)(2,1)S(1)}, bf16[512,384]{1,0:T(8,128)(2,1)S(1)}, u32[]{:S(2)}, u32[]{:S(2)}) collective-permute-start(bf16[512,384]{1,0:T(8,128)(2,1)S(1)} %add_convert_fusion.1), channel_id=1, source_target_pairs={{0,16},{8,24},{16,0},{24,8},{1,17},{9,25},{17,1},{25,9},{2,18},{10... | collective-permute-start | bytes 1179656 | tf_op jit(solution)/shard_map/ppermute | solution.py:372
  51.4 0.8 %shard_map.83.grad_ref = f32[1024,512]{1,0:T(8,128)S(1)} custom-call(bf16[64,2048]{1,0:T(8,128)(2,1)S(1)} %collective-permute-done.9.up_ref, bf16[64,2048]{1,0:T(8,128)(2,1)S(1)} %collective-permute-done.11.down_ref, f32[1,2048]{1,0:T(1,128)S(1)} %copy-done.2, bf16[512,2048]{1,0:T(8,128)(2,1)S(1)} %copy-done, ...), custom_call_target="tpu_custom_call", output_to_operand_aliasing={{}: (4, {})} | custom-call | flops 1 | bytes 1 | tf_op jit(solution)/shard_map/pallas_call | solution.py:244
  52.3 6.5 %shard_map.84 = (bf16[2,8,128,512]{3,2,1,0:T(8,128)(2,1)S(1)}, f32[3,3,2,512]{3,2,1,0:T(2,128)S(1)}) custom-call(f32[1024,512]{1,0:T(8,128)S(1)} %shard_map.83.grad_ref, bf16[8,128,512]{2,1,0:T(8,128)(2,1)S(1)} %get-tuple-element.205.gate_ref, bf16[8,128,512]{2,1,0:T(8,128)(2,1)S(1)} %get-tuple-element.206.value_ref, bf16[2,8,128,512]{3,2,1,0:T(8,128)(2,1)S(1)} %bitcast.18, ...), custom_call_target="tpu_custom_call" | custom-call | flops 1 | bytes 1 | tf_op jit(solution)/shard_map/pallas_call | solution.py:301
  58.8 3.5 %copy.20 = bf16[2,8,128,512]{3,0,2,1:T(2,128)(2,1)} copy(bf16[2,8,128,512]{3,2,1,0:T(8,128)(2,1)S(1)} %get-tuple-element.210) | data formatting | bytes 4194304 | tf_op jit(solution)/shard_map/optimization_barrier | solution.py:366
  63.0 2.3 %collective-permute-done.18 = bf16[512,384]{1,0:T(8,128)(2,1)S(1)} collective-permute-done((bf16[512,384]{1,0:T(8,128)(2,1)S(1)}, bf16[512,384]{1,0:T(8,128)(2,1)S(1)}, u32[]{:S(2)}, u32[]{:S(2)}) %collective-permute-start.18) | collective-permute-done | bytes 393248 | tf_op jit(solution)/shard_map/ppermute | solution.py:372
  66.1 1.6 %collective-permute-done.19 = f32[3,3,2,512]{3,2,1,0:T(2,128)S(1)} collective-permute-done((f32[3,3,2,512]{3,2,1,0:T(2,128)S(1)}, f32[3,3,2,512]{3,2,1,0:T(2,128)S(1)}, u32[]{:S(2)}, u32[]{:S(2)}) %collective-permute-start.19) | collective-permute-done | bytes 36896 | tf_op jit(solution)/shard_map/ppermute | solution.py:372
  67.7 2.2 %collective-permute-start.20 = (f32[3,3,2,512]{3,2,1,0:T(2,128)S(1)}, f32[3,3,2,512]{3,2,1,0:T(2,128)S(1)}, u32[]{:S(2)}, u32[]{:S(2)}) collective-permute-start(f32[3,3,2,512]{3,2,1,0:T(2,128)S(1)} %add.31.refs_5_), channel_id=1, source_target_pairs={{0,16},{8,24},{16,0},{24,8},{1,17},{9,25},{17,1},{25,9},{2,18},{10... | collective-permute-start | bytes 110600 | tf_op jit(solution)/shard_map/ppermute | solution.py:372
  69.9 4.1 %collective-permute-done.21 = bf16[512,384]{1,0:T(8,128)(2,1)S(1)} collective-permute-done((bf16[512,384]{1,0:T(8,128)(2,1)S(1)}, bf16[512,384]{1,0:T(8,128)(2,1)S(1)}, u32[]{:S(2)}, u32[]{:S(2)}) %collective-permute-start.21) | collective-permute-done | bytes 393248 | tf_op jit(solution)/shard_map/ppermute | solution.py:372
  74.6 1.4 %shard_map.85 = (bf16[512,2048]{1,0:T(8,128)(2,1)}, f32[3,3,2,512]{3,2,1,0:T(2,128)}) custom-call(bf16[512,256]{1,0:T(8,128)(2,1)S(1)} %multiply_convert_fusion.2.refs_0_, bf16[512,384]{1,0:T(8,128)(2,1)S(1)} %multiply_convert_fusion.1.refs_1_, bf16[512,384]{1,0:T(8,128)(2,1)S(1)} %multiply_convert_fusion.refs_2_, ...), custom_call_target="tpu_custom_call" | custom-call | flops 1 | bytes 1 | tf_op jit(solution)/shard_map/pallas_call | solution.py:345
  (47 shorter events, 6.7 us)
Async XLA Ops:
  1.7 12.5 %collective-permute-start = (bf16[64,2048]{1,0:T(8,128)(2,1)S(1)}, bf16[64,2048]{1,0:T(8,128)(2,1)S(1)}, u32[]{:S(2)}, u32[]{:S(2)}) collective-permute-start(bf16[64,2048]{1,0:T(8,128)(2,1)S(1)} %get-tuple-element.246), channel_id=1, source_target_pairs={{0,2},{2,4},{4,6},{6,7},{7,5},{5,3},{3,1},{1,0},{8,10},{10,12},{12... | collective-permute-start | bytes 786440 | tf_op jit(solution)/shard_map/ppermute | solution.py:423
  4.8 11.5 %collective-permute-start.3 = (bf16[64,2048]{1,0:T(8,128)(2,1)S(1)}, bf16[64,2048]{1,0:T(8,128)(2,1)S(1)}, u32[]{:S(2)}, u32[]{:S(2)}) collective-permute-start(bf16[64,2048]{1,0:T(8,128)(2,1)S(1)} %get-tuple-element.245), channel_id=1, source_target_pairs={{0,1},{2,0},{4,2},{6,4},{7,6},{5,7},{3,5},{1,3},{8,9},{10,8},{12,1... | collective-permute-start | bytes 786440 | tf_op jit(solution)/shard_map/ppermute | solution.py:423
  4.8 13.1 %collective-permute-start.2 = (bf16[64,2048]{1,0:T(8,128)(2,1)S(1)}, bf16[64,2048]{1,0:T(8,128)(2,1)S(1)}, u32[]{:S(2)}, u32[]{:S(2)}) collective-permute-start(bf16[64,2048]{1,0:T(8,128)(2,1)S(1)} %get-tuple-element.245), channel_id=1, source_target_pairs={{0,2},{2,4},{4,6},{6,7},{7,5},{5,3},{3,1},{1,0},{8,10},{10,12},{12... | collective-permute-start | bytes 786440 | tf_op jit(solution)/shard_map/ppermute | solution.py:423
  6.8 12.1 %collective-permute-start.4 = (bf16[64,2048]{1,0:T(8,128)(2,1)S(1)}, bf16[64,2048]{1,0:T(8,128)(2,1)S(1)}, u32[]{:S(2)}, u32[]{:S(2)}) collective-permute-start(bf16[64,2048]{1,0:T(8,128)(2,1)S(1)} %get-tuple-element.246), channel_id=1, source_target_pairs={{0,1},{2,0},{4,2},{6,4},{7,6},{5,7},{3,5},{1,3},{8,9},{10,8},{12,1... | collective-permute-start | bytes 786440 | tf_op jit(solution)/shard_map/ppermute | solution.py:423
  14.2 6.8 %copy-start = (bf16[512,2048]{1,0:T(8,128)(2,1)S(1)}, bf16[512,2048]{1,0:T(8,128)(2,1)}, u32[]{:S(2)}) copy-start(bf16[512,2048]{1,0:T(8,128)(2,1)} %weight_ref.1) | copy-start | bytes 6291460
  14.2 6.8 %copy-start.1 = (bf16[1,1,128,2048]{3,2,1,0:T(8,128)(2,1)S(1)}, bf16[1,1,128,2048]{3,2,1,0:T(8,128)(2,1)}, u32[]{:S(2)}) copy-start(bf16[1,1,128,2048]{3,2,1,0:T(8,128)(2,1)} %param.8) | copy-start | bytes 1572868
  14.2 6.8 %copy-start.2 = (f32[1,2048]{1,0:T(1,128)S(1)}, f32[1,2048]{1,0:T(1,128)}, u32[]{:S(2)}) copy-start(f32[1,2048]{1,0:T(1,128)} %gate_ref.5) | copy-start | bytes 24580
  14.2 9.3 %collective-permute-start.1 = (bf16[64,2048]{1,0:T(8,128)(2,1)S(1)}, bf16[64,2048]{1,0:T(8,128)(2,1)S(1)}, u32[]{:S(2)}, u32[]{:S(2)}) collective-permute-start(bf16[64,2048]{1,0:T(8,128)(2,1)S(1)} %collective-permute-done.refs_1_), channel_id=1, source_target_pairs={{0,2},{2,4},{4,6},{6,7},{7,5},{5,3},{3,1},{1,0},{8,10},{10,12},{12... | collective-permute-start | bytes 786440 | tf_op jit(solution)/shard_map/ppermute | solution.py:423
  16.3 9.2 %collective-permute-start.7 = (bf16[64,2048]{1,0:T(8,128)(2,1)S(1)}, bf16[64,2048]{1,0:T(8,128)(2,1)S(1)}, u32[]{:S(2)}, u32[]{:S(2)}) collective-permute-start(bf16[64,2048]{1,0:T(8,128)(2,1)S(1)} %collective-permute-done.3.refs_4_), channel_id=1, source_target_pairs={{0,1},{2,0},{4,2},{6,4},{7,6},{5,7},{3,5},{1,3},{8,9},{10,8},{12,1... | collective-permute-start | bytes 786440 | tf_op jit(solution)/shard_map/ppermute | solution.py:423
  18.9 12.2 %collective-permute-start.8 = (bf16[64,2048]{1,0:T(8,128)(2,1)S(1)}, bf16[64,2048]{1,0:T(8,128)(2,1)S(1)}, u32[]{:S(2)}, u32[]{:S(2)}) collective-permute-start(bf16[64,2048]{1,0:T(8,128)(2,1)S(1)} %collective-permute-done.4.refs_3_), channel_id=1, source_target_pairs={{0,1},{2,0},{4,2},{6,4},{7,6},{5,7},{3,5},{1,3},{8,9},{10,8},{12,1... | collective-permute-start | bytes 786440 | tf_op jit(solution)/shard_map/ppermute | solution.py:423
  19.9 9.2 %collective-permute-start.6 = (bf16[64,2048]{1,0:T(8,128)(2,1)S(1)}, bf16[64,2048]{1,0:T(8,128)(2,1)S(1)}, u32[]{:S(2)}, u32[]{:S(2)}) collective-permute-start(bf16[64,2048]{1,0:T(8,128)(2,1)S(1)} %collective-permute-done.2.refs_2_), channel_id=1, source_target_pairs={{0,2},{2,4},{4,6},{6,7},{7,5},{5,3},{3,1},{1,0},{8,10},{10,12},{12... | collective-permute-start | bytes 786440 | tf_op jit(solution)/shard_map/ppermute | solution.py:423
  23.5 11.3 %collective-permute-start.5 = (bf16[64,2048]{1,0:T(8,128)(2,1)S(1)}, bf16[64,2048]{1,0:T(8,128)(2,1)S(1)}, u32[]{:S(2)}, u32[]{:S(2)}) collective-permute-start(bf16[64,2048]{1,0:T(8,128)(2,1)S(1)} %collective-permute-done.1.refs_0_), channel_id=1, source_target_pairs={{0,2},{2,4},{4,6},{6,7},{7,5},{5,3},{3,1},{1,0},{8,10},{10,12},{12... | collective-permute-start | bytes 786440 | tf_op jit(solution)/shard_map/ppermute | solution.py:423
  25.5 11.2 %collective-permute-start.10 = (bf16[64,2048]{1,0:T(8,128)(2,1)S(1)}, bf16[64,2048]{1,0:T(8,128)(2,1)S(1)}, u32[]{:S(2)}, u32[]{:S(2)}) collective-permute-start(bf16[64,2048]{1,0:T(8,128)(2,1)S(1)} %collective-permute-done.7.refs_3_), channel_id=1, source_target_pairs={{0,1},{2,0},{4,2},{6,4},{7,6},{5,7},{3,5},{1,3},{8,9},{10,8},{12,1... | collective-permute-start | bytes 786440 | tf_op jit(solution)/shard_map/ppermute | solution.py:423
  31.2 11.2 %collective-permute-start.13 = (bf16[64,2048]{1,0:T(8,128)(2,1)S(1)}, bf16[64,2048]{1,0:T(8,128)(2,1)S(1)}, u32[]{:S(2)}, u32[]{:S(2)}) collective-permute-start(bf16[64,2048]{1,0:T(8,128)(2,1)S(1)} %collective-permute-done.8.refs_2_), channel_id=1, source_target_pairs={{0,1},{2,0},{4,2},{6,4},{7,6},{5,7},{3,5},{1,3},{8,9},{10,8},{12,1... | collective-permute-start | bytes 786440 | tf_op jit(solution)/shard_map/ppermute | solution.py:423
  31.2 9.2 %collective-permute-start.12 = (bf16[64,2048]{1,0:T(8,128)(2,1)S(1)}, bf16[64,2048]{1,0:T(8,128)(2,1)S(1)}, u32[]{:S(2)}, u32[]{:S(2)}) collective-permute-start(bf16[64,2048]{1,0:T(8,128)(2,1)S(1)} %collective-permute-done.6.refs_1_), channel_id=1, source_target_pairs={{0,2},{2,4},{4,6},{6,7},{7,5},{5,3},{3,1},{1,0},{8,10},{10,12},{12... | collective-permute-start | bytes 786440 | tf_op jit(solution)/shard_map/ppermute | solution.py:423
  36.8 9.5 %collective-permute-start.11 = (bf16[64,2048]{1,0:T(8,128)(2,1)S(1)}, bf16[64,2048]{1,0:T(8,128)(2,1)S(1)}, u32[]{:S(2)}, u32[]{:S(2)}) collective-permute-start(bf16[64,2048]{1,0:T(8,128)(2,1)S(1)} %collective-permute-done.10.refs_3_), channel_id=1, source_target_pairs={{0,1},{2,0},{4,2},{6,4},{7,6},{5,7},{3,5},{1,3},{8,9},{10,8},{12,1... | collective-permute-start | bytes 786440 | tf_op jit(solution)/shard_map/ppermute | solution.py:423
  36.8 9.5 %collective-permute-start.9 = (bf16[64,2048]{1,0:T(8,128)(2,1)S(1)}, bf16[64,2048]{1,0:T(8,128)(2,1)S(1)}, u32[]{:S(2)}, u32[]{:S(2)}) collective-permute-start(bf16[64,2048]{1,0:T(8,128)(2,1)S(1)} %collective-permute-done.5.refs_0_), channel_id=1, source_target_pairs={{0,2},{2,4},{4,6},{6,7},{7,5},{5,3},{3,1},{1,0},{8,10},{10,12},{12... | collective-permute-start | bytes 786440 | tf_op jit(solution)/shard_map/ppermute | solution.py:423
  46.6 1.6 %collective-permute-start.16 = (bf16[512,256]{1,0:T(8,128)(2,1)S(1)}, bf16[512,256]{1,0:T(8,128)(2,1)S(1)}, u32[]{:S(2)}, u32[]{:S(2)}) collective-permute-start(bf16[512,256]{1,0:T(8,128)(2,1)S(1)} %get-tuple-element.193), channel_id=1, source_target_pairs={{0,8},{8,0},{16,24},{24,16},{1,9},{9,1},{17,25},{25,17},{2,10},{10... | collective-permute-start | bytes 786440 | tf_op jit(solution)/shard_map/ppermute | solution.py:372
  47.3 2.5 %collective-permute-start.15 = (bf16[512,384]{1,0:T(8,128)(2,1)S(1)}, bf16[512,384]{1,0:T(8,128)(2,1)S(1)}, u32[]{:S(2)}, u32[]{:S(2)}) collective-permute-start(bf16[512,384]{1,0:T(8,128)(2,1)S(1)} %get-tuple-element.191), channel_id=1, source_target_pairs={{0,8},{8,0},{16,24},{24,16},{1,9},{9,1},{17,25},{25,17},{2,10},{10... | collective-permute-start | bytes 1179656 | tf_op jit(solution)/shard_map/ppermute | solution.py:372
  47.9 2.0 %collective-permute-start.14 = (bf16[512,384]{1,0:T(8,128)(2,1)S(1)}, bf16[512,384]{1,0:T(8,128)(2,1)S(1)}, u32[]{:S(2)}, u32[]{:S(2)}) collective-permute-start(bf16[512,384]{1,0:T(8,128)(2,1)S(1)} %get-tuple-element.189), channel_id=1, source_target_pairs={{0,8},{8,0},{16,24},{24,16},{1,9},{9,1},{17,25},{25,17},{2,10},{10... | collective-permute-start | bytes 1179656 | tf_op jit(solution)/shard_map/ppermute | solution.py:372
  48.3 14.7 %collective-permute-start.17 = (bf16[512,256]{1,0:T(8,128)(2,1)S(1)}, bf16[512,256]{1,0:T(8,128)(2,1)S(1)}, u32[]{:S(2)}, u32[]{:S(2)}) collective-permute-start(bf16[512,256]{1,0:T(8,128)(2,1)S(1)} %add_convert_fusion.2), channel_id=1, source_target_pairs={{0,16},{8,24},{16,0},{24,8},{1,17},{9,25},{17,1},{25,9},{2,18},{10... | collective-permute-start | bytes 786440 | tf_op jit(solution)/shard_map/ppermute | solution.py:372
  49.9 15.4 %collective-permute-start.18 = (bf16[512,384]{1,0:T(8,128)(2,1)S(1)}, bf16[512,384]{1,0:T(8,128)(2,1)S(1)}, u32[]{:S(2)}, u32[]{:S(2)}) collective-permute-start(bf16[512,384]{1,0:T(8,128)(2,1)S(1)} %add_convert_fusion.1), channel_id=1, source_target_pairs={{0,16},{8,24},{16,0},{24,8},{1,17},{9,25},{17,1},{25,9},{2,18},{10... | collective-permute-start | bytes 1179656 | tf_op jit(solution)/shard_map/ppermute | solution.py:372
  62.3 11.7 %collective-permute-start.21 = (bf16[512,384]{1,0:T(8,128)(2,1)S(1)}, bf16[512,384]{1,0:T(8,128)(2,1)S(1)}, u32[]{:S(2)}, u32[]{:S(2)}) collective-permute-start(bf16[512,384]{1,0:T(8,128)(2,1)S(1)} %add_convert_fusion), channel_id=1, source_target_pairs={{0,16},{8,24},{16,0},{24,8},{1,17},{9,25},{17,1},{25,9},{2,18},{10... | collective-permute-start | bytes 1179656 | tf_op jit(solution)/shard_map/ppermute | solution.py:372
  65.5 8.9 %collective-permute-start.22 = (bf16[512,384]{1,0:T(8,128)(2,1)S(1)}, bf16[512,384]{1,0:T(8,128)(2,1)S(1)}, u32[]{:S(2)}, u32[]{:S(2)}) collective-permute-start(bf16[512,384]{1,0:T(8,128)(2,1)S(1)} %multiply_convert_fusion.1.refs_1_), channel_id=1, source_target_pairs={{0,8},{8,0},{16,24},{24,16},{1,9},{9,1},{17,25},{25,17},{2,10},{10... | collective-permute-start | bytes 1179656 | tf_op jit(solution)/shard_map/ppermute | solution.py:372
  65.5 8.8 %collective-permute-start.23 = (bf16[512,256]{1,0:T(8,128)(2,1)S(1)}, bf16[512,256]{1,0:T(8,128)(2,1)S(1)}, u32[]{:S(2)}, u32[]{:S(2)}) collective-permute-start(bf16[512,256]{1,0:T(8,128)(2,1)S(1)} %multiply_convert_fusion.2.refs_0_), channel_id=1, source_target_pairs={{0,8},{8,0},{16,24},{24,16},{1,9},{9,1},{17,25},{25,17},{2,10},{10... | collective-permute-start | bytes 786440 | tf_op jit(solution)/shard_map/ppermute | solution.py:372
  66.0 1.6 %collective-permute-start.19 = (f32[3,3,2,512]{3,2,1,0:T(2,128)S(1)}, f32[3,3,2,512]{3,2,1,0:T(2,128)S(1)}, u32[]{:S(2)}, u32[]{:S(2)}) collective-permute-start(f32[3,3,2,512]{3,2,1,0:T(2,128)S(1)} %get-tuple-element.224), channel_id=1, source_target_pairs={{0,8},{8,0},{16,24},{24,16},{1,9},{9,1},{17,25},{25,17},{2,10},{10... | collective-permute-start | bytes 110600 | tf_op jit(solution)/shard_map/ppermute | solution.py:372
  67.7 6.7 %collective-permute-start.20 = (f32[3,3,2,512]{3,2,1,0:T(2,128)S(1)}, f32[3,3,2,512]{3,2,1,0:T(2,128)S(1)}, u32[]{:S(2)}, u32[]{:S(2)}) collective-permute-start(f32[3,3,2,512]{3,2,1,0:T(2,128)S(1)} %add.31.refs_5_), channel_id=1, source_target_pairs={{0,16},{8,24},{16,0},{24,8},{1,17},{9,25},{17,1},{25,9},{2,18},{10... | collective-permute-start | bytes 110600 | tf_op jit(solution)/shard_map/ppermute | solution.py:372
  74.5 1.8 %collective-permute-start.24 = (bf16[512,384]{1,0:T(8,128)(2,1)S(1)}, bf16[512,384]{1,0:T(8,128)(2,1)S(1)}, u32[]{:S(2)}, u32[]{:S(2)}) collective-permute-start(bf16[512,384]{1,0:T(8,128)(2,1)S(1)} %multiply_convert_fusion.refs_2_), channel_id=1, source_target_pairs={{0,8},{8,0},{16,24},{24,16},{1,9},{9,1},{17,25},{25,17},{2,10},{10... | collective-permute-start | bytes 1179656 | tf_op jit(solution)/shard_map/ppermute | solution.py:372

commit v8 on v7

--- a/solution.py
+++ b/solution.py
@@ -475,7 +475,7 @@
     hidden_grad = order.after(hidden_grad, ())
     finish(1)
     received = order.after(received, ())
-    terms = order.after(terms + received, ())
+    terms = order.after((terms + received).astype(BF16), ())
     received = swap(terms, 2)
     received, far_sums[2] = order.after((received, far_sums[2]), ())
     others[0] = order.after(others[0], ())
@@ -483,7 +483,7 @@
     finish(2)
     shape = (channels, depth)
     whole, conv_grad = put(
-        order.token, mines, others[:2], firsts, shape, terms, received
+        order.token, mines, others[:2], firsts, shape, terms.astype(F32), received.astype(F32)
     )
     bit = 4
     while bit < dp:

time: 77.3 us -> 76.9 us (level)
  no operation moved by 1% of the time
where the time goes in v8:
time: 76.9 us; the launch traced here: 76.7 us
  waiting for transfers between devices  23.4 us (30%)
  starting transfers between devices  22.5 us (29%)
  Pallas kernels  21.1 us (27%)
  local copies, waits for them, and re-layouts  8.08 us (11%)
  between operations  0.86 us (1%)
    ppermute x14, starting transfers between devices, on_device(): lax.ppermute(state[way, part], 'tensor', right if way == 'up' else left)  15.3 us
    ppermute x14, waiting for transfers between devices, on_device(): lax.ppermute(state[way, part], 'tensor', right if way == 'up' else left)  14.9 us
    ppermute x11, waiting for transfers between devices, swap(): return lax.ppermute(value, 'dp', [(i, i ^ bit) for i in range(n)])  8.5 us
    ppermute x11, starting transfers between devices, swap(): return lax.ppermute(value, 'dp', [(i, i ^ bit) for i in range(n)])  7.25 us
    pallas_call x1, Pallas kernels, grads(): pl.pallas_call(functools.partial(grads_kernel, scale), in_specs=[VMEM] *...  6.54 us
    pallas_call x2, Pallas kernels, conv_parts(): pl.pallas_call(functools.partial(conv_kernel, first, count), in_specs=[VM...  6.1 us
    pallas_call x3, Pallas kernels, rows_parts(): pl.pallas_call(functools.partial(rows_kernel, n, len(pieces), numbers, be...  5.31 us
    optimization_barrier x1, local copies, waits for them, and re-layouts, after(): lax.optimization_barrier(flat)  3.48 us
  transfers between devices with their start and end apart: 25, of which 14 were waited for; matrix products, arithmetic and copies ran while one was open for 9% of the time, Pallas kernels for 27%

profile of v8, /device:TPU:0, one launch (start us, length us, event | category | flops | bytes accessed | tf_op | source)
XLA Modules:
  0.0 76.7 jit_solution(3442100018916818659)
XLA Ops:
  0.6 1.1 %slice_bitcast_fusion = (bf16[64,2048]{1,0:T(8,128)(2,1)S(1)}, bf16[64,2048]{1,0:T(8,128)(2,1)S(1)}) fusion(bf16[1,1,128,2048]{3,2,1,0:T(8,128)(2,1)} %param.8), kind=kLoop, calls=%fused_computation.8 | loop fusion | bytes 1048576 | tf_op jit(solution)/shard_map/slice | solution.py:410
  1.7 3.1 %collective-permute-start = (bf16[64,2048]{1,0:T(8,128)(2,1)S(1)}, bf16[64,2048]{1,0:T(8,128)(2,1)S(1)}, u32[]{:S(2)}, u32[]{:S(2)}) collective-permute-start(bf16[64,2048]{1,0:T(8,128)(2,1)S(1)} %get-tuple-element.246), channel_id=1, source_target_pairs={{0,2},{2,4},{4,6},{6,7},{7,5},{5,3},{3,1},{1,0},{8,10},{10,12},{12... | collective-permute-start | bytes 786440 | tf_op jit(solution)/shard_map/ppermute | solution.py:423
  4.8 2.0 %collective-permute-start.2 = (bf16[64,2048]{1,0:T(8,128)(2,1)S(1)}, bf16[64,2048]{1,0:T(8,128)(2,1)S(1)}, u32[]{:S(2)}, u32[]{:S(2)}) collective-permute-start(bf16[64,2048]{1,0:T(8,128)(2,1)S(1)} %get-tuple-element.245), channel_id=1, source_target_pairs={{0,2},{2,4},{4,6},{6,7},{7,5},{5,3},{3,1},{1,0},{8,10},{10,12},{12... | collective-permute-start | bytes 786440 | tf_op jit(solution)/shard_map/ppermute | solution.py:423
  7.6 2.0 %copy.21 = bf16[1,8,128,2,512]{4,2,1,3,0:T(8,128)(2,1)S(1)} copy(bf16[1,8,128,2,512]{4,3,2,1,0:T(2,128)(2,1)} %param.5) | data formatting | bytes 4194304 | tf_op args[0]
  9.6 4.5 %shard_map.76 = (bf16[8,128,512]{2,1,0:T(8,128)(2,1)S(1)}, bf16[8,128,512]{2,1,0:T(8,128)(2,1)S(1)}, bf16[512,1024]{1,0:T(8,128)(2,1)S(1)}) custom-call(bf16[2,8,128,512]{3,2,1,0:T(8,128)(2,1)S(1)} %bitcast.16, f32[18,512]{1,0:T(8,128)S(1)} %reshape.24.weight_ref.taps_ref), custom_call_target="tpu_custom_call" | custom-call | flops 1 | bytes 1 | tf_op jit(solution)/shard_map/pallas_call | solution.py:103
  14.2 2.1 %collective-permute-start.1 = (bf16[64,2048]{1,0:T(8,128)(2,1)S(1)}, bf16[64,2048]{1,0:T(8,128)(2,1)S(1)}, u32[]{:S(2)}, u32[]{:S(2)}) collective-permute-start(bf16[64,2048]{1,0:T(8,128)(2,1)S(1)} %collective-permute-done.refs_1_), channel_id=1, source_target_pairs={{0,2},{2,4},{4,6},{6,7},{7,5},{5,3},{3,1},{1,0},{8,10},{10,12},{12... | collective-permute-start | bytes 786440 | tf_op jit(solution)/shard_map/ppermute | solution.py:423
  16.3 1.6 %shard_map.77 = (bf16[8,128,512]{2,1,0:T(8,128)(2,1)S(1)}, bf16[8,128,512]{2,1,0:T(8,128)(2,1)S(1)}, bf16[512,1024]{1,0:T(8,128)(2,1)S(1)}) custom-call(bf16[2,8,128,512]{3,2,1,0:T(8,128)(2,1)S(1)} %bitcast.17, f32[18,512]{1,0:T(8,128)S(1)} %reshape.24.weight_ref.taps_ref, ...), custom_call_target="tpu_custom_call", output_to_operand_aliasing={{0}: (2, {}), {1}: (3, {}), {2}: (4, {})} | custom-call | flops 1 | bytes 1 | tf_op jit(solution)/shard_map/pallas_call | solution.py:103
  17.9 1.0 %collective-permute-done.4.refs_3_ = bf16[64,2048]{1,0:T(8,128)(2,1)S(1)} collective-permute-done((bf16[64,2048]{1,0:T(8,128)(2,1)S(1)}, bf16[64,2048]{1,0:T(8,128)(2,1)S(1)}, u32[]{:S(2)}, u32[]{:S(2)}) %collective-permute-start.4) | collective-permute-done | bytes 262176 | tf_op jit(solution)/shard_map/ppermute | solution.py:423
  18.9 1.0 %collective-permute-start.8 = (bf16[64,2048]{1,0:T(8,128)(2,1)S(1)}, bf16[64,2048]{1,0:T(8,128)(2,1)S(1)}, u32[]{:S(2)}, u32[]{:S(2)}) collective-permute-start(bf16[64,2048]{1,0:T(8,128)(2,1)S(1)} %collective-permute-done.4.refs_3_), channel_id=1, source_target_pairs={{0,1},{2,0},{4,2},{6,4},{7,6},{5,7},{3,5},{1,3},{8,9},{10,8},{12,1... | collective-permute-start | bytes 786440 | tf_op jit(solution)/shard_map/ppermute | solution.py:423
  19.9 1.1 %collective-permute-start.6 = (bf16[64,2048]{1,0:T(8,128)(2,1)S(1)}, bf16[64,2048]{1,0:T(8,128)(2,1)S(1)}, u32[]{:S(2)}, u32[]{:S(2)}) collective-permute-start(bf16[64,2048]{1,0:T(8,128)(2,1)S(1)} %collective-permute-done.2.refs_2_), channel_id=1, source_target_pairs={{0,2},{2,4},{4,6},{6,7},{7,5},{5,3},{3,1},{1,0},{8,10},{10,12},{12... | collective-permute-start | bytes 786440 | tf_op jit(solution)/shard_map/ppermute | solution.py:423
  21.0 2.1 %shard_map.78 = (f32[512,2048]{1,0:T(8,128)S(1)}, f32[1024,512]{1,0:T(8,128)S(1)}) custom-call(bf16[128,2048]{1,0:T(8,128)(2,1)S(1)} %bitcast.19, bf16[64,2048]{1,0:T(8,128)(2,1)S(1)} %collective-permute-done.refs_1_, bf16[64,2048]{1,0:T(8,128)(2,1)S(1)} %collective-permute-done.2.refs_2_, bf16[64,2048]{1,0:T(8,128)(2,1)S(1)} %collective-permute-done.4.refs_3_, ...), custom_call_target="tpu_custom_call" | custom-call | flops 1 | bytes 1 | tf_op jit(solution)/shard_map/pallas_call | solution.py:164
  23.5 2.0 %collective-permute-start.5 = (bf16[64,2048]{1,0:T(8,128)(2,1)S(1)}, bf16[64,2048]{1,0:T(8,128)(2,1)S(1)}, u32[]{:S(2)}, u32[]{:S(2)}) collective-permute-start(bf16[64,2048]{1,0:T(8,128)(2,1)S(1)} %collective-permute-done.1.refs_0_), channel_id=1, source_target_pairs={{0,2},{2,4},{4,6},{6,7},{7,5},{5,3},{3,1},{1,0},{8,10},{10,12},{12... | collective-permute-start | bytes 786440 | tf_op jit(solution)/shard_map/ppermute | solution.py:423
  25.5 3.6 %collective-permute-done.6.refs_1_ = bf16[64,2048]{1,0:T(8,128)(2,1)S(1)} collective-permute-done((bf16[64,2048]{1,0:T(8,128)(2,1)S(1)}, bf16[64,2048]{1,0:T(8,128)(2,1)S(1)}, u32[]{:S(2)}, u32[]{:S(2)}) %collective-permute-start.6) | collective-permute-done | bytes 262176 | tf_op jit(solution)/shard_map/ppermute | solution.py:423
  29.1 2.0 %collective-permute-done.8.refs_2_ = bf16[64,2048]{1,0:T(8,128)(2,1)S(1)} collective-permute-done((bf16[64,2048]{1,0:T(8,128)(2,1)S(1)}, bf16[64,2048]{1,0:T(8,128)(2,1)S(1)}, u32[]{:S(2)}, u32[]{:S(2)}) %collective-permute-start.8) | collective-permute-done | bytes 262176 | tf_op jit(solution)/shard_map/ppermute | solution.py:423
  31.2 2.0 %collective-permute-start.12 = (bf16[64,2048]{1,0:T(8,128)(2,1)S(1)}, bf16[64,2048]{1,0:T(8,128)(2,1)S(1)}, u32[]{:S(2)}, u32[]{:S(2)}) collective-permute-start(bf16[64,2048]{1,0:T(8,128)(2,1)S(1)} %collective-permute-done.6.refs_1_), channel_id=1, source_target_pairs={{0,2},{2,4},{4,6},{6,7},{7,5},{5,3},{3,1},{1,0},{8,10},{10,12},{12... | collective-permute-start | bytes 786440 | tf_op jit(solution)/shard_map/ppermute | solution.py:423
  33.2 1.6 %shard_map.79 = (f32[512,2048]{1,0:T(8,128)S(1)}, f32[1024,512]{1,0:T(8,128)S(1)}) custom-call(bf16[64,2048]{1,0:T(8,128)(2,1)S(1)} %collective-permute-done.1.refs_0_, bf16[64,2048]{1,0:T(8,128)(2,1)S(1)} %collective-permute-done.6.refs_1_, bf16[64,2048]{1,0:T(8,128)(2,1)S(1)} %collective-permute-done.8.refs_2_, ...), custom_call_target="tpu_custom_call", output_to_operand_aliasing={{0}: (7, {}), {1}: (8, {})} | custom-call | flops 1 | bytes 1 | tf_op jit(solution)/shard_map/pallas_call | solution.py:164
  34.8 2.0 %collective-permute-done.10.refs_3_ = bf16[64,2048]{1,0:T(8,128)(2,1)S(1)} collective-permute-done((bf16[64,2048]{1,0:T(8,128)(2,1)S(1)}, bf16[64,2048]{1,0:T(8,128)(2,1)S(1)}, u32[]{:S(2)}, u32[]{:S(2)}) %collective-permute-start.10) | collective-permute-done | bytes 262176 | tf_op jit(solution)/shard_map/ppermute | solution.py:423
  36.8 2.0 %collective-permute-start.9 = (bf16[64,2048]{1,0:T(8,128)(2,1)S(1)}, bf16[64,2048]{1,0:T(8,128)(2,1)S(1)}, u32[]{:S(2)}, u32[]{:S(2)}) collective-permute-start(bf16[64,2048]{1,0:T(8,128)(2,1)S(1)} %collective-permute-done.5.refs_0_), channel_id=1, source_target_pairs={{0,2},{2,4},{4,6},{6,7},{7,5},{5,3},{3,1},{1,0},{8,10},{10,12},{12... | collective-permute-start | bytes 786440 | tf_op jit(solution)/shard_map/ppermute | solution.py:423
  38.8 1.6 %collective-permute-done.12.refs_1_ = bf16[64,2048]{1,0:T(8,128)(2,1)S(1)} collective-permute-done((bf16[64,2048]{1,0:T(8,128)(2,1)S(1)}, bf16[64,2048]{1,0:T(8,128)(2,1)S(1)}, u32[]{:S(2)}, u32[]{:S(2)}) %collective-permute-start.12) | collective-permute-done | bytes 262176 | tf_op jit(solution)/shard_map/ppermute | solution.py:423
  40.4 2.0 %collective-permute-done.13.refs_2_ = bf16[64,2048]{1,0:T(8,128)(2,1)S(1)} collective-permute-done((bf16[64,2048]{1,0:T(8,128)(2,1)S(1)}, bf16[64,2048]{1,0:T(8,128)(2,1)S(1)}, u32[]{:S(2)}, u32[]{:S(2)}) %collective-permute-start.13) | collective-permute-done | bytes 262176 | tf_op jit(solution)/shard_map/ppermute | solution.py:423
  42.4 1.6 %shard_map.80 = (f32[512,2048]{1,0:T(8,128)S(1)}, f32[1024,512]{1,0:T(8,128)S(1)}) custom-call(bf16[64,2048]{1,0:T(8,128)(2,1)S(1)} %collective-permute-done.5.refs_0_, bf16[64,2048]{1,0:T(8,128)(2,1)S(1)} %collective-permute-done.12.refs_1_, bf16[64,2048]{1,0:T(8,128)(2,1)S(1)} %collective-permute-done.13.refs_2_, ...), custom_call_target="tpu_custom_call", output_to_operand_aliasing={{0}: (7, {}), {1}: (8, {})} | custom-call | flops 1 | bytes 1 | tf_op jit(solution)/shard_map/pallas_call | solution.py:164
  44.0 2.3 %collective-permute-done.11.down_ref = bf16[64,2048]{1,0:T(8,128)(2,1)S(1)} collective-permute-done((bf16[64,2048]{1,0:T(8,128)(2,1)S(1)}, bf16[64,2048]{1,0:T(8,128)(2,1)S(1)}, u32[]{:S(2)}, u32[]{:S(2)}) %collective-permute-start.11) | collective-permute-done | bytes 262176 | tf_op jit(solution)/shard_map/ppermute | solution.py:423
  48.2 1.6 %collective-permute-start.17 = (bf16[512,256]{1,0:T(8,128)(2,1)S(1)}, bf16[512,256]{1,0:T(8,128)(2,1)S(1)}, u32[]{:S(2)}, u32[]{:S(2)}) collective-permute-start(bf16[512,256]{1,0:T(8,128)(2,1)S(1)} %add_convert_fusion.2), channel_id=1, source_target_pairs={{0,16},{8,24},{16,0},{24,8},{1,17},{9,25},{17,1},{25,9},{2,18},{10... | collective-permute-start | bytes 786440 | tf_op jit(solution)/shard_map/ppermute | solution.py:372
  49.9 1.4 %collective-permute-start.18 = (bf16[512,384]{1,0:T(8,128)(2,1)S(1)}, bf16[512,384]{1,0:T(8,128)(2,1)S(1)}, u32[]{:S(2)}, u32[]{:S(2)}) collective-permute-start(bf16[512,384]{1,0:T(8,128)(2,1)S(1)} %add_convert_fusion.1), channel_id=1, source_target_pairs={{0,16},{8,24},{16,0},{24,8},{1,17},{9,25},{17,1},{25,9},{2,18},{10... | collective-permute-start | bytes 1179656 | tf_op jit(solution)/shard_map/ppermute | solution.py:372
  51.4 0.8 %shard_map.83.grad_ref = f32[1024,512]{1,0:T(8,128)S(1)} custom-call(bf16[64,2048]{1,0:T(8,128)(2,1)S(1)} %collective-permute-done.9.up_ref, bf16[64,2048]{1,0:T(8,128)(2,1)S(1)} %collective-permute-done.11.down_ref, f32[1,2048]{1,0:T(1,128)S(1)} %copy-done.2, bf16[512,2048]{1,0:T(8,128)(2,1)S(1)} %copy-done, ...), custom_call_target="tpu_custom_call", output_to_operand_aliasing={{}: (4, {})} | custom-call | flops 1 | bytes 1 | tf_op jit(solution)/shard_map/pallas_call | solution.py:244
  52.2 6.5 %shard_map.84 = (bf16[2,8,128,512]{3,2,1,0:T(8,128)(2,1)S(1)}, f32[3,3,2,512]{3,2,1,0:T(2,128)S(1)}) custom-call(f32[1024,512]{1,0:T(8,128)S(1)} %shard_map.83.grad_ref, bf16[8,128,512]{2,1,0:T(8,128)(2,1)S(1)} %get-tuple-element.205.gate_ref, bf16[8,128,512]{2,1,0:T(8,128)(2,1)S(1)} %get-tuple-element.206.value_ref, bf16[2,8,128,512]{3,2,1,0:T(8,128)(2,1)S(1)} %bitcast.18, ...), custom_call_target="tpu_custom_call" | custom-call | flops 1 | bytes 1 | tf_op jit(solution)/shard_map/pallas_call | solution.py:301
  58.8 3.5 %copy.20 = bf16[2,8,128,512]{3,0,2,1:T(2,128)(2,1)} copy(bf16[2,8,128,512]{3,2,1,0:T(8,128)(2,1)S(1)} %get-tuple-element.210) | data formatting | bytes 4194304 | tf_op jit(solution)/shard_map/optimization_barrier | solution.py:366
  63.0 2.3 %collective-permute-done.18 = bf16[512,384]{1,0:T(8,128)(2,1)S(1)} collective-permute-done((bf16[512,384]{1,0:T(8,128)(2,1)S(1)}, bf16[512,384]{1,0:T(8,128)(2,1)S(1)}, u32[]{:S(2)}, u32[]{:S(2)}) %collective-permute-start.18) | collective-permute-done | bytes 393248 | tf_op jit(solution)/shard_map/ppermute | solution.py:372
  66.1 1.2 %collective-permute-done.19 = f32[3,3,2,512]{3,2,1,0:T(2,128)S(1)} collective-permute-done((f32[3,3,2,512]{3,2,1,0:T(2,128)S(1)}, f32[3,3,2,512]{3,2,1,0:T(2,128)S(1)}, u32[]{:S(2)}, u32[]{:S(2)}) %collective-permute-start.19) | collective-permute-done | bytes 36896 | tf_op jit(solution)/shard_map/ppermute | solution.py:372
  67.3 2.2 %collective-permute-start.20 = (bf16[3,3,2,512]{3,2,1,0:T(2,128)(2,1)S(1)}, bf16[3,3,2,512]{3,2,1,0:T(2,128)(2,1)S(1)}, u32[]{:S(2)}, u32[]{:S(2)}) collective-permute-start(bf16[3,3,2,512]{3,2,1,0:T(2,128)(2,1)S(1)} %add_convert_fusion.3), channel_id=1, source_target_pairs={{0,16},{8,24},{16,0},{24,8},{1,17},{9,25},{17,1},{25,9},{2,18},{10... | collective-permute-start | bytes 55304 | tf_op jit(solution)/shard_map/ppermute | solution.py:372
  69.5 4.3 %collective-permute-done.21 = bf16[512,384]{1,0:T(8,128)(2,1)S(1)} collective-permute-done((bf16[512,384]{1,0:T(8,128)(2,1)S(1)}, bf16[512,384]{1,0:T(8,128)(2,1)S(1)}, u32[]{:S(2)}, u32[]{:S(2)}) %collective-permute-start.21) | collective-permute-done | bytes 393248 | tf_op jit(solution)/shard_map/ppermute | solution.py:372
  74.2 1.4 %shard_map.85 = (bf16[512,2048]{1,0:T(8,128)(2,1)}, f32[3,3,2,512]{3,2,1,0:T(2,128)}) custom-call(bf16[512,256]{1,0:T(8,128)(2,1)S(1)} %multiply_convert_fusion.2.refs_0_, bf16[512,384]{1,0:T(8,128)(2,1)S(1)} %multiply_convert_fusion.1.refs_1_, bf16[512,384]{1,0:T(8,128)(2,1)S(1)} %multiply_convert_fusion.refs_2_, ...), custom_call_target="tpu_custom_call" | custom-call | flops 1 | bytes 1 | tf_op jit(solution)/shard_map/pallas_call | solution.py:345
  (49 shorter events, 6.5 us)
Async XLA Ops:
  1.7 12.5 %collective-permute-start = (bf16[64,2048]{1,0:T(8,128)(2,1)S(1)}, bf16[64,2048]{1,0:T(8,128)(2,1)S(1)}, u32[]{:S(2)}, u32[]{:S(2)}) collective-permute-start(bf16[64,2048]{1,0:T(8,128)(2,1)S(1)} %get-tuple-element.246), channel_id=1, source_target_pairs={{0,2},{2,4},{4,6},{6,7},{7,5},{5,3},{3,1},{1,0},{8,10},{10,12},{12... | collective-permute-start | bytes 786440 | tf_op jit(solution)/shard_map/ppermute | solution.py:423
  4.8 11.5 %collective-permute-start.3 = (bf16[64,2048]{1,0:T(8,128)(2,1)S(1)}, bf16[64,2048]{1,0:T(8,128)(2,1)S(1)}, u32[]{:S(2)}, u32[]{:S(2)}) collective-permute-start(bf16[64,2048]{1,0:T(8,128)(2,1)S(1)} %get-tuple-element.245), channel_id=1, source_target_pairs={{0,1},{2,0},{4,2},{6,4},{7,6},{5,7},{3,5},{1,3},{8,9},{10,8},{12,1... | collective-permute-start | bytes 786440 | tf_op jit(solution)/shard_map/ppermute | solution.py:423
  4.8 13.1 %collective-permute-start.2 = (bf16[64,2048]{1,0:T(8,128)(2,1)S(1)}, bf16[64,2048]{1,0:T(8,128)(2,1)S(1)}, u32[]{:S(2)}, u32[]{:S(2)}) collective-permute-start(bf16[64,2048]{1,0:T(8,128)(2,1)S(1)} %get-tuple-element.245), channel_id=1, source_target_pairs={{0,2},{2,4},{4,6},{6,7},{7,5},{5,3},{3,1},{1,0},{8,10},{10,12},{12... | collective-permute-start | bytes 786440 | tf_op jit(solution)/shard_map/ppermute | solution.py:423
  6.8 12.1 %collective-permute-start.4 = (bf16[64,2048]{1,0:T(8,128)(2,1)S(1)}, bf16[64,2048]{1,0:T(8,128)(2,1)S(1)}, u32[]{:S(2)}, u32[]{:S(2)}) collective-permute-start(bf16[64,2048]{1,0:T(8,128)(2,1)S(1)} %get-tuple-element.246), channel_id=1, source_target_pairs={{0,1},{2,0},{4,2},{6,4},{7,6},{5,7},{3,5},{1,3},{8,9},{10,8},{12,1... | collective-permute-start | bytes 786440 | tf_op jit(solution)/shard_map/ppermute | solution.py:423
  14.2 6.8 %copy-start = (bf16[512,2048]{1,0:T(8,128)(2,1)S(1)}, bf16[512,2048]{1,0:T(8,128)(2,1)}, u32[]{:S(2)}) copy-start(bf16[512,2048]{1,0:T(8,128)(2,1)} %weight_ref.1) | copy-start | bytes 6291460
  14.2 6.8 %copy-start.1 = (bf16[1,1,128,2048]{3,2,1,0:T(8,128)(2,1)S(1)}, bf16[1,1,128,2048]{3,2,1,0:T(8,128)(2,1)}, u32[]{:S(2)}) copy-start(bf16[1,1,128,2048]{3,2,1,0:T(8,128)(2,1)} %param.8) | copy-start | bytes 1572868
  14.2 6.8 %copy-start.2 = (f32[1,2048]{1,0:T(1,128)S(1)}, f32[1,2048]{1,0:T(1,128)}, u32[]{:S(2)}) copy-start(f32[1,2048]{1,0:T(1,128)} %gate_ref.5) | copy-start | bytes 24580
  14.2 9.3 %collective-permute-start.1 = (bf16[64,2048]{1,0:T(8,128)(2,1)S(1)}, bf16[64,2048]{1,0:T(8,128)(2,1)S(1)}, u32[]{:S(2)}, u32[]{:S(2)}) collective-permute-start(bf16[64,2048]{1,0:T(8,128)(2,1)S(1)} %collective-permute-done.refs_1_), channel_id=1, source_target_pairs={{0,2},{2,4},{4,6},{6,7},{7,5},{5,3},{3,1},{1,0},{8,10},{10,12},{12... | collective-permute-start | bytes 786440 | tf_op jit(solution)/shard_map/ppermute | solution.py:423
  16.3 9.2 %collective-permute-start.7 = (bf16[64,2048]{1,0:T(8,128)(2,1)S(1)}, bf16[64,2048]{1,0:T(8,128)(2,1)S(1)}, u32[]{:S(2)}, u32[]{:S(2)}) collective-permute-start(bf16[64,2048]{1,0:T(8,128)(2,1)S(1)} %collective-permute-done.3.refs_4_), channel_id=1, source_target_pairs={{0,1},{2,0},{4,2},{6,4},{7,6},{5,7},{3,5},{1,3},{8,9},{10,8},{12,1... | collective-permute-start | bytes 786440 | tf_op jit(solution)/shard_map/ppermute | solution.py:423
  18.9 12.2 %collective-permute-start.8 = (bf16[64,2048]{1,0:T(8,128)(2,1)S(1)}, bf16[64,2048]{1,0:T(8,128)(2,1)S(1)}, u32[]{:S(2)}, u32[]{:S(2)}) collective-permute-start(bf16[64,2048]{1,0:T(8,128)(2,1)S(1)} %collective-permute-done.4.refs_3_), channel_id=1, source_target_pairs={{0,1},{2,0},{4,2},{6,4},{7,6},{5,7},{3,5},{1,3},{8,9},{10,8},{12,1... | collective-permute-start | bytes 786440 | tf_op jit(solution)/shard_map/ppermute | solution.py:423
  19.9 9.2 %collective-permute-start.6 = (bf16[64,2048]{1,0:T(8,128)(2,1)S(1)}, bf16[64,2048]{1,0:T(8,128)(2,1)S(1)}, u32[]{:S(2)}, u32[]{:S(2)}) collective-permute-start(bf16[64,2048]{1,0:T(8,128)(2,1)S(1)} %collective-permute-done.2.refs_2_), channel_id=1, source_target_pairs={{0,2},{2,4},{4,6},{6,7},{7,5},{5,3},{3,1},{1,0},{8,10},{10,12},{12... | collective-permute-start | bytes 786440 | tf_op jit(solution)/shard_map/ppermute | solution.py:423
  23.5 11.3 %collective-permute-start.5 = (bf16[64,2048]{1,0:T(8,128)(2,1)S(1)}, bf16[64,2048]{1,0:T(8,128)(2,1)S(1)}, u32[]{:S(2)}, u32[]{:S(2)}) collective-permute-start(bf16[64,2048]{1,0:T(8,128)(2,1)S(1)} %collective-permute-done.1.refs_0_), channel_id=1, source_target_pairs={{0,2},{2,4},{4,6},{6,7},{7,5},{5,3},{3,1},{1,0},{8,10},{10,12},{12... | collective-permute-start | bytes 786440 | tf_op jit(solution)/shard_map/ppermute | solution.py:423
  25.5 11.2 %collective-permute-start.10 = (bf16[64,2048]{1,0:T(8,128)(2,1)S(1)}, bf16[64,2048]{1,0:T(8,128)(2,1)S(1)}, u32[]{:S(2)}, u32[]{:S(2)}) collective-permute-start(bf16[64,2048]{1,0:T(8,128)(2,1)S(1)} %collective-permute-done.7.refs_3_), channel_id=1, source_target_pairs={{0,1},{2,0},{4,2},{6,4},{7,6},{5,7},{3,5},{1,3},{8,9},{10,8},{12,1... | collective-permute-start | bytes 786440 | tf_op jit(solution)/shard_map/ppermute | solution.py:423
  31.2 11.2 %collective-permute-start.13 = (bf16[64,2048]{1,0:T(8,128)(2,1)S(1)}, bf16[64,2048]{1,0:T(8,128)(2,1)S(1)}, u32[]{:S(2)}, u32[]{:S(2)}) collective-permute-start(bf16[64,2048]{1,0:T(8,128)(2,1)S(1)} %collective-permute-done.8.refs_2_), channel_id=1, source_target_pairs={{0,1},{2,0},{4,2},{6,4},{7,6},{5,7},{3,5},{1,3},{8,9},{10,8},{12,1... | collective-permute-start | bytes 786440 | tf_op jit(solution)/shard_map/ppermute | solution.py:423
  31.2 9.2 %collective-permute-start.12 = (bf16[64,2048]{1,0:T(8,128)(2,1)S(1)}, bf16[64,2048]{1,0:T(8,128)(2,1)S(1)}, u32[]{:S(2)}, u32[]{:S(2)}) collective-permute-start(bf16[64,2048]{1,0:T(8,128)(2,1)S(1)} %collective-permute-done.6.refs_1_), channel_id=1, source_target_pairs={{0,2},{2,4},{4,6},{6,7},{7,5},{5,3},{3,1},{1,0},{8,10},{10,12},{12... | collective-permute-start | bytes 786440 | tf_op jit(solution)/shard_map/ppermute | solution.py:423
  36.8 9.5 %collective-permute-start.11 = (bf16[64,2048]{1,0:T(8,128)(2,1)S(1)}, bf16[64,2048]{1,0:T(8,128)(2,1)S(1)}, u32[]{:S(2)}, u32[]{:S(2)}) collective-permute-start(bf16[64,2048]{1,0:T(8,128)(2,1)S(1)} %collective-permute-done.10.refs_3_), channel_id=1, source_target_pairs={{0,1},{2,0},{4,2},{6,4},{7,6},{5,7},{3,5},{1,3},{8,9},{10,8},{12,1... | collective-permute-start | bytes 786440 | tf_op jit(solution)/shard_map/ppermute | solution.py:423
  36.8 9.5 %collective-permute-start.9 = (bf16[64,2048]{1,0:T(8,128)(2,1)S(1)}, bf16[64,2048]{1,0:T(8,128)(2,1)S(1)}, u32[]{:S(2)}, u32[]{:S(2)}) collective-permute-start(bf16[64,2048]{1,0:T(8,128)(2,1)S(1)} %collective-permute-done.5.refs_0_), channel_id=1, source_target_pairs={{0,2},{2,4},{4,6},{6,7},{7,5},{5,3},{3,1},{1,0},{8,10},{10,12},{12... | collective-permute-start | bytes 786440 | tf_op jit(solution)/shard_map/ppermute | solution.py:423
  46.6 1.6 %collective-permute-start.16 = (bf16[512,256]{1,0:T(8,128)(2,1)S(1)}, bf16[512,256]{1,0:T(8,128)(2,1)S(1)}, u32[]{:S(2)}, u32[]{:S(2)}) collective-permute-start(bf16[512,256]{1,0:T(8,128)(2,1)S(1)} %get-tuple-element.193), channel_id=1, source_target_pairs={{0,8},{8,0},{16,24},{24,16},{1,9},{9,1},{17,25},{25,17},{2,10},{10... | collective-permute-start | bytes 786440 | tf_op jit(solution)/shard_map/ppermute | solution.py:372
  47.3 2.5 %collective-permute-start.15 = (bf16[512,384]{1,0:T(8,128)(2,1)S(1)}, bf16[512,384]{1,0:T(8,128)(2,1)S(1)}, u32[]{:S(2)}, u32[]{:S(2)}) collective-permute-start(bf16[512,384]{1,0:T(8,128)(2,1)S(1)} %get-tuple-element.191), channel_id=1, source_target_pairs={{0,8},{8,0},{16,24},{24,16},{1,9},{9,1},{17,25},{25,17},{2,10},{10... | collective-permute-start | bytes 1179656 | tf_op jit(solution)/shard_map/ppermute | solution.py:372
  47.9 2.0 %collective-permute-start.14 = (bf16[512,384]{1,0:T(8,128)(2,1)S(1)}, bf16[512,384]{1,0:T(8,128)(2,1)S(1)}, u32[]{:S(2)}, u32[]{:S(2)}) collective-permute-start(bf16[512,384]{1,0:T(8,128)(2,1)S(1)} %get-tuple-element.189), channel_id=1, source_target_pairs={{0,8},{8,0},{16,24},{24,16},{1,9},{9,1},{17,25},{25,17},{2,10},{10... | collective-permute-start | bytes 1179656 | tf_op jit(solution)/shard_map/ppermute | solution.py:372
  48.2 14.7 %collective-permute-start.17 = (bf16[512,256]{1,0:T(8,128)(2,1)S(1)}, bf16[512,256]{1,0:T(8,128)(2,1)S(1)}, u32[]{:S(2)}, u32[]{:S(2)}) collective-permute-start(bf16[512,256]{1,0:T(8,128)(2,1)S(1)} %add_convert_fusion.2), channel_id=1, source_target_pairs={{0,16},{8,24},{16,0},{24,8},{1,17},{9,25},{17,1},{25,9},{2,18},{10... | collective-permute-start | bytes 786440 | tf_op jit(solution)/shard_map/ppermute | solution.py:372
  49.9 15.4 %collective-permute-start.18 = (bf16[512,384]{1,0:T(8,128)(2,1)S(1)}, bf16[512,384]{1,0:T(8,128)(2,1)S(1)}, u32[]{:S(2)}, u32[]{:S(2)}) collective-permute-start(bf16[512,384]{1,0:T(8,128)(2,1)S(1)} %add_convert_fusion.1), channel_id=1, source_target_pairs={{0,16},{8,24},{16,0},{24,8},{1,17},{9,25},{17,1},{25,9},{2,18},{10... | collective-permute-start | bytes 1179656 | tf_op jit(solution)/shard_map/ppermute | solution.py:372
  62.3 11.5 %collective-permute-start.21 = (bf16[512,384]{1,0:T(8,128)(2,1)S(1)}, bf16[512,384]{1,0:T(8,128)(2,1)S(1)}, u32[]{:S(2)}, u32[]{:S(2)}) collective-permute-start(bf16[512,384]{1,0:T(8,128)(2,1)S(1)} %add_convert_fusion), channel_id=1, source_target_pairs={{0,16},{8,24},{16,0},{24,8},{1,17},{9,25},{17,1},{25,9},{2,18},{10... | collective-permute-start | bytes 1179656 | tf_op jit(solution)/shard_map/ppermute | solution.py:372
  65.4 8.5 %collective-permute-start.22 = (bf16[512,384]{1,0:T(8,128)(2,1)S(1)}, bf16[512,384]{1,0:T(8,128)(2,1)S(1)}, u32[]{:S(2)}, u32[]{:S(2)}) collective-permute-start(bf16[512,384]{1,0:T(8,128)(2,1)S(1)} %multiply_convert_fusion.1.refs_1_), channel_id=1, source_target_pairs={{0,8},{8,0},{16,24},{24,16},{1,9},{9,1},{17,25},{25,17},{2,10},{10... | collective-permute-start | bytes 1179656 | tf_op jit(solution)/shard_map/ppermute | solution.py:372
  65.5 1.8 %collective-permute-start.19 = (f32[3,3,2,512]{3,2,1,0:T(2,128)S(1)}, f32[3,3,2,512]{3,2,1,0:T(2,128)S(1)}, u32[]{:S(2)}, u32[]{:S(2)}) collective-permute-start(f32[3,3,2,512]{3,2,1,0:T(2,128)S(1)} %get-tuple-element.224), channel_id=1, source_target_pairs={{0,8},{8,0},{16,24},{24,16},{1,9},{9,1},{17,25},{25,17},{2,10},{10... | collective-permute-start | bytes 110600 | tf_op jit(solution)/shard_map/ppermute | solution.py:372
  66.0 8.0 %collective-permute-start.23 = (bf16[512,256]{1,0:T(8,128)(2,1)S(1)}, bf16[512,256]{1,0:T(8,128)(2,1)S(1)}, u32[]{:S(2)}, u32[]{:S(2)}) collective-permute-start(bf16[512,256]{1,0:T(8,128)(2,1)S(1)} %multiply_convert_fusion.2.refs_0_), channel_id=1, source_target_pairs={{0,8},{8,0},{16,24},{24,16},{1,9},{9,1},{17,25},{25,17},{2,10},{10... | collective-permute-start | bytes 786440 | tf_op jit(solution)/shard_map/ppermute | solution.py:372
  67.3 6.7 %collective-permute-start.20 = (bf16[3,3,2,512]{3,2,1,0:T(2,128)(2,1)S(1)}, bf16[3,3,2,512]{3,2,1,0:T(2,128)(2,1)S(1)}, u32[]{:S(2)}, u32[]{:S(2)}) collective-permute-start(bf16[3,3,2,512]{3,2,1,0:T(2,128)(2,1)S(1)} %add_convert_fusion.3), channel_id=1, source_target_pairs={{0,16},{8,24},{16,0},{24,8},{1,17},{9,25},{17,1},{25,9},{2,18},{10... | collective-permute-start | bytes 55304 | tf_op jit(solution)/shard_map/ppermute | solution.py:372
  74.1 1.8 %collective-permute-start.24 = (bf16[512,384]{1,0:T(8,128)(2,1)S(1)}, bf16[512,384]{1,0:T(8,128)(2,1)S(1)}, u32[]{:S(2)}, u32[]{:S(2)}) collective-permute-start(bf16[512,384]{1,0:T(8,128)(2,1)S(1)} %multiply_convert_fusion.refs_2_), channel_id=1, source_target_pairs={{0,8},{8,0},{16,24},{24,16},{1,9},{9,1},{17,25},{25,17},{2,10},{10... | collective-permute-start | bytes 1179656 | tf_op jit(solution)/shard_map/ppermute | solution.py:372

commit v9 on v8

--- a/solution.py
+++ b/solution.py
@@ -474,13 +474,20 @@
     )
     hidden_grad = order.after(hidden_grad, ())
     finish(1)
+    pair_there = swap(pairs[2], 1)
     received = order.after(received, ())
     terms = order.after((terms + received).astype(BF16), ())
     received = swap(terms, 2)
     received, far_sums[2] = order.after((received, far_sums[2]), ())
     others[0] = order.after(others[0], ())
     others[1] = order.after(others[1], ())
-    finish(2)
+    if dp == 4:
+        arrived = order.after(far_sums[2], ())
+        there = swap(arrived, 1)
+        mines.append((sum_far(pairs[2], arrived) * grad_scale).astype(BF16))
+        pair_there = order.after(pair_there, ())
+    else:
+        finish(2)
     shape = (channels, depth)
     whole, conv_grad = put(
         order.token, mines, others[:2], firsts, shape, terms.astype(F32), received.astype(F32)
@@ -489,7 +496,11 @@
     while bit < dp:
         conv_grad = conv_grad + swap(conv_grad, bit)
         bit *= 2
-    whole, others[2] = order.after((whole, others[2]), ())
+    if dp == 4:
+        whole, there = order.after((whole, there), ())
+        others.append((sum_far(pair_there, there) * grad_scale).astype(BF16))
+    else:
+        whole, others[2] = order.after((whole, others[2]), ())
     column = firsts[2] + (1 - place[1]) * widths[2]
     whole = lax.dynamic_update_slice(whole, others[2], (0, column))
     return (hidden_grad[None], whole, conv_grad)

time: 76.9 us -> 76.8 us (level)
  other arithmetic: 0.67 us -> 1.61 us
  local copies, waits for them, and re-layouts: 8.08 us -> 7.3 us
    dynamic_update_slice x0 -> x1, other arithmetic: none -> 0.87 us  [on_device(): whole = lax.dynamic_update_slice(whole, others[2], (0, column))]
    dynamic_update_slice x1 -> x0, local copies, waits for them, and re-layouts: 0.79 us -> none  [on_device(): whole = lax.dynamic_update_slice(whole, others[2], (0, column))]
    ppermute x11 -> x12, waiting for transfers between devices: 8.5 us -> 7.86 us  [swap(): return lax.ppermute(value, 'dp', [(i, i ^ bit) for i in range(n)])]
    ppermute x11 -> x12, starting transfers between devices: 7.25 us -> 7.63 us  [swap(): return lax.ppermute(value, 'dp', [(i, i ^ bit) for i in range(n)])]
  transfers between devices with their start and end apart: 25 -> 26, of which waited for: 14 -> 14; matrix products, arithmetic and copies ran while one was open for 9% -> 9% of each run, Pallas kernels for 27% -> 27%
where the time goes in v9:
time: 76.8 us; the launch traced here: 76.6 us
  starting transfers between devices  22.9 us (30%)
  waiting for transfers between devices  22.8 us (30%)
  Pallas kernels  21.1 us (27%)
  local copies, waits for them, and re-layouts  7.3 us (10%)
  other arithmetic  1.61 us (2%)
  between operations  0.87 us (1%)
    ppermute x14, starting transfers between devices, on_device(): lax.ppermute(state[way, part], 'tensor', right if way == 'up' else left)  15.3 us
    ppermute x14, waiting for transfers between devices, on_device(): lax.ppermute(state[way, part], 'tensor', right if way == 'up' else left)  14.9 us
    ppermute x12, waiting for transfers between devices, swap(): return lax.ppermute(value, 'dp', [(i, i ^ bit) for i in range(n)])  7.86 us
    ppermute x12, starting transfers between devices, swap(): return lax.ppermute(value, 'dp', [(i, i ^ bit) for i in range(n)])  7.63 us
    pallas_call x1, Pallas kernels, grads(): pl.pallas_call(functools.partial(grads_kernel, scale), in_specs=[VMEM] *...  6.52 us
    pallas_call x2, Pallas kernels, conv_parts(): pl.pallas_call(functools.partial(conv_kernel, first, count), in_specs=[VM...  6.09 us
    pallas_call x3, Pallas kernels, rows_parts(): pl.pallas_call(functools.partial(rows_kernel, n, len(pieces), numbers, be...  5.31 us
    optimization_barrier x1, local copies, waits for them, and re-layouts, after(): lax.optimization_barrier(flat)  3.48 us
  transfers between devices with their start and end apart: 26, of which 14 were waited for; matrix products, arithmetic and copies ran while one was open for 9% of the time, Pallas kernels for 27%

profile of v9, /device:TPU:0, one launch (start us, length us, event | category | flops | bytes accessed | tf_op | source)
XLA Modules:
  0.0 76.6 jit_solution(13992739465469486812)
XLA Ops:
  0.6 1.1 %slice_bitcast_fusion = (bf16[64,2048]{1,0:T(8,128)(2,1)S(1)}, bf16[64,2048]{1,0:T(8,128)(2,1)S(1)}) fusion(bf16[1,1,128,2048]{3,2,1,0:T(8,128)(2,1)} %param.8), kind=kLoop, calls=%fused_computation.10 | loop fusion | bytes 1048576 | tf_op jit(solution)/shard_map/slice | solution.py:410
  1.7 3.1 %collective-permute-start = (bf16[64,2048]{1,0:T(8,128)(2,1)S(1)}, bf16[64,2048]{1,0:T(8,128)(2,1)S(1)}, u32[]{:S(2)}, u32[]{:S(2)}) collective-permute-start(bf16[64,2048]{1,0:T(8,128)(2,1)S(1)} %get-tuple-element.246), channel_id=1, source_target_pairs={{0,2},{2,4},{4,6},{6,7},{7,5},{5,3},{3,1},{1,0},{8,10},{10,12},{12... | collective-permute-start | bytes 786440 | tf_op jit(solution)/shard_map/ppermute | solution.py:423
  4.8 2.0 %collective-permute-start.2 = (bf16[64,2048]{1,0:T(8,128)(2,1)S(1)}, bf16[64,2048]{1,0:T(8,128)(2,1)S(1)}, u32[]{:S(2)}, u32[]{:S(2)}) collective-permute-start(bf16[64,2048]{1,0:T(8,128)(2,1)S(1)} %get-tuple-element.245), channel_id=1, source_target_pairs={{0,2},{2,4},{4,6},{6,7},{7,5},{5,3},{3,1},{1,0},{8,10},{10,12},{12... | collective-permute-start | bytes 786440 | tf_op jit(solution)/shard_map/ppermute | solution.py:423
  7.6 2.0 %copy.21 = bf16[1,8,128,2,512]{4,2,1,3,0:T(8,128)(2,1)S(1)} copy(bf16[1,8,128,2,512]{4,3,2,1,0:T(2,128)(2,1)} %param.5) | data formatting | bytes 4194304 | tf_op args[0]
  9.6 4.5 %shard_map.76 = (bf16[8,128,512]{2,1,0:T(8,128)(2,1)S(1)}, bf16[8,128,512]{2,1,0:T(8,128)(2,1)S(1)}, bf16[512,1024]{1,0:T(8,128)(2,1)S(1)}) custom-call(bf16[2,8,128,512]{3,2,1,0:T(8,128)(2,1)S(1)} %bitcast.16, f32[18,512]{1,0:T(8,128)S(1)} %reshape.24.weight_ref.taps_ref), custom_call_target="tpu_custom_call" | custom-call | flops 1 | bytes 1 | tf_op jit(solution)/shard_map/pallas_call | solution.py:103
  14.2 2.1 %collective-permute-start.1 = (bf16[64,2048]{1,0:T(8,128)(2,1)S(1)}, bf16[64,2048]{1,0:T(8,128)(2,1)S(1)}, u32[]{:S(2)}, u32[]{:S(2)}) collective-permute-start(bf16[64,2048]{1,0:T(8,128)(2,1)S(1)} %collective-permute-done.refs_1_), channel_id=1, source_target_pairs={{0,2},{2,4},{4,6},{6,7},{7,5},{5,3},{3,1},{1,0},{8,10},{10,12},{12... | collective-permute-start | bytes 786440 | tf_op jit(solution)/shard_map/ppermute | solution.py:423
  16.3 1.6 %shard_map.77 = (bf16[8,128,512]{2,1,0:T(8,128)(2,1)S(1)}, bf16[8,128,512]{2,1,0:T(8,128)(2,1)S(1)}, bf16[512,1024]{1,0:T(8,128)(2,1)S(1)}) custom-call(bf16[2,8,128,512]{3,2,1,0:T(8,128)(2,1)S(1)} %bitcast.17, f32[18,512]{1,0:T(8,128)S(1)} %reshape.24.weight_ref.taps_ref, ...), custom_call_target="tpu_custom_call", output_to_operand_aliasing={{0}: (2, {}), {1}: (3, {}), {2}: (4, {})} | custom-call | flops 1 | bytes 1 | tf_op jit(solution)/shard_map/pallas_call | solution.py:103
  17.9 1.1 %collective-permute-done.4.refs_3_ = bf16[64,2048]{1,0:T(8,128)(2,1)S(1)} collective-permute-done((bf16[64,2048]{1,0:T(8,128)(2,1)S(1)}, bf16[64,2048]{1,0:T(8,128)(2,1)S(1)}, u32[]{:S(2)}, u32[]{:S(2)}) %collective-permute-start.4) | collective-permute-done | bytes 262176 | tf_op jit(solution)/shard_map/ppermute | solution.py:423
  18.9 0.9 %collective-permute-start.8 = (bf16[64,2048]{1,0:T(8,128)(2,1)S(1)}, bf16[64,2048]{1,0:T(8,128)(2,1)S(1)}, u32[]{:S(2)}, u32[]{:S(2)}) collective-permute-start(bf16[64,2048]{1,0:T(8,128)(2,1)S(1)} %collective-permute-done.4.refs_3_), channel_id=1, source_target_pairs={{0,1},{2,0},{4,2},{6,4},{7,6},{5,7},{3,5},{1,3},{8,9},{10,8},{12,1... | collective-permute-start | bytes 786440 | tf_op jit(solution)/shard_map/ppermute | solution.py:423
  19.9 1.1 %collective-permute-start.6 = (bf16[64,2048]{1,0:T(8,128)(2,1)S(1)}, bf16[64,2048]{1,0:T(8,128)(2,1)S(1)}, u32[]{:S(2)}, u32[]{:S(2)}) collective-permute-start(bf16[64,2048]{1,0:T(8,128)(2,1)S(1)} %collective-permute-done.2.refs_2_), channel_id=1, source_target_pairs={{0,2},{2,4},{4,6},{6,7},{7,5},{5,3},{3,1},{1,0},{8,10},{10,12},{12... | collective-permute-start | bytes 786440 | tf_op jit(solution)/shard_map/ppermute | solution.py:423
  21.0 2.1 %shard_map.78 = (f32[512,2048]{1,0:T(8,128)S(1)}, f32[1024,512]{1,0:T(8,128)S(1)}) custom-call(bf16[128,2048]{1,0:T(8,128)(2,1)S(1)} %bitcast.19, bf16[64,2048]{1,0:T(8,128)(2,1)S(1)} %collective-permute-done.refs_1_, bf16[64,2048]{1,0:T(8,128)(2,1)S(1)} %collective-permute-done.2.refs_2_, bf16[64,2048]{1,0:T(8,128)(2,1)S(1)} %collective-permute-done.4.refs_3_, ...), custom_call_target="tpu_custom_call" | custom-call | flops 1 | bytes 1 | tf_op jit(solution)/shard_map/pallas_call | solution.py:164
  23.5 2.0 %collective-permute-start.5 = (bf16[64,2048]{1,0:T(8,128)(2,1)S(1)}, bf16[64,2048]{1,0:T(8,128)(2,1)S(1)}, u32[]{:S(2)}, u32[]{:S(2)}) collective-permute-start(bf16[64,2048]{1,0:T(8,128)(2,1)S(1)} %collective-permute-done.1.refs_0_), channel_id=1, source_target_pairs={{0,2},{2,4},{4,6},{6,7},{7,5},{5,3},{3,1},{1,0},{8,10},{10,12},{12... | collective-permute-start | bytes 786440 | tf_op jit(solution)/shard_map/ppermute | solution.py:423
  25.5 3.6 %collective-permute-done.6.refs_1_ = bf16[64,2048]{1,0:T(8,128)(2,1)S(1)} collective-permute-done((bf16[64,2048]{1,0:T(8,128)(2,1)S(1)}, bf16[64,2048]{1,0:T(8,128)(2,1)S(1)}, u32[]{:S(2)}, u32[]{:S(2)}) %collective-permute-start.6) | collective-permute-done | bytes 262176 | tf_op jit(solution)/shard_map/ppermute | solution.py:423
  29.1 2.0 %collective-permute-done.8.refs_2_ = bf16[64,2048]{1,0:T(8,128)(2,1)S(1)} collective-permute-done((bf16[64,2048]{1,0:T(8,128)(2,1)S(1)}, bf16[64,2048]{1,0:T(8,128)(2,1)S(1)}, u32[]{:S(2)}, u32[]{:S(2)}) %collective-permute-start.8) | collective-permute-done | bytes 262176 | tf_op jit(solution)/shard_map/ppermute | solution.py:423
  31.2 2.0 %collective-permute-start.12 = (bf16[64,2048]{1,0:T(8,128)(2,1)S(1)}, bf16[64,2048]{1,0:T(8,128)(2,1)S(1)}, u32[]{:S(2)}, u32[]{:S(2)}) collective-permute-start(bf16[64,2048]{1,0:T(8,128)(2,1)S(1)} %collective-permute-done.6.refs_1_), channel_id=1, source_target_pairs={{0,2},{2,4},{4,6},{6,7},{7,5},{5,3},{3,1},{1,0},{8,10},{10,12},{12... | collective-permute-start | bytes 786440 | tf_op jit(solution)/shard_map/ppermute | solution.py:423
  33.2 1.6 %shard_map.79 = (f32[512,2048]{1,0:T(8,128)S(1)}, f32[1024,512]{1,0:T(8,128)S(1)}) custom-call(bf16[64,2048]{1,0:T(8,128)(2,1)S(1)} %collective-permute-done.1.refs_0_, bf16[64,2048]{1,0:T(8,128)(2,1)S(1)} %collective-permute-done.6.refs_1_, bf16[64,2048]{1,0:T(8,128)(2,1)S(1)} %collective-permute-done.8.refs_2_, ...), custom_call_target="tpu_custom_call", output_to_operand_aliasing={{0}: (7, {}), {1}: (8, {})} | custom-call | flops 1 | bytes 1 | tf_op jit(solution)/shard_map/pallas_call | solution.py:164
  34.8 2.0 %collective-permute-done.10.refs_3_ = bf16[64,2048]{1,0:T(8,128)(2,1)S(1)} collective-permute-done((bf16[64,2048]{1,0:T(8,128)(2,1)S(1)}, bf16[64,2048]{1,0:T(8,128)(2,1)S(1)}, u32[]{:S(2)}, u32[]{:S(2)}) %collective-permute-start.10) | collective-permute-done | bytes 262176 | tf_op jit(solution)/shard_map/ppermute | solution.py:423
  36.8 2.0 %collective-permute-start.9 = (bf16[64,2048]{1,0:T(8,128)(2,1)S(1)}, bf16[64,2048]{1,0:T(8,128)(2,1)S(1)}, u32[]{:S(2)}, u32[]{:S(2)}) collective-permute-start(bf16[64,2048]{1,0:T(8,128)(2,1)S(1)} %collective-permute-done.5.refs_0_), channel_id=1, source_target_pairs={{0,2},{2,4},{4,6},{6,7},{7,5},{5,3},{3,1},{1,0},{8,10},{10,12},{12... | collective-permute-start | bytes 786440 | tf_op jit(solution)/shard_map/ppermute | solution.py:423
  38.8 1.6 %collective-permute-done.12.refs_1_ = bf16[64,2048]{1,0:T(8,128)(2,1)S(1)} collective-permute-done((bf16[64,2048]{1,0:T(8,128)(2,1)S(1)}, bf16[64,2048]{1,0:T(8,128)(2,1)S(1)}, u32[]{:S(2)}, u32[]{:S(2)}) %collective-permute-start.12) | collective-permute-done | bytes 262176 | tf_op jit(solution)/shard_map/ppermute | solution.py:423
  40.4 2.0 %collective-permute-done.13.refs_2_ = bf16[64,2048]{1,0:T(8,128)(2,1)S(1)} collective-permute-done((bf16[64,2048]{1,0:T(8,128)(2,1)S(1)}, bf16[64,2048]{1,0:T(8,128)(2,1)S(1)}, u32[]{:S(2)}, u32[]{:S(2)}) %collective-permute-start.13) | collective-permute-done | bytes 262176 | tf_op jit(solution)/shard_map/ppermute | solution.py:423
  42.4 1.6 %shard_map.80 = (f32[512,2048]{1,0:T(8,128)S(1)}, f32[1024,512]{1,0:T(8,128)S(1)}) custom-call(bf16[64,2048]{1,0:T(8,128)(2,1)S(1)} %collective-permute-done.5.refs_0_, bf16[64,2048]{1,0:T(8,128)(2,1)S(1)} %collective-permute-done.12.refs_1_, bf16[64,2048]{1,0:T(8,128)(2,1)S(1)} %collective-permute-done.13.refs_2_, ...), custom_call_target="tpu_custom_call", output_to_operand_aliasing={{0}: (7, {}), {1}: (8, {})} | custom-call | flops 1 | bytes 1 | tf_op jit(solution)/shard_map/pallas_call | solution.py:164
  44.0 2.3 %collective-permute-done.11.down_ref = bf16[64,2048]{1,0:T(8,128)(2,1)S(1)} collective-permute-done((bf16[64,2048]{1,0:T(8,128)(2,1)S(1)}, bf16[64,2048]{1,0:T(8,128)(2,1)S(1)}, u32[]{:S(2)}, u32[]{:S(2)}) %collective-permute-start.11) | collective-permute-done | bytes 262176 | tf_op jit(solution)/shard_map/ppermute | solution.py:423
  48.2 1.6 %collective-permute-start.17 = (bf16[512,256]{1,0:T(8,128)(2,1)S(1)}, bf16[512,256]{1,0:T(8,128)(2,1)S(1)}, u32[]{:S(2)}, u32[]{:S(2)}) collective-permute-start(bf16[512,256]{1,0:T(8,128)(2,1)S(1)} %add_convert_fusion.2), channel_id=1, source_target_pairs={{0,16},{8,24},{16,0},{24,8},{1,17},{9,25},{17,1},{25,9},{2,18},{10... | collective-permute-start | bytes 786440 | tf_op jit(solution)/shard_map/ppermute | solution.py:372
  50.0 1.4 %collective-permute-start.18 = (bf16[512,384]{1,0:T(8,128)(2,1)S(1)}, bf16[512,384]{1,0:T(8,128)(2,1)S(1)}, u32[]{:S(2)}, u32[]{:S(2)}) collective-permute-start(bf16[512,384]{1,0:T(8,128)(2,1)S(1)} %add_convert_fusion.1), channel_id=1, source_target_pairs={{0,16},{8,24},{16,0},{24,8},{1,17},{9,25},{17,1},{25,9},{2,18},{10... | collective-permute-start | bytes 1179656 | tf_op jit(solution)/shard_map/ppermute | solution.py:372
  51.4 0.8 %shard_map.83.grad_ref = f32[1024,512]{1,0:T(8,128)S(1)} custom-call(bf16[64,2048]{1,0:T(8,128)(2,1)S(1)} %collective-permute-done.9.up_ref, bf16[64,2048]{1,0:T(8,128)(2,1)S(1)} %collective-permute-done.11.down_ref, f32[1,2048]{1,0:T(1,128)S(1)} %copy-done.2, bf16[512,2048]{1,0:T(8,128)(2,1)S(1)} %copy-done, ...), custom_call_target="tpu_custom_call", output_to_operand_aliasing={{}: (4, {})} | custom-call | flops 1 | bytes 1 | tf_op jit(solution)/shard_map/pallas_call | solution.py:244
  52.3 6.5 %shard_map.84 = (bf16[2,8,128,512]{3,2,1,0:T(8,128)(2,1)S(1)}, f32[3,3,2,512]{3,2,1,0:T(2,128)S(1)}) custom-call(f32[1024,512]{1,0:T(8,128)S(1)} %shard_map.83.grad_ref, bf16[8,128,512]{2,1,0:T(8,128)(2,1)S(1)} %get-tuple-element.205.gate_ref, bf16[8,128,512]{2,1,0:T(8,128)(2,1)S(1)} %get-tuple-element.206.value_ref, bf16[2,8,128,512]{3,2,1,0:T(8,128)(2,1)S(1)} %bitcast.18, ...), custom_call_target="tpu_custom_call" | custom-call | flops 1 | bytes 1 | tf_op jit(solution)/shard_map/pallas_call | solution.py:301
  58.8 3.5 %copy.20 = bf16[2,8,128,512]{3,0,2,1:T(2,128)(2,1)} copy(bf16[2,8,128,512]{3,2,1,0:T(8,128)(2,1)S(1)} %get-tuple-element.210) | data formatting | bytes 4194304 | tf_op jit(solution)/shard_map/optimization_barrier | solution.py:366
  63.1 2.2 %collective-permute-done.18 = bf16[512,384]{1,0:T(8,128)(2,1)S(1)} collective-permute-done((bf16[512,384]{1,0:T(8,128)(2,1)S(1)}, bf16[512,384]{1,0:T(8,128)(2,1)S(1)}, u32[]{:S(2)}, u32[]{:S(2)}) %collective-permute-start.18) | collective-permute-done | bytes 393248 | tf_op jit(solution)/shard_map/ppermute | solution.py:372
  67.3 2.2 %collective-permute-start.20 = (bf16[3,3,2,512]{3,2,1,0:T(2,128)(2,1)S(1)}, bf16[3,3,2,512]{3,2,1,0:T(2,128)(2,1)S(1)}, u32[]{:S(2)}, u32[]{:S(2)}) collective-permute-start(bf16[3,3,2,512]{3,2,1,0:T(2,128)(2,1)S(1)} %add_convert_fusion.3), channel_id=1, source_target_pairs={{0,16},{8,24},{16,0},{24,8},{1,17},{9,25},{17,1},{25,9},{2,18},{10... | collective-permute-start | bytes 55304 | tf_op jit(solution)/shard_map/ppermute | solution.py:372
  69.5 4.3 %collective-permute-done.21 = bf16[512,384]{1,0:T(8,128)(2,1)S(1)} collective-permute-done((bf16[512,384]{1,0:T(8,128)(2,1)S(1)}, bf16[512,384]{1,0:T(8,128)(2,1)S(1)}, u32[]{:S(2)}, u32[]{:S(2)}) %collective-permute-start.21) | collective-permute-done | bytes 393248 | tf_op jit(solution)/shard_map/ppermute | solution.py:372
  74.2 1.4 %shard_map.85 = (bf16[512,2048]{1,0:T(8,128)(2,1)}, f32[3,3,2,512]{3,2,1,0:T(2,128)}) custom-call(bf16[512,256]{1,0:T(8,128)(2,1)S(1)} %multiply_convert_fusion.3.refs_0_, bf16[512,384]{1,0:T(8,128)(2,1)S(1)} %multiply_convert_fusion.2.refs_1_, bf16[512,384]{1,0:T(8,128)(2,1)S(1)} %multiply_convert_fusion.1.refs_2_, ...), custom_call_target="tpu_custom_call" | custom-call | flops 1 | bytes 1 | tf_op jit(solution)/shard_map/pallas_call | solution.py:345
  75.7 0.9 %fusion = bf16[512,2048]{1,0:T(8,128)(2,1)} fusion(bf16[512,2048]{1,0:T(8,128)(2,1)} %get-tuple-element.241, s32[]{:T(128)S(6)} %select_n.3, bf16[512,384]{1,0:T(8,128)(2,1)S(1)} %collective-permute-done.25, bf16[512,384]{1,0:T(8,128)(2,1)S(1)} %collective-permute-done.24), kind=kLoop, calls=%fused_computation.9 | loop fusion | flops 983040 | bytes 1179652 | tf_op jit(solution)/shard_map/dynamic_update_slice | solution.py:505
  (51 shorter events, 6.8 us)
Async XLA Ops:
  1.7 12.5 %collective-permute-start = (bf16[64,2048]{1,0:T(8,128)(2,1)S(1)}, bf16[64,2048]{1,0:T(8,128)(2,1)S(1)}, u32[]{:S(2)}, u32[]{:S(2)}) collective-permute-start(bf16[64,2048]{1,0:T(8,128)(2,1)S(1)} %get-tuple-element.246), channel_id=1, source_target_pairs={{0,2},{2,4},{4,6},{6,7},{7,5},{5,3},{3,1},{1,0},{8,10},{10,12},{12... | collective-permute-start | bytes 786440 | tf_op jit(solution)/shard_map/ppermute | solution.py:423
  4.8 11.5 %collective-permute-start.3 = (bf16[64,2048]{1,0:T(8,128)(2,1)S(1)}, bf16[64,2048]{1,0:T(8,128)(2,1)S(1)}, u32[]{:S(2)}, u32[]{:S(2)}) collective-permute-start(bf16[64,2048]{1,0:T(8,128)(2,1)S(1)} %get-tuple-element.245), channel_id=1, source_target_pairs={{0,1},{2,0},{4,2},{6,4},{7,6},{5,7},{3,5},{1,3},{8,9},{10,8},{12,1... | collective-permute-start | bytes 786440 | tf_op jit(solution)/shard_map/ppermute | solution.py:423
  4.8 13.1 %collective-permute-start.2 = (bf16[64,2048]{1,0:T(8,128)(2,1)S(1)}, bf16[64,2048]{1,0:T(8,128)(2,1)S(1)}, u32[]{:S(2)}, u32[]{:S(2)}) collective-permute-start(bf16[64,2048]{1,0:T(8,128)(2,1)S(1)} %get-tuple-element.245), channel_id=1, source_target_pairs={{0,2},{2,4},{4,6},{6,7},{7,5},{5,3},{3,1},{1,0},{8,10},{10,12},{12... | collective-permute-start | bytes 786440 | tf_op jit(solution)/shard_map/ppermute | solution.py:423
  6.8 12.1 %collective-permute-start.4 = (bf16[64,2048]{1,0:T(8,128)(2,1)S(1)}, bf16[64,2048]{1,0:T(8,128)(2,1)S(1)}, u32[]{:S(2)}, u32[]{:S(2)}) collective-permute-start(bf16[64,2048]{1,0:T(8,128)(2,1)S(1)} %get-tuple-element.246), channel_id=1, source_target_pairs={{0,1},{2,0},{4,2},{6,4},{7,6},{5,7},{3,5},{1,3},{8,9},{10,8},{12,1... | collective-permute-start | bytes 786440 | tf_op jit(solution)/shard_map/ppermute | solution.py:423
  14.2 6.8 %copy-start = (bf16[512,2048]{1,0:T(8,128)(2,1)S(1)}, bf16[512,2048]{1,0:T(8,128)(2,1)}, u32[]{:S(2)}) copy-start(bf16[512,2048]{1,0:T(8,128)(2,1)} %weight_ref.1) | copy-start | bytes 6291460
  14.2 6.8 %copy-start.1 = (bf16[1,1,128,2048]{3,2,1,0:T(8,128)(2,1)S(1)}, bf16[1,1,128,2048]{3,2,1,0:T(8,128)(2,1)}, u32[]{:S(2)}) copy-start(bf16[1,1,128,2048]{3,2,1,0:T(8,128)(2,1)} %param.8) | copy-start | bytes 1572868
  14.2 6.8 %copy-start.2 = (f32[1,2048]{1,0:T(1,128)S(1)}, f32[1,2048]{1,0:T(1,128)}, u32[]{:S(2)}) copy-start(f32[1,2048]{1,0:T(1,128)} %gate_ref.5) | copy-start | bytes 24580
  14.2 9.3 %collective-permute-start.1 = (bf16[64,2048]{1,0:T(8,128)(2,1)S(1)}, bf16[64,2048]{1,0:T(8,128)(2,1)S(1)}, u32[]{:S(2)}, u32[]{:S(2)}) collective-permute-start(bf16[64,2048]{1,0:T(8,128)(2,1)S(1)} %collective-permute-done.refs_1_), channel_id=1, source_target_pairs={{0,2},{2,4},{4,6},{6,7},{7,5},{5,3},{3,1},{1,0},{8,10},{10,12},{12... | collective-permute-start | bytes 786440 | tf_op jit(solution)/shard_map/ppermute | solution.py:423
  16.3 9.2 %collective-permute-start.7 = (bf16[64,2048]{1,0:T(8,128)(2,1)S(1)}, bf16[64,2048]{1,0:T(8,128)(2,1)S(1)}, u32[]{:S(2)}, u32[]{:S(2)}) collective-permute-start(bf16[64,2048]{1,0:T(8,128)(2,1)S(1)} %collective-permute-done.3.refs_4_), channel_id=1, source_target_pairs={{0,1},{2,0},{4,2},{6,4},{7,6},{5,7},{3,5},{1,3},{8,9},{10,8},{12,1... | collective-permute-start | bytes 786440 | tf_op jit(solution)/shard_map/ppermute | solution.py:423
  18.9 12.2 %collective-permute-start.8 = (bf16[64,2048]{1,0:T(8,128)(2,1)S(1)}, bf16[64,2048]{1,0:T(8,128)(2,1)S(1)}, u32[]{:S(2)}, u32[]{:S(2)}) collective-permute-start(bf16[64,2048]{1,0:T(8,128)(2,1)S(1)} %collective-permute-done.4.refs_3_), channel_id=1, source_target_pairs={{0,1},{2,0},{4,2},{6,4},{7,6},{5,7},{3,5},{1,3},{8,9},{10,8},{12,1... | collective-permute-start | bytes 786440 | tf_op jit(solution)/shard_map/ppermute | solution.py:423
  19.9 9.2 %collective-permute-start.6 = (bf16[64,2048]{1,0:T(8,128)(2,1)S(1)}, bf16[64,2048]{1,0:T(8,128)(2,1)S(1)}, u32[]{:S(2)}, u32[]{:S(2)}) collective-permute-start(bf16[64,2048]{1,0:T(8,128)(2,1)S(1)} %collective-permute-done.2.refs_2_), channel_id=1, source_target_pairs={{0,2},{2,4},{4,6},{6,7},{7,5},{5,3},{3,1},{1,0},{8,10},{10,12},{12... | collective-permute-start | bytes 786440 | tf_op jit(solution)/shard_map/ppermute | solution.py:423
  23.5 11.3 %collective-permute-start.5 = (bf16[64,2048]{1,0:T(8,128)(2,1)S(1)}, bf16[64,2048]{1,0:T(8,128)(2,1)S(1)}, u32[]{:S(2)}, u32[]{:S(2)}) collective-permute-start(bf16[64,2048]{1,0:T(8,128)(2,1)S(1)} %collective-permute-done.1.refs_0_), channel_id=1, source_target_pairs={{0,2},{2,4},{4,6},{6,7},{7,5},{5,3},{3,1},{1,0},{8,10},{10,12},{12... | collective-permute-start | bytes 786440 | tf_op jit(solution)/shard_map/ppermute | solution.py:423
  25.5 11.2 %collective-permute-start.10 = (bf16[64,2048]{1,0:T(8,128)(2,1)S(1)}, bf16[64,2048]{1,0:T(8,128)(2,1)S(1)}, u32[]{:S(2)}, u32[]{:S(2)}) collective-permute-start(bf16[64,2048]{1,0:T(8,128)(2,1)S(1)} %collective-permute-done.7.refs_3_), channel_id=1, source_target_pairs={{0,1},{2,0},{4,2},{6,4},{7,6},{5,7},{3,5},{1,3},{8,9},{10,8},{12,1... | collective-permute-start | bytes 786440 | tf_op jit(solution)/shard_map/ppermute | solution.py:423
  31.1 11.2 %collective-permute-start.13 = (bf16[64,2048]{1,0:T(8,128)(2,1)S(1)}, bf16[64,2048]{1,0:T(8,128)(2,1)S(1)}, u32[]{:S(2)}, u32[]{:S(2)}) collective-permute-start(bf16[64,2048]{1,0:T(8,128)(2,1)S(1)} %collective-permute-done.8.refs_2_), channel_id=1, source_target_pairs={{0,1},{2,0},{4,2},{6,4},{7,6},{5,7},{3,5},{1,3},{8,9},{10,8},{12,1... | collective-permute-start | bytes 786440 | tf_op jit(solution)/shard_map/ppermute | solution.py:423
  31.2 9.2 %collective-permute-start.12 = (bf16[64,2048]{1,0:T(8,128)(2,1)S(1)}, bf16[64,2048]{1,0:T(8,128)(2,1)S(1)}, u32[]{:S(2)}, u32[]{:S(2)}) collective-permute-start(bf16[64,2048]{1,0:T(8,128)(2,1)S(1)} %collective-permute-done.6.refs_1_), channel_id=1, source_target_pairs={{0,2},{2,4},{4,6},{6,7},{7,5},{5,3},{3,1},{1,0},{8,10},{10,12},{12... | collective-permute-start | bytes 786440 | tf_op jit(solution)/shard_map/ppermute | solution.py:423
  36.8 9.5 %collective-permute-start.11 = (bf16[64,2048]{1,0:T(8,128)(2,1)S(1)}, bf16[64,2048]{1,0:T(8,128)(2,1)S(1)}, u32[]{:S(2)}, u32[]{:S(2)}) collective-permute-start(bf16[64,2048]{1,0:T(8,128)(2,1)S(1)} %collective-permute-done.10.refs_3_), channel_id=1, source_target_pairs={{0,1},{2,0},{4,2},{6,4},{7,6},{5,7},{3,5},{1,3},{8,9},{10,8},{12,1... | collective-permute-start | bytes 786440 | tf_op jit(solution)/shard_map/ppermute | solution.py:423
  36.8 9.5 %collective-permute-start.9 = (bf16[64,2048]{1,0:T(8,128)(2,1)S(1)}, bf16[64,2048]{1,0:T(8,128)(2,1)S(1)}, u32[]{:S(2)}, u32[]{:S(2)}) collective-permute-start(bf16[64,2048]{1,0:T(8,128)(2,1)S(1)} %collective-permute-done.5.refs_0_), channel_id=1, source_target_pairs={{0,2},{2,4},{4,6},{6,7},{7,5},{5,3},{3,1},{1,0},{8,10},{10,12},{12... | collective-permute-start | bytes 786440 | tf_op jit(solution)/shard_map/ppermute | solution.py:423
  46.6 1.6 %collective-permute-start.16 = (bf16[512,256]{1,0:T(8,128)(2,1)S(1)}, bf16[512,256]{1,0:T(8,128)(2,1)S(1)}, u32[]{:S(2)}, u32[]{:S(2)}) collective-permute-start(bf16[512,256]{1,0:T(8,128)(2,1)S(1)} %get-tuple-element.193), channel_id=1, source_target_pairs={{0,8},{8,0},{16,24},{24,16},{1,9},{9,1},{17,25},{25,17},{2,10},{10... | collective-permute-start | bytes 786440 | tf_op jit(solution)/shard_map/ppermute | solution.py:372
  47.3 2.5 %collective-permute-start.15 = (bf16[512,384]{1,0:T(8,128)(2,1)S(1)}, bf16[512,384]{1,0:T(8,128)(2,1)S(1)}, u32[]{:S(2)}, u32[]{:S(2)}) collective-permute-start(bf16[512,384]{1,0:T(8,128)(2,1)S(1)} %get-tuple-element.191), channel_id=1, source_target_pairs={{0,8},{8,0},{16,24},{24,16},{1,9},{9,1},{17,25},{25,17},{2,10},{10... | collective-permute-start | bytes 1179656 | tf_op jit(solution)/shard_map/ppermute | solution.py:372
  47.9 2.1 %collective-permute-start.14 = (bf16[512,384]{1,0:T(8,128)(2,1)S(1)}, bf16[512,384]{1,0:T(8,128)(2,1)S(1)}, u32[]{:S(2)}, u32[]{:S(2)}) collective-permute-start(bf16[512,384]{1,0:T(8,128)(2,1)S(1)} %get-tuple-element.189), channel_id=1, source_target_pairs={{0,8},{8,0},{16,24},{24,16},{1,9},{9,1},{17,25},{25,17},{2,10},{10... | collective-permute-start | bytes 1179656 | tf_op jit(solution)/shard_map/ppermute | solution.py:372
  48.2 14.8 %collective-permute-start.17 = (bf16[512,256]{1,0:T(8,128)(2,1)S(1)}, bf16[512,256]{1,0:T(8,128)(2,1)S(1)}, u32[]{:S(2)}, u32[]{:S(2)}) collective-permute-start(bf16[512,256]{1,0:T(8,128)(2,1)S(1)} %add_convert_fusion.2), channel_id=1, source_target_pairs={{0,16},{8,24},{16,0},{24,8},{1,17},{9,25},{17,1},{25,9},{2,18},{10... | collective-permute-start | bytes 786440 | tf_op jit(solution)/shard_map/ppermute | solution.py:372
  50.0 15.3 %collective-permute-start.18 = (bf16[512,384]{1,0:T(8,128)(2,1)S(1)}, bf16[512,384]{1,0:T(8,128)(2,1)S(1)}, u32[]{:S(2)}, u32[]{:S(2)}) collective-permute-start(bf16[512,384]{1,0:T(8,128)(2,1)S(1)} %add_convert_fusion.1), channel_id=1, source_target_pairs={{0,16},{8,24},{16,0},{24,8},{1,17},{9,25},{17,1},{25,9},{2,18},{10... | collective-permute-start | bytes 1179656 | tf_op jit(solution)/shard_map/ppermute | solution.py:372
  62.3 11.5 %collective-permute-start.21 = (bf16[512,384]{1,0:T(8,128)(2,1)S(1)}, bf16[512,384]{1,0:T(8,128)(2,1)S(1)}, u32[]{:S(2)}, u32[]{:S(2)}) collective-permute-start(bf16[512,384]{1,0:T(8,128)(2,1)S(1)} %add_convert_fusion), channel_id=1, source_target_pairs={{0,16},{8,24},{16,0},{24,8},{1,17},{9,25},{17,1},{25,9},{2,18},{10... | collective-permute-start | bytes 1179656 | tf_op jit(solution)/shard_map/ppermute | solution.py:372
  65.4 8.6 %collective-permute-start.22 = (bf16[512,384]{1,0:T(8,128)(2,1)S(1)}, bf16[512,384]{1,0:T(8,128)(2,1)S(1)}, u32[]{:S(2)}, u32[]{:S(2)}) collective-permute-start(bf16[512,384]{1,0:T(8,128)(2,1)S(1)} %multiply_convert_fusion.2.refs_1_), channel_id=1, source_target_pairs={{0,8},{8,0},{16,24},{24,16},{1,9},{9,1},{17,25},{25,17},{2,10},{10... | collective-permute-start | bytes 1179656 | tf_op jit(solution)/shard_map/ppermute | solution.py:372
  65.5 1.8 %collective-permute-start.19 = (f32[3,3,2,512]{3,2,1,0:T(2,128)S(1)}, f32[3,3,2,512]{3,2,1,0:T(2,128)S(1)}, u32[]{:S(2)}, u32[]{:S(2)}) collective-permute-start(f32[3,3,2,512]{3,2,1,0:T(2,128)S(1)} %get-tuple-element.224), channel_id=1, source_target_pairs={{0,8},{8,0},{16,24},{24,16},{1,9},{9,1},{17,25},{25,17},{2,10},{10... | collective-permute-start | bytes 110600 | tf_op jit(solution)/shard_map/ppermute | solution.py:372
  66.0 8.0 %collective-permute-start.23 = (bf16[512,256]{1,0:T(8,128)(2,1)S(1)}, bf16[512,256]{1,0:T(8,128)(2,1)S(1)}, u32[]{:S(2)}, u32[]{:S(2)}) collective-permute-start(bf16[512,256]{1,0:T(8,128)(2,1)S(1)} %multiply_convert_fusion.3.refs_0_), channel_id=1, source_target_pairs={{0,8},{8,0},{16,24},{24,16},{1,9},{9,1},{17,25},{25,17},{2,10},{10... | collective-permute-start | bytes 786440 | tf_op jit(solution)/shard_map/ppermute | solution.py:372
  66.1 8.0 %collective-permute-start.24 = (bf16[512,384]{1,0:T(8,128)(2,1)S(1)}, bf16[512,384]{1,0:T(8,128)(2,1)S(1)}, u32[]{:S(2)}, u32[]{:S(2)}) collective-permute-start(bf16[512,384]{1,0:T(8,128)(2,1)S(1)} %add_convert_fusion), channel_id=1, source_target_pairs={{0,8},{8,0},{16,24},{24,16},{1,9},{9,1},{17,25},{25,17},{2,10},{10... | collective-permute-start | bytes 1179656 | tf_op jit(solution)/shard_map/ppermute | solution.py:372
  67.3 6.7 %collective-permute-start.20 = (bf16[3,3,2,512]{3,2,1,0:T(2,128)(2,1)S(1)}, bf16[3,3,2,512]{3,2,1,0:T(2,128)(2,1)S(1)}, u32[]{:S(2)}, u32[]{:S(2)}) collective-permute-start(bf16[3,3,2,512]{3,2,1,0:T(2,128)(2,1)S(1)} %add_convert_fusion.3), channel_id=1, source_target_pairs={{0,16},{8,24},{16,0},{24,8},{1,17},{9,25},{17,1},{25,9},{2,18},{10... | collective-permute-start | bytes 55304 | tf_op jit(solution)/shard_map/ppermute | solution.py:372
  74.0 1.7 %collective-permute-start.25 = (bf16[512,384]{1,0:T(8,128)(2,1)S(1)}, bf16[512,384]{1,0:T(8,128)(2,1)S(1)}, u32[]{:S(2)}, u32[]{:S(2)}) collective-permute-start(bf16[512,384]{1,0:T(8,128)(2,1)S(1)} %collective-permute-done.21), channel_id=1, source_target_pairs={{0,8},{8,0},{16,24},{24,16},{1,9},{9,1},{17,25},{25,17},{2,10},{10... | collective-permute-start | bytes 1179656 | tf_op jit(solution)/shard_map/ppermute | solution.py:372

commit v10 on v8

--- a/solution.py
+++ b/solution.py
@@ -410,7 +410,7 @@
     state = {("up", 0): own[:half], ("down", 1): own[half:], ("up", 1): own[half:], ("down", 0): own[:half]}
     pieces, numbers, before = [own], [0], None
     blocks = channels // LANES
-    early = blocks - blocks // 4
+    early = blocks - blocks // 2
     for stage in range(1, last + 1):
         arrived = {}
         for way, part in state:

time: 76.9 us -> 76.9 us (level)
  no operation moved by 1% of the time
where the time goes in v10:
time: 76.9 us; the launch traced here: 76.7 us
  waiting for transfers between devices  23.4 us (30%)
  starting transfers between devices  22.6 us (29%)
  Pallas kernels  21.1 us (27%)
  local copies, waits for them, and re-layouts  8.08 us (11%)
  between operations  0.86 us (1%)
    ppermute x14, starting transfers between devices, on_device(): lax.ppermute(state[way, part], 'tensor', right if way == 'up' else left)  15.3 us
    ppermute x14, waiting for transfers between devices, on_device(): lax.ppermute(state[way, part], 'tensor', right if way == 'up' else left)  14.9 us
    ppermute x11, waiting for transfers between devices, swap(): return lax.ppermute(value, 'dp', [(i, i ^ bit) for i in range(n)])  8.5 us
    ppermute x11, starting transfers between devices, swap(): return lax.ppermute(value, 'dp', [(i, i ^ bit) for i in range(n)])  7.25 us
    pallas_call x1, Pallas kernels, grads(): pl.pallas_call(functools.partial(grads_kernel, scale), in_specs=[VMEM] *...  6.54 us
    pallas_call x2, Pallas kernels, conv_parts(): pl.pallas_call(functools.partial(conv_kernel, first, count), in_specs=[VM...  6.12 us
    pallas_call x3, Pallas kernels, rows_parts(): pl.pallas_call(functools.partial(rows_kernel, n, len(pieces), numbers, be...  5.3 us
    optimization_barrier x1, local copies, waits for them, and re-layouts, after(): lax.optimization_barrier(flat)  3.48 us
  transfers between devices with their start and end apart: 25, of which 14 were waited for; matrix products, arithmetic and copies ran while one was open for 9% of the time, Pallas kernels for 27%

profile of v10, /device:TPU:0, one launch (start us, length us, event | category | flops | bytes accessed | tf_op | source)
XLA Modules:
  0.0 76.7 jit_solution(16450837482321769629)
XLA Ops:
  0.6 1.1 %slice_bitcast_fusion = (bf16[64,2048]{1,0:T(8,128)(2,1)S(1)}, bf16[64,2048]{1,0:T(8,128)(2,1)S(1)}) fusion(bf16[1,1,128,2048]{3,2,1,0:T(8,128)(2,1)} %param.8), kind=kLoop, calls=%fused_computation.8 | loop fusion | bytes 1048576 | tf_op jit(solution)/shard_map/slice | solution.py:410
  1.7 3.1 %collective-permute-start = (bf16[64,2048]{1,0:T(8,128)(2,1)S(1)}, bf16[64,2048]{1,0:T(8,128)(2,1)S(1)}, u32[]{:S(2)}, u32[]{:S(2)}) collective-permute-start(bf16[64,2048]{1,0:T(8,128)(2,1)S(1)} %get-tuple-element.246), channel_id=1, source_target_pairs={{0,2},{2,4},{4,6},{6,7},{7,5},{5,3},{3,1},{1,0},{8,10},{10,12},{12... | collective-permute-start | bytes 786440 | tf_op jit(solution)/shard_map/ppermute | solution.py:423
  4.8 2.0 %collective-permute-start.2 = (bf16[64,2048]{1,0:T(8,128)(2,1)S(1)}, bf16[64,2048]{1,0:T(8,128)(2,1)S(1)}, u32[]{:S(2)}, u32[]{:S(2)}) collective-permute-start(bf16[64,2048]{1,0:T(8,128)(2,1)S(1)} %get-tuple-element.245), channel_id=1, source_target_pairs={{0,2},{2,4},{4,6},{6,7},{7,5},{5,3},{3,1},{1,0},{8,10},{10,12},{12... | collective-permute-start | bytes 786440 | tf_op jit(solution)/shard_map/ppermute | solution.py:423
  7.6 2.0 %copy.21 = bf16[1,8,128,2,512]{4,2,1,3,0:T(8,128)(2,1)S(1)} copy(bf16[1,8,128,2,512]{4,3,2,1,0:T(2,128)(2,1)} %param.5) | data formatting | bytes 4194304 | tf_op args[0]
  9.6 3.1 %shard_map.76 = (bf16[8,128,512]{2,1,0:T(8,128)(2,1)S(1)}, bf16[8,128,512]{2,1,0:T(8,128)(2,1)S(1)}, bf16[512,1024]{1,0:T(8,128)(2,1)S(1)}) custom-call(bf16[2,8,128,512]{3,2,1,0:T(8,128)(2,1)S(1)} %bitcast.16, f32[18,512]{1,0:T(8,128)S(1)} %reshape.24.weight_ref.taps_ref), custom_call_target="tpu_custom_call" | custom-call | flops 1 | bytes 1 | tf_op jit(solution)/shard_map/pallas_call | solution.py:103
  12.7 2.1 %collective-permute-start.1 = (bf16[64,2048]{1,0:T(8,128)(2,1)S(1)}, bf16[64,2048]{1,0:T(8,128)(2,1)S(1)}, u32[]{:S(2)}, u32[]{:S(2)}) collective-permute-start(bf16[64,2048]{1,0:T(8,128)(2,1)S(1)} %collective-permute-done.refs_1_), channel_id=1, source_target_pairs={{0,2},{2,4},{4,6},{6,7},{7,5},{5,3},{3,1},{1,0},{8,10},{10,12},{12... | collective-permute-start | bytes 786440 | tf_op jit(solution)/shard_map/ppermute | solution.py:423
  14.8 3.1 %shard_map.77 = (bf16[8,128,512]{2,1,0:T(8,128)(2,1)S(1)}, bf16[8,128,512]{2,1,0:T(8,128)(2,1)S(1)}, bf16[512,1024]{1,0:T(8,128)(2,1)S(1)}) custom-call(bf16[2,8,128,512]{3,2,1,0:T(8,128)(2,1)S(1)} %bitcast.17, f32[18,512]{1,0:T(8,128)S(1)} %reshape.24.weight_ref.taps_ref, ...), custom_call_target="tpu_custom_call", output_to_operand_aliasing={{0}: (2, {}), {1}: (3, {}), {2}: (4, {})} | custom-call | flops 1 | bytes 1 | tf_op jit(solution)/shard_map/pallas_call | solution.py:103
  17.9 1.7 %collective-permute-done.4.refs_3_ = bf16[64,2048]{1,0:T(8,128)(2,1)S(1)} collective-permute-done((bf16[64,2048]{1,0:T(8,128)(2,1)S(1)}, bf16[64,2048]{1,0:T(8,128)(2,1)S(1)}, u32[]{:S(2)}, u32[]{:S(2)}) %collective-permute-start.4) | collective-permute-done | bytes 262176 | tf_op jit(solution)/shard_map/ppermute | solution.py:423
  19.9 1.8 %collective-permute-start.6 = (bf16[64,2048]{1,0:T(8,128)(2,1)S(1)}, bf16[64,2048]{1,0:T(8,128)(2,1)S(1)}, u32[]{:S(2)}, u32[]{:S(2)}) collective-permute-start(bf16[64,2048]{1,0:T(8,128)(2,1)S(1)} %collective-permute-done.2.refs_2_), channel_id=1, source_target_pairs={{0,2},{2,4},{4,6},{6,7},{7,5},{5,3},{3,1},{1,0},{8,10},{10,12},{12... | collective-permute-start | bytes 786440 | tf_op jit(solution)/shard_map/ppermute | solution.py:423
  21.7 2.1 %shard_map.78 = (f32[512,2048]{1,0:T(8,128)S(1)}, f32[1024,512]{1,0:T(8,128)S(1)}) custom-call(bf16[128,2048]{1,0:T(8,128)(2,1)S(1)} %bitcast.19, bf16[64,2048]{1,0:T(8,128)(2,1)S(1)} %collective-permute-done.refs_1_, bf16[64,2048]{1,0:T(8,128)(2,1)S(1)} %collective-permute-done.2.refs_2_, bf16[64,2048]{1,0:T(8,128)(2,1)S(1)} %collective-permute-done.4.refs_3_, ...), custom_call_target="tpu_custom_call" | custom-call | flops 1 | bytes 1 | tf_op jit(solution)/shard_map/pallas_call | solution.py:164
  23.8 1.6 %collective-permute-start.5 = (bf16[64,2048]{1,0:T(8,128)(2,1)S(1)}, bf16[64,2048]{1,0:T(8,128)(2,1)S(1)}, u32[]{:S(2)}, u32[]{:S(2)}) collective-permute-start(bf16[64,2048]{1,0:T(8,128)(2,1)S(1)} %collective-permute-done.1.refs_0_), channel_id=1, source_target_pairs={{0,2},{2,4},{4,6},{6,7},{7,5},{5,3},{3,1},{1,0},{8,10},{10,12},{12... | collective-permute-start | bytes 786440 | tf_op jit(solution)/shard_map/ppermute | solution.py:423
  25.9 3.3 %collective-permute-done.6.refs_1_ = bf16[64,2048]{1,0:T(8,128)(2,1)S(1)} collective-permute-done((bf16[64,2048]{1,0:T(8,128)(2,1)S(1)}, bf16[64,2048]{1,0:T(8,128)(2,1)S(1)}, u32[]{:S(2)}, u32[]{:S(2)}) %collective-permute-start.6) | collective-permute-done | bytes 262176 | tf_op jit(solution)/shard_map/ppermute | solution.py:423
  29.1 1.7 %collective-permute-done.8.refs_2_ = bf16[64,2048]{1,0:T(8,128)(2,1)S(1)} collective-permute-done((bf16[64,2048]{1,0:T(8,128)(2,1)S(1)}, bf16[64,2048]{1,0:T(8,128)(2,1)S(1)}, u32[]{:S(2)}, u32[]{:S(2)}) %collective-permute-start.8) | collective-permute-done | bytes 262176 | tf_op jit(solution)/shard_map/ppermute | solution.py:423
  30.9 2.0 %collective-permute-start.12 = (bf16[64,2048]{1,0:T(8,128)(2,1)S(1)}, bf16[64,2048]{1,0:T(8,128)(2,1)S(1)}, u32[]{:S(2)}, u32[]{:S(2)}) collective-permute-start(bf16[64,2048]{1,0:T(8,128)(2,1)S(1)} %collective-permute-done.6.refs_1_), channel_id=1, source_target_pairs={{0,2},{2,4},{4,6},{6,7},{7,5},{5,3},{3,1},{1,0},{8,10},{10,12},{12... | collective-permute-start | bytes 786440 | tf_op jit(solution)/shard_map/ppermute | solution.py:423
  32.9 1.6 %shard_map.79 = (f32[512,2048]{1,0:T(8,128)S(1)}, f32[1024,512]{1,0:T(8,128)S(1)}) custom-call(bf16[64,2048]{1,0:T(8,128)(2,1)S(1)} %collective-permute-done.1.refs_0_, bf16[64,2048]{1,0:T(8,128)(2,1)S(1)} %collective-permute-done.6.refs_1_, bf16[64,2048]{1,0:T(8,128)(2,1)S(1)} %collective-permute-done.8.refs_2_, ...), custom_call_target="tpu_custom_call", output_to_operand_aliasing={{0}: (7, {}), {1}: (8, {})} | custom-call | flops 1 | bytes 1 | tf_op jit(solution)/shard_map/pallas_call | solution.py:164
  34.8 1.7 %collective-permute-done.10.refs_3_ = bf16[64,2048]{1,0:T(8,128)(2,1)S(1)} collective-permute-done((bf16[64,2048]{1,0:T(8,128)(2,1)S(1)}, bf16[64,2048]{1,0:T(8,128)(2,1)S(1)}, u32[]{:S(2)}, u32[]{:S(2)}) %collective-permute-start.10) | collective-permute-done | bytes 262176 | tf_op jit(solution)/shard_map/ppermute | solution.py:423
  36.5 2.0 %collective-permute-start.9 = (bf16[64,2048]{1,0:T(8,128)(2,1)S(1)}, bf16[64,2048]{1,0:T(8,128)(2,1)S(1)}, u32[]{:S(2)}, u32[]{:S(2)}) collective-permute-start(bf16[64,2048]{1,0:T(8,128)(2,1)S(1)} %collective-permute-done.5.refs_0_), channel_id=1, source_target_pairs={{0,2},{2,4},{4,6},{6,7},{7,5},{5,3},{3,1},{1,0},{8,10},{10,12},{12... | collective-permute-start | bytes 786440 | tf_op jit(solution)/shard_map/ppermute | solution.py:423
  38.5 1.9 %collective-permute-done.12.refs_1_ = bf16[64,2048]{1,0:T(8,128)(2,1)S(1)} collective-permute-done((bf16[64,2048]{1,0:T(8,128)(2,1)S(1)}, bf16[64,2048]{1,0:T(8,128)(2,1)S(1)}, u32[]{:S(2)}, u32[]{:S(2)}) %collective-permute-start.12) | collective-permute-done | bytes 262176 | tf_op jit(solution)/shard_map/ppermute | solution.py:423
  40.4 1.7 %collective-permute-done.13.refs_2_ = bf16[64,2048]{1,0:T(8,128)(2,1)S(1)} collective-permute-done((bf16[64,2048]{1,0:T(8,128)(2,1)S(1)}, bf16[64,2048]{1,0:T(8,128)(2,1)S(1)}, u32[]{:S(2)}, u32[]{:S(2)}) %collective-permute-start.13) | collective-permute-done | bytes 262176 | tf_op jit(solution)/shard_map/ppermute | solution.py:423
  42.1 1.6 %shard_map.80 = (f32[512,2048]{1,0:T(8,128)S(1)}, f32[1024,512]{1,0:T(8,128)S(1)}) custom-call(bf16[64,2048]{1,0:T(8,128)(2,1)S(1)} %collective-permute-done.5.refs_0_, bf16[64,2048]{1,0:T(8,128)(2,1)S(1)} %collective-permute-done.12.refs_1_, bf16[64,2048]{1,0:T(8,128)(2,1)S(1)} %collective-permute-done.13.refs_2_, ...), custom_call_target="tpu_custom_call", output_to_operand_aliasing={{0}: (7, {}), {1}: (8, {})} | custom-call | flops 1 | bytes 1 | tf_op jit(solution)/shard_map/pallas_call | solution.py:164
  43.7 2.6 %collective-permute-done.11.down_ref = bf16[64,2048]{1,0:T(8,128)(2,1)S(1)} collective-permute-done((bf16[64,2048]{1,0:T(8,128)(2,1)S(1)}, bf16[64,2048]{1,0:T(8,128)(2,1)S(1)}, u32[]{:S(2)}, u32[]{:S(2)}) %collective-permute-start.11) | collective-permute-done | bytes 262176 | tf_op jit(solution)/shard_map/ppermute | solution.py:423
  48.2 1.6 %collective-permute-start.17 = (bf16[512,256]{1,0:T(8,128)(2,1)S(1)}, bf16[512,256]{1,0:T(8,128)(2,1)S(1)}, u32[]{:S(2)}, u32[]{:S(2)}) collective-permute-start(bf16[512,256]{1,0:T(8,128)(2,1)S(1)} %add_convert_fusion.2), channel_id=1, source_target_pairs={{0,16},{8,24},{16,0},{24,8},{1,17},{9,25},{17,1},{25,9},{2,18},{10... | collective-permute-start | bytes 786440 | tf_op jit(solution)/shard_map/ppermute | solution.py:372
  49.9 1.4 %collective-permute-start.18 = (bf16[512,384]{1,0:T(8,128)(2,1)S(1)}, bf16[512,384]{1,0:T(8,128)(2,1)S(1)}, u32[]{:S(2)}, u32[]{:S(2)}) collective-permute-start(bf16[512,384]{1,0:T(8,128)(2,1)S(1)} %add_convert_fusion.1), channel_id=1, source_target_pairs={{0,16},{8,24},{16,0},{24,8},{1,17},{9,25},{17,1},{25,9},{2,18},{10... | collective-permute-start | bytes 1179656 | tf_op jit(solution)/shard_map/ppermute | solution.py:372
  51.4 0.8 %shard_map.83.grad_ref = f32[1024,512]{1,0:T(8,128)S(1)} custom-call(bf16[64,2048]{1,0:T(8,128)(2,1)S(1)} %collective-permute-done.9.up_ref, bf16[64,2048]{1,0:T(8,128)(2,1)S(1)} %collective-permute-done.11.down_ref, f32[1,2048]{1,0:T(1,128)S(1)} %copy-done.2, bf16[512,2048]{1,0:T(8,128)(2,1)S(1)} %copy-done, ...), custom_call_target="tpu_custom_call", output_to_operand_aliasing={{}: (4, {})} | custom-call | flops 1 | bytes 1 | tf_op jit(solution)/shard_map/pallas_call | solution.py:244
  52.2 6.5 %shard_map.84 = (bf16[2,8,128,512]{3,2,1,0:T(8,128)(2,1)S(1)}, f32[3,3,2,512]{3,2,1,0:T(2,128)S(1)}) custom-call(f32[1024,512]{1,0:T(8,128)S(1)} %shard_map.83.grad_ref, bf16[8,128,512]{2,1,0:T(8,128)(2,1)S(1)} %get-tuple-element.205.gate_ref, bf16[8,128,512]{2,1,0:T(8,128)(2,1)S(1)} %get-tuple-element.206.value_ref, bf16[2,8,128,512]{3,2,1,0:T(8,128)(2,1)S(1)} %bitcast.18, ...), custom_call_target="tpu_custom_call" | custom-call | flops 1 | bytes 1 | tf_op jit(solution)/shard_map/pallas_call | solution.py:301
  58.8 3.5 %copy.20 = bf16[2,8,128,512]{3,0,2,1:T(2,128)(2,1)} copy(bf16[2,8,128,512]{3,2,1,0:T(8,128)(2,1)S(1)} %get-tuple-element.210) | data formatting | bytes 4194304 | tf_op jit(solution)/shard_map/optimization_barrier | solution.py:366
  63.0 2.3 %collective-permute-done.18 = bf16[512,384]{1,0:T(8,128)(2,1)S(1)} collective-permute-done((bf16[512,384]{1,0:T(8,128)(2,1)S(1)}, bf16[512,384]{1,0:T(8,128)(2,1)S(1)}, u32[]{:S(2)}, u32[]{:S(2)}) %collective-permute-start.18) | collective-permute-done | bytes 393248 | tf_op jit(solution)/shard_map/ppermute | solution.py:372
  66.1 1.2 %collective-permute-done.19 = f32[3,3,2,512]{3,2,1,0:T(2,128)S(1)} collective-permute-done((f32[3,3,2,512]{3,2,1,0:T(2,128)S(1)}, f32[3,3,2,512]{3,2,1,0:T(2,128)S(1)}, u32[]{:S(2)}, u32[]{:S(2)}) %collective-permute-start.19) | collective-permute-done | bytes 36896 | tf_op jit(solution)/shard_map/ppermute | solution.py:372
  67.3 2.2 %collective-permute-start.20 = (bf16[3,3,2,512]{3,2,1,0:T(2,128)(2,1)S(1)}, bf16[3,3,2,512]{3,2,1,0:T(2,128)(2,1)S(1)}, u32[]{:S(2)}, u32[]{:S(2)}) collective-permute-start(bf16[3,3,2,512]{3,2,1,0:T(2,128)(2,1)S(1)} %add_convert_fusion.3), channel_id=1, source_target_pairs={{0,16},{8,24},{16,0},{24,8},{1,17},{9,25},{17,1},{25,9},{2,18},{10... | collective-permute-start | bytes 55304 | tf_op jit(solution)/shard_map/ppermute | solution.py:372
  69.5 4.3 %collective-permute-done.21 = bf16[512,384]{1,0:T(8,128)(2,1)S(1)} collective-permute-done((bf16[512,384]{1,0:T(8,128)(2,1)S(1)}, bf16[512,384]{1,0:T(8,128)(2,1)S(1)}, u32[]{:S(2)}, u32[]{:S(2)}) %collective-permute-start.21) | collective-permute-done | bytes 393248 | tf_op jit(solution)/shard_map/ppermute | solution.py:372
  74.2 1.4 %shard_map.85 = (bf16[512,2048]{1,0:T(8,128)(2,1)}, f32[3,3,2,512]{3,2,1,0:T(2,128)}) custom-call(bf16[512,256]{1,0:T(8,128)(2,1)S(1)} %multiply_convert_fusion.2.refs_0_, bf16[512,384]{1,0:T(8,128)(2,1)S(1)} %multiply_convert_fusion.1.refs_1_, bf16[512,384]{1,0:T(8,128)(2,1)S(1)} %multiply_convert_fusion.refs_2_, ...), custom_call_target="tpu_custom_call" | custom-call | flops 1 | bytes 1 | tf_op jit(solution)/shard_map/pallas_call | solution.py:345
  75.9 0.8 %constant_dynamic-update-slice_fusion = bf16[512,2048]{1,0:T(8,128)(2,1)} fusion(bf16[512,2048]{1,0:T(8,128)(2,1)} %get-tuple-element.242, bf16[512,384]{1,0:T(8,128)(2,1)S(1)} %collective-permute-done.24, s32[]{:T(128)S(6)} %select_n.3), kind=kLoop, calls=%fused_computation.12 | loop fusion | bytes 786436 | tf_op jit(solution)/shard_map/dynamic_update_slice | solution.py:494
  (49 shorter events, 6.3 us)
Async XLA Ops:
  1.7 11.0 %collective-permute-start = (bf16[64,2048]{1,0:T(8,128)(2,1)S(1)}, bf16[64,2048]{1,0:T(8,128)(2,1)S(1)}, u32[]{:S(2)}, u32[]{:S(2)}) collective-permute-start(bf16[64,2048]{1,0:T(8,128)(2,1)S(1)} %get-tuple-element.246), channel_id=1, source_target_pairs={{0,2},{2,4},{4,6},{6,7},{7,5},{5,3},{3,1},{1,0},{8,10},{10,12},{12... | collective-permute-start | bytes 786440 | tf_op jit(solution)/shard_map/ppermute | solution.py:423
  4.8 10.0 %collective-permute-start.3 = (bf16[64,2048]{1,0:T(8,128)(2,1)S(1)}, bf16[64,2048]{1,0:T(8,128)(2,1)S(1)}, u32[]{:S(2)}, u32[]{:S(2)}) collective-permute-start(bf16[64,2048]{1,0:T(8,128)(2,1)S(1)} %get-tuple-element.245), channel_id=1, source_target_pairs={{0,1},{2,0},{4,2},{6,4},{7,6},{5,7},{3,5},{1,3},{8,9},{10,8},{12,1... | collective-permute-start | bytes 786440 | tf_op jit(solution)/shard_map/ppermute | solution.py:423
  4.8 13.1 %collective-permute-start.2 = (bf16[64,2048]{1,0:T(8,128)(2,1)S(1)}, bf16[64,2048]{1,0:T(8,128)(2,1)S(1)}, u32[]{:S(2)}, u32[]{:S(2)}) collective-permute-start(bf16[64,2048]{1,0:T(8,128)(2,1)S(1)} %get-tuple-element.245), channel_id=1, source_target_pairs={{0,2},{2,4},{4,6},{6,7},{7,5},{5,3},{3,1},{1,0},{8,10},{10,12},{12... | collective-permute-start | bytes 786440 | tf_op jit(solution)/shard_map/ppermute | solution.py:423
  6.8 12.8 %collective-permute-start.4 = (bf16[64,2048]{1,0:T(8,128)(2,1)S(1)}, bf16[64,2048]{1,0:T(8,128)(2,1)S(1)}, u32[]{:S(2)}, u32[]{:S(2)}) collective-permute-start(bf16[64,2048]{1,0:T(8,128)(2,1)S(1)} %get-tuple-element.246), channel_id=1, source_target_pairs={{0,1},{2,0},{4,2},{6,4},{7,6},{5,7},{3,5},{1,3},{8,9},{10,8},{12,1... | collective-permute-start | bytes 786440 | tf_op jit(solution)/shard_map/ppermute | solution.py:423
  12.7 9.0 %copy-start = (bf16[512,2048]{1,0:T(8,128)(2,1)S(1)}, bf16[512,2048]{1,0:T(8,128)(2,1)}, u32[]{:S(2)}) copy-start(bf16[512,2048]{1,0:T(8,128)(2,1)} %weight_ref.1) | copy-start | bytes 6291460
  12.7 9.0 %copy-start.1 = (bf16[1,1,128,2048]{3,2,1,0:T(8,128)(2,1)S(1)}, bf16[1,1,128,2048]{3,2,1,0:T(8,128)(2,1)}, u32[]{:S(2)}) copy-start(bf16[1,1,128,2048]{3,2,1,0:T(8,128)(2,1)} %param.8) | copy-start | bytes 1572868
  12.7 8.9 %copy-start.2 = (f32[1,2048]{1,0:T(1,128)S(1)}, f32[1,2048]{1,0:T(1,128)}, u32[]{:S(2)}) copy-start(f32[1,2048]{1,0:T(1,128)} %gate_ref.5) | copy-start | bytes 24580
  12.7 11.1 %collective-permute-start.1 = (bf16[64,2048]{1,0:T(8,128)(2,1)S(1)}, bf16[64,2048]{1,0:T(8,128)(2,1)S(1)}, u32[]{:S(2)}, u32[]{:S(2)}) collective-permute-start(bf16[64,2048]{1,0:T(8,128)(2,1)S(1)} %collective-permute-done.refs_1_), channel_id=1, source_target_pairs={{0,2},{2,4},{4,6},{6,7},{7,5},{5,3},{3,1},{1,0},{8,10},{10,12},{12... | collective-permute-start | bytes 786440 | tf_op jit(solution)/shard_map/ppermute | solution.py:423
  14.8 10.6 %collective-permute-start.7 = (bf16[64,2048]{1,0:T(8,128)(2,1)S(1)}, bf16[64,2048]{1,0:T(8,128)(2,1)S(1)}, u32[]{:S(2)}, u32[]{:S(2)}) collective-permute-start(bf16[64,2048]{1,0:T(8,128)(2,1)S(1)} %collective-permute-done.3.refs_4_), channel_id=1, source_target_pairs={{0,1},{2,0},{4,2},{6,4},{7,6},{5,7},{3,5},{1,3},{8,9},{10,8},{12,1... | collective-permute-start | bytes 786440 | tf_op jit(solution)/shard_map/ppermute | solution.py:423
  19.6 11.2 %collective-permute-start.8 = (bf16[64,2048]{1,0:T(8,128)(2,1)S(1)}, bf16[64,2048]{1,0:T(8,128)(2,1)S(1)}, u32[]{:S(2)}, u32[]{:S(2)}) collective-permute-start(bf16[64,2048]{1,0:T(8,128)(2,1)S(1)} %collective-permute-done.4.refs_3_), channel_id=1, source_target_pairs={{0,1},{2,0},{4,2},{6,4},{7,6},{5,7},{3,5},{1,3},{8,9},{10,8},{12,1... | collective-permute-start | bytes 786440 | tf_op jit(solution)/shard_map/ppermute | solution.py:423
  19.9 9.2 %collective-permute-start.6 = (bf16[64,2048]{1,0:T(8,128)(2,1)S(1)}, bf16[64,2048]{1,0:T(8,128)(2,1)S(1)}, u32[]{:S(2)}, u32[]{:S(2)}) collective-permute-start(bf16[64,2048]{1,0:T(8,128)(2,1)S(1)} %collective-permute-done.2.refs_2_), channel_id=1, source_target_pairs={{0,2},{2,4},{4,6},{6,7},{7,5},{5,3},{3,1},{1,0},{8,10},{10,12},{12... | collective-permute-start | bytes 786440 | tf_op jit(solution)/shard_map/ppermute | solution.py:423
  23.8 11.0 %collective-permute-start.5 = (bf16[64,2048]{1,0:T(8,128)(2,1)S(1)}, bf16[64,2048]{1,0:T(8,128)(2,1)S(1)}, u32[]{:S(2)}, u32[]{:S(2)}) collective-permute-start(bf16[64,2048]{1,0:T(8,128)(2,1)S(1)} %collective-permute-done.1.refs_0_), channel_id=1, source_target_pairs={{0,2},{2,4},{4,6},{6,7},{7,5},{5,3},{3,1},{1,0},{8,10},{10,12},{12... | collective-permute-start | bytes 786440 | tf_op jit(solution)/shard_map/ppermute | solution.py:423
  25.4 11.0 %collective-permute-start.10 = (bf16[64,2048]{1,0:T(8,128)(2,1)S(1)}, bf16[64,2048]{1,0:T(8,128)(2,1)S(1)}, u32[]{:S(2)}, u32[]{:S(2)}) collective-permute-start(bf16[64,2048]{1,0:T(8,128)(2,1)S(1)} %collective-permute-done.7.refs_3_), channel_id=1, source_target_pairs={{0,1},{2,0},{4,2},{6,4},{7,6},{5,7},{3,5},{1,3},{8,9},{10,8},{12,1... | collective-permute-start | bytes 786440 | tf_op jit(solution)/shard_map/ppermute | solution.py:423
  30.9 11.2 %collective-permute-start.13 = (bf16[64,2048]{1,0:T(8,128)(2,1)S(1)}, bf16[64,2048]{1,0:T(8,128)(2,1)S(1)}, u32[]{:S(2)}, u32[]{:S(2)}) collective-permute-start(bf16[64,2048]{1,0:T(8,128)(2,1)S(1)} %collective-permute-done.8.refs_2_), channel_id=1, source_target_pairs={{0,1},{2,0},{4,2},{6,4},{7,6},{5,7},{3,5},{1,3},{8,9},{10,8},{12,1... | collective-permute-start | bytes 786440 | tf_op jit(solution)/shard_map/ppermute | solution.py:423
  30.9 9.5 %collective-permute-start.12 = (bf16[64,2048]{1,0:T(8,128)(2,1)S(1)}, bf16[64,2048]{1,0:T(8,128)(2,1)S(1)}, u32[]{:S(2)}, u32[]{:S(2)}) collective-permute-start(bf16[64,2048]{1,0:T(8,128)(2,1)S(1)} %collective-permute-done.6.refs_1_), channel_id=1, source_target_pairs={{0,2},{2,4},{4,6},{6,7},{7,5},{5,3},{3,1},{1,0},{8,10},{10,12},{12... | collective-permute-start | bytes 786440 | tf_op jit(solution)/shard_map/ppermute | solution.py:423
  36.5 9.8 %collective-permute-start.11 = (bf16[64,2048]{1,0:T(8,128)(2,1)S(1)}, bf16[64,2048]{1,0:T(8,128)(2,1)S(1)}, u32[]{:S(2)}, u32[]{:S(2)}) collective-permute-start(bf16[64,2048]{1,0:T(8,128)(2,1)S(1)} %collective-permute-done.10.refs_3_), channel_id=1, source_target_pairs={{0,1},{2,0},{4,2},{6,4},{7,6},{5,7},{3,5},{1,3},{8,9},{10,8},{12,1... | collective-permute-start | bytes 786440 | tf_op jit(solution)/shard_map/ppermute | solution.py:423
  36.5 9.8 %collective-permute-start.9 = (bf16[64,2048]{1,0:T(8,128)(2,1)S(1)}, bf16[64,2048]{1,0:T(8,128)(2,1)S(1)}, u32[]{:S(2)}, u32[]{:S(2)}) collective-permute-start(bf16[64,2048]{1,0:T(8,128)(2,1)S(1)} %collective-permute-done.5.refs_0_), channel_id=1, source_target_pairs={{0,2},{2,4},{4,6},{6,7},{7,5},{5,3},{3,1},{1,0},{8,10},{10,12},{12... | collective-permute-start | bytes 786440 | tf_op jit(solution)/shard_map/ppermute | solution.py:423
  46.6 1.6 %collective-permute-start.16 = (bf16[512,256]{1,0:T(8,128)(2,1)S(1)}, bf16[512,256]{1,0:T(8,128)(2,1)S(1)}, u32[]{:S(2)}, u32[]{:S(2)}) collective-permute-start(bf16[512,256]{1,0:T(8,128)(2,1)S(1)} %get-tuple-element.193), channel_id=1, source_target_pairs={{0,8},{8,0},{16,24},{24,16},{1,9},{9,1},{17,25},{25,17},{2,10},{10... | collective-permute-start | bytes 786440 | tf_op jit(solution)/shard_map/ppermute | solution.py:372
  47.3 2.5 %collective-permute-start.15 = (bf16[512,384]{1,0:T(8,128)(2,1)S(1)}, bf16[512,384]{1,0:T(8,128)(2,1)S(1)}, u32[]{:S(2)}, u32[]{:S(2)}) collective-permute-start(bf16[512,384]{1,0:T(8,128)(2,1)S(1)} %get-tuple-element.191), channel_id=1, source_target_pairs={{0,8},{8,0},{16,24},{24,16},{1,9},{9,1},{17,25},{25,17},{2,10},{10... | collective-permute-start | bytes 1179656 | tf_op jit(solution)/shard_map/ppermute | solution.py:372
  47.9 2.0 %collective-permute-start.14 = (bf16[512,384]{1,0:T(8,128)(2,1)S(1)}, bf16[512,384]{1,0:T(8,128)(2,1)S(1)}, u32[]{:S(2)}, u32[]{:S(2)}) collective-permute-start(bf16[512,384]{1,0:T(8,128)(2,1)S(1)} %get-tuple-element.189), channel_id=1, source_target_pairs={{0,8},{8,0},{16,24},{24,16},{1,9},{9,1},{17,25},{25,17},{2,10},{10... | collective-permute-start | bytes 1179656 | tf_op jit(solution)/shard_map/ppermute | solution.py:372
  48.2 14.7 %collective-permute-start.17 = (bf16[512,256]{1,0:T(8,128)(2,1)S(1)}, bf16[512,256]{1,0:T(8,128)(2,1)S(1)}, u32[]{:S(2)}, u32[]{:S(2)}) collective-permute-start(bf16[512,256]{1,0:T(8,128)(2,1)S(1)} %add_convert_fusion.2), channel_id=1, source_target_pairs={{0,16},{8,24},{16,0},{24,8},{1,17},{9,25},{17,1},{25,9},{2,18},{10... | collective-permute-start | bytes 786440 | tf_op jit(solution)/shard_map/ppermute | solution.py:372
  49.9 15.4 %collective-permute-start.18 = (bf16[512,384]{1,0:T(8,128)(2,1)S(1)}, bf16[512,384]{1,0:T(8,128)(2,1)S(1)}, u32[]{:S(2)}, u32[]{:S(2)}) collective-permute-start(bf16[512,384]{1,0:T(8,128)(2,1)S(1)} %add_convert_fusion.1), channel_id=1, source_target_pairs={{0,16},{8,24},{16,0},{24,8},{1,17},{9,25},{17,1},{25,9},{2,18},{10... | collective-permute-start | bytes 1179656 | tf_op jit(solution)/shard_map/ppermute | solution.py:372
  62.3 11.5 %collective-permute-start.21 = (bf16[512,384]{1,0:T(8,128)(2,1)S(1)}, bf16[512,384]{1,0:T(8,128)(2,1)S(1)}, u32[]{:S(2)}, u32[]{:S(2)}) collective-permute-start(bf16[512,384]{1,0:T(8,128)(2,1)S(1)} %add_convert_fusion), channel_id=1, source_target_pairs={{0,16},{8,24},{16,0},{24,8},{1,17},{9,25},{17,1},{25,9},{2,18},{10... | collective-permute-start | bytes 1179656 | tf_op jit(solution)/shard_map/ppermute | solution.py:372
  65.4 8.5 %collective-permute-start.22 = (bf16[512,384]{1,0:T(8,128)(2,1)S(1)}, bf16[512,384]{1,0:T(8,128)(2,1)S(1)}, u32[]{:S(2)}, u32[]{:S(2)}) collective-permute-start(bf16[512,384]{1,0:T(8,128)(2,1)S(1)} %multiply_convert_fusion.1.refs_1_), channel_id=1, source_target_pairs={{0,8},{8,0},{16,24},{24,16},{1,9},{9,1},{17,25},{25,17},{2,10},{10... | collective-permute-start | bytes 1179656 | tf_op jit(solution)/shard_map/ppermute | solution.py:372
  65.5 1.8 %collective-permute-start.19 = (f32[3,3,2,512]{3,2,1,0:T(2,128)S(1)}, f32[3,3,2,512]{3,2,1,0:T(2,128)S(1)}, u32[]{:S(2)}, u32[]{:S(2)}) collective-permute-start(f32[3,3,2,512]{3,2,1,0:T(2,128)S(1)} %get-tuple-element.224), channel_id=1, source_target_pairs={{0,8},{8,0},{16,24},{24,16},{1,9},{9,1},{17,25},{25,17},{2,10},{10... | collective-permute-start | bytes 110600 | tf_op jit(solution)/shard_map/ppermute | solution.py:372
  66.0 8.0 %collective-permute-start.23 = (bf16[512,256]{1,0:T(8,128)(2,1)S(1)}, bf16[512,256]{1,0:T(8,128)(2,1)S(1)}, u32[]{:S(2)}, u32[]{:S(2)}) collective-permute-start(bf16[512,256]{1,0:T(8,128)(2,1)S(1)} %multiply_convert_fusion.2.refs_0_), channel_id=1, source_target_pairs={{0,8},{8,0},{16,24},{24,16},{1,9},{9,1},{17,25},{25,17},{2,10},{10... | collective-permute-start | bytes 786440 | tf_op jit(solution)/shard_map/ppermute | solution.py:372
  67.3 6.7 %collective-permute-start.20 = (bf16[3,3,2,512]{3,2,1,0:T(2,128)(2,1)S(1)}, bf16[3,3,2,512]{3,2,1,0:T(2,128)(2,1)S(1)}, u32[]{:S(2)}, u32[]{:S(2)}) collective-permute-start(bf16[3,3,2,512]{3,2,1,0:T(2,128)(2,1)S(1)} %add_convert_fusion.3), channel_id=1, source_target_pairs={{0,16},{8,24},{16,0},{24,8},{1,17},{9,25},{17,1},{25,9},{2,18},{10... | collective-permute-start | bytes 55304 | tf_op jit(solution)/shard_map/ppermute | solution.py:372
  74.1 1.8 %collective-permute-start.24 = (bf16[512,384]{1,0:T(8,128)(2,1)S(1)}, bf16[512,384]{1,0:T(8,128)(2,1)S(1)}, u32[]{:S(2)}, u32[]{:S(2)}) collective-permute-start(bf16[512,384]{1,0:T(8,128)(2,1)S(1)} %multiply_convert_fusion.refs_2_), channel_id=1, source_target_pairs={{0,8},{8,0},{16,24},{24,16},{1,9},{9,1},{17,25},{25,17},{2,10},{10... | collective-permute-start | bytes 1179656 | tf_op jit(solution)/shard_map/ppermute | solution.py:372
